TPU v7x, 128 devices: a whole 4x4x4 slice. The times are simulated.
128 devices in a mesh: tm: 32 (over x, y, core), row: 4 (over z).
Axes of the slice: x: 4, y: 4, z: 4, core: 2. Of those that a mesh axis runs over, the one named last changes fastest.
Arguments:
- prior: float32 [256], replicated, may hold values from -6 to 6
- dynamics: float32 [2048, 256, 256], P('tm', 'row'), as said below
- gains: float32 [2048, 256, 256], P('tm', 'row'), may hold values from -0.0048828125 to 0.0048828125
- observed: float32 [131072, 256], P('tm', 'row'), may hold values from -6 to 6
- owner: int32 [131072, 1], P('tm'), may hold values from 0 to 31; in each aligned block of 4096 rows (0 to 4095, 4096 to 8191, ...) at most 512 rows name the same one
- step: int32 [131072], P('tm'), may hold values from 0 to 63
Outputs:
- states: float32 [2048, 256], P('tm', 'row')
Inputs may be any that keep to these rules, and one draw needn't show every extreme that they name: Among the rows of one index of tm, no owner is named more than 512 times, a bound that some block reaches. Each dynamics[k] is a diagonal plus a dense part of small independent entries.
All inputs are finite; a program needn't handle non-finite values.
Results may differ from a plain program's by a relative error of at most 0.0003.
Values sent between devices are 32-bit elements; how exact they have to be, the bound alone decides.
No kernel may reach another device: no remote copies, remote signals or barrier semaphores. Data moves between devices by JAX's collectives and lax.ppermute only.
A program may use at most 128 MiB of HBM per device.

v0:
```python
import jax
import jax.numpy as jnp
from jax import lax
from jax.sharding import PartitionSpec as P

HIGH = lax.Precision.HIGHEST


def passed_along(block, axis, distance):
    devices = range(lax.axis_size(axis))
    route = [(i - distance, i) for i in devices if i - distance in devices]
    return lax.ppermute(block, axis, route)


def product(left, right):
    return jnp.dot(left, right, precision=HIGH, preferred_element_type=jnp.float32)


def shards(prior, dynamics, gains, observed, owner, step):
    steps_dev = dynamics.shape[0]
    rows_dev = dynamics.shape[1]
    width = dynamics.shape[2]
    time_devs = lax.axis_size("tm")
    obs_rows = observed.shape[0]
    capacity = 4 * obs_rows // time_devs
    target_state = owner[:, 0]
    owner_onehot = (
        target_state[:, None] == jnp.arange(time_devs, dtype=jnp.int32)[None, :]
    ).astype(jnp.int32)
    ranking = jnp.sum((jnp.cumsum(owner_onehot, axis=0) - 1) * owner_onehot, axis=1)
    slot_index = target_state * capacity + ranking
    send_rows = (
        jnp.zeros((time_devs * capacity, observed.shape[1]), jnp.float32)
        .at[slot_index]
        .set(observed)
    )
    send_tags = (
        jnp.full((time_devs * capacity,), -1.0, jnp.float32)
        .at[slot_index]
        .set(step.astype(jnp.float32))
    )
    recv_rows, recv_tags = (
        lax.all_to_all(send_rows, "tm", split_axis=0, concat_axis=0, tiled=True),
        lax.all_to_all(send_tags, "tm", split_axis=0, concat_axis=0, tiled=True),
    )
    select = (recv_tags[None, :] == jnp.arange(steps_dev, dtype=jnp.float32)[:, None]).astype(
        jnp.float32
    )
    local_sums = product(select, recv_rows)
    full_sums = lax.all_gather(local_sums, "row", axis=1, tiled=True)
    offset_vectors = jnp.einsum("kij,kj->ki", gains, full_sums, precision=HIGH)
    row_index = lax.axis_index("row")

    def compose_step(carry, element):
        cols_map, shift_vec = carry
        matrix, offset = element
        return ((product(matrix, cols_map), product(matrix, shift_vec) + offset), None)

    def filter_step(state, element):
        matrix, offset = element
        fresh = product(matrix, state) + offset
        return (fresh, fresh)

    whole_dyn, whole_off = (
        lax.all_gather(dynamics, "row", axis=1, tiled=True),
        lax.all_gather(offset_vectors, "row", axis=1, tiled=True),
    )
    wanted = row_index * rows_dev + jnp.arange(rows_dev, dtype=jnp.int32)
    identity_cols = (jnp.arange(width, dtype=jnp.int32)[:, None] == wanted[None, :]).astype(
        jnp.float32
    )
    (cols_map, block_shift), _ = lax.scan(
        compose_step, (identity_cols, jnp.zeros((width,), jnp.float32)), (whole_dyn, whole_off)
    )
    block_map = lax.all_gather(cols_map, "row", axis=1, tiled=True)
    time_index = lax.axis_index("tm")

    def passing_round(turn, incoming):
        departing_messages = product(block_map, incoming) + block_shift
        moved = passed_along(departing_messages, "tm", 1)
        return jnp.where(time_index == 0, prior, moved)

    incoming = lax.fori_loop(0, time_devs - 1, passing_round, prior)
    _, swept = lax.scan(filter_step, incoming, (whole_dyn, whole_off))
    states = lax.dynamic_slice_in_dim(swept, row_index * rows_dev, rows_dev, 1)
    return states


def solution(mesh):
    return jax.shard_map(
        shards,
        mesh=mesh,
        in_specs=(
            P(),
            P("tm", "row", None),
            P("tm", "row", None),
            P("tm", "row"),
            P("tm", None),
            P("tm"),
        ),
        out_specs=P("tm", "row"),
        check_vma=False,
    )
```

profile of v0, /device:TPU:6, one launch (start us, length us, event | category | flops | bytes accessed | tf_op | source)
XLA Modules:
  0.0 673.5 jit_solution(12060424392617440511)
XLA Ops:
  7.3 9.2 %reduce-window.6 = s32[32,32,128]{2,1,0:T(8,128)S(1)} reduce-window(s32[32,32,128]{2,1,0:T(8,128)S(1)} %fusion.18, s32[]{:T(128)} %constant.52.clone.1), window={size=1x1x128 pad=0_0x0_0x127_0}, to_apply=%region_0.0 | reduce-window | flops 16646144 | bytes 1048580 | tf_op jit(solution)/shard_map/reduce-window
  20.0 14.4 %scatter_custom_fusion.1 = f32[16384,64]{1,0:T(8,128)} fusion(s32[4096]{0:T(1024)S(1)} %bitcast.99, f32[4096,64]{1,0:T(8,128)S(1)} %copy.18, f32[]{:T(128)} %constant.55.clone.1), kind=kCustom, calls=%fused_computation.19 | custom fusion | bytes 4194308 | tf_op jit(solution)/shard_map/scatter | solution.py:35
  34.3 6.8 %copy.19 = f32[32,512,64]{1,2,0:T(8,128)} copy(f32[32,512,64]{2,1,0:T(8,128)} %bitcast.82) | data formatting | bytes 8388608 | tf_op jit(solution)/shard_map/all_to_all | solution.py:43
  41.1 7.8 %all-to-all-start.1 = ((f32[32,512,64]{1,2,0:T(8,128)}), f32[32,512,64]{1,2,0:T(8,128)}, u32[]{:S(2)}, u32[]{:S(2)}) async-start(f32[32,512,64]{1,2,0:T(8,128)} %copy.19), calls=%async_computation.1 | async-start | bytes 8388608 | tf_op jit(solution)/shard_map/all_to_all | solution.py:43
  48.9 16.1 %scatter_custom_fusion = f32[16384]{0:T(1024)} fusion(s32[4096]{0:T(1024)S(1)} %bitcast.100, f32[4096]{0:T(1024)S(1)} %convert_element_type.14, f32[]{:T(128)} %constant.56.clone.1), kind=kCustom, calls=%fused_computation.35 | custom fusion | bytes 65540 | tf_op jit(solution)/shard_map/scatter | solution.py:40
  65.0 35.0 %all-to-all-done.1 = f32[32,512,64]{1,2,0:T(8,128)} async-done(((f32[32,512,64]{1,2,0:T(8,128)}), f32[32,512,64]{1,2,0:T(8,128)}, u32[]{:S(2)}, u32[]{:S(2)}) %all-to-all-start.1) | async-done | bytes 4194336 | tf_op jit(solution)/shard_map/all_to_all | solution.py:43
  100.1 8.2 %all-to-all-start = ((f32[32,512,1]{1,2,0:T(1,128)}), f32[32,512,1]{1,2,0:T(1,128)S(1)}, u32[]{:S(2)}, u32[]{:S(2)}) async-start(f32[32,512,1]{1,2,0:T(1,128)} %bitcast.13), calls=%async_computation | async-start | bytes 131072 | tf_op jit(solution)/shard_map/all_to_all | solution.py:44
  118.6 13.6 %all_gather.13 = f32[64,256]{0,1:T(8,128)S(1)} all-gather(f32[64,64]{0,1:T(8,128)S(1)} %fusion.14), channel_id=1, replica_groups=mesh['tm'=32,'row'=4] {'row'}, dimensions={1}, use_global_device_ids=true | all-gather | bytes 81920 | tf_op jit(solution)/shard_map/all_gather | solution.py:50
  135.1 12.4 %all_gather.14 = f32[64,256]{0,1:T(8,128)S(1)} all-gather(f32[64,64]{0,1:T(8,128)S(1)} %copy.30), channel_id=1, replica_groups=mesh['tm'=32,'row'=4] {'row'}, dimensions={1}, use_global_device_ids=true | all-gather | bytes 81920 | tf_op jit(solution)/shard_map/all_gather | solution.py:66
  147.7 19.9 %all-gather.2.cloned.1.call-done = f32[64,256,256]{2,1,0:T(8,128)} async-done(((f32[64,64,256]{2,1,0:T(8,128)}), f32[64,256,256]{2,1,0:T(8,128)}) %all-gather.2.cloned.1.call-update) | async-done | bytes 16777232 | tf_op jit(solution)/shard_map/all_gather | solution.py:65
  167.6 171.2 %while.39 = (s32[]{:T(128)}, f32[256,64]{0,1:T(8,128)S(1)}, f32[256]{0:T(256)S(1)}, f32[64,256,256]{2,1,0:T(8,128)}, f32[64,256]{1,0:T(8,128)S(1)}, /*index=5*/s32[]{:T(128)}, s32[]{:T(128)}) while((s32[]{:T(128)}, f32[256,64]{0,1:T(8,128)S(1)}, f32[256]{0:T(256)S(1)}, f32[64,256,256]{2,1,0:T(8,128)}, f32[64,256]{1,0:T(8,128)S(1)}, ...), condition=%wide.region_6.7_spmd.clone, body=%wide.region_5.6_spmd.clone.sunk | while | flops 51118592 | bytes 796763 | solution.py:72
  338.8 12.6 %all_gather.15 = f32[256,256]{0,1:T(8,128)S(1)} all-gather(f32[256,64]{0,1:T(8,128)S(1)} %get-tuple-element.132), channel_id=1, replica_groups=mesh['tm'=32,'row'=4] {'row'}, dimensions={1}, use_global_device_ids=true | all-gather | bytes 327680 | tf_op jit(solution)/shard_map/all_gather | solution.py:75
  351.5 227.1 %while.37 = (s32[]{:T(128)}, f32[256]{0:T(256)S(1)}, pred[]{:T(512)}, f32[256,256]{1,0:T(8,128)S(1)}, f32[256]{0:T(256)S(1)}, /*index=5*/f32[256]{0:T(256)S(1)}, s32[]{:T(128)}) while((s32[]{:T(128)}, f32[256]{0:T(256)S(1)}, pred[]{:T(512)}, f32[256,256]{1,0:T(8,128)S(1)}, f32[256]{0:T(256)S(1)}, /*index=5*/f32[256]{0:T(256)S(1)}, ...), condition=%wide.region_8.9_spmd, body=%wide.region_7.8_spmd.sunk | while | flops 786946 | bytes 274550 | solution.py:83
  353.7 5.1 collective-permute-done
  361.1 5.1 collective-permute-done
  368.4 5.1 collective-permute-done
  375.7 5.1 collective-permute-done
  383.0 5.1 collective-permute-done
  390.4 5.1 collective-permute-done
  397.7 5.1 collective-permute-done
  405.0 5.1 collective-permute-done
  412.4 5.1 collective-permute-done
  419.7 5.1 collective-permute-done
  427.0 5.1 collective-permute-done
  456.3 5.1 collective-permute-done
  463.6 5.1 collective-permute-done
  492.9 5.1 collective-permute-done
  522.2 5.1 collective-permute-done
  529.6 5.1 collective-permute-done
  558.9 5.1 collective-permute-done
  566.2 5.1 collective-permute-done
  578.6 87.4 %while.38 = (s32[]{:T(128)}, f32[256]{0:T(256)S(1)}, f32[64,256]{1,0:T(8,128)S(1)}, f32[64,256,256]{2,1,0:T(8,128)}, f32[64,256]{1,0:T(8,128)S(1)}, /*index=5*/s32[]{:T(128)}, s32[]{:T(128)}) while((s32[]{:T(128)}, f32[256]{0:T(256)S(1)}, f32[64,256]{1,0:T(8,128)S(1)}, f32[64,256,256]{2,1,0:T(8,128)}, f32[64,256]{1,0:T(8,128)S(1)}, ...), condition=%wide.region_10.11_spmd, body=%wide.region_9.10_spmd.sunk | while | flops 786690 | bytes 271957 | solution.py:84
  (807 shorter events, 407.3 us)
Async XLA Ops:
  6.5 161.1 %all-gather.2.cloned.1.call-start = ((), (), s32[]{:S(2)}) async-start(), calls=%async_computation.2 | async-start | bytes 20971520 | tf_op jit(solution)/shard_map/all_gather | solution.py:65
  41.1 58.9 %all-to-all-start.1 = ((f32[32,512,64]{1,2,0:T(8,128)}), f32[32,512,64]{1,2,0:T(8,128)}, u32[]{:S(2)}, u32[]{:S(2)}) async-start(f32[32,512,64]{1,2,0:T(8,128)} %copy.19), calls=%async_computation.1 | async-start | bytes 8388608 | tf_op jit(solution)/shard_map/all_to_all | solution.py:43
  100.1 13.8 %all-to-all-start = ((f32[32,512,1]{1,2,0:T(1,128)}), f32[32,512,1]{1,2,0:T(1,128)S(1)}, u32[]{:S(2)}, u32[]{:S(2)}) async-start(f32[32,512,1]{1,2,0:T(1,128)} %bitcast.13), calls=%async_computation | async-start | bytes 131072 | tf_op jit(solution)/shard_map/all_to_all | solution.py:44
  351.8 7.0 %collective-permute-start = (f32[256]{0:T(256)S(1)}, f32[256]{0:T(256)S(1)}, u32[]{:S(2)}, u32[]{:S(2)}) collective-permute-start(f32[256]{0:T(256)S(1)} %add.67), channel_id=1, source_target_pairs={{0,4},{4,8},{8,12},{12,16},{16,20},{20,24},{24,28},{28,32},{32,36}... | collective-permute-start | bytes 3080 | tf_op jit(solution)/shard_map/while/body/eval_jaxpr/ppermute | solution.py:12
  359.1 7.0 %collective-permute-start = (f32[256]{0:T(256)S(1)}, f32[256]{0:T(256)S(1)}, u32[]{:S(2)}, u32[]{:S(2)}) collective-permute-start(f32[256]{0:T(256)S(1)} %add.67), channel_id=1, source_target_pairs={{0,4},{4,8},{8,12},{12,16},{16,20},{20,24},{24,28},{28,32},{32,36}... | collective-permute-start | bytes 3080 | tf_op jit(solution)/shard_map/while/body/eval_jaxpr/ppermute | solution.py:12
  366.4 7.0 %collective-permute-start = (f32[256]{0:T(256)S(1)}, f32[256]{0:T(256)S(1)}, u32[]{:S(2)}, u32[]{:S(2)}) collective-permute-start(f32[256]{0:T(256)S(1)} %add.67), channel_id=1, source_target_pairs={{0,4},{4,8},{8,12},{12,16},{16,20},{20,24},{24,28},{28,32},{32,36}... | collective-permute-start | bytes 3080 | tf_op jit(solution)/shard_map/while/body/eval_jaxpr/ppermute | solution.py:12
  373.7 7.0 %collective-permute-start = (f32[256]{0:T(256)S(1)}, f32[256]{0:T(256)S(1)}, u32[]{:S(2)}, u32[]{:S(2)}) collective-permute-start(f32[256]{0:T(256)S(1)} %add.67), channel_id=1, source_target_pairs={{0,4},{4,8},{8,12},{12,16},{16,20},{20,24},{24,28},{28,32},{32,36}... | collective-permute-start | bytes 3080 | tf_op jit(solution)/shard_map/while/body/eval_jaxpr/ppermute | solution.py:12
  381.1 7.0 %collective-permute-start = (f32[256]{0:T(256)S(1)}, f32[256]{0:T(256)S(1)}, u32[]{:S(2)}, u32[]{:S(2)}) collective-permute-start(f32[256]{0:T(256)S(1)} %add.67), channel_id=1, source_target_pairs={{0,4},{4,8},{8,12},{12,16},{16,20},{20,24},{24,28},{28,32},{32,36}... | collective-permute-start | bytes 3080 | tf_op jit(solution)/shard_map/while/body/eval_jaxpr/ppermute | solution.py:12
  388.4 7.0 %collective-permute-start = (f32[256]{0:T(256)S(1)}, f32[256]{0:T(256)S(1)}, u32[]{:S(2)}, u32[]{:S(2)}) collective-permute-start(f32[256]{0:T(256)S(1)} %add.67), channel_id=1, source_target_pairs={{0,4},{4,8},{8,12},{12,16},{16,20},{20,24},{24,28},{28,32},{32,36}... | collective-permute-start | bytes 3080 | tf_op jit(solution)/shard_map/while/body/eval_jaxpr/ppermute | solution.py:12
  395.7 7.0 %collective-permute-start = (f32[256]{0:T(256)S(1)}, f32[256]{0:T(256)S(1)}, u32[]{:S(2)}, u32[]{:S(2)}) collective-permute-start(f32[256]{0:T(256)S(1)} %add.67), channel_id=1, source_target_pairs={{0,4},{4,8},{8,12},{12,16},{16,20},{20,24},{24,28},{28,32},{32,36}... | collective-permute-start | bytes 3080 | tf_op jit(solution)/shard_map/while/body/eval_jaxpr/ppermute | solution.py:12
  403.0 7.0 %collective-permute-start = (f32[256]{0:T(256)S(1)}, f32[256]{0:T(256)S(1)}, u32[]{:S(2)}, u32[]{:S(2)}) collective-permute-start(f32[256]{0:T(256)S(1)} %add.67), channel_id=1, source_target_pairs={{0,4},{4,8},{8,12},{12,16},{16,20},{20,24},{24,28},{28,32},{32,36}... | collective-permute-start | bytes 3080 | tf_op jit(solution)/shard_map/while/body/eval_jaxpr/ppermute | solution.py:12
  410.4 7.0 %collective-permute-start = (f32[256]{0:T(256)S(1)}, f32[256]{0:T(256)S(1)}, u32[]{:S(2)}, u32[]{:S(2)}) collective-permute-start(f32[256]{0:T(256)S(1)} %add.67), channel_id=1, source_target_pairs={{0,4},{4,8},{8,12},{12,16},{16,20},{20,24},{24,28},{28,32},{32,36}... | collective-permute-start | bytes 3080 | tf_op jit(solution)/shard_map/while/body/eval_jaxpr/ppermute | solution.py:12
  417.7 7.0 %collective-permute-start = (f32[256]{0:T(256)S(1)}, f32[256]{0:T(256)S(1)}, u32[]{:S(2)}, u32[]{:S(2)}) collective-permute-start(f32[256]{0:T(256)S(1)} %add.67), channel_id=1, source_target_pairs={{0,4},{4,8},{8,12},{12,16},{16,20},{20,24},{24,28},{28,32},{32,36}... | collective-permute-start | bytes 3080 | tf_op jit(solution)/shard_map/while/body/eval_jaxpr/ppermute | solution.py:12
  425.0 7.0 %collective-permute-start = (f32[256]{0:T(256)S(1)}, f32[256]{0:T(256)S(1)}, u32[]{:S(2)}, u32[]{:S(2)}) collective-permute-start(f32[256]{0:T(256)S(1)} %add.67), channel_id=1, source_target_pairs={{0,4},{4,8},{8,12},{12,16},{16,20},{20,24},{24,28},{28,32},{32,36}... | collective-permute-start | bytes 3080 | tf_op jit(solution)/shard_map/while/body/eval_jaxpr/ppermute | solution.py:12
  432.4 7.0 %collective-permute-start = (f32[256]{0:T(256)S(1)}, f32[256]{0:T(256)S(1)}, u32[]{:S(2)}, u32[]{:S(2)}) collective-permute-start(f32[256]{0:T(256)S(1)} %add.67), channel_id=1, source_target_pairs={{0,4},{4,8},{8,12},{12,16},{16,20},{20,24},{24,28},{28,32},{32,36}... | collective-permute-start | bytes 3080 | tf_op jit(solution)/shard_map/while/body/eval_jaxpr/ppermute | solution.py:12
  439.7 7.0 %collective-permute-start = (f32[256]{0:T(256)S(1)}, f32[256]{0:T(256)S(1)}, u32[]{:S(2)}, u32[]{:S(2)}) collective-permute-start(f32[256]{0:T(256)S(1)} %add.67), channel_id=1, source_target_pairs={{0,4},{4,8},{8,12},{12,16},{16,20},{20,24},{24,28},{28,32},{32,36}... | collective-permute-start | bytes 3080 | tf_op jit(solution)/shard_map/while/body/eval_jaxpr/ppermute | solution.py:12
  447.0 7.0 %collective-permute-start = (f32[256]{0:T(256)S(1)}, f32[256]{0:T(256)S(1)}, u32[]{:S(2)}, u32[]{:S(2)}) collective-permute-start(f32[256]{0:T(256)S(1)} %add.67), channel_id=1, source_target_pairs={{0,4},{4,8},{8,12},{12,16},{16,20},{20,24},{24,28},{28,32},{32,36}... | collective-permute-start | bytes 3080 | tf_op jit(solution)/shard_map/while/body/eval_jaxpr/ppermute | solution.py:12
  454.3 7.0 %collective-permute-start = (f32[256]{0:T(256)S(1)}, f32[256]{0:T(256)S(1)}, u32[]{:S(2)}, u32[]{:S(2)}) collective-permute-start(f32[256]{0:T(256)S(1)} %add.67), channel_id=1, source_target_pairs={{0,4},{4,8},{8,12},{12,16},{16,20},{20,24},{24,28},{28,32},{32,36}... | collective-permute-start | bytes 3080 | tf_op jit(solution)/shard_map/while/body/eval_jaxpr/ppermute | solution.py:12
  461.7 7.0 %collective-permute-start = (f32[256]{0:T(256)S(1)}, f32[256]{0:T(256)S(1)}, u32[]{:S(2)}, u32[]{:S(2)}) collective-permute-start(f32[256]{0:T(256)S(1)} %add.67), channel_id=1, source_target_pairs={{0,4},{4,8},{8,12},{12,16},{16,20},{20,24},{24,28},{28,32},{32,36}... | collective-permute-start | bytes 3080 | tf_op jit(solution)/shard_map/while/body/eval_jaxpr/ppermute | solution.py:12
  469.0 7.0 %collective-permute-start = (f32[256]{0:T(256)S(1)}, f32[256]{0:T(256)S(1)}, u32[]{:S(2)}, u32[]{:S(2)}) collective-permute-start(f32[256]{0:T(256)S(1)} %add.67), channel_id=1, source_target_pairs={{0,4},{4,8},{8,12},{12,16},{16,20},{20,24},{24,28},{28,32},{32,36}... | collective-permute-start | bytes 3080 | tf_op jit(solution)/shard_map/while/body/eval_jaxpr/ppermute | solution.py:12
  476.3 7.0 %collective-permute-start = (f32[256]{0:T(256)S(1)}, f32[256]{0:T(256)S(1)}, u32[]{:S(2)}, u32[]{:S(2)}) collective-permute-start(f32[256]{0:T(256)S(1)} %add.67), channel_id=1, source_target_pairs={{0,4},{4,8},{8,12},{12,16},{16,20},{20,24},{24,28},{28,32},{32,36}... | collective-permute-start | bytes 3080 | tf_op jit(solution)/shard_map/while/body/eval_jaxpr/ppermute | solution.py:12
  483.6 7.0 %collective-permute-start = (f32[256]{0:T(256)S(1)}, f32[256]{0:T(256)S(1)}, u32[]{:S(2)}, u32[]{:S(2)}) collective-permute-start(f32[256]{0:T(256)S(1)} %add.67), channel_id=1, source_target_pairs={{0,4},{4,8},{8,12},{12,16},{16,20},{20,24},{24,28},{28,32},{32,36}... | collective-permute-start | bytes 3080 | tf_op jit(solution)/shard_map/while/body/eval_jaxpr/ppermute | solution.py:12
  491.0 7.0 %collective-permute-start = (f32[256]{0:T(256)S(1)}, f32[256]{0:T(256)S(1)}, u32[]{:S(2)}, u32[]{:S(2)}) collective-permute-start(f32[256]{0:T(256)S(1)} %add.67), channel_id=1, source_target_pairs={{0,4},{4,8},{8,12},{12,16},{16,20},{20,24},{24,28},{28,32},{32,36}... | collective-permute-start | bytes 3080 | tf_op jit(solution)/shard_map/while/body/eval_jaxpr/ppermute | solution.py:12
  498.3 7.0 %collective-permute-start = (f32[256]{0:T(256)S(1)}, f32[256]{0:T(256)S(1)}, u32[]{:S(2)}, u32[]{:S(2)}) collective-permute-start(f32[256]{0:T(256)S(1)} %add.67), channel_id=1, source_target_pairs={{0,4},{4,8},{8,12},{12,16},{16,20},{20,24},{24,28},{28,32},{32,36}... | collective-permute-start | bytes 3080 | tf_op jit(solution)/shard_map/while/body/eval_jaxpr/ppermute | solution.py:12
  505.6 7.0 %collective-permute-start = (f32[256]{0:T(256)S(1)}, f32[256]{0:T(256)S(1)}, u32[]{:S(2)}, u32[]{:S(2)}) collective-permute-start(f32[256]{0:T(256)S(1)} %add.67), channel_id=1, source_target_pairs={{0,4},{4,8},{8,12},{12,16},{16,20},{20,24},{24,28},{28,32},{32,36}... | collective-permute-start | bytes 3080 | tf_op jit(solution)/shard_map/while/body/eval_jaxpr/ppermute | solution.py:12
  512.9 7.0 %collective-permute-start = (f32[256]{0:T(256)S(1)}, f32[256]{0:T(256)S(1)}, u32[]{:S(2)}, u32[]{:S(2)}) collective-permute-start(f32[256]{0:T(256)S(1)} %add.67), channel_id=1, source_target_pairs={{0,4},{4,8},{8,12},{12,16},{16,20},{20,24},{24,28},{28,32},{32,36}... | collective-permute-start | bytes 3080 | tf_op jit(solution)/shard_map/while/body/eval_jaxpr/ppermute | solution.py:12
  520.3 7.0 %collective-permute-start = (f32[256]{0:T(256)S(1)}, f32[256]{0:T(256)S(1)}, u32[]{:S(2)}, u32[]{:S(2)}) collective-permute-start(f32[256]{0:T(256)S(1)} %add.67), channel_id=1, source_target_pairs={{0,4},{4,8},{8,12},{12,16},{16,20},{20,24},{24,28},{28,32},{32,36}... | collective-permute-start | bytes 3080 | tf_op jit(solution)/shard_map/while/body/eval_jaxpr/ppermute | solution.py:12
  527.6 7.0 %collective-permute-start = (f32[256]{0:T(256)S(1)}, f32[256]{0:T(256)S(1)}, u32[]{:S(2)}, u32[]{:S(2)}) collective-permute-start(f32[256]{0:T(256)S(1)} %add.67), channel_id=1, source_target_pairs={{0,4},{4,8},{8,12},{12,16},{16,20},{20,24},{24,28},{28,32},{32,36}... | collective-permute-start | bytes 3080 | tf_op jit(solution)/shard_map/while/body/eval_jaxpr/ppermute | solution.py:12
  534.9 7.0 %collective-permute-start = (f32[256]{0:T(256)S(1)}, f32[256]{0:T(256)S(1)}, u32[]{:S(2)}, u32[]{:S(2)}) collective-permute-start(f32[256]{0:T(256)S(1)} %add.67), channel_id=1, source_target_pairs={{0,4},{4,8},{8,12},{12,16},{16,20},{20,24},{24,28},{28,32},{32,36}... | collective-permute-start | bytes 3080 | tf_op jit(solution)/shard_map/while/body/eval_jaxpr/ppermute | solution.py:12
  542.2 7.0 %collective-permute-start = (f32[256]{0:T(256)S(1)}, f32[256]{0:T(256)S(1)}, u32[]{:S(2)}, u32[]{:S(2)}) collective-permute-start(f32[256]{0:T(256)S(1)} %add.67), channel_id=1, source_target_pairs={{0,4},{4,8},{8,12},{12,16},{16,20},{20,24},{24,28},{28,32},{32,36}... | collective-permute-start | bytes 3080 | tf_op jit(solution)/shard_map/while/body/eval_jaxpr/ppermute | solution.py:12
  549.6 7.0 %collective-permute-start = (f32[256]{0:T(256)S(1)}, f32[256]{0:T(256)S(1)}, u32[]{:S(2)}, u32[]{:S(2)}) collective-permute-start(f32[256]{0:T(256)S(1)} %add.67), channel_id=1, source_target_pairs={{0,4},{4,8},{8,12},{12,16},{16,20},{20,24},{24,28},{28,32},{32,36}... | collective-permute-start | bytes 3080 | tf_op jit(solution)/shard_map/while/body/eval_jaxpr/ppermute | solution.py:12
  564.2 7.0 %collective-permute-start = (f32[256]{0:T(256)S(1)}, f32[256]{0:T(256)S(1)}, u32[]{:S(2)}, u32[]{:S(2)}) collective-permute-start(f32[256]{0:T(256)S(1)} %add.67), channel_id=1, source_target_pairs={{0,4},{4,8},{8,12},{12,16},{16,20},{20,24},{24,28},{28,32},{32,36}... | collective-permute-start | bytes 3080 | tf_op jit(solution)/shard_map/while/body/eval_jaxpr/ppermute | solution.py:12
  (5 other events, 89.8 us)
Sparse Core Ops, SparseCore 0:
  9.0 158.5 all-gather.1
where the time goes:
time: 681 us; the launch traced here: 674 us
  matrix products  255 us (37%)
  waiting for transfers between devices  213 us (31%)
  starting transfers between devices  77 us (11%)
  local copies, waits for them, and re-layouts  56.7 us (8%)
  blocking collectives  38.6 us (6%)
  other arithmetic  14.2 us (2%)
  between operations  13.6 us (2%)
    dot_general x224, matrix products, product(): jnp.dot(left, right, precision=HIGH, preferred_element_type=jnp.float32)  255 us
    ppermute x31, waiting for transfers between devices, passed_along(): return lax.ppermute(block, axis, route)  157 us
    ppermute x31, starting transfers between devices, passed_along(): return lax.ppermute(block, axis, route)  61 us
    all_to_all x1, waiting for transfers between devices, shards(): lax.all_to_all(send_rows, 'tm', split_axis=0, concat_axis=0, tiled=True)  35 us
    all_gather x1, waiting for transfers between devices, shards(): lax.all_gather(dynamics, 'row', axis=1, tiled=True)  19.9 us
    scatter x1, local copies, waits for them, and re-layouts, shards(): send_tags = jnp.full((time_devs * capacity,), -1.0, jnp.float32).at[slot_...  16.1 us
    scatter x1, local copies, waits for them, and re-layouts, shards(): send_rows = jnp.zeros((time_devs * capacity, observed.shape[1]), jnp.floa...  14.4 us
  transfers between devices with their start and end apart: 34, of which 34 were waited for; matrix products, arithmetic and copies ran while one was open for 9% of the time, Pallas kernels for 0%

commit v1 on v0

v1 whole, which is shorter than its diff:
```python
import functools

import jax
import jax.numpy as jnp
from jax import lax
from jax.experimental import pallas as pl
from jax.experimental.pallas import tpu as pltpu
from jax.sharding import PartitionSpec as P

F32 = jnp.float32
BF16 = jnp.bfloat16
PARAMS = pltpu.CompilerParams(vmem_limit_bytes=56 * 1024 * 1024)
VM = pl.BlockSpec(memory_space=pltpu.VMEM)
SM = pl.BlockSpec(memory_space=pltpu.SMEM)
N = 256
PAD = 16
R = N + PAD
ROWS = 4
SUB = 16
SEG = 4


def split(x):
    hi = x.astype(BF16)
    return hi, (x - hi.astype(F32)).astype(BF16)


def dot_nn(a, b):
    return lax.dot_general(a, b, (((1,), (0,)), ((), ())), preferred_element_type=F32)


def dot_nt(a, b):
    return lax.dot_general(a, b, (((1,), (1,)), ((), ())), preferred_element_type=F32)


def mm(a, b, dot=dot_nn):
    ah, al = split(a)
    bh, bl = split(b)
    return dot(ah, bh) + dot(al, bh) + dot(ah, bl)


def then(first, second):
    out = mm(first, second[:N])
    return jnp.concatenate([out[:N], out[N:] + second[N:]], axis=0)


def apply(s, m):
    return mm(s, m[:N]) + m[N:]


def eye_map():
    r = lax.broadcasted_iota(jnp.int32, (R, N), 0)
    c = lax.broadcasted_iota(jnp.int32, (R, N), 1)
    return jnp.where(r == c, 1.0, 0.0).astype(F32)


def call(kernel, outs, args, specs=None, scratch=(), **kw):
    return pl.pallas_call(
        kernel,
        out_shape=[jax.ShapeDtypeStruct(s, F32) for s in outs],
        in_specs=specs,
        out_specs=[VM] * len(outs),
        scratch_shapes=list(scratch),
        compiler_params=PARAMS,
        **kw,
    )(*args)


BIN_M = 256


def bin_kernel(rid_ref, obs_ref, out_ref, rhs, acc):
    i = pl.program_id(0)
    n_m = pl.num_programs(0)

    @pl.when(i == 0)
    def _():
        x = obs_ref[...]
        hi = x.astype(BF16)
        rest = x - hi.astype(F32)
        mid = rest.astype(BF16)
        low = (rest - mid.astype(F32)).astype(BF16)
        rhs[...] = jnp.concatenate([hi, mid, low, jnp.zeros_like(hi)], axis=1)

    rows = lax.broadcasted_iota(jnp.int32, (BIN_M, rid_ref.shape[1]), 0) + i * BIN_M
    onehot = jnp.where(rows == rid_ref[...], 1.0, 0.0).astype(BF16)
    got = dot_nn(onehot, rhs[...])
    a = got[:, :128]
    b = got[:, 128:]
    ab = a + b
    acc[pl.ds(pl.multiple_of(i * BIN_M, BIN_M), BIN_M), :] = a + pltpu.roll(a, 64, 1) + b + pltpu.roll(b, 64, 1)

    @pl.when(i == n_m - 1)
    def _():
        half = out_ref.shape[0]
        lane = lax.broadcasted_iota(jnp.int32, (half, 128), 1)
        out_ref[...] = jnp.where(lane < 64, acc[:half, :], acc[half:, :])


def binned(rid, observed):
    n_bins = 2048
    obs_rows, width = observed.shape
    return pl.pallas_call(
        bin_kernel,
        out_shape=jax.ShapeDtypeStruct((n_bins // 2, 128), F32),
        grid=(n_bins // BIN_M,),
        in_specs=[
            pl.BlockSpec((1, obs_rows), lambda i: (0, 0)),
            pl.BlockSpec((obs_rows, width), lambda i: (0, 0)),
        ],
        out_specs=pl.BlockSpec((n_bins // 2, 128), lambda i: (0, 0)),
        scratch_shapes=[pltpu.VMEM((obs_rows, 4 * width), BF16), pltpu.VMEM((n_bins, 128), F32)],
        compiler_params=PARAMS,
    )(rid, observed)


def compose_kernel(z_ref, a0, a1, a2, a3, b0, b1, b2, b3, pref, whole, a_s, b_s):
    z = z_ref[0]
    for d, (a, b) in enumerate(((a0, b0), (a1, b1), (a2, b2), (a3, b3))):
        slot = lax.rem(z - d + ROWS, ROWS)
        a_s[:, pl.ds(pl.multiple_of(slot * 64, 64), 64), :] = a[...]
        b_s[slot] = b[...]
    b = jnp.concatenate([b_s[i] for i in range(ROWS)], axis=1)
    first = lax.broadcasted_iota(jnp.int32, (PAD, N), 0) == 0
    cur = [eye_map()] * (SUB // SEG)
    for t in range(SEG):
        for c in range(SUB // SEG):
            k = c * SEG + t
            out = mm(cur[c], a_s[k], dot_nt)
            pref[k, :N, :] = out[:N]
            pref[k, N:, :] = out[N:] + jnp.where(first, b[k : k + 1, :], 0.0)
            cur[c] = pref[k]
    whole[...] = then(then(cur[0], cur[1]), then(cur[2], cur[3]))


def four_kernel(pos_ref, m0, m1, m2, m3, total, before, m_s):
    pos = pos_ref[0]
    for d, m in enumerate((m0, m1, m2, m3)):
        m_s[lax.rem(pos - d + 4, 4)] = m[...]
    m01 = then(m_s[0], m_s[1])
    m23 = then(m_s[2], m_s[3])
    total[...] = then(m01, m23)
    before[...] = eye_map()

    @pl.when(pos == 1)
    def _():
        before[...] = m_s[0]

    @pl.when(pos == 2)
    def _():
        before[...] = m01

    @pl.when(pos == 3)
    def _():
        before[...] = then(m01, m_s[2])


def pair_kernel(c_ref, own, other, before_in, total, before):
    c = c_ref[0]
    swap = c == 1

    @pl.when(swap)
    def _():
        total[...] = then(other[...], own[...])
        before[...] = then(other[...], before_in[...])

    @pl.when(jnp.logical_not(swap))
    def _():
        total[...] = then(own[...], other[...])
        before[...] = before_in[...]


def top_kernel(pos_ref, prior, m0, m1, m2, m3, ybefore, out, m_s, s_s):
    pos = pos_ref[0]
    for d, m in enumerate((m0, m1, m2, m3)):
        m_s[lax.rem(pos - d + 4, 4)] = m[...]
    r = lax.broadcasted_iota(jnp.int32, (PAD, N), 0)
    s_s[...] = jnp.where(r == 0, prior[...], 0.0)
    for i in range(3):

        @pl.when(i < pos)
        def _(i=i):
            s_s[...] = apply(s_s[...], m_s[i])

    out[...] = apply(s_s[...], ybefore[...])


def states_kernel(idx_ref, mine, other, before, pref, o0, o1, o2, o3, st_s, s_s):
    z = idx_ref[0]
    c = idx_ref[1]
    s_s[...] = jnp.where(c == 0, mine[...], other[...])
    s = apply(s_s[...], before[...])
    eye = lax.broadcasted_iota(jnp.int32, (N, N), 0) == lax.broadcasted_iota(jnp.int32, (N, N), 1)
    for q in range(SUB // SEG):
        col = jnp.sum(jnp.where(eye, s[0:1, :], 0.0), axis=1, keepdims=True)
        for t in range(SEG):
            k = q * SEG + t
            row = jnp.sum(pref[k, :N, :] * col, axis=0, keepdims=True) + pref[k, N : N + 1, :]
            for j in range(ROWS):
                st_s[j, k : k + 1, :] = row[:, j * 64 : (j + 1) * 64]
        if q < SUB // SEG - 1:
            s = apply(s, pref[q * SEG + SEG - 1])
    for d, o in enumerate((o0, o1, o2, o3)):
        o[...] = st_s[lax.rem(z + d, ROWS)]


def place_kernel(z_ref, r0, r1, r2, r3, out):
    z = z_ref[0]
    for d, r in enumerate((r0, r1, r2, r3)):
        slot = lax.rem(z - d + ROWS, ROWS)
        out[pl.ds(pl.multiple_of(slot * SUB, SUB), SUB), :] = r[...]


def along_row(x, d):
    return lax.ppermute(x, "row", [(i, (i + d) % ROWS) for i in range(ROWS)])


def pick(x, i):
    return lax.dynamic_index_in_dim(x, i, 0, keepdims=False)


def shards(prior, dynamics, gains, observed, owner, step):
    tm = lax.axis_index("tm").astype(jnp.int32)
    z = lax.axis_index("row").astype(jnp.int32)
    x, y, c = tm // 8, (tm // 2) % 4, tm % 2
    z1 = z.reshape(1)

    parts = dynamics.reshape(ROWS, SUB, 64, N)
    mats = [pick(parts, z)] + [along_row(pick(parts, (z + d) % ROWS), d) for d in (1, 2, 3)]

    rid = owner[:, 0] * 32 + step % 32 + 1024 * (step // 32)
    partial = binned(rid.reshape(1, -1), observed)
    sums = lax.all_to_all(partial, "tm", 0, 0, tiled=True)
    info = jnp.sum(sums.reshape(32, 32, 128), axis=0)
    infos = [info] + [along_row(info, d) for d in (1, 2, 3)]
    cyc = [infos[3], infos[2], infos[1], infos[0]] * 2
    ordered = lax.dynamic_slice_in_dim(jnp.stack(cyc), 3 - z, ROWS, 0)
    full = ordered.reshape(ROWS, 32, 2, 64).transpose(2, 1, 0, 3).reshape(64, N)
    offset = jnp.sum(gains * full[:, None, :], axis=2)
    off = offset.reshape(ROWS, SUB, 64)
    offs = [pick(off, z)] + [along_row(pick(off, (z + d) % ROWS), d) for d in (1, 2, 3)]

    pref, whole = call(
        compose_kernel,
        [(SUB, R, N), (R, N)],
        (z1, *mats, *offs),
        [SM] + [VM] * 8,
        [pltpu.VMEM((SUB, N, N), F32), pltpu.VMEM((ROWS, SUB, 64), F32)],
    )

    four = functools.partial(
        call, four_kernel, [(R, N), (R, N)], specs=[SM] + [VM] * 4, scratch=[pltpu.VMEM((4, R, N), F32)]
    )
    block, before = four(args=(z1, whole, *[along_row(whole, d) for d in (1, 2, 3)]))
    swapped = lax.ppermute(block, "tm", [(i, i ^ 1) for i in range(32)])
    column, before = call(
        pair_kernel, [(R, N), (R, N)], (c.reshape(1), block, swapped, before), [SM] + [VM] * 3
    )

    def along_y(m, d):
        return lax.ppermute(
            m, "tm", [(8 * i + 2 * j, 8 * i + 2 * ((j + d) % 4)) for i in range(4) for j in range(4)]
        )

    def along_x(m, d):
        return lax.ppermute(
            m, "tm", [(8 * i + 2 * j, 8 * (i + d) + 2 * j) for i in range(4 - d) for j in range(4)]
        )

    plane, ybefore = four(args=(y.reshape(1), column, *[along_y(column, d) for d in (1, 2, 3)]))
    (entry,) = call(
        top_kernel,
        [(PAD, N)],
        (x.reshape(1), prior.reshape(1, N), plane, *[along_x(plane, d) for d in (1, 2, 3)], ybefore),
        [SM] + [VM] * 6,
        [pltpu.VMEM((4, R, N), F32), pltpu.VMEM((PAD, N), F32)],
    )
    handed = lax.ppermute(entry, "tm", [(2 * i, 2 * i + 1) for i in range(16)])
    outs = call(
        states_kernel,
        [(SUB, 64)] * 4,
        (jnp.stack([z, c]), entry, handed, before, pref),
        [SM] + [VM] * 4,
        [pltpu.VMEM((ROWS, SUB, 64), F32), pltpu.VMEM((PAD, N), F32)],
    )
    got = [outs[0]] + [along_row(outs[d], d) for d in (1, 2, 3)]
    (states,) = call(place_kernel, [(64, 64)], (z1, *got), [SM] + [VM] * 4)
    return states


def solution(mesh):
    return jax.shard_map(
        shards,
        mesh=mesh,
        in_specs=(
            P(),
            P("tm", "row", None),
            P("tm", "row", None),
            P("tm", "row"),
            P("tm", None),
            P("tm"),
        ),
        out_specs=P("tm", "row"),
        check_vma=False,
    )
```

time: 681 us -> 187 us (0.27); the launches traced: 674 us -> 187 us
  matrix products: 255 us -> 0 us
  waiting for transfers between devices: 213 us -> 88 us
  local copies, waits for them, and re-layouts: 56.7 us -> 14 us
  blocking collectives: 38.6 us -> 0 us
  Pallas kernels: 0 us -> 32.4 us
  starting transfers between devices: 77 us -> 46.3 us
  between operations: 13.6 us -> 0.3 us
  other arithmetic: 14.2 us -> 5.59 us
    dot_general x224 -> x0, matrix products: 255 us -> none  [product(): jnp.dot(left, right, precision=HIGH, preferred_element_type=jnp.float32)]
    ppermute x31 -> x23, waiting for transfers between devices: 157 us -> 78.7 us  [the longest x15 59.7 us: along_row(): return lax.ppermute(x, 'row', [(i, (i + d) % ROWS) for i in range(ROWS)])]
    all_gather x3 -> x0, blocking collectives: 38.6 us -> none  [the longest x1 13.6 us: shards(): full_sums = lax.all_gather(local_sums, 'row', axis=1, tiled=True)]
    pallas_call x0 -> x8, Pallas kernels: none -> 32.4 us  [the longest x7 23.1 us: call(): pl.pallas_call(kernel, out_shape=[jax.ShapeDtypeStruct(s, F32) for s in o...]
    scatter x2 -> x0, local copies, waits for them, and re-layouts: 30.5 us -> none  [the longest x1 16.1 us: shards(): send_tags = jnp.full((time_devs * capacity,), -1.0, jnp.float32).at[slot_...]
    all_to_all x2 -> x1, waiting for transfers between devices: 35.7 us -> 9.24 us  [shards(): sums = lax.all_to_all(partial, 'tm', 0, 0, tiled=True)]
    ppermute x31 -> x23, starting transfers between devices: 61 us -> 38.7 us  [the longest x15 24.3 us: along_row(): return lax.ppermute(x, 'row', [(i, (i + d) % ROWS) for i in range(ROWS)])]
    all_gather x1 -> x0, waiting for transfers between devices: 19.9 us -> none  [shards(): lax.all_gather(dynamics, 'row', axis=1, tiled=True)]
  transfers between devices with their start and end apart: 34 -> 24, of which waited for: 34 -> 19; matrix products, arithmetic and copies ran while one was open for 9% -> 4% of each run, Pallas kernels for 0% -> 0%
where the time goes in v1:
time: 187 us
  waiting for transfers between devices  88 us (47%)
  starting transfers between devices  46.3 us (25%)
  Pallas kernels  32.4 us (17%)
  local copies, waits for them, and re-layouts  14 us (7%)
  other arithmetic  5.59 us (3%)
    ppermute x15, waiting for transfers between devices, along_row(): return lax.ppermute(x, 'row', [(i, (i + d) % ROWS) for i in range(ROWS)])  59.7 us
    ppermute x15, starting transfers between devices, along_row(): return lax.ppermute(x, 'row', [(i, (i + d) % ROWS) for i in range(ROWS)])  24.3 us
    pallas_call x7, Pallas kernels, call(): pl.pallas_call(kernel, out_shape=[jax.ShapeDtypeStruct(s, F32) for s in o...  23.1 us
    ppermute x3, waiting for transfers between devices, along_x(): lax.ppermute(m, 'tm', [(8 * i + 2 * j, 8 * (i + d) + 2 * j) for i in rang...  10.6 us
    pallas_call x1, Pallas kernels, binned(): pl.pallas_call(bin_kernel, out_shape=jax.ShapeDtypeStruct((n_bins // 2, 1...  9.35 us
    ppermute x3, starting transfers between devices, along_y(): lax.ppermute(m, 'tm', [(8 * i + 2 * j, 8 * i + 2 * ((j + d) % 4)) for i i...  9.26 us
    all_to_all x1, waiting for transfers between devices, shards(): sums = lax.all_to_all(partial, 'tm', 0, 0, tiled=True)  9.24 us
    unnamed x46, local copies, waits for them, and re-layouts  9.12 us
  transfers between devices with their start and end apart: 24, of which 19 were waited for; matrix products, arithmetic and copies ran while one was open for 4% of the time, Pallas kernels for 0%

profile of v1, /device:TPU:6, one launch (start us, length us, event | category | flops | bytes accessed | tf_op | source)
XLA Modules:
  0.0 186.7 jit_solution(2970140274684063437)
XLA Ops:
  0.0 3.2 %copy.9.obs_ref = f32[4096,64]{1,0:T(8,128)} copy(f32[4096,64]{0,1:T(8,128)} %param.9) | data formatting | bytes 2097152 | tf_op args[3]
  5.3 9.3 %shard_map.64 = f32[1024,128]{1,0:T(8,128)} custom-call(s32[1,4096]{1,0:T(1,128)} %bitcast.43, f32[4096,64]{1,0:T(8,128)} %copy.9.obs_ref), custom_call_target="tpu_custom_call" | custom-call | tf_op jit(solution)/shard_map/pallas_call | solution.py:103
  14.6 7.6 %all-to-all-start = ((f32[32,32,128]{2,1,0:T(8,128)}), f32[32,32,128]{2,1,0:T(8,128)S(1)}, u32[]{:S(2)}, u32[]{:S(2)}) async-start(f32[32,32,128]{2,1,0:T(8,128)} %bitcast.40), calls=%async_computation | async-start | bytes 1048576 | tf_op jit(solution)/shard_map/all_to_all | solution.py:233
  22.3 9.2 %all-to-all-done = f32[32,32,128]{2,1,0:T(8,128)S(1)} async-done(((f32[32,32,128]{2,1,0:T(8,128)}), f32[32,32,128]{2,1,0:T(8,128)S(1)}, u32[]{:S(2)}, u32[]{:S(2)}) %all-to-all-start) | async-done | bytes 524320 | tf_op jit(solution)/shard_map/all_to_all | solution.py:233
  31.6 4.1 %collective-permute-start.3 = (f32[32,128]{1,0:T(8,128)S(1)}, f32[32,128]{1,0:T(8,128)S(1)}, u32[]{:S(2)}, u32[]{:S(2)}) collective-permute-start(f32[32,128]{1,0:T(8,128)S(1)} %reduce_sum.18), channel_id=1, source_target_pairs={{0,3},{1,0},{2,1},{3,2},{4,7},{5,4},{6,5},{7,6},{8,11},{9,8},{10,9... | collective-permute-start | bytes 49160 | tf_op jit(solution)/shard_map/ppermute | solution.py:215
  35.7 3.9 %dynamic-slice_bitcast_fusion = (f32[16,64,256]{2,1,0:T(8,128)S(1)}, f32[16,64,256]{2,1,0:T(8,128)}, f32[16,64,256]{2,1,0:T(8,128)}, f32[16,64,256]{2,1,0:T(8,128)}) fusion(f32[4,16,64,256]{3,2,1,0:T(8,128)} %bitcast.39, s32[]{:T(128)S(6)} %select_n.78, s32[]{:T(128)S(6)} %select_n.76, s32[]{:T(128)S(6)} %select_n.74, s32[]{:T(128)S(6)} %select_n.72), kind=kLoop, calls=%fused_computation.1 | loop fusion | bytes 8388624 | tf_op jit(solution)/shard_map/jit(dynamic_index_in_dim)/squeeze | solution.py:219
  39.6 1.9 collective-permute-start.1
  42.8 2.9 %collective-permute-start.4 = (f32[32,128]{1,0:T(8,128)S(1)}, f32[32,128]{1,0:T(8,128)S(1)}, u32[]{:S(2)}, u32[]{:S(2)}) collective-permute-start(f32[32,128]{1,0:T(8,128)S(1)} %reduce_sum.18), channel_id=1, source_target_pairs={{0,2},{1,3},{2,0},{3,1},{4,6},{5,7},{6,4},{7,5},{8,10},{9,11},{10,... | collective-permute-start | bytes 49160 | tf_op jit(solution)/shard_map/ppermute | solution.py:215
  45.8 42.2 %collective-permute-done.4 = f32[32,128]{1,0:T(8,128)S(1)} collective-permute-done((f32[32,128]{1,0:T(8,128)S(1)}, f32[32,128]{1,0:T(8,128)S(1)}, u32[]{:S(2)}, u32[]{:S(2)}) %collective-permute-start.4) | collective-permute-done | bytes 16416 | tf_op jit(solution)/shard_map/ppermute | solution.py:215
  89.9 2.8 %multiply_reduce_fusion = f32[64,64]{1,0:T(8,128)S(1)} fusion(f32[64,64,256]{2,1,0:T(8,128)} %param.8, f32[64,256]{1,0:T(8,128)S(1)} %mul.33), kind=kLoop, calls=%fused_computation | loop fusion | flops 2093056 | bytes 4276224 | tf_op jit(solution)/shard_map/reduce_sum | solution.py:239
  93.9 3.9 %collective-permute-start.7 = (f32[16,64]{1,0:T(8,128)S(1)}, f32[16,64]{1,0:T(8,128)S(1)}, u32[]{:S(2)}, u32[]{:S(2)}) collective-permute-start(f32[16,64]{1,0:T(8,128)S(1)} %get-tuple-element.34), channel_id=1, source_target_pairs={{0,2},{1,3},{2,0},{3,1},{4,6},{5,7},{6,4},{7,5},{8,10},{9,11},{10,... | collective-permute-start | bytes 12296 | tf_op jit(solution)/shard_map/ppermute | solution.py:215
  99.9 1.9 %collective-permute-done.8.b3 = f32[16,64]{1,0:T(8,128)S(1)} collective-permute-done((f32[16,64]{1,0:T(8,128)S(1)}, f32[16,64]{1,0:T(8,128)S(1)}, u32[]{:S(2)}, u32[]{:S(2)}) %collective-permute-start.8) | collective-permute-done | bytes 4128 | tf_op jit(solution)/shard_map/ppermute | solution.py:215
  103.2 6.8 %shard_map.65 = (f32[16,272,256]{2,1,0:T(8,128)}, f32[272,256]{1,0:T(8,128)}) custom-call(s32[1]{0:T(128)} %bitcast.z_ref.pos_ref, f32[16,64,256]{2,1,0:T(8,128)} %get-tuple-element.32.a0, f32[16,64,256]{2,1,0:T(8,128)} %copy-done, f32[16,64,256]{2,1,0:T(8,128)} %copy-done.1, f32[16,64,256]{2,1,0:T(8,128)} %collective-permute-done.2.a3, ...), custom_call_target="tpu_custom_call" | custom-call | tf_op jit(solution)/shard_map/pallas_call | solution.py:58
  111.2 1.8 collective-permute-start.11
  113.8 6.9 %collective-permute-done.10.m2 = f32[272,256]{1,0:T(8,128)S(1)} collective-permute-done((f32[272,256]{1,0:T(8,128)}, f32[272,256]{1,0:T(8,128)S(1)}, u32[]{:S(2)}, u32[]{:S(2)}) %collective-permute-start.10) | collective-permute-done | bytes 278560 | tf_op jit(solution)/shard_map/ppermute | solution.py:215
  120.7 2.7 %collective-permute-done.11.m3 = f32[272,256]{1,0:T(8,128)S(1)} collective-permute-done((f32[272,256]{1,0:T(8,128)}, f32[272,256]{1,0:T(8,128)S(1)}, u32[]{:S(2)}, u32[]{:S(2)}) %collective-permute-start.11) | collective-permute-done | bytes 278560 | tf_op jit(solution)/shard_map/ppermute | solution.py:215
  124.9 3.0 %shard_map.66 = (f32[272,256]{1,0:T(8,128)}, f32[272,256]{1,0:T(8,128)}) custom-call(s32[1]{0:T(128)} %bitcast.z_ref.pos_ref, f32[272,256]{1,0:T(8,128)} %get-tuple-element.17.m0, f32[272,256]{1,0:T(8,128)} %copy-done.11, f32[272,256]{1,0:T(8,128)} %copy-done.9, f32[272,256]{1,0:T(8,128)} %copy-done.10), custom_call_target="tpu_custom_call" | custom-call | tf_op jit(solution)/shard_map/pallas_call | solution.py:58
  127.9 1.8 collective-permute-done.12.other
  130.3 2.2 %shard_map.67 = (f32[272,256]{1,0:T(8,128)}, f32[272,256]{1,0:T(8,128)}) custom-call(s32[1]{0:T(128)} %bitcast.1.c_ref, f32[272,256]{1,0:T(8,128)} %get-tuple-element.18.own, f32[272,256]{1,0:T(8,128)} %copy-done.8, f32[272,256]{1,0:T(8,128)} %get-tuple-element.19.before_in), custom_call_target="tpu_custom_call" | custom-call | tf_op jit(solution)/shard_map/pallas_call | solution.py:58
  132.6 2.8 %collective-permute-start.13 = (f32[272,256]{1,0:T(8,128)}, f32[272,256]{1,0:T(8,128)S(1)}, u32[]{:S(2)}, u32[]{:S(2)}) collective-permute-start(f32[272,256]{1,0:T(8,128)} %get-tuple-element.20.m0), channel_id=1, source_target_pairs={{0,8},{8,16},{16,24},{24,0},{32,40},{40,48},{48,56},{56,32},{64,72... | collective-permute-start | bytes 835592 | tf_op jit(solution)/shard_map/ppermute | solution.py:261
  135.3 4.1 %collective-permute-start.14 = (f32[272,256]{1,0:T(8,128)}, f32[272,256]{1,0:T(8,128)S(1)}, u32[]{:S(2)}, u32[]{:S(2)}) collective-permute-start(f32[272,256]{1,0:T(8,128)} %get-tuple-element.20.m0), channel_id=1, source_target_pairs={{0,16},{8,24},{16,0},{24,8},{32,48},{40,56},{48,32},{56,40},{64,80... | collective-permute-start | bytes 835592 | tf_op jit(solution)/shard_map/ppermute | solution.py:261
  139.5 2.4 %collective-permute-start.15 = (f32[272,256]{1,0:T(8,128)}, f32[272,256]{1,0:T(8,128)S(1)}, u32[]{:S(2)}, u32[]{:S(2)}) collective-permute-start(f32[272,256]{1,0:T(8,128)} %get-tuple-element.20.m0), channel_id=1, source_target_pairs={{0,24},{8,0},{16,8},{24,16},{32,56},{40,32},{48,40},{56,48},{64,88... | collective-permute-start | bytes 835592 | tf_op jit(solution)/shard_map/ppermute | solution.py:261
  142.4 3.1 %collective-permute-done.14.m2 = f32[272,256]{1,0:T(8,128)S(1)} collective-permute-done((f32[272,256]{1,0:T(8,128)}, f32[272,256]{1,0:T(8,128)S(1)}, u32[]{:S(2)}, u32[]{:S(2)}) %collective-permute-start.14) | collective-permute-done | bytes 278560 | tf_op jit(solution)/shard_map/ppermute | solution.py:261
  145.5 2.7 %collective-permute-done.15.m3 = f32[272,256]{1,0:T(8,128)S(1)} collective-permute-done((f32[272,256]{1,0:T(8,128)}, f32[272,256]{1,0:T(8,128)S(1)}, u32[]{:S(2)}, u32[]{:S(2)}) %collective-permute-start.15) | collective-permute-done | bytes 278560 | tf_op jit(solution)/shard_map/ppermute | solution.py:261
  148.9 3.0 %shard_map.68 = (f32[272,256]{1,0:T(8,128)}, f32[272,256]{1,0:T(8,128)}) custom-call(s32[1]{0:T(128)} %bitcast.4.pos_ref, f32[272,256]{1,0:T(8,128)} %get-tuple-element.20.m0, f32[272,256]{1,0:T(8,128)} %copy-done.2, f32[272,256]{1,0:T(8,128)} %copy-done.3, f32[272,256]{1,0:T(8,128)} %copy-done.4), custom_call_target="tpu_custom_call" | custom-call | tf_op jit(solution)/shard_map/pallas_call | solution.py:58
  155.8 4.7 %collective-permute-done.16.m1 = f32[272,256]{1,0:T(8,128)S(1)} collective-permute-done((f32[272,256]{1,0:T(8,128)}, f32[272,256]{1,0:T(8,128)S(1)}, u32[]{:S(2)}, u32[]{:S(2)}) %collective-permute-start.16) | collective-permute-done | bytes 278560 | tf_op jit(solution)/shard_map/ppermute | solution.py:266
  160.5 2.8 %collective-permute-done.17.m2 = f32[272,256]{1,0:T(8,128)S(1)} collective-permute-done((f32[272,256]{1,0:T(8,128)}, f32[272,256]{1,0:T(8,128)S(1)}, u32[]{:S(2)}, u32[]{:S(2)}) %collective-permute-start.17) | collective-permute-done | bytes 278560 | tf_op jit(solution)/shard_map/ppermute | solution.py:266
  163.3 3.1 %collective-permute-done.18.m3 = f32[272,256]{1,0:T(8,128)S(1)} collective-permute-done((f32[272,256]{1,0:T(8,128)}, f32[272,256]{1,0:T(8,128)S(1)}, u32[]{:S(2)}, u32[]{:S(2)}) %collective-permute-start.18) | collective-permute-done | bytes 278560 | tf_op jit(solution)/shard_map/ppermute | solution.py:266
  167.1 2.7 %shard_map.69.mine = f32[16,256]{1,0:T(8,128)} custom-call(s32[1]{0:T(128)} %bitcast.2.pos_ref, f32[1,256]{1,0:T(1,128)} %bitcast.45, f32[272,256]{1,0:T(8,128)} %get-tuple-element.21.m0, f32[272,256]{1,0:T(8,128)} %copy-done.5, f32[272,256]{1,0:T(8,128)} %copy-done.6, f32[272,256]{1,0:T(8,128)} %copy-done.7, f32[272,256]{1,0:T(8,128)} %get-tuple-element.22.ybefore), custom_call_target="tpu_custom_call" | custom-call | tf_op jit(solution)/shard_map/pallas_call | solution.py:58
  172.8 4.1 %shard_map.70 = (f32[16,64]{1,0:T(8,128)}, f32[16,64]{1,0:T(8,128)}, f32[16,64]{1,0:T(8,128)}, f32[16,64]{1,0:T(8,128)}) custom-call(s32[2]{0:T(128)} %pad_add_fusion.idx_ref, f32[16,256]{1,0:T(8,128)} %shard_map.69.mine, f32[16,256]{1,0:T(8,128)} %copy-done.12, f32[272,256]{1,0:T(8,128)} %get-tuple-element.23.before, f32[16,272,256]{2,1,0:T(8,128)} %get-tuple-element.24.pref), custom_call_target="tpu_custom_call" | custom-call | tf_op jit(solution)/shard_map/pallas_call | solution.py:58
  177.0 3.8 %collective-permute-start.21 = (f32[16,64]{1,0:T(8,128)}, f32[16,64]{1,0:T(8,128)S(1)}, u32[]{:S(2)}, u32[]{:S(2)}) collective-permute-start(f32[16,64]{1,0:T(8,128)} %get-tuple-element.27), channel_id=1, source_target_pairs={{0,2},{1,3},{2,0},{3,1},{4,6},{5,7},{6,4},{7,5},{8,10},{9,11},{10,... | collective-permute-start | bytes 12296 | tf_op jit(solution)/shard_map/ppermute | solution.py:215
  182.8 1.9 %collective-permute-done.22.r3 = f32[16,64]{1,0:T(8,128)S(1)} collective-permute-done((f32[16,64]{1,0:T(8,128)}, f32[16,64]{1,0:T(8,128)S(1)}, u32[]{:S(2)}, u32[]{:S(2)}) %collective-permute-start.22) | collective-permute-done | bytes 4128 | tf_op jit(solution)/shard_map/ppermute | solution.py:215
  (82 shorter events, 27.1 us)
Async XLA Ops:
  14.6 16.9 %all-to-all-start = ((f32[32,32,128]{2,1,0:T(8,128)}), f32[32,32,128]{2,1,0:T(8,128)S(1)}, u32[]{:S(2)}, u32[]{:S(2)}) async-start(f32[32,32,128]{2,1,0:T(8,128)} %bitcast.40), calls=%async_computation | async-start | bytes 1048576 | tf_op jit(solution)/shard_map/all_to_all | solution.py:233
  31.6 14.2 %collective-permute-start.3 = (f32[32,128]{1,0:T(8,128)S(1)}, f32[32,128]{1,0:T(8,128)S(1)}, u32[]{:S(2)}, u32[]{:S(2)}) collective-permute-start(f32[32,128]{1,0:T(8,128)S(1)} %reduce_sum.18), channel_id=1, source_target_pairs={{0,3},{1,0},{2,1},{3,2},{4,7},{5,4},{6,5},{7,6},{8,11},{9,8},{10,9... | collective-permute-start | bytes 49160 | tf_op jit(solution)/shard_map/ppermute | solution.py:215
  39.6 62.3 %collective-permute-start = (f32[16,64,256]{2,1,0:T(8,128)}, f32[16,64,256]{2,1,0:T(8,128)S(1)}, u32[]{:S(2)}, u32[]{:S(2)}) collective-permute-start(f32[16,64,256]{2,1,0:T(8,128)} %get-tuple-element.31), channel_id=1, source_target_pairs={{0,1},{1,2},{2,3},{3,0},{4,5},{5,6},{6,7},{7,4},{8,9},{9,10},{10,1... | collective-permute-start | bytes 3145736 | tf_op jit(solution)/shard_map/ppermute | solution.py:215
  39.6 62.3 %collective-permute-start.1 = (f32[16,64,256]{2,1,0:T(8,128)}, f32[16,64,256]{2,1,0:T(8,128)S(1)}, u32[]{:S(2)}, u32[]{:S(2)}) collective-permute-start(f32[16,64,256]{2,1,0:T(8,128)} %get-tuple-element.30), channel_id=1, source_target_pairs={{0,2},{1,3},{2,0},{3,1},{4,6},{5,7},{6,4},{7,5},{8,10},{9,11},{10,... | collective-permute-start | bytes 3145736 | tf_op jit(solution)/shard_map/ppermute | solution.py:215
  41.5 60.4 %collective-permute-start.2 = (f32[16,64,256]{2,1,0:T(8,128)S(1)}, f32[16,64,256]{2,1,0:T(8,128)}, u32[]{:S(2)}, u32[]{:S(2)}) collective-permute-start(f32[16,64,256]{2,1,0:T(8,128)S(1)} %get-tuple-element.29), channel_id=1, source_target_pairs={{0,3},{1,0},{2,1},{3,2},{4,7},{5,4},{6,5},{7,6},{8,11},{9,8},{10,9... | collective-permute-start | bytes 3145736 | tf_op jit(solution)/shard_map/ppermute | solution.py:215
  42.8 45.2 %collective-permute-start.4 = (f32[32,128]{1,0:T(8,128)S(1)}, f32[32,128]{1,0:T(8,128)S(1)}, u32[]{:S(2)}, u32[]{:S(2)}) collective-permute-start(f32[32,128]{1,0:T(8,128)S(1)} %reduce_sum.18), channel_id=1, source_target_pairs={{0,2},{1,3},{2,0},{3,1},{4,6},{5,7},{6,4},{7,5},{8,10},{9,11},{10,... | collective-permute-start | bytes 49160 | tf_op jit(solution)/shard_map/ppermute | solution.py:215
  45.8 43.7 %collective-permute-start.5 = (f32[32,128]{1,0:T(8,128)S(1)}, f32[32,128]{1,0:T(8,128)S(1)}, u32[]{:S(2)}, u32[]{:S(2)}) collective-permute-start(f32[32,128]{1,0:T(8,128)S(1)} %reduce_sum.18), channel_id=1, source_target_pairs={{0,1},{1,2},{2,3},{3,0},{4,5},{5,6},{6,7},{7,4},{8,9},{9,10},{10,1... | collective-permute-start | bytes 49160 | tf_op jit(solution)/shard_map/ppermute | solution.py:215
  93.3 4.9 %collective-permute-start.6 = (f32[16,64]{1,0:T(8,128)S(1)}, f32[16,64]{1,0:T(8,128)S(1)}, u32[]{:S(2)}, u32[]{:S(2)}) collective-permute-start(f32[16,64]{1,0:T(8,128)S(1)} %get-tuple-element.35), channel_id=1, source_target_pairs={{0,1},{1,2},{2,3},{3,0},{4,5},{5,6},{6,7},{7,4},{8,9},{9,10},{10,1... | collective-permute-start | bytes 12296 | tf_op jit(solution)/shard_map/ppermute | solution.py:215
  93.9 6.0 %collective-permute-start.7 = (f32[16,64]{1,0:T(8,128)S(1)}, f32[16,64]{1,0:T(8,128)S(1)}, u32[]{:S(2)}, u32[]{:S(2)}) collective-permute-start(f32[16,64]{1,0:T(8,128)S(1)} %get-tuple-element.34), channel_id=1, source_target_pairs={{0,2},{1,3},{2,0},{3,1},{4,6},{5,7},{6,4},{7,5},{8,10},{9,11},{10,... | collective-permute-start | bytes 12296 | tf_op jit(solution)/shard_map/ppermute | solution.py:215
  98.2 3.7 %copy-start.13 = (f32[16,64]{1,0:T(8,128)}, f32[16,64]{1,0:T(8,128)S(1)}, u32[]{:S(2)}) copy-start(f32[16,64]{1,0:T(8,128)S(1)} %collective-permute-done.6.b1) | copy-start | bytes 12292
  98.2 3.7 %collective-permute-start.8 = (f32[16,64]{1,0:T(8,128)S(1)}, f32[16,64]{1,0:T(8,128)S(1)}, u32[]{:S(2)}, u32[]{:S(2)}) collective-permute-start(f32[16,64]{1,0:T(8,128)S(1)} %get-tuple-element.33), channel_id=1, source_target_pairs={{0,3},{1,0},{2,1},{3,2},{4,7},{5,4},{6,5},{7,6},{8,11},{9,8},{10,9... | collective-permute-start | bytes 12296 | tf_op jit(solution)/shard_map/ppermute | solution.py:215
  110.0 10.7 %collective-permute-start.10 = (f32[272,256]{1,0:T(8,128)}, f32[272,256]{1,0:T(8,128)S(1)}, u32[]{:S(2)}, u32[]{:S(2)}) collective-permute-start(f32[272,256]{1,0:T(8,128)} %get-tuple-element.17.m0), channel_id=1, source_target_pairs={{0,2},{1,3},{2,0},{3,1},{4,6},{5,7},{6,4},{7,5},{8,10},{9,11},{10,... | collective-permute-start | bytes 835592 | tf_op jit(solution)/shard_map/ppermute | solution.py:215
  111.2 12.3 %collective-permute-start.11 = (f32[272,256]{1,0:T(8,128)}, f32[272,256]{1,0:T(8,128)S(1)}, u32[]{:S(2)}, u32[]{:S(2)}) collective-permute-start(f32[272,256]{1,0:T(8,128)} %get-tuple-element.17.m0), channel_id=1, source_target_pairs={{0,3},{1,0},{2,1},{3,2},{4,7},{5,4},{6,5},{7,6},{8,11},{9,8},{10,9... | collective-permute-start | bytes 835592 | tf_op jit(solution)/shard_map/ppermute | solution.py:215
  113.0 10.7 %collective-permute-start.9 = (f32[272,256]{1,0:T(8,128)}, f32[272,256]{1,0:T(8,128)S(1)}, u32[]{:S(2)}, u32[]{:S(2)}) collective-permute-start(f32[272,256]{1,0:T(8,128)} %get-tuple-element.17.m0), channel_id=1, source_target_pairs={{0,1},{1,2},{2,3},{3,0},{4,5},{5,6},{6,7},{7,4},{8,9},{9,10},{10,1... | collective-permute-start | bytes 835592 | tf_op jit(solution)/shard_map/ppermute | solution.py:215
  120.7 2.9 %copy-start.9 = (f32[272,256]{1,0:T(8,128)}, f32[272,256]{1,0:T(8,128)S(1)}, u32[]{:S(2)}) copy-start(f32[272,256]{1,0:T(8,128)S(1)} %collective-permute-done.10.m2) | copy-start | bytes 835588
  127.9 1.8 collective-permute-start.12
  132.6 9.8 %collective-permute-start.13 = (f32[272,256]{1,0:T(8,128)}, f32[272,256]{1,0:T(8,128)S(1)}, u32[]{:S(2)}, u32[]{:S(2)}) collective-permute-start(f32[272,256]{1,0:T(8,128)} %get-tuple-element.20.m0), channel_id=1, source_target_pairs={{0,8},{8,16},{16,24},{24,0},{32,40},{40,48},{48,56},{56,32},{64,72... | collective-permute-start | bytes 835592 | tf_op jit(solution)/shard_map/ppermute | solution.py:261
  135.3 10.2 %collective-permute-start.14 = (f32[272,256]{1,0:T(8,128)}, f32[272,256]{1,0:T(8,128)S(1)}, u32[]{:S(2)}, u32[]{:S(2)}) collective-permute-start(f32[272,256]{1,0:T(8,128)} %get-tuple-element.20.m0), channel_id=1, source_target_pairs={{0,16},{8,24},{16,0},{24,8},{32,48},{40,56},{48,32},{56,40},{64,80... | collective-permute-start | bytes 835592 | tf_op jit(solution)/shard_map/ppermute | solution.py:261
  139.5 8.7 %collective-permute-start.15 = (f32[272,256]{1,0:T(8,128)}, f32[272,256]{1,0:T(8,128)S(1)}, u32[]{:S(2)}, u32[]{:S(2)}) collective-permute-start(f32[272,256]{1,0:T(8,128)} %get-tuple-element.20.m0), channel_id=1, source_target_pairs={{0,24},{8,0},{16,8},{24,16},{32,56},{40,32},{48,40},{56,48},{64,88... | collective-permute-start | bytes 835592 | tf_op jit(solution)/shard_map/ppermute | solution.py:261
  142.4 5.8 %copy-start.2 = (f32[272,256]{1,0:T(8,128)}, f32[272,256]{1,0:T(8,128)S(1)}, u32[]{:S(2)}) copy-start(f32[272,256]{1,0:T(8,128)S(1)} %collective-permute-done.13.m1) | copy-start | bytes 835588
  145.5 2.7 %copy-start.3 = (f32[272,256]{1,0:T(8,128)}, f32[272,256]{1,0:T(8,128)S(1)}, u32[]{:S(2)}) copy-start(f32[272,256]{1,0:T(8,128)S(1)} %collective-permute-done.14.m2) | copy-start | bytes 835588
  151.9 8.6 %collective-permute-start.16 = (f32[272,256]{1,0:T(8,128)}, f32[272,256]{1,0:T(8,128)S(1)}, u32[]{:S(2)}, u32[]{:S(2)}) collective-permute-start(f32[272,256]{1,0:T(8,128)} %get-tuple-element.21.m0), channel_id=1, source_target_pairs={{0,32},{8,40},{16,48},{24,56},{32,64},{40,72},{48,80},{56,88},{64,... | collective-permute-start | bytes 835592 | tf_op jit(solution)/shard_map/ppermute | solution.py:266
  153.1 10.2 %collective-permute-start.17 = (f32[272,256]{1,0:T(8,128)}, f32[272,256]{1,0:T(8,128)S(1)}, u32[]{:S(2)}, u32[]{:S(2)}) collective-permute-start(f32[272,256]{1,0:T(8,128)} %get-tuple-element.21.m0), channel_id=1, source_target_pairs={{0,64},{8,72},{16,80},{24,88},{32,96},{40,104},{48,112},{56,120},{... | collective-permute-start | bytes 835592 | tf_op jit(solution)/shard_map/ppermute | solution.py:266
  154.4 12.0 %collective-permute-start.18 = (f32[272,256]{1,0:T(8,128)}, f32[272,256]{1,0:T(8,128)S(1)}, u32[]{:S(2)}, u32[]{:S(2)}) collective-permute-start(f32[272,256]{1,0:T(8,128)} %get-tuple-element.21.m0), channel_id=1, source_target_pairs={{0,96},{8,104},{16,112},{24,120},{1,97},{9,105},{17,113},{25,121},... | collective-permute-start | bytes 835592 | tf_op jit(solution)/shard_map/ppermute | solution.py:266
  160.5 5.9 %copy-start.5 = (f32[272,256]{1,0:T(8,128)}, f32[272,256]{1,0:T(8,128)S(1)}, u32[]{:S(2)}) copy-start(f32[272,256]{1,0:T(8,128)S(1)} %collective-permute-done.16.m1) | copy-start | bytes 835588
  163.3 3.1 %copy-start.6 = (f32[272,256]{1,0:T(8,128)}, f32[272,256]{1,0:T(8,128)S(1)}, u32[]{:S(2)}) copy-start(f32[272,256]{1,0:T(8,128)S(1)} %collective-permute-done.17.m2) | copy-start | bytes 835588
  169.8 2.3 %collective-permute-start.19 = (f32[16,256]{1,0:T(8,128)}, f32[16,256]{1,0:T(8,128)S(1)}, u32[]{:S(2)}, u32[]{:S(2)}) collective-permute-start(f32[16,256]{1,0:T(8,128)} %shard_map.69.mine), channel_id=1, source_target_pairs={{0,4},{8,12},{16,20},{24,28},{32,36},{40,44},{48,52},{56,60},{64,6... | collective-permute-start | bytes 49160 | tf_op jit(solution)/shard_map/ppermute | solution.py:278
  176.8 5.1 %collective-permute-start.20 = (f32[16,64]{1,0:T(8,128)}, f32[16,64]{1,0:T(8,128)S(1)}, u32[]{:S(2)}, u32[]{:S(2)}) collective-permute-start(f32[16,64]{1,0:T(8,128)} %get-tuple-element.26), channel_id=1, source_target_pairs={{0,1},{1,2},{2,3},{3,0},{4,5},{5,6},{6,7},{7,4},{8,9},{9,10},{10,1... | collective-permute-start | bytes 12296 | tf_op jit(solution)/shard_map/ppermute | solution.py:215
  177.0 5.8 %collective-permute-start.21 = (f32[16,64]{1,0:T(8,128)}, f32[16,64]{1,0:T(8,128)S(1)}, u32[]{:S(2)}, u32[]{:S(2)}) collective-permute-start(f32[16,64]{1,0:T(8,128)} %get-tuple-element.27), channel_id=1, source_target_pairs={{0,2},{1,3},{2,0},{3,1},{4,6},{5,7},{6,4},{7,5},{8,10},{9,11},{10,... | collective-permute-start | bytes 12296 | tf_op jit(solution)/shard_map/ppermute | solution.py:215
  180.8 3.9 %collective-permute-start.22 = (f32[16,64]{1,0:T(8,128)}, f32[16,64]{1,0:T(8,128)S(1)}, u32[]{:S(2)}, u32[]{:S(2)}) collective-permute-start(f32[16,64]{1,0:T(8,128)} %get-tuple-element.28), channel_id=1, source_target_pairs={{0,3},{1,0},{2,1},{3,2},{4,7},{5,4},{6,5},{7,6},{8,11},{9,8},{10,9... | collective-permute-start | bytes 12296 | tf_op jit(solution)/shard_map/ppermute | solution.py:215
  181.9 2.8 %copy-start.16 = (f32[16,64]{1,0:T(8,128)}, f32[16,64]{1,0:T(8,128)S(1)}, u32[]{:S(2)}) copy-start(f32[16,64]{1,0:T(8,128)S(1)} %collective-permute-done.20.r1) | copy-start | bytes 12292
  182.8 1.9 %copy-start.17 = (f32[16,64]{1,0:T(8,128)}, f32[16,64]{1,0:T(8,128)S(1)}, u32[]{:S(2)}) copy-start(f32[16,64]{1,0:T(8,128)S(1)} %collective-permute-done.21.r2) | copy-start | bytes 12292
  (11 other events, 9.6 us)

commit v2 on v1

--- a/solution.py
+++ b/solution.py
@@ -80,57 +80,113 @@
         rest = x - hi.astype(F32)
         mid = rest.astype(BF16)
         low = (rest - mid.astype(F32)).astype(BF16)
-        rhs[...] = jnp.concatenate([hi, mid, low, jnp.zeros_like(hi)], axis=1)
+        rhs[...] = jnp.concatenate([hi, mid, low, jnp.zeros_like(hi)], axis=0)
 
     rows = lax.broadcasted_iota(jnp.int32, (BIN_M, rid_ref.shape[1]), 0) + i * BIN_M
     onehot = jnp.where(rows == rid_ref[...], 1.0, 0.0).astype(BF16)
-    got = dot_nn(onehot, rhs[...])
-    a = got[:, :128]
-    b = got[:, 128:]
-    ab = a + b
-    acc[pl.ds(pl.multiple_of(i * BIN_M, BIN_M), BIN_M), :] = a + pltpu.roll(a, 64, 1) + b + pltpu.roll(b, 64, 1)
+    got = dot_nt(onehot, rhs[...])
+    a = got[:, :128] + got[:, 128:]
+    acc[pl.ds(pl.multiple_of(i * BIN_M, BIN_M), BIN_M), :] = a + pltpu.roll(a, 64, 1)
 
     @pl.when(i == n_m - 1)
     def _():
-        half = out_ref.shape[0]
-        lane = lax.broadcasted_iota(jnp.int32, (half, 128), 1)
-        out_ref[...] = jnp.where(lane < 64, acc[:half, :], acc[half:, :])
+        part = out_ref.shape[0]
+        low_half = lax.broadcasted_iota(jnp.int32, (part, 128), 1) < 64
+        for h in range(2):
+            even = acc[2 * h * part : (2 * h + 1) * part, :]
+            odd = acc[(2 * h + 1) * part : (2 * h + 2) * part, :]
+            out_ref[:, h * 128 : (h + 1) * 128] = jnp.where(low_half, even, odd)
 
 
 def binned(rid, observed):
     n_bins = 2048
-    obs_rows, width = observed.shape
+    width, obs_rows = observed.shape
     return pl.pallas_call(
         bin_kernel,
-        out_shape=jax.ShapeDtypeStruct((n_bins // 2, 128), F32),
+        out_shape=jax.ShapeDtypeStruct((n_bins // 4, N), F32),
         grid=(n_bins // BIN_M,),
         in_specs=[
             pl.BlockSpec((1, obs_rows), lambda i: (0, 0)),
-            pl.BlockSpec((obs_rows, width), lambda i: (0, 0)),
+            pl.BlockSpec((width, obs_rows), lambda i: (0, 0)),
         ],
-        out_specs=pl.BlockSpec((n_bins // 2, 128), lambda i: (0, 0)),
-        scratch_shapes=[pltpu.VMEM((obs_rows, 4 * width), BF16), pltpu.VMEM((n_bins, 128), F32)],
+        out_specs=pl.BlockSpec((n_bins // 4, N), lambda i: (0, 0)),
+        scratch_shapes=[pltpu.VMEM((4 * width, obs_rows), BF16), pltpu.VMEM((n_bins, 128), F32)],
         compiler_params=PARAMS,
     )(rid, observed)
 
 
-def compose_kernel(z_ref, a0, a1, a2, a3, b0, b1, b2, b3, pref, whole, a_s, b_s):
+def assemble(z, parts, ah, al):
+    for d, part in enumerate(parts):
+        slot = lax.rem(z - d + ROWS, ROWS)
+        rows = pl.ds(pl.multiple_of(slot * 64, 64), 64)
+        for k in range(ah.shape[0]):
+            hi, lo = split(part[k * 64 : (k + 1) * 64, :])
+            ah[k, rows, :] = hi
+            al[k, rows, :] = lo
+
+
+def by_step(x, ah, al):
+    xh, xl = split(x)
+    return dot_nt(xh, ah) + dot_nt(xl, ah) + dot_nt(xh, al)
+
+
+def chains(ah, al, pref):
+    n_chains = ah.shape[0] // SEG
+    eye = jnp.where(
+        lax.broadcasted_iota(jnp.int32, (N, N), 0) == lax.broadcasted_iota(jnp.int32, (N, N), 1), 1.0, 0.0
+    ).astype(BF16)
+    for t in range(SEG):
+        for c in range(n_chains):
+            k = c * SEG + t
+            if t == 0:
+                pref[k] = dot_nt(eye, ah[k]) + dot_nt(eye, al[k])
+            else:
+                pref[k] = by_step(pref[k - 1], ah[k], al[k])
+
+
+def first_kernel(z_ref, a0, a1, a2, a3, pref, ah, al, both):
+    assemble(z_ref[0], (a0, a1, a2, a3), ah, al)
+    chains(ah, al, pref)
+    both[...] = mm(pref[SEG - 1], pref[2 * SEG - 1])
+
+
+def second_kernel(z_ref, a0, a1, a2, a3, both, pref, ah, al, three):
+    assemble(z_ref[0], (a0, a1, a2, a3), ah, al)
+    chains(ah, al, pref)
+    three[...] = mm(both[...], pref[SEG - 1])
+
+
+def third_kernel(
+    z_ref, a0, a1, a2, a3, b0, p01, ah01, al01, p2, ah2, al2, three, pref, shifts, whole, ah, al, b_s
+):
     z = z_ref[0]
-    for d, (a, b) in enumerate(((a0, b0), (a1, b1), (a2, b2), (a3, b3))):
-        slot = lax.rem(z - d + ROWS, ROWS)
-        a_s[:, pl.ds(pl.multiple_of(slot * 64, 64), 64), :] = a[...]
-        b_s[slot] = b[...]
-    b = jnp.concatenate([b_s[i] for i in range(ROWS)], axis=1)
+    assemble(z, (a0, a1, a2, a3), ah, al)
+    b_s[z] = b0[...]
+    for d, a in ((1, a1), (2, a2), (3, a3)):
+        b_s[lax.rem(z - d + ROWS, ROWS)] = a[SEG * 64 :, :]
+    b = jnp.concatenate([b_s[i, :, :64] for i in range(ROWS)], axis=1)
     first = lax.broadcasted_iota(jnp.int32, (PAD, N), 0) == 0
-    cur = [eye_map()] * (SUB // SEG)
-    for t in range(SEG):
+
+    def row(k):
+        return jnp.where(first, b[k : k + 1, :], 0.0)
+
+    mats = [(ah01, al01, i) for i in range(2 * SEG)] + [(ah2, al2, i) for i in range(SEG)]
+    mats += [(ah, al, i) for i in range(SEG)]
+    p = [row(c * SEG) for c in range(SUB // SEG)]
+    for c in range(SUB // SEG):
+        shifts[c * SEG : c * SEG + 1, :] = p[c][:1]
+    for t in range(1, SEG):
         for c in range(SUB // SEG):
             k = c * SEG + t
-            out = mm(cur[c], a_s[k], dot_nt)
-            pref[k, :N, :] = out[:N]
-            pref[k, N:, :] = out[N:] + jnp.where(first, b[k : k + 1, :], 0.0)
-            cur[c] = pref[k]
-    whole[...] = then(then(cur[0], cur[1]), then(cur[2], cur[3]))
+            h, l, i = mats[k]
+            p[c] = by_step(p[c], h[i], l[i]) + row(k)
+            shifts[k : k + 1, :] = p[c][:1]
+    chains(ah, al, pref)
+    v = mm(p[0], p01[2 * SEG - 1]) + p[1]
+    v = mm(v, p2[SEG - 1]) + p[2]
+    v = mm(v, pref[SEG - 1]) + p[3]
+    whole[:N, :] = mm(three[...], pref[SEG - 1])
+    whole[N:, :] = v
 
 
 def four_kernel(pos_ref, m0, m1, m2, m3, total, before, m_s):
@@ -185,23 +241,46 @@
     out[...] = apply(s_s[...], ybefore[...])
 
 
-def states_kernel(idx_ref, mine, other, before, pref, o0, o1, o2, o3, st_s, s_s):
+def states_kernel(idx_ref, mine, other, before, p01, p2, p3, shifts, o0, o1, o2, o3, st_s, s_s):
     z = idx_ref[0]
     c = idx_ref[1]
     s_s[...] = jnp.where(c == 0, mine[...], other[...])
     s = apply(s_s[...], before[...])
     eye = lax.broadcasted_iota(jnp.int32, (N, N), 0) == lax.broadcasted_iota(jnp.int32, (N, N), 1)
+    first = lax.broadcasted_iota(jnp.int32, (PAD, N), 0) == 0
+    prefs = [(p01, i) for i in range(2 * SEG)] + [(p2, i) for i in range(SEG)] + [(p3, i) for i in range(SEG)]
     for q in range(SUB // SEG):
         col = jnp.sum(jnp.where(eye, s[0:1, :], 0.0), axis=1, keepdims=True)
         for t in range(SEG):
             k = q * SEG + t
-            row = jnp.sum(pref[k, :N, :] * col, axis=0, keepdims=True) + pref[k, N : N + 1, :]
+            m, i = prefs[k]
+            row = jnp.sum(m[i] * col, axis=0, keepdims=True) + shifts[k : k + 1, :]
             for j in range(ROWS):
                 st_s[j, k : k + 1, :] = row[:, j * 64 : (j + 1) * 64]
         if q < SUB // SEG - 1:
-            s = apply(s, pref[q * SEG + SEG - 1])
+            m, i = prefs[q * SEG + SEG - 1]
+            k = q * SEG + SEG - 1
+            s = mm(s, m[i]) + jnp.where(first, shifts[k : k + 1, :], 0.0)
     for d, o in enumerate((o0, o1, o2, o3)):
         o[...] = st_s[lax.rem(z + d, ROWS)]
+
+
+def offset_kernel(z_ref, g, i0, r1, r2, r3, o0, o1, o2, o3, info_s, off_s):
+    z = z_ref[0]
+    info_s[z] = i0[...]
+    for d, r in ((1, r1), (2, r2), (3, r3)):
+        info_s[lax.rem(z - d + ROWS, ROWS)] = r[r.shape[0] - 16 :, :]
+    lane = lax.broadcasted_iota(jnp.int32, (64, 128), 1)
+    for q in range(4):
+        full = jnp.concatenate([info_s[i, :, q * 64 : (q + 1) * 64] for i in range(ROWS)], axis=1)
+        acc = jnp.zeros((64, 128), F32)
+        for k in range(16):
+            col = jnp.sum(g[16 * q + k] * full[k : k + 1, :], axis=1, keepdims=True)
+            acc = jnp.where(lane == k, col, acc)
+        off_s[q] = jnp.concatenate([acc, jnp.zeros((64, 128), F32)], axis=0).T[:16, :]
+    for d, o in enumerate((o0, o1, o2, o3)):
+        o[:, :128] = off_s[lax.rem(z + d, ROWS)]
+        o[:, 128:] = jnp.zeros((16, 128), F32)
 
 
 def place_kernel(z_ref, r0, r1, r2, r3, out):
@@ -215,37 +294,66 @@
     return lax.ppermute(x, "row", [(i, (i + d) % ROWS) for i in range(ROWS)])
 
 
-def pick(x, i):
-    return lax.dynamic_index_in_dim(x, i, 0, keepdims=False)
-
-
 def shards(prior, dynamics, gains, observed, owner, step):
     tm = lax.axis_index("tm").astype(jnp.int32)
     z = lax.axis_index("row").astype(jnp.int32)
     x, y, c = tm // 8, (tm // 2) % 4, tm % 2
     z1 = z.reshape(1)
 
-    parts = dynamics.reshape(ROWS, SUB, 64, N)
-    mats = [pick(parts, z)] + [along_row(pick(parts, (z + d) % ROWS), d) for d in (1, 2, 3)]
-
-    rid = owner[:, 0] * 32 + step % 32 + 1024 * (step // 32)
-    partial = binned(rid.reshape(1, -1), observed)
+    flat = dynamics.reshape(ROWS * SUB * 64, N)
+
+    def piece(d, start, count):
+        return lax.dynamic_slice_in_dim(flat, ((z + d) % ROWS) * (SUB * 64) + start * 64, count * 64, 0)
+
+    part_a = [piece(0, 0, 8)] + [along_row(piece(d, 0, 8), d) for d in (1, 2, 3)]
+
+    rid = owner[:, 0] * 16 + step % 16 + 512 * (step // 16)
+    partial = binned(rid.reshape(1, -1), observed.T)
     sums = lax.all_to_all(partial, "tm", 0, 0, tiled=True)
-    info = jnp.sum(sums.reshape(32, 32, 128), axis=0)
-    infos = [info] + [along_row(info, d) for d in (1, 2, 3)]
-    cyc = [infos[3], infos[2], infos[1], infos[0]] * 2
-    ordered = lax.dynamic_slice_in_dim(jnp.stack(cyc), 3 - z, ROWS, 0)
-    full = ordered.reshape(ROWS, 32, 2, 64).transpose(2, 1, 0, 3).reshape(64, N)
-    offset = jnp.sum(gains * full[:, None, :], axis=2)
-    off = offset.reshape(ROWS, SUB, 64)
-    offs = [pick(off, z)] + [along_row(pick(off, (z + d) % ROWS), d) for d in (1, 2, 3)]
-
-    pref, whole = call(
-        compose_kernel,
-        [(SUB, R, N), (R, N)],
-        (z1, *mats, *offs),
-        [SM] + [VM] * 8,
-        [pltpu.VMEM((SUB, N, N), F32), pltpu.VMEM((ROWS, SUB, 64), F32)],
+    info = jnp.sum(sums.reshape(32, 16, N), axis=0)
+    info, *part_a = lax.optimization_barrier((info, *part_a))
+
+    sent_b = [jnp.concatenate([piece(d, 8, 4), info], axis=0) for d in (1, 2, 3)]
+    part_b = [piece(0, 8, 4)] + [along_row(sent_b[d - 1], d) for d in (1, 2, 3)]
+    p01, ah01, al01, both = pl.pallas_call(
+        first_kernel,
+        out_shape=[
+            jax.ShapeDtypeStruct((8, N, N), F32),
+            jax.ShapeDtypeStruct((8, N, N), BF16),
+            jax.ShapeDtypeStruct((8, N, N), BF16),
+            jax.ShapeDtypeStruct((N, N), F32),
+        ],
+        in_specs=[SM] + [VM] * 4,
+        out_specs=[VM] * 4,
+        compiler_params=PARAMS,
+    )(z1, *part_a)
+    offs = call(
+        offset_kernel,
+        [(16, N)] * 4,
+        (z1, gains, info, *part_b[1:]),
+        [SM] + [VM] * 5,
+        [pltpu.VMEM((ROWS, 16, N), F32), pltpu.VMEM((ROWS, 16, 128), F32)],
+    )
+    sent_c = [jnp.concatenate([piece(d, 12, 4), offs[d]], axis=0) for d in (1, 2, 3)]
+    part_c = [piece(0, 12, 4)] + [along_row(sent_c[d - 1], d) for d in (1, 2, 3)]
+    p2, ah2, al2, three = pl.pallas_call(
+        second_kernel,
+        out_shape=[
+            jax.ShapeDtypeStruct((4, N, N), F32),
+            jax.ShapeDtypeStruct((4, N, N), BF16),
+            jax.ShapeDtypeStruct((4, N, N), BF16),
+            jax.ShapeDtypeStruct((N, N), F32),
+        ],
+        in_specs=[SM] + [VM] * 5,
+        out_specs=[VM] * 4,
+        compiler_params=PARAMS,
+    )(z1, *part_b, both)
+    p3, shifts, whole = call(
+        third_kernel,
+        [(4, N, N), (SUB, N), (R, N)],
+        (z1, *part_c, offs[0], p01, ah01, al01, p2, ah2, al2, three),
+        [SM] + [VM] * 12,
+        [pltpu.VMEM((4, N, N), BF16), pltpu.VMEM((4, N, N), BF16), pltpu.VMEM((ROWS, 16, N), F32)],
     )
 
     four = functools.partial(
@@ -279,8 +387,8 @@
     outs = call(
         states_kernel,
         [(SUB, 64)] * 4,
-        (jnp.stack([z, c]), entry, handed, before, pref),
-        [SM] + [VM] * 4,
+        (jnp.stack([z, c]), entry, handed, before, p01, p2, p3, shifts),
+        [SM] + [VM] * 7,
         [pltpu.VMEM((ROWS, SUB, 64), F32), pltpu.VMEM((PAD, N), F32)],
     )
     got = [outs[0]] + [along_row(outs[d], d) for d in (1, 2, 3)]

time: 187 us -> 163 us (0.87)
  waiting for transfers between devices: 88 us -> 61.9 us
  Pallas kernels: 32.4 us -> 43.9 us
  starting transfers between devices: 46.3 us -> 41.8 us
  local copies, waits for them, and re-layouts: 14 us -> 11 us
  other arithmetic: 5.59 us -> 3.61 us
    ppermute x15, waiting for transfers between devices: 59.7 us -> 36.2 us  [along_row(): return lax.ppermute(x, 'row', [(i, (i + d) % ROWS) for i in range(ROWS)])]
    pallas_call x1 -> x3, Pallas kernels: 9.35 us -> 16.8 us  [the longest x1 8.96 us: binned(): pl.pallas_call(bin_kernel, out_shape=jax.ShapeDtypeStruct((n_bins // 4, N...]
    dynamic_slice x1 -> x2, local copies, waits for them, and re-layouts: 0.01 us -> 5.45 us  [piece(): lax.dynamic_slice_in_dim(flat, (z + d) % ROWS * (SUB * 64) + start * 64,...]
    ppermute x15, starting transfers between devices: 24.3 us -> 19.6 us  [along_row(): return lax.ppermute(x, 'row', [(i, (i + d) % ROWS) for i in range(ROWS)])]
    squeeze x2 -> x0, local copies, waits for them, and re-layouts: 4.53 us -> none  [pick(): return lax.dynamic_index_in_dim(x, i, 0, keepdims=False)]
    pallas_call x7 -> x8, Pallas kernels: 23.1 us -> 27.1 us  [call(): pl.pallas_call(kernel, out_shape=[jax.ShapeDtypeStruct(s, F32) for s in o...]
    unnamed x46 -> x50, local copies, waits for them, and re-layouts: 9.12 us -> 5.5 us
    reduce_sum x2 -> x1, other arithmetic: 2.85 us -> 0.05 us  [shards(): info = jnp.sum(sums.reshape(32, 16, N), axis=0)]
  transfers between devices with their start and end apart: 24 -> 24, of which waited for: 19 -> 19; matrix products, arithmetic and copies ran while one was open for 4% -> 3% of each run, Pallas kernels for 0% -> 10%
where the time goes in v2:
time: 163 us; the launch traced here: 162 us
  waiting for transfers between devices  61.9 us (38%)
  Pallas kernels  43.9 us (27%)
  starting transfers between devices  41.8 us (26%)
  local copies, waits for them, and re-layouts  11 us (7%)
  other arithmetic  3.61 us (2%)
    ppermute x15, waiting for transfers between devices, along_row(): return lax.ppermute(x, 'row', [(i, (i + d) % ROWS) for i in range(ROWS)])  36.2 us
    pallas_call x8, Pallas kernels, call(): pl.pallas_call(kernel, out_shape=[jax.ShapeDtypeStruct(s, F32) for s in o...  27.1 us
    ppermute x15, starting transfers between devices, along_row(): return lax.ppermute(x, 'row', [(i, (i + d) % ROWS) for i in range(ROWS)])  19.6 us
    ppermute x3, waiting for transfers between devices, along_x(): lax.ppermute(m, 'tm', [(8 * i + 2 * j, 8 * (i + d) + 2 * j) for i in rang...  10.6 us
    ppermute x3, starting transfers between devices, along_y(): lax.ppermute(m, 'tm', [(8 * i + 2 * j, 8 * i + 2 * ((j + d) % 4)) for i i...  9.37 us
    pallas_call x1, Pallas kernels, binned(): pl.pallas_call(bin_kernel, out_shape=jax.ShapeDtypeStruct((n_bins // 4, N...  8.96 us
    all_to_all x1, starting transfers between devices, shards(): sums = lax.all_to_all(partial, 'tm', 0, 0, tiled=True)  7.6 us
    all_to_all x1, waiting for transfers between devices, shards(): sums = lax.all_to_all(partial, 'tm', 0, 0, tiled=True)  6.72 us
  transfers between devices with their start and end apart: 24, of which 19 were waited for; matrix products, arithmetic and copies ran while one was open for 3% of the time, Pallas kernels for 10%

profile of v2, /device:TPU:6, one launch (start us, length us, event | category | flops | bytes accessed | tf_op | source)
XLA Modules:
  0.0 162.4 jit_solution(10370540816564779705)
XLA Ops:
  0.0 2.9 %constant_dynamic-slice_fusion.6 = (f32[512,256]{1,0:T(8,128)}, f32[512,256]{1,0:T(8,128)}, f32[512,256]{1,0:T(8,128)}, f32[512,256]{1,0:T(8,128)}) fusion(f32[4096,256]{1,0:T(8,128)} %bitcast.10, s32[]{:T(128)S(6)} %select_n.112, s32[]{:T(128)S(6)} %select_n.110, s32[]{:T(128)S(6)} %select_n.108, s32[]{:T(128)S(6)} %select_n.107), kind=kLoop, calls=%fused_computation.26 | loop fusion | bytes 4194320 | tf_op jit(solution)/shard_map/dynamic_slice | solution.py:306
  2.9 1.9 %collective-permute-start = (f32[512,256]{1,0:T(8,128)}, f32[512,256]{1,0:T(8,128)S(1)}, u32[]{:S(2)}, u32[]{:S(2)}) collective-permute-start(f32[512,256]{1,0:T(8,128)} %get-tuple-element.75), channel_id=1, source_target_pairs={{0,1},{1,2},{2,3},{3,0},{4,5},{5,6},{6,7},{7,4},{8,9},{9,10},{10,1... | collective-permute-start | bytes 1572872 | tf_op jit(solution)/shard_map/ppermute | solution.py:294
  4.9 3.6 %collective-permute-start.1 = (f32[512,256]{1,0:T(8,128)}, f32[512,256]{1,0:T(8,128)S(1)}, u32[]{:S(2)}, u32[]{:S(2)}) collective-permute-start(f32[512,256]{1,0:T(8,128)} %get-tuple-element.74), channel_id=1, source_target_pairs={{0,2},{1,3},{2,0},{3,1},{4,6},{5,7},{6,4},{7,5},{8,10},{9,11},{10,... | collective-permute-start | bytes 1572872 | tf_op jit(solution)/shard_map/ppermute | solution.py:294
  10.1 9.0 %shard_map.64 = f32[512,256]{1,0:T(8,128)} custom-call(s32[1,4096]{1,0:T(1,128)} %bitcast.14, f32[64,4096]{1,0:T(8,128)} %bitcast.13), custom_call_target="tpu_custom_call" | custom-call | tf_op jit(solution)/shard_map/pallas_call | solution.py:104
  19.1 7.6 %all-to-all-start = ((f32[32,16,256]{2,1,0:T(8,128)}), f32[32,16,256]{2,1,0:T(8,128)S(1)}, u32[]{:S(2)}, u32[]{:S(2)}) async-start(f32[32,16,256]{2,1,0:T(8,128)} %bitcast.12), calls=%async_computation | async-start | bytes 1048576 | tf_op jit(solution)/shard_map/all_to_all | solution.py:312
  26.7 2.5 %constant_dynamic-slice_fusion = (f32[256,256]{1,0:T(8,128)}, f32[256,256]{1,0:T(8,128)S(1)}, f32[256,256]{1,0:T(8,128)S(1)}, f32[256,256]{1,0:T(8,128)S(1)}, f3...) fusion(f32[4096,256]{1,0:T(8,128)} %bitcast.11, ...), kind=kLoop, calls=%fused_computation.20 | loop fusion | bytes 4194336 | tf_op jit(solution)/shard_map/dynamic_slice | solution.py:306
  29.2 6.7 %all-to-all-done = f32[32,16,256]{2,1,0:T(8,128)S(1)} async-done(((f32[32,16,256]{2,1,0:T(8,128)}), f32[32,16,256]{2,1,0:T(8,128)S(1)}, u32[]{:S(2)}, u32[]{:S(2)}) %all-to-all-start) | async-done | bytes 524320 | tf_op jit(solution)/shard_map/all_to_all | solution.py:312
  37.7 2.3 %collective-permute-start.5 = (f32[272,256]{1,0:T(8,128)S(1)}, f32[272,256]{1,0:T(8,128)S(1)}, u32[]{:S(2)}, u32[]{:S(2)}) collective-permute-start(f32[272,256]{1,0:T(8,128)S(1)} %get-tuple-element.77), channel_id=1, source_target_pairs={{0,3},{1,0},{2,1},{3,2},{4,7},{5,4},{6,5},{7,6},{8,11},{9,8},{10,9... | collective-permute-start | bytes 835592 | tf_op jit(solution)/shard_map/ppermute | solution.py:294
  40.0 12.4 %collective-permute-done.3.r1.a1 = f32[272,256]{1,0:T(8,128)S(1)} collective-permute-done((f32[272,256]{1,0:T(8,128)S(1)}, f32[272,256]{1,0:T(8,128)S(1)}, u32[]{:S(2)}, u32[]{:S(2)}) %collective-permute-start.3) | collective-permute-done | bytes 278560 | tf_op jit(solution)/shard_map/ppermute | solution.py:294
  53.8 4.0 %shard_map.65 = (f32[16,256]{1,0:T(8,128)}, f32[16,256]{1,0:T(8,128)}, f32[16,256]{1,0:T(8,128)}, f32[16,256]{1,0:T(8,128)}) custom-call(s32[1]{0:T(128)} %bitcast.z_ref.pos_ref, f32[64,64,256]{2,1,0:T(8,128)} %g.1, f32[16,256]{1,0:T(8,128)} %copy-done.18, f32[272,256]{1,0:T(8,128)} %copy-done, f32[272,256]{1,0:T(8,128)} %copy-done.1, f32[272,256]{1,0:T(8,128)} %copy-done.2), custom_call_target="tpu_custom_call" | custom-call | tf_op jit(solution)/shard_map/pallas_call | solution.py:58
  58.6 2.7 %collective-permute-start.8 = (f32[272,256]{1,0:T(8,128)S(1)}, f32[272,256]{1,0:T(8,128)S(1)}, u32[]{:S(2)}, u32[]{:S(2)}) collective-permute-start(f32[272,256]{1,0:T(8,128)S(1)} %pad_maximum_fusion.5), channel_id=1, source_target_pairs={{0,3},{1,0},{2,1},{3,2},{4,7},{5,4},{6,5},{7,6},{8,11},{9,8},{10,9... | collective-permute-start | bytes 835592 | tf_op jit(solution)/shard_map/ppermute | solution.py:294
  63.8 4.3 %shard_map.66 = (f32[8,256,256]{2,1,0:T(8,128)}, bf16[8,256,256]{2,1,0:T(8,128)(2,1)}, bf16[8,256,256]{2,1,0:T(8,128)(2,1)}, f32[256,256]{1,0:T(8,128)}) custom-call(s32[1]{0:T(128)} %bitcast.z_ref.pos_ref, f32[512,256]{1,0:T(8,128)} %get-tuple-element.40.a0, f32[512,256]{1,0:T(8,128)} %copy-done.3, f32[512,256]{1,0:T(8,128)} %copy-done.4, ...), custom_call_target="tpu_custom_call" | custom-call | tf_op jit(solution)/shard_map/pallas_call | solution.py:318
  68.1 3.5 %shard_map.67 = (f32[4,256,256]{2,1,0:T(8,128)}, bf16[4,256,256]{2,1,0:T(8,128)(2,1)}, bf16[4,256,256]{2,1,0:T(8,128)(2,1)}, f32[256,256]{1,0:T(8,128)}) custom-call(s32[1]{0:T(128)} %bitcast.z_ref.pos_ref, f32[256,256]{1,0:T(8,128)} %get-tuple-element.65.a0, f32[272,256]{1,0:T(8,128)} %copy-done, f32[272,256]{1,0:T(8,128)} %copy-done.1, ...), custom_call_target="tpu_custom_call" | custom-call | tf_op jit(solution)/shard_map/pallas_call | solution.py:339
  73.4 4.5 %collective-permute-done.6.a1 = f32[272,256]{1,0:T(8,128)S(1)} collective-permute-done((f32[272,256]{1,0:T(8,128)S(1)}, f32[272,256]{1,0:T(8,128)S(1)}, u32[]{:S(2)}, u32[]{:S(2)}) %collective-permute-start.6) | collective-permute-done | bytes 278560 | tf_op jit(solution)/shard_map/ppermute | solution.py:294
  78.6 6.7 %shard_map.68 = (f32[4,256,256]{2,1,0:T(8,128)}, f32[16,256]{1,0:T(8,128)}, f32[272,256]{1,0:T(8,128)}) custom-call(s32[1]{0:T(128)} %bitcast.z_ref.pos_ref, f32[256,256]{1,0:T(8,128)} %get-tuple-element.72.a0, f32[272,256]{1,0:T(8,128)} %copy-done.7, f32[272,256]{1,0:T(8,128)} %copy-done.6, f32[272,256]{1,0:T(8,128)} %copy-done.5, ...), custom_call_target="tpu_custom_call" | custom-call | tf_op jit(solution)/shard_map/pallas_call | solution.py:58
  87.6 9.0 %collective-permute-done.10.m2 = f32[272,256]{1,0:T(8,128)S(1)} collective-permute-done((f32[272,256]{1,0:T(8,128)}, f32[272,256]{1,0:T(8,128)S(1)}, u32[]{:S(2)}, u32[]{:S(2)}) %collective-permute-start.10) | collective-permute-done | bytes 278560 | tf_op jit(solution)/shard_map/ppermute | solution.py:294
  96.5 1.9 %collective-permute-done.11.m3 = f32[272,256]{1,0:T(8,128)S(1)} collective-permute-done((f32[272,256]{1,0:T(8,128)}, f32[272,256]{1,0:T(8,128)S(1)}, u32[]{:S(2)}, u32[]{:S(2)}) %collective-permute-start.11) | collective-permute-done | bytes 278560 | tf_op jit(solution)/shard_map/ppermute | solution.py:294
  98.4 3.1 %collective-permute-done.9.m1 = f32[272,256]{1,0:T(8,128)S(1)} collective-permute-done((f32[272,256]{1,0:T(8,128)}, f32[272,256]{1,0:T(8,128)S(1)}, u32[]{:S(2)}, u32[]{:S(2)}) %collective-permute-start.9) | collective-permute-done | bytes 278560 | tf_op jit(solution)/shard_map/ppermute | solution.py:294
  102.2 3.2 %shard_map.69 = (f32[272,256]{1,0:T(8,128)}, f32[272,256]{1,0:T(8,128)}) custom-call(s32[1]{0:T(128)} %bitcast.z_ref.pos_ref, f32[272,256]{1,0:T(8,128)} %get-tuple-element.52.m0, f32[272,256]{1,0:T(8,128)} %copy-done.17, f32[272,256]{1,0:T(8,128)} %copy-done.15, f32[272,256]{1,0:T(8,128)} %copy-done.16), custom_call_target="tpu_custom_call" | custom-call | tf_op jit(solution)/shard_map/pallas_call | solution.py:58
  107.9 2.2 %shard_map.70 = (f32[272,256]{1,0:T(8,128)}, f32[272,256]{1,0:T(8,128)}) custom-call(s32[1]{0:T(128)} %bitcast.1.c_ref, f32[272,256]{1,0:T(8,128)} %get-tuple-element.53.own, f32[272,256]{1,0:T(8,128)} %copy-done.14, f32[272,256]{1,0:T(8,128)} %get-tuple-element.54.before_in), custom_call_target="tpu_custom_call" | custom-call | tf_op jit(solution)/shard_map/pallas_call | solution.py:58
  110.1 2.7 %collective-permute-start.13 = (f32[272,256]{1,0:T(8,128)}, f32[272,256]{1,0:T(8,128)S(1)}, u32[]{:S(2)}, u32[]{:S(2)}) collective-permute-start(f32[272,256]{1,0:T(8,128)} %get-tuple-element.55.m0), channel_id=1, source_target_pairs={{0,8},{8,16},{16,24},{24,0},{32,40},{40,48},{48,56},{56,32},{64,72... | collective-permute-start | bytes 835592 | tf_op jit(solution)/shard_map/ppermute | solution.py:369
  112.8 4.1 %collective-permute-start.14 = (f32[272,256]{1,0:T(8,128)}, f32[272,256]{1,0:T(8,128)S(1)}, u32[]{:S(2)}, u32[]{:S(2)}) collective-permute-start(f32[272,256]{1,0:T(8,128)} %get-tuple-element.55.m0), channel_id=1, source_target_pairs={{0,16},{8,24},{16,0},{24,8},{32,48},{40,56},{48,32},{56,40},{64,80... | collective-permute-start | bytes 835592 | tf_op jit(solution)/shard_map/ppermute | solution.py:369
  117.0 2.5 %collective-permute-start.15 = (f32[272,256]{1,0:T(8,128)}, f32[272,256]{1,0:T(8,128)S(1)}, u32[]{:S(2)}, u32[]{:S(2)}) collective-permute-start(f32[272,256]{1,0:T(8,128)} %get-tuple-element.55.m0), channel_id=1, source_target_pairs={{0,24},{8,0},{16,8},{24,16},{32,56},{40,32},{48,40},{56,48},{64,88... | collective-permute-start | bytes 835592 | tf_op jit(solution)/shard_map/ppermute | solution.py:369
  120.0 3.0 %collective-permute-done.14.m2 = f32[272,256]{1,0:T(8,128)S(1)} collective-permute-done((f32[272,256]{1,0:T(8,128)}, f32[272,256]{1,0:T(8,128)S(1)}, u32[]{:S(2)}, u32[]{:S(2)}) %collective-permute-start.14) | collective-permute-done | bytes 278560 | tf_op jit(solution)/shard_map/ppermute | solution.py:369
  123.0 2.7 %collective-permute-done.15.m3 = f32[272,256]{1,0:T(8,128)S(1)} collective-permute-done((f32[272,256]{1,0:T(8,128)}, f32[272,256]{1,0:T(8,128)S(1)}, u32[]{:S(2)}, u32[]{:S(2)}) %collective-permute-start.15) | collective-permute-done | bytes 278560 | tf_op jit(solution)/shard_map/ppermute | solution.py:369
  126.4 3.0 %shard_map.71 = (f32[272,256]{1,0:T(8,128)}, f32[272,256]{1,0:T(8,128)}) custom-call(s32[1]{0:T(128)} %bitcast.4.pos_ref, f32[272,256]{1,0:T(8,128)} %get-tuple-element.55.m0, f32[272,256]{1,0:T(8,128)} %copy-done.8, f32[272,256]{1,0:T(8,128)} %copy-done.9, f32[272,256]{1,0:T(8,128)} %copy-done.10), custom_call_target="tpu_custom_call" | custom-call | tf_op jit(solution)/shard_map/pallas_call | solution.py:58
  133.3 4.7 %collective-permute-done.16.m1 = f32[272,256]{1,0:T(8,128)S(1)} collective-permute-done((f32[272,256]{1,0:T(8,128)}, f32[272,256]{1,0:T(8,128)S(1)}, u32[]{:S(2)}, u32[]{:S(2)}) %collective-permute-start.16) | collective-permute-done | bytes 278560 | tf_op jit(solution)/shard_map/ppermute | solution.py:374
  138.0 2.8 %collective-permute-done.17.m2 = f32[272,256]{1,0:T(8,128)S(1)} collective-permute-done((f32[272,256]{1,0:T(8,128)}, f32[272,256]{1,0:T(8,128)S(1)}, u32[]{:S(2)}, u32[]{:S(2)}) %collective-permute-start.17) | collective-permute-done | bytes 278560 | tf_op jit(solution)/shard_map/ppermute | solution.py:374
  140.8 3.1 %collective-permute-done.18.m3 = f32[272,256]{1,0:T(8,128)S(1)} collective-permute-done((f32[272,256]{1,0:T(8,128)}, f32[272,256]{1,0:T(8,128)S(1)}, u32[]{:S(2)}, u32[]{:S(2)}) %collective-permute-start.18) | collective-permute-done | bytes 278560 | tf_op jit(solution)/shard_map/ppermute | solution.py:374
  144.6 2.7 %shard_map.72.mine = f32[16,256]{1,0:T(8,128)} custom-call(s32[1]{0:T(128)} %bitcast.2.pos_ref, f32[1,256]{1,0:T(1,128)} %bitcast.16, f32[272,256]{1,0:T(8,128)} %get-tuple-element.56.m0, f32[272,256]{1,0:T(8,128)} %copy-done.11, f32[272,256]{1,0:T(8,128)} %copy-done.12, f32[272,256]{1,0:T(8,128)} %copy-done.13, f32[272,256]{1,0:T(8,128)} %get-tuple-element.57.ybefore), custom_call_target="tpu_custom_call" | custom-call | tf_op jit(solution)/shard_map/pallas_call | solution.py:58
  150.3 4.0 %shard_map.73 = (f32[16,64]{1,0:T(8,128)}, f32[16,64]{1,0:T(8,128)}, f32[16,64]{1,0:T(8,128)}, f32[16,64]{1,0:T(8,128)}) custom-call(s32[2]{0:T(128)} %pad_add_fusion.idx_ref, f32[16,256]{1,0:T(8,128)} %shard_map.72.mine, f32[16,256]{1,0:T(8,128)} %copy-done.19, f32[272,256]{1,0:T(8,128)} %get-tuple-element.58.before, f32[8,256,256]{2,1,0:T(8,128)} %get-tuple-element.44.p01, ...), custom_call_target="tpu_custom_call" | custom-call | tf_op jit(solution)/shard_map/pallas_call | solution.py:58
  154.3 2.3 %collective-permute-start.21 = (f32[16,64]{1,0:T(8,128)}, f32[16,64]{1,0:T(8,128)S(1)}, u32[]{:S(2)}, u32[]{:S(2)}) collective-permute-start(f32[16,64]{1,0:T(8,128)} %get-tuple-element.63), channel_id=1, source_target_pairs={{0,2},{1,3},{2,0},{3,1},{4,6},{5,7},{6,4},{7,5},{8,10},{9,11},{10,... | collective-permute-start | bytes 12296 | tf_op jit(solution)/shard_map/ppermute | solution.py:294
  (87 shorter events, 30.3 us)
Async XLA Ops:
  0.0 9.5 %copy-start.21 = (s32[4096,1]{0,1:T(1,128)S(1)}, s32[4096,1]{0,1:T(1,128)}, u32[]{:S(2)}) copy-start(s32[4096,1]{0,1:T(1,128)} %param.10) | copy-start | bytes 49156
  0.0 9.5 %copy-start.20 = (s32[4096]{0:T(1024)S(1)}, s32[4096]{0:T(1024)}, u32[]{:S(2)}) copy-start(s32[4096]{0:T(1024)} %param.11) | copy-start | bytes 49156
  2.9 33.1 %collective-permute-start = (f32[512,256]{1,0:T(8,128)}, f32[512,256]{1,0:T(8,128)S(1)}, u32[]{:S(2)}, u32[]{:S(2)}) collective-permute-start(f32[512,256]{1,0:T(8,128)} %get-tuple-element.75), channel_id=1, source_target_pairs={{0,1},{1,2},{2,3},{3,0},{4,5},{5,6},{6,7},{7,4},{8,9},{9,10},{10,1... | collective-permute-start | bytes 1572872 | tf_op jit(solution)/shard_map/ppermute | solution.py:294
  4.9 31.2 %collective-permute-start.1 = (f32[512,256]{1,0:T(8,128)}, f32[512,256]{1,0:T(8,128)S(1)}, u32[]{:S(2)}, u32[]{:S(2)}) collective-permute-start(f32[512,256]{1,0:T(8,128)} %get-tuple-element.74), channel_id=1, source_target_pairs={{0,2},{1,3},{2,0},{3,1},{4,6},{5,7},{6,4},{7,5},{8,10},{9,11},{10,... | collective-permute-start | bytes 1572872 | tf_op jit(solution)/shard_map/ppermute | solution.py:294
  8.4 27.6 %collective-permute-start.2 = (f32[512,256]{1,0:T(8,128)}, f32[512,256]{1,0:T(8,128)}, u32[]{:S(2)}, u32[]{:S(2)}) collective-permute-start(f32[512,256]{1,0:T(8,128)} %get-tuple-element.73), channel_id=1, source_target_pairs={{0,3},{1,0},{2,1},{3,2},{4,7},{5,4},{6,5},{7,6},{8,11},{9,8},{10,9... | collective-permute-start | bytes 1572872 | tf_op jit(solution)/shard_map/ppermute | solution.py:294
  19.1 16.9 %all-to-all-start = ((f32[32,16,256]{2,1,0:T(8,128)}), f32[32,16,256]{2,1,0:T(8,128)S(1)}, u32[]{:S(2)}, u32[]{:S(2)}) async-start(f32[32,16,256]{2,1,0:T(8,128)} %bitcast.12), calls=%async_computation | async-start | bytes 1048576 | tf_op jit(solution)/shard_map/all_to_all | solution.py:312
  36.0 17.1 %copy-start.18 = (f32[16,256]{1,0:T(8,128)}, f32[16,256]{1,0:T(8,128)S(1)}, u32[]{:S(2)}) copy-start(f32[16,256]{1,0:T(8,128)S(1)} %reduce_sum.9.i0) | copy-start | bytes 49156
  36.0 27.7 %copy-start.3 = (f32[512,256]{1,0:T(8,128)}, f32[512,256]{1,0:T(8,128)S(1)}, u32[]{:S(2)}) copy-start(f32[512,256]{1,0:T(8,128)S(1)} %collective-permute-done.a1) | copy-start | bytes 1572868
  36.1 27.7 %copy-start.4 = (f32[512,256]{1,0:T(8,128)}, f32[512,256]{1,0:T(8,128)S(1)}, u32[]{:S(2)}) copy-start(f32[512,256]{1,0:T(8,128)S(1)} %collective-permute-done.1.a2) | copy-start | bytes 1572868
  36.1 16.3 %collective-permute-start.3 = (f32[272,256]{1,0:T(8,128)S(1)}, f32[272,256]{1,0:T(8,128)S(1)}, u32[]{:S(2)}, u32[]{:S(2)}) collective-permute-start(f32[272,256]{1,0:T(8,128)S(1)} %get-tuple-element.79), channel_id=1, source_target_pairs={{0,1},{1,2},{2,3},{3,0},{4,5},{5,6},{6,7},{7,4},{8,9},{9,10},{10,1... | collective-permute-start | bytes 835592 | tf_op jit(solution)/shard_map/ppermute | solution.py:294
  37.2 15.2 %collective-permute-start.4 = (f32[272,256]{1,0:T(8,128)S(1)}, f32[272,256]{1,0:T(8,128)S(1)}, u32[]{:S(2)}, u32[]{:S(2)}) collective-permute-start(f32[272,256]{1,0:T(8,128)S(1)} %get-tuple-element.78), channel_id=1, source_target_pairs={{0,2},{1,3},{2,0},{3,1},{4,6},{5,7},{6,4},{7,5},{8,10},{9,11},{10,... | collective-permute-start | bytes 835592 | tf_op jit(solution)/shard_map/ppermute | solution.py:294
  37.7 15.4 %collective-permute-start.5 = (f32[272,256]{1,0:T(8,128)S(1)}, f32[272,256]{1,0:T(8,128)S(1)}, u32[]{:S(2)}, u32[]{:S(2)}) collective-permute-start(f32[272,256]{1,0:T(8,128)S(1)} %get-tuple-element.77), channel_id=1, source_target_pairs={{0,3},{1,0},{2,1},{3,2},{4,7},{5,4},{6,5},{7,6},{8,11},{9,8},{10,9... | collective-permute-start | bytes 835592 | tf_op jit(solution)/shard_map/ppermute | solution.py:294
  58.6 14.8 %collective-permute-start.8 = (f32[272,256]{1,0:T(8,128)S(1)}, f32[272,256]{1,0:T(8,128)S(1)}, u32[]{:S(2)}, u32[]{:S(2)}) collective-permute-start(f32[272,256]{1,0:T(8,128)S(1)} %pad_maximum_fusion.5), channel_id=1, source_target_pairs={{0,3},{1,0},{2,1},{3,2},{4,7},{5,4},{6,5},{7,6},{8,11},{9,8},{10,9... | collective-permute-start | bytes 835592 | tf_op jit(solution)/shard_map/ppermute | solution.py:294
  62.0 11.4 %collective-permute-start.7 = (f32[272,256]{1,0:T(8,128)S(1)}, f32[272,256]{1,0:T(8,128)S(1)}, u32[]{:S(2)}, u32[]{:S(2)}) collective-permute-start(f32[272,256]{1,0:T(8,128)S(1)} %pad_maximum_fusion.4), channel_id=1, source_target_pairs={{0,2},{1,3},{2,0},{3,1},{4,6},{5,7},{6,4},{7,5},{8,10},{9,11},{10,... | collective-permute-start | bytes 835592 | tf_op jit(solution)/shard_map/ppermute | solution.py:294
  63.1 14.8 %collective-permute-start.6 = (f32[272,256]{1,0:T(8,128)S(1)}, f32[272,256]{1,0:T(8,128)S(1)}, u32[]{:S(2)}, u32[]{:S(2)}) collective-permute-start(f32[272,256]{1,0:T(8,128)S(1)} %pad_maximum_fusion.3), channel_id=1, source_target_pairs={{0,1},{1,2},{2,3},{3,0},{4,5},{5,6},{6,7},{7,4},{8,9},{9,10},{10,1... | collective-permute-start | bytes 835592 | tf_op jit(solution)/shard_map/ppermute | solution.py:294
  85.3 11.3 %collective-permute-start.10 = (f32[272,256]{1,0:T(8,128)}, f32[272,256]{1,0:T(8,128)S(1)}, u32[]{:S(2)}, u32[]{:S(2)}) collective-permute-start(f32[272,256]{1,0:T(8,128)} %get-tuple-element.52.m0), channel_id=1, source_target_pairs={{0,2},{1,3},{2,0},{3,1},{4,6},{5,7},{6,4},{7,5},{8,10},{9,11},{10,... | collective-permute-start | bytes 835592 | tf_op jit(solution)/shard_map/ppermute | solution.py:294
  85.5 12.9 %collective-permute-start.11 = (f32[272,256]{1,0:T(8,128)}, f32[272,256]{1,0:T(8,128)S(1)}, u32[]{:S(2)}, u32[]{:S(2)}) collective-permute-start(f32[272,256]{1,0:T(8,128)} %get-tuple-element.52.m0), channel_id=1, source_target_pairs={{0,3},{1,0},{2,1},{3,2},{4,7},{5,4},{6,5},{7,6},{8,11},{9,8},{10,9... | collective-permute-start | bytes 835592 | tf_op jit(solution)/shard_map/ppermute | solution.py:294
  86.8 14.8 %collective-permute-start.9 = (f32[272,256]{1,0:T(8,128)}, f32[272,256]{1,0:T(8,128)S(1)}, u32[]{:S(2)}, u32[]{:S(2)}) collective-permute-start(f32[272,256]{1,0:T(8,128)} %get-tuple-element.52.m0), channel_id=1, source_target_pairs={{0,1},{1,2},{2,3},{3,0},{4,5},{5,6},{6,7},{7,4},{8,9},{9,10},{10,1... | collective-permute-start | bytes 835592 | tf_op jit(solution)/shard_map/ppermute | solution.py:294
  96.5 5.0 %copy-start.15 = (f32[272,256]{1,0:T(8,128)}, f32[272,256]{1,0:T(8,128)S(1)}, u32[]{:S(2)}) copy-start(f32[272,256]{1,0:T(8,128)S(1)} %collective-permute-done.10.m2) | copy-start | bytes 835588
  105.4 1.8 %collective-permute-start.12 = (f32[272,256]{1,0:T(8,128)}, f32[272,256]{1,0:T(8,128)S(1)}, u32[]{:S(2)}, u32[]{:S(2)}) collective-permute-start(f32[272,256]{1,0:T(8,128)} %get-tuple-element.53.own), channel_id=1, source_target_pairs={{0,4},{4,0},{8,12},{12,8},{16,20},{20,16},{24,28},{28,24},{32,36},... | collective-permute-start | bytes 835592 | tf_op jit(solution)/shard_map/ppermute | solution.py:363
  110.1 9.8 %collective-permute-start.13 = (f32[272,256]{1,0:T(8,128)}, f32[272,256]{1,0:T(8,128)S(1)}, u32[]{:S(2)}, u32[]{:S(2)}) collective-permute-start(f32[272,256]{1,0:T(8,128)} %get-tuple-element.55.m0), channel_id=1, source_target_pairs={{0,8},{8,16},{16,24},{24,0},{32,40},{40,48},{48,56},{56,32},{64,72... | collective-permute-start | bytes 835592 | tf_op jit(solution)/shard_map/ppermute | solution.py:369
  112.8 10.2 %collective-permute-start.14 = (f32[272,256]{1,0:T(8,128)}, f32[272,256]{1,0:T(8,128)S(1)}, u32[]{:S(2)}, u32[]{:S(2)}) collective-permute-start(f32[272,256]{1,0:T(8,128)} %get-tuple-element.55.m0), channel_id=1, source_target_pairs={{0,16},{8,24},{16,0},{24,8},{32,48},{40,56},{48,32},{56,40},{64,80... | collective-permute-start | bytes 835592 | tf_op jit(solution)/shard_map/ppermute | solution.py:369
  117.0 8.7 %collective-permute-start.15 = (f32[272,256]{1,0:T(8,128)}, f32[272,256]{1,0:T(8,128)S(1)}, u32[]{:S(2)}, u32[]{:S(2)}) collective-permute-start(f32[272,256]{1,0:T(8,128)} %get-tuple-element.55.m0), channel_id=1, source_target_pairs={{0,24},{8,0},{16,8},{24,16},{32,56},{40,32},{48,40},{56,48},{64,88... | collective-permute-start | bytes 835592 | tf_op jit(solution)/shard_map/ppermute | solution.py:369
  119.9 5.8 %copy-start.8 = (f32[272,256]{1,0:T(8,128)}, f32[272,256]{1,0:T(8,128)S(1)}, u32[]{:S(2)}) copy-start(f32[272,256]{1,0:T(8,128)S(1)} %collective-permute-done.13.m1) | copy-start | bytes 835588
  129.4 8.6 %collective-permute-start.16 = (f32[272,256]{1,0:T(8,128)}, f32[272,256]{1,0:T(8,128)S(1)}, u32[]{:S(2)}, u32[]{:S(2)}) collective-permute-start(f32[272,256]{1,0:T(8,128)} %get-tuple-element.56.m0), channel_id=1, source_target_pairs={{0,32},{8,40},{16,48},{24,56},{32,64},{40,72},{48,80},{56,88},{64,... | collective-permute-start | bytes 835592 | tf_op jit(solution)/shard_map/ppermute | solution.py:374
  130.7 10.2 %collective-permute-start.17 = (f32[272,256]{1,0:T(8,128)}, f32[272,256]{1,0:T(8,128)S(1)}, u32[]{:S(2)}, u32[]{:S(2)}) collective-permute-start(f32[272,256]{1,0:T(8,128)} %get-tuple-element.56.m0), channel_id=1, source_target_pairs={{0,64},{8,72},{16,80},{24,88},{32,96},{40,104},{48,112},{56,120},{... | collective-permute-start | bytes 835592 | tf_op jit(solution)/shard_map/ppermute | solution.py:374
  132.0 12.0 %collective-permute-start.18 = (f32[272,256]{1,0:T(8,128)}, f32[272,256]{1,0:T(8,128)S(1)}, u32[]{:S(2)}, u32[]{:S(2)}) collective-permute-start(f32[272,256]{1,0:T(8,128)} %get-tuple-element.56.m0), channel_id=1, source_target_pairs={{0,96},{8,104},{16,112},{24,120},{1,97},{9,105},{17,113},{25,121},... | collective-permute-start | bytes 835592 | tf_op jit(solution)/shard_map/ppermute | solution.py:374
  138.0 5.9 %copy-start.11 = (f32[272,256]{1,0:T(8,128)}, f32[272,256]{1,0:T(8,128)S(1)}, u32[]{:S(2)}) copy-start(f32[272,256]{1,0:T(8,128)S(1)} %collective-permute-done.16.m1) | copy-start | bytes 835588
  147.4 2.3 %collective-permute-start.19 = (f32[16,256]{1,0:T(8,128)}, f32[16,256]{1,0:T(8,128)S(1)}, u32[]{:S(2)}, u32[]{:S(2)}) collective-permute-start(f32[16,256]{1,0:T(8,128)} %shard_map.72.mine), channel_id=1, source_target_pairs={{0,4},{8,12},{16,20},{24,28},{32,36},{40,44},{48,52},{56,60},{64,6... | collective-permute-start | bytes 49160 | tf_op jit(solution)/shard_map/ppermute | solution.py:386
  154.3 5.1 %collective-permute-start.20 = (f32[16,64]{1,0:T(8,128)}, f32[16,64]{1,0:T(8,128)S(1)}, u32[]{:S(2)}, u32[]{:S(2)}) collective-permute-start(f32[16,64]{1,0:T(8,128)} %get-tuple-element.62), channel_id=1, source_target_pairs={{0,1},{1,2},{2,3},{3,0},{4,5},{5,6},{6,7},{7,4},{8,9},{9,10},{10,1... | collective-permute-start | bytes 12296 | tf_op jit(solution)/shard_map/ppermute | solution.py:294
  154.3 5.4 %collective-permute-start.21 = (f32[16,64]{1,0:T(8,128)}, f32[16,64]{1,0:T(8,128)S(1)}, u32[]{:S(2)}, u32[]{:S(2)}) collective-permute-start(f32[16,64]{1,0:T(8,128)} %get-tuple-element.63), channel_id=1, source_target_pairs={{0,2},{1,3},{2,0},{3,1},{4,6},{5,7},{6,4},{7,5},{8,10},{9,11},{10,... | collective-permute-start | bytes 12296 | tf_op jit(solution)/shard_map/ppermute | solution.py:294
  156.6 3.9 %collective-permute-start.22 = (f32[16,64]{1,0:T(8,128)}, f32[16,64]{1,0:T(8,128)S(1)}, u32[]{:S(2)}, u32[]{:S(2)}) collective-permute-start(f32[16,64]{1,0:T(8,128)} %get-tuple-element.64), channel_id=1, source_target_pairs={{0,3},{1,0},{2,1},{3,2},{4,7},{5,4},{6,5},{7,6},{8,11},{9,8},{10,9... | collective-permute-start | bytes 12296 | tf_op jit(solution)/shard_map/ppermute | solution.py:294
  (17 other events, 26.9 us)

commit v3 on v2

--- a/solution.py
+++ b/solution.py
@@ -1,5 +1,3 @@
-import functools
-
 import jax
 import jax.numpy as jnp
 from jax import lax
@@ -9,7 +7,7 @@
 
 F32 = jnp.float32
 BF16 = jnp.bfloat16
-PARAMS = pltpu.CompilerParams(vmem_limit_bytes=56 * 1024 * 1024)
+PARAMS = pltpu.CompilerParams(vmem_limit_bytes=24 * 1024 * 1024)
 VM = pl.BlockSpec(memory_space=pltpu.VMEM)
 SM = pl.BlockSpec(memory_space=pltpu.SMEM)
 N = 256
@@ -17,7 +15,10 @@
 R = N + PAD
 ROWS = 4
 SUB = 16
-SEG = 4
+CHUNKS = ((5, 5), (3,), (3,))
+SEGS = tuple(n for chunk in CHUNKS for n in chunk)
+SIZES = tuple(sum(chunk) for chunk in CHUNKS)
+ENDS = tuple(sum(SEGS[: i + 1]) for i in range(len(SEGS)))
 
 
 def split(x):
@@ -54,16 +55,20 @@
     return jnp.where(r == c, 1.0, 0.0).astype(F32)
 
 
-def call(kernel, outs, args, specs=None, scratch=(), **kw):
+def near(x):
+    return pltpu.with_memory_space_constraint(x, pltpu.VMEM)
+
+
+def call(kernel, outs, scalars, args, scratch=(), far=()):
+    outs = [o if isinstance(o[0], tuple) else (o, F32) for o in outs]
     return pl.pallas_call(
         kernel,
-        out_shape=[jax.ShapeDtypeStruct(s, F32) for s in outs],
-        in_specs=specs,
+        out_shape=[pltpu.VMEM(s, t) for s, t in outs],
+        in_specs=[SM] * len(scalars) + [VM] * (len(far) + len(args)),
         out_specs=[VM] * len(outs),
         scratch_shapes=list(scratch),
         compiler_params=PARAMS,
-        **kw,
-    )(*args)
+    )(*scalars, *far, *[near(a) for a in args])
 
 
 BIN_M = 256
@@ -130,14 +135,15 @@
     return dot_nt(xh, ah) + dot_nt(xl, ah) + dot_nt(xh, al)
 
 
-def chains(ah, al, pref):
-    n_chains = ah.shape[0] // SEG
+def chains(lengths, ah, al, pref):
     eye = jnp.where(
         lax.broadcasted_iota(jnp.int32, (N, N), 0) == lax.broadcasted_iota(jnp.int32, (N, N), 1), 1.0, 0.0
     ).astype(BF16)
-    for t in range(SEG):
-        for c in range(n_chains):
-            k = c * SEG + t
+    for t in range(max(lengths)):
+        for c, length in enumerate(lengths):
+            if t >= length:
+                continue
+            k = sum(lengths[:c]) + t
             if t == 0:
                 pref[k] = dot_nt(eye, ah[k]) + dot_nt(eye, al[k])
             else:
@@ -146,14 +152,14 @@
 
 def first_kernel(z_ref, a0, a1, a2, a3, pref, ah, al, both):
     assemble(z_ref[0], (a0, a1, a2, a3), ah, al)
-    chains(ah, al, pref)
-    both[...] = mm(pref[SEG - 1], pref[2 * SEG - 1])
+    chains(CHUNKS[0], ah, al, pref)
+    both[...] = mm(pref[CHUNKS[0][0] - 1], pref[SIZES[0] - 1])
 
 
 def second_kernel(z_ref, a0, a1, a2, a3, both, pref, ah, al, three):
     assemble(z_ref[0], (a0, a1, a2, a3), ah, al)
-    chains(ah, al, pref)
-    three[...] = mm(both[...], pref[SEG - 1])
+    chains(CHUNKS[1], ah, al, pref)
+    three[...] = mm(both[...], pref[SIZES[1] - 1])
 
 
 def third_kernel(
@@ -163,29 +169,32 @@
     assemble(z, (a0, a1, a2, a3), ah, al)
     b_s[z] = b0[...]
     for d, a in ((1, a1), (2, a2), (3, a3)):
-        b_s[lax.rem(z - d + ROWS, ROWS)] = a[SEG * 64 :, :]
+        b_s[lax.rem(z - d + ROWS, ROWS)] = a[SIZES[2] * 64 :, :]
     b = jnp.concatenate([b_s[i, :, :64] for i in range(ROWS)], axis=1)
     first = lax.broadcasted_iota(jnp.int32, (PAD, N), 0) == 0
 
     def row(k):
         return jnp.where(first, b[k : k + 1, :], 0.0)
 
-    mats = [(ah01, al01, i) for i in range(2 * SEG)] + [(ah2, al2, i) for i in range(SEG)]
-    mats += [(ah, al, i) for i in range(SEG)]
-    p = [row(c * SEG) for c in range(SUB // SEG)]
-    for c in range(SUB // SEG):
-        shifts[c * SEG : c * SEG + 1, :] = p[c][:1]
-    for t in range(1, SEG):
-        for c in range(SUB // SEG):
-            k = c * SEG + t
+    mats = [(ah01, al01, i) for i in range(SIZES[0])] + [(ah2, al2, i) for i in range(SIZES[1])]
+    mats += [(ah, al, i) for i in range(SIZES[2])]
+    starts = [end - n for end, n in zip(ENDS, SEGS)]
+    p = [row(k) for k in starts]
+    for c, k in enumerate(starts):
+        shifts[k : k + 1, :] = p[c][:1]
+    for t in range(1, max(SEGS)):
+        for c, start in enumerate(starts):
+            if t >= SEGS[c]:
+                continue
+            k = start + t
             h, l, i = mats[k]
             p[c] = by_step(p[c], h[i], l[i]) + row(k)
             shifts[k : k + 1, :] = p[c][:1]
-    chains(ah, al, pref)
-    v = mm(p[0], p01[2 * SEG - 1]) + p[1]
-    v = mm(v, p2[SEG - 1]) + p[2]
-    v = mm(v, pref[SEG - 1]) + p[3]
-    whole[:N, :] = mm(three[...], pref[SEG - 1])
+    chains(CHUNKS[2], ah, al, pref)
+    v = mm(p[0], p01[SIZES[0] - 1]) + p[1]
+    v = mm(v, p2[SIZES[1] - 1]) + p[2]
+    v = mm(v, pref[SIZES[2] - 1]) + p[3]
+    whole[:N, :] = mm(three[...], pref[SIZES[2] - 1])
     whole[N:, :] = v
 
 
@@ -241,26 +250,25 @@
     out[...] = apply(s_s[...], ybefore[...])
 
 
-def states_kernel(idx_ref, mine, other, before, p01, p2, p3, shifts, o0, o1, o2, o3, st_s, s_s):
-    z = idx_ref[0]
-    c = idx_ref[1]
+def states_kernel(z_ref, c_ref, mine, other, before, p01, p2, p3, shifts, o0, o1, o2, o3, st_s, s_s):
+    z = z_ref[0]
+    c = c_ref[0]
     s_s[...] = jnp.where(c == 0, mine[...], other[...])
     s = apply(s_s[...], before[...])
     eye = lax.broadcasted_iota(jnp.int32, (N, N), 0) == lax.broadcasted_iota(jnp.int32, (N, N), 1)
     first = lax.broadcasted_iota(jnp.int32, (PAD, N), 0) == 0
-    prefs = [(p01, i) for i in range(2 * SEG)] + [(p2, i) for i in range(SEG)] + [(p3, i) for i in range(SEG)]
-    for q in range(SUB // SEG):
+    prefs = [(p01, i) for i in range(SIZES[0])] + [(p2, i) for i in range(SIZES[1])]
+    prefs += [(p3, i) for i in range(SIZES[2])]
+    for end, n in zip(ENDS, SEGS):
         col = jnp.sum(jnp.where(eye, s[0:1, :], 0.0), axis=1, keepdims=True)
-        for t in range(SEG):
-            k = q * SEG + t
+        for k in range(end - n, end):
             m, i = prefs[k]
             row = jnp.sum(m[i] * col, axis=0, keepdims=True) + shifts[k : k + 1, :]
             for j in range(ROWS):
                 st_s[j, k : k + 1, :] = row[:, j * 64 : (j + 1) * 64]
-        if q < SUB // SEG - 1:
-            m, i = prefs[q * SEG + SEG - 1]
-            k = q * SEG + SEG - 1
-            s = mm(s, m[i]) + jnp.where(first, shifts[k : k + 1, :], 0.0)
+        if end < SUB:
+            m, i = prefs[end - 1]
+            s = mm(s, m[i]) + jnp.where(first, shifts[end - 1 : end, :], 0.0)
     for d, o in enumerate((o0, o1, o2, o3)):
         o[...] = st_s[lax.rem(z + d, ROWS)]
 
@@ -305,7 +313,8 @@
     def piece(d, start, count):
         return lax.dynamic_slice_in_dim(flat, ((z + d) % ROWS) * (SUB * 64) + start * 64, count * 64, 0)
 
-    part_a = [piece(0, 0, 8)] + [along_row(piece(d, 0, 8), d) for d in (1, 2, 3)]
+    at_b, at_c = SIZES[0], SIZES[0] + SIZES[1]
+    part_a = [piece(0, 0, SIZES[0])] + [along_row(piece(d, 0, SIZES[0]), d) for d in (1, 2, 3)]
 
     rid = owner[:, 0] * 16 + step % 16 + 512 * (step // 16)
     partial = binned(rid.reshape(1, -1), observed.T)
@@ -313,57 +322,45 @@
     info = jnp.sum(sums.reshape(32, 16, N), axis=0)
     info, *part_a = lax.optimization_barrier((info, *part_a))
 
-    sent_b = [jnp.concatenate([piece(d, 8, 4), info], axis=0) for d in (1, 2, 3)]
-    part_b = [piece(0, 8, 4)] + [along_row(sent_b[d - 1], d) for d in (1, 2, 3)]
-    p01, ah01, al01, both = pl.pallas_call(
+    sent_b = [jnp.concatenate([piece(d, at_b, SIZES[1]), info], axis=0) for d in (1, 2, 3)]
+    part_b = [piece(0, at_b, SIZES[1])] + [along_row(sent_b[d - 1], d) for d in (1, 2, 3)]
+    p01, ah01, al01, both = call(
         first_kernel,
-        out_shape=[
-            jax.ShapeDtypeStruct((8, N, N), F32),
-            jax.ShapeDtypeStruct((8, N, N), BF16),
-            jax.ShapeDtypeStruct((8, N, N), BF16),
-            jax.ShapeDtypeStruct((N, N), F32),
-        ],
-        in_specs=[SM] + [VM] * 4,
-        out_specs=[VM] * 4,
-        compiler_params=PARAMS,
-    )(z1, *part_a)
+        [(SIZES[0], N, N), ((SIZES[0], N, N), BF16), ((SIZES[0], N, N), BF16), (N, N)],
+        (z1,),
+        part_a,
+    )
+    p01, ah01, al01, both, *part_b = lax.optimization_barrier((p01, ah01, al01, both, *part_b))
     offs = call(
         offset_kernel,
         [(16, N)] * 4,
-        (z1, gains, info, *part_b[1:]),
-        [SM] + [VM] * 5,
+        (z1,),
+        (info, *part_b[1:]),
         [pltpu.VMEM((ROWS, 16, N), F32), pltpu.VMEM((ROWS, 16, 128), F32)],
-    )
-    sent_c = [jnp.concatenate([piece(d, 12, 4), offs[d]], axis=0) for d in (1, 2, 3)]
-    part_c = [piece(0, 12, 4)] + [along_row(sent_c[d - 1], d) for d in (1, 2, 3)]
-    p2, ah2, al2, three = pl.pallas_call(
+        far=(gains,),
+    )
+    sent_c = [jnp.concatenate([piece(d, at_c, SIZES[2]), offs[d]], axis=0) for d in (1, 2, 3)]
+    part_c = [piece(0, at_c, SIZES[2])] + [along_row(sent_c[d - 1], d) for d in (1, 2, 3)]
+    p2, ah2, al2, three = call(
         second_kernel,
-        out_shape=[
-            jax.ShapeDtypeStruct((4, N, N), F32),
-            jax.ShapeDtypeStruct((4, N, N), BF16),
-            jax.ShapeDtypeStruct((4, N, N), BF16),
-            jax.ShapeDtypeStruct((N, N), F32),
-        ],
-        in_specs=[SM] + [VM] * 5,
-        out_specs=[VM] * 4,
-        compiler_params=PARAMS,
-    )(z1, *part_b, both)
+        [(SIZES[1], N, N), ((SIZES[1], N, N), BF16), ((SIZES[1], N, N), BF16), (N, N)],
+        (z1,),
+        (*part_b, both),
+    )
     p3, shifts, whole = call(
         third_kernel,
-        [(4, N, N), (SUB, N), (R, N)],
-        (z1, *part_c, offs[0], p01, ah01, al01, p2, ah2, al2, three),
-        [SM] + [VM] * 12,
-        [pltpu.VMEM((4, N, N), BF16), pltpu.VMEM((4, N, N), BF16), pltpu.VMEM((ROWS, 16, N), F32)],
-    )
-
-    four = functools.partial(
-        call, four_kernel, [(R, N), (R, N)], specs=[SM] + [VM] * 4, scratch=[pltpu.VMEM((4, R, N), F32)]
-    )
-    block, before = four(args=(z1, whole, *[along_row(whole, d) for d in (1, 2, 3)]))
+        [(SIZES[2], N, N), (SUB, N), (R, N)],
+        (z1,),
+        (*part_c, offs[0], p01, ah01, al01, p2, ah2, al2, three),
+        [pltpu.VMEM((SIZES[2], N, N), BF16)] * 2 + [pltpu.VMEM((ROWS, 16, N), F32)],
+    )
+
+    def four(pos, maps):
+        return call(four_kernel, [(R, N), (R, N)], (pos.reshape(1),), maps, [pltpu.VMEM((4, R, N), F32)])
+
+    block, before = four(z, [whole] + [along_row(whole, d) for d in (1, 2, 3)])
     swapped = lax.ppermute(block, "tm", [(i, i ^ 1) for i in range(32)])
-    column, before = call(
-        pair_kernel, [(R, N), (R, N)], (c.reshape(1), block, swapped, before), [SM] + [VM] * 3
-    )
+    column, before = call(pair_kernel, [(R, N), (R, N)], (c.reshape(1),), (block, swapped, before))
 
     def along_y(m, d):
         return lax.ppermute(
@@ -375,24 +372,30 @@
             m, "tm", [(8 * i + 2 * j, 8 * (i + d) + 2 * j) for i in range(4 - d) for j in range(4)]
         )
 
-    plane, ybefore = four(args=(y.reshape(1), column, *[along_y(column, d) for d in (1, 2, 3)]))
+    plane, ybefore = four(y, [column] + [along_y(column, d) for d in (1, 2, 3)])
     (entry,) = call(
         top_kernel,
         [(PAD, N)],
-        (x.reshape(1), prior.reshape(1, N), plane, *[along_x(plane, d) for d in (1, 2, 3)], ybefore),
-        [SM] + [VM] * 6,
+        (x.reshape(1),),
+        (prior.reshape(1, N), plane, *[along_x(plane, d) for d in (1, 2, 3)], ybefore),
         [pltpu.VMEM((4, R, N), F32), pltpu.VMEM((PAD, N), F32)],
     )
     handed = lax.ppermute(entry, "tm", [(2 * i, 2 * i + 1) for i in range(16)])
     outs = call(
         states_kernel,
         [(SUB, 64)] * 4,
-        (jnp.stack([z, c]), entry, handed, before, p01, p2, p3, shifts),
-        [SM] + [VM] * 7,
+        (z1, c.reshape(1)),
+        (entry, handed, before, p01, p2, p3, shifts),
         [pltpu.VMEM((ROWS, SUB, 64), F32), pltpu.VMEM((PAD, N), F32)],
     )
     got = [outs[0]] + [along_row(outs[d], d) for d in (1, 2, 3)]
-    (states,) = call(place_kernel, [(64, 64)], (z1, *got), [SM] + [VM] * 4)
+    states = pl.pallas_call(
+        place_kernel,
+        out_shape=jax.ShapeDtypeStruct((64, 64), F32),
+        in_specs=[SM] + [VM] * 4,
+        out_specs=VM,
+        compiler_params=PARAMS,
+    )(z1, *[near(g) for g in got])
     return states
 
 

time: 163 us -> 148 us (0.908)
  Pallas kernels: 43.9 us -> 25.8 us
  local copies, waits for them, and re-layouts: 11 us -> 17.8 us
  waiting for transfers between devices: 61.9 us -> 56.7 us
  starting transfers between devices: 41.8 us -> 46.9 us
  other arithmetic: 3.61 us -> 0.18 us
    pallas_call x10, Pallas kernels: 35 us -> 18.1 us  [the longest x9 17.5 us: call(): pl.pallas_call(kernel, out_shape=[pltpu.VMEM(s, t) for s, t in outs], in_...]
    unnamed x50 -> x42, local copies, waits for them, and re-layouts: 5.5 us -> 12.3 us
    ppermute x15, waiting for transfers between devices: 36.2 us -> 30.3 us  [along_row(): return lax.ppermute(x, 'row', [(i, (i + d) % ROWS) for i in range(ROWS)])]
    ppermute x15, starting transfers between devices: 19.6 us -> 22.5 us  [along_row(): return lax.ppermute(x, 'row', [(i, (i + d) % ROWS) for i in range(ROWS)])]
    ppermute x3, starting transfers between devices: 9.37 us -> 11.5 us  [along_y(): lax.ppermute(m, 'tm', [(8 * i + 2 * j, 8 * i + 2 * ((j + d) % 4)) for i i...]
    concatenate x4, other arithmetic: 2.27 us -> 0.09 us  [the longest x1 0.05 us: shards(): jnp.concatenate([piece(d, at_b, SIZES[1]), info], axis=0)]
  transfers between devices with their start and end apart: 24 -> 24, of which waited for: 19 -> 17; matrix products, arithmetic and copies ran while one was open for 3% -> 2% of each run, Pallas kernels for 10% -> 8%
where the time goes in v3:
time: 148 us
  waiting for transfers between devices  56.7 us (38%)
  starting transfers between devices  46.9 us (32%)
  Pallas kernels  25.8 us (17%)
  local copies, waits for them, and re-layouts  17.8 us (12%)
    ppermute x15, waiting for transfers between devices, along_row(): return lax.ppermute(x, 'row', [(i, (i + d) % ROWS) for i in range(ROWS)])  30.3 us
    ppermute x15, starting transfers between devices, along_row(): return lax.ppermute(x, 'row', [(i, (i + d) % ROWS) for i in range(ROWS)])  22.5 us
    pallas_call x9, Pallas kernels, call(): pl.pallas_call(kernel, out_shape=[pltpu.VMEM(s, t) for s, t in outs], in_...  17.5 us
    unnamed x42, local copies, waits for them, and re-layouts  12.3 us
    ppermute x3, starting transfers between devices, along_y(): lax.ppermute(m, 'tm', [(8 * i + 2 * j, 8 * i + 2 * ((j + d) % 4)) for i i...  11.5 us
    ppermute x3, waiting for transfers between devices, along_x(): lax.ppermute(m, 'tm', [(8 * i + 2 * j, 8 * (i + d) + 2 * j) for i in rang...  11.4 us
    pallas_call x1, Pallas kernels, binned(): pl.pallas_call(bin_kernel, out_shape=jax.ShapeDtypeStruct((n_bins // 4, N...  7.7 us
    all_to_all x1, starting transfers between devices, shards(): sums = lax.all_to_all(partial, 'tm', 0, 0, tiled=True)  7.61 us
  transfers between devices with their start and end apart: 24, of which 17 were waited for; matrix products, arithmetic and copies ran while one was open for 2% of the time, Pallas kernels for 8%

profile of v3, /device:TPU:6, one launch (start us, length us, event | category | flops | bytes accessed | tf_op | source)
XLA Modules:
  0.0 147.7 jit_solution(9061599287505770394)
XLA Ops:
  0.1 3.1 %constant_dynamic-slice_fusion.6 = (f32[640,256]{1,0:T(8,128)}, f32[640,256]{1,0:T(8,128)}, f32[640,256]{1,0:T(8,128)}, f32[640,256]{1,0:T(8,128)S(1)}) fusion(f32[4096,256]{1,0:T(8,128)} %bitcast.13, s32[]{:T(128)S(6)} %select_n.112, s32[]{:T(128)S(6)} %select_n.110, s32[]{:T(128)S(6)} %select_n.108, s32[]{:T(128)S(6)} %select_n.107), kind=kLoop, calls=%fused_computation.26 | loop fusion | bytes 5242896 | tf_op jit(solution)/shard_map/dynamic_slice | solution.py:314
  3.2 1.9 %collective-permute-start = (f32[640,256]{1,0:T(8,128)}, f32[640,256]{1,0:T(8,128)S(1)}, u32[]{:S(2)}, u32[]{:S(2)}) collective-permute-start(f32[640,256]{1,0:T(8,128)} %get-tuple-element.91), channel_id=1, source_target_pairs={{0,1},{1,2},{2,3},{3,0},{4,5},{5,6},{6,7},{7,4},{8,9},{9,10},{10,1... | collective-permute-start | bytes 1966088 | tf_op jit(solution)/shard_map/ppermute | solution.py:302
  5.1 3.6 %collective-permute-start.1 = (f32[640,256]{1,0:T(8,128)}, f32[640,256]{1,0:T(8,128)S(1)}, u32[]{:S(2)}, u32[]{:S(2)}) collective-permute-start(f32[640,256]{1,0:T(8,128)} %get-tuple-element.90), channel_id=1, source_target_pairs={{0,2},{1,3},{2,0},{3,1},{4,6},{5,7},{6,4},{7,5},{8,10},{9,11},{10,... | collective-permute-start | bytes 1966088 | tf_op jit(solution)/shard_map/ppermute | solution.py:302
  9.7 7.7 %shard_map.64 = f32[512,256]{1,0:T(8,128)} custom-call(s32[1,4096]{1,0:T(1,128)S(1)} %bitcast.11, f32[64,4096]{1,0:T(8,128)S(1)} %bitcast.10), custom_call_target="tpu_custom_call" | custom-call | tf_op jit(solution)/shard_map/pallas_call | solution.py:109
  17.4 7.6 %all-to-all-start = ((f32[32,16,256]{2,1,0:T(8,128)}), f32[32,16,256]{2,1,0:T(8,128)S(1)}, u32[]{:S(2)}, u32[]{:S(2)}) async-start(f32[32,16,256]{2,1,0:T(8,128)} %bitcast.9), calls=%async_computation | async-start | bytes 1048576 | tf_op jit(solution)/shard_map/all_to_all | solution.py:321
  25.1 2.4 %constant_dynamic-slice_fusion = (f32[192,256]{1,0:T(8,128)S(1)}, f32[192,256]{1,0:T(8,128)}, f32[192,256]{1,0:T(8,128)S(1)}, f32[192,256]{1,0:T(8,128)S(1)}, f3...) fusion(f32[4096,256]{1,0:T(8,128)} %bitcast.14, s32[]{:T(128)S(6)} %select_n.118, ...), kind=kLoop, calls=%fused_computation.20 | loop fusion | bytes 3145760 | tf_op jit(solution)/shard_map/dynamic_slice | solution.py:314
  27.6 6.8 %all-to-all-done = f32[32,16,256]{2,1,0:T(8,128)S(1)} async-done(((f32[32,16,256]{2,1,0:T(8,128)}), f32[32,16,256]{2,1,0:T(8,128)S(1)}, u32[]{:S(2)}, u32[]{:S(2)}) %all-to-all-start) | async-done | bytes 524320 | tf_op jit(solution)/shard_map/all_to_all | solution.py:321
  34.4 3.0 %collective-permute-done.1.a2 = f32[640,256]{1,0:T(8,128)S(1)} collective-permute-done((f32[640,256]{1,0:T(8,128)}, f32[640,256]{1,0:T(8,128)S(1)}, u32[]{:S(2)}, u32[]{:S(2)}) %collective-permute-start.1) | collective-permute-done | bytes 655392 | tf_op jit(solution)/shard_map/ppermute | solution.py:302
  38.8 2.4 %collective-permute-start.4 = (f32[208,256]{1,0:T(8,128)S(1)}, f32[208,256]{1,0:T(8,128)S(1)}, u32[]{:S(2)}, u32[]{:S(2)}) collective-permute-start(f32[208,256]{1,0:T(8,128)S(1)} %get-tuple-element.94), channel_id=1, source_target_pairs={{0,2},{1,3},{2,0},{3,1},{4,6},{5,7},{6,4},{7,5},{8,10},{9,11},{10,... | collective-permute-start | bytes 638984 | tf_op jit(solution)/shard_map/ppermute | solution.py:302
  44.7 3.1 %shard_map.65 = (f32[10,256,256]{2,1,0:T(8,128)S(1)}, bf16[10,256,256]{2,1,0:T(8,128)(2,1)S(1)}, bf16[10,256,256]{2,1,0:T(8,128)(2,1)S(1)}, f32[256,256]{1,0:T(8,128)S(1)}) custom-call(s32[1]{0:T(128)} %bitcast.z_ref.pos_ref, f32[640,256]{1,0:T(8,128)S(1)} %get-tuple-element.44.a0, f32[640,256]{1,0:T(8,128)S(1)} %copy-done.7, f32[640,256]{1,0:T(8,128)S(1)} %copy-done.9, ...), custom_call_target="tpu_custom_call" | custom-call | tf_op jit(solution)/shard_map/pallas_call | solution.py:64
  47.8 3.1 %collective-permute-done.4.r2.a2 = f32[208,256]{1,0:T(8,128)S(1)} collective-permute-done((f32[208,256]{1,0:T(8,128)S(1)}, f32[208,256]{1,0:T(8,128)S(1)}, u32[]{:S(2)}, u32[]{:S(2)}) %collective-permute-start.4) | collective-permute-done | bytes 213024 | tf_op jit(solution)/shard_map/ppermute | solution.py:302
  50.9 2.2 %copy-done = f32[64,64,256]{2,1,0:T(8,128)S(1)} copy-done((f32[64,64,256]{2,1,0:T(8,128)S(1)}, f32[64,64,256]{2,1,0:T(8,128)}, u32[]{:S(2)}) %copy-start) | copy-done | bytes 4194328
  54.9 3.5 %collective-permute-start.7 = (f32[208,256]{1,0:T(8,128)S(1)}, f32[208,256]{1,0:T(8,128)S(1)}, u32[]{:S(2)}, u32[]{:S(2)}) collective-permute-start(f32[208,256]{1,0:T(8,128)S(1)} %pad_maximum_fusion.4), channel_id=1, source_target_pairs={{0,2},{1,3},{2,0},{3,1},{4,6},{5,7},{6,4},{7,5},{8,10},{9,11},{10,... | collective-permute-start | bytes 638984 | tf_op jit(solution)/shard_map/ppermute | solution.py:302
  59.7 2.3 %collective-permute-done.6.a1 = f32[208,256]{1,0:T(8,128)S(1)} collective-permute-done((f32[208,256]{1,0:T(8,128)S(1)}, f32[208,256]{1,0:T(8,128)S(1)}, u32[]{:S(2)}, u32[]{:S(2)}) %collective-permute-start.6) | collective-permute-done | bytes 213024 | tf_op jit(solution)/shard_map/ppermute | solution.py:302
  62.0 5.7 %collective-permute-done.7.a2 = f32[208,256]{1,0:T(8,128)S(1)} collective-permute-done((f32[208,256]{1,0:T(8,128)S(1)}, f32[208,256]{1,0:T(8,128)S(1)}, u32[]{:S(2)}, u32[]{:S(2)}) %collective-permute-start.7) | collective-permute-done | bytes 213024 | tf_op jit(solution)/shard_map/ppermute | solution.py:302
  67.8 2.7 %shard_map.68 = (f32[3,256,256]{2,1,0:T(8,128)S(1)}, f32[16,256]{1,0:T(8,128)S(1)}, f32[272,256]{1,0:T(8,128)S(1)}) custom-call(s32[1]{0:T(128)} %bitcast.z_ref.pos_ref, f32[192,256]{1,0:T(8,128)S(1)} %copy-done.5, f32[208,256]{1,0:T(8,128)S(1)} %collective-permute-done.6.a1, f32[208,256]{1,0:T(8,128)S(1)} %collective-permute-done.7.a2, ...), custom_call_target="tpu_custom_call" | custom-call | tf_op jit(solution)/shard_map/pallas_call | solution.py:64
  71.3 3.6 %collective-permute-start.10 = (f32[272,256]{1,0:T(8,128)S(1)}, f32[272,256]{1,0:T(8,128)S(1)}, u32[]{:S(2)}, u32[]{:S(2)}) collective-permute-start(f32[272,256]{1,0:T(8,128)S(1)} %get-tuple-element.68.m0), channel_id=1, source_target_pairs={{0,2},{1,3},{2,0},{3,1},{4,6},{5,7},{6,4},{7,5},{8,10},{9,11},{10,... | collective-permute-start | bytes 835592 | tf_op jit(solution)/shard_map/ppermute | solution.py:302
  75.0 5.4 %collective-permute-done.9.m1 = f32[272,256]{1,0:T(8,128)S(1)} collective-permute-done((f32[272,256]{1,0:T(8,128)S(1)}, f32[272,256]{1,0:T(8,128)S(1)}, u32[]{:S(2)}, u32[]{:S(2)}) %collective-permute-start.9) | collective-permute-done | bytes 278560 | tf_op jit(solution)/shard_map/ppermute | solution.py:302
  80.3 7.1 %collective-permute-done.10.m2 = f32[272,256]{1,0:T(8,128)S(1)} collective-permute-done((f32[272,256]{1,0:T(8,128)S(1)}, f32[272,256]{1,0:T(8,128)S(1)}, u32[]{:S(2)}, u32[]{:S(2)}) %collective-permute-start.10) | collective-permute-done | bytes 278560 | tf_op jit(solution)/shard_map/ppermute | solution.py:302
  92.7 2.0 %shard_map.70 = (f32[272,256]{1,0:T(8,128)}, f32[272,256]{1,0:T(8,128)S(1)}) custom-call(s32[1]{0:T(128)} %bitcast.1.c_ref, f32[272,256]{1,0:T(8,128)} %get-tuple-element.69.own, f32[272,256]{1,0:T(8,128)} %collective-permute-done.12.other, f32[272,256]{1,0:T(8,128)S(1)} %copy-done.15), custom_call_target="tpu_custom_call" | custom-call | tf_op jit(solution)/shard_map/pallas_call | solution.py:64
  95.4 3.5 %collective-permute-start.13 = (f32[272,256]{1,0:T(8,128)}, f32[272,256]{1,0:T(8,128)}, u32[]{:S(2)}, u32[]{:S(2)}) collective-permute-start(f32[272,256]{1,0:T(8,128)} %get-tuple-element.71.m0), channel_id=1, source_target_pairs={{0,8},{8,16},{16,24},{24,0},{32,40},{40,48},{48,56},{56,32},{64,72... | collective-permute-start | bytes 835592 | tf_op jit(solution)/shard_map/ppermute | solution.py:366
  98.9 4.8 %collective-permute-start.14 = (f32[272,256]{1,0:T(8,128)}, f32[272,256]{1,0:T(8,128)}, u32[]{:S(2)}, u32[]{:S(2)}) collective-permute-start(f32[272,256]{1,0:T(8,128)} %get-tuple-element.71.m0), channel_id=1, source_target_pairs={{0,16},{8,24},{16,0},{24,8},{32,48},{40,56},{48,32},{56,40},{64,80... | collective-permute-start | bytes 835592 | tf_op jit(solution)/shard_map/ppermute | solution.py:366
  103.7 3.3 %collective-permute-start.15 = (f32[272,256]{1,0:T(8,128)}, f32[272,256]{1,0:T(8,128)}, u32[]{:S(2)}, u32[]{:S(2)}) collective-permute-start(f32[272,256]{1,0:T(8,128)} %get-tuple-element.71.m0), channel_id=1, source_target_pairs={{0,24},{8,0},{16,8},{24,16},{32,56},{40,32},{48,40},{56,48},{64,88... | collective-permute-start | bytes 835592 | tf_op jit(solution)/shard_map/ppermute | solution.py:366
  107.0 2.6 %collective-permute-done.14.m2 = f32[272,256]{1,0:T(8,128)} collective-permute-done((f32[272,256]{1,0:T(8,128)}, f32[272,256]{1,0:T(8,128)}, u32[]{:S(2)}, u32[]{:S(2)}) %collective-permute-start.14) | collective-permute-done | bytes 278560 | tf_op jit(solution)/shard_map/ppermute | solution.py:366
  109.6 2.9 %collective-permute-done.15.m3 = f32[272,256]{1,0:T(8,128)} collective-permute-done((f32[272,256]{1,0:T(8,128)}, f32[272,256]{1,0:T(8,128)}, u32[]{:S(2)}, u32[]{:S(2)}) %collective-permute-start.15) | collective-permute-done | bytes 278560 | tf_op jit(solution)/shard_map/ppermute | solution.py:366
  112.4 2.9 %shard_map.71 = (f32[272,256]{1,0:T(8,128)}, f32[272,256]{1,0:T(8,128)S(1)}) custom-call(s32[1]{0:T(128)} %bitcast.4.pos_ref, f32[272,256]{1,0:T(8,128)} %get-tuple-element.71.m0, f32[272,256]{1,0:T(8,128)} %collective-permute-done.13.m1, f32[272,256]{1,0:T(8,128)} %collective-permute-done.14.m2, f32[272,256]{1,0:T(8,128)} %collective-permute-done.15.m3), custom_call_target="tpu_custom_call" | custom-call | tf_op jit(solution)/shard_map/pallas_call | solution.py:64
  119.9 4.8 %collective-permute-done.16.m1 = f32[272,256]{1,0:T(8,128)} collective-permute-done((f32[272,256]{1,0:T(8,128)}, f32[272,256]{1,0:T(8,128)}, u32[]{:S(2)}, u32[]{:S(2)}) %collective-permute-start.16) | collective-permute-done | bytes 278560 | tf_op jit(solution)/shard_map/ppermute | solution.py:371
  124.8 2.8 %collective-permute-done.17.m2 = f32[272,256]{1,0:T(8,128)} collective-permute-done((f32[272,256]{1,0:T(8,128)}, f32[272,256]{1,0:T(8,128)}, u32[]{:S(2)}, u32[]{:S(2)}) %collective-permute-start.17) | collective-permute-done | bytes 278560 | tf_op jit(solution)/shard_map/ppermute | solution.py:371
  127.6 3.8 %collective-permute-done.18.m3 = f32[272,256]{1,0:T(8,128)} collective-permute-done((f32[272,256]{1,0:T(8,128)}, f32[272,256]{1,0:T(8,128)}, u32[]{:S(2)}, u32[]{:S(2)}) %collective-permute-start.18) | collective-permute-done | bytes 278560 | tf_op jit(solution)/shard_map/ppermute | solution.py:371
  132.3 2.0 %shard_map.72.mine = f32[16,256]{1,0:T(8,128)S(1)} custom-call(s32[1]{0:T(128)} %bitcast.2.pos_ref, f32[1,256]{1,0:T(1,128)S(1)} %bitcast.12, f32[272,256]{1,0:T(8,128)} %get-tuple-element.72.m0, f32[272,256]{1,0:T(8,128)} %collective-permute-done.16.m1, f32[272,256]{1,0:T(8,128)} %collective-permute-done.17.m2, f32[272,256]{1,0:T(8,128)} %collective-permute-done.18.m3, ...), custom_call_target="tpu_custom_call" | custom-call | tf_op jit(solution)/shard_map/pallas_call | solution.py:64
  139.7 3.8 %collective-permute-start.21 = (f32[16,64]{1,0:T(8,128)S(1)}, f32[16,64]{1,0:T(8,128)S(1)}, u32[]{:S(2)}, u32[]{:S(2)}) collective-permute-start(f32[16,64]{1,0:T(8,128)S(1)} %get-tuple-element.79), channel_id=1, source_target_pairs={{0,2},{1,3},{2,0},{3,1},{4,6},{5,7},{6,4},{7,5},{8,10},{9,11},{10,... | collective-permute-start | bytes 12296 | tf_op jit(solution)/shard_map/ppermute | solution.py:302
  145.2 1.9 %collective-permute-done.22.r3 = f32[16,64]{1,0:T(8,128)S(1)} collective-permute-done((f32[16,64]{1,0:T(8,128)S(1)}, f32[16,64]{1,0:T(8,128)S(1)}, u32[]{:S(2)}, u32[]{:S(2)}) %collective-permute-start.22) | collective-permute-done | bytes 4128 | tf_op jit(solution)/shard_map/ppermute | solution.py:302
  (78 shorter events, 29.1 us)
Async XLA Ops:
  0.0 9.7 %copy-start.20 = (s32[4096,1]{0,1:T(1,128)S(1)}, s32[4096,1]{0,1:T(1,128)}, u32[]{:S(2)}) copy-start(s32[4096,1]{0,1:T(1,128)} %param.10) | copy-start | bytes 49156
  0.0 9.7 %copy-start.19 = (s32[4096]{0:T(1024)S(1)}, s32[4096]{0:T(1024)}, u32[]{:S(2)}) copy-start(s32[4096]{0:T(1024)} %param.11) | copy-start | bytes 49156
  0.0 9.7 %copy-start.1 = (f32[4096,64]{0,1:T(8,128)S(1)}, f32[4096,64]{0,1:T(8,128)}, u32[]{:S(2)}) copy-start(f32[4096,64]{0,1:T(8,128)} %param.9) | copy-start | bytes 3145732
  3.2 31.2 %collective-permute-start = (f32[640,256]{1,0:T(8,128)}, f32[640,256]{1,0:T(8,128)S(1)}, u32[]{:S(2)}, u32[]{:S(2)}) collective-permute-start(f32[640,256]{1,0:T(8,128)} %get-tuple-element.91), channel_id=1, source_target_pairs={{0,1},{1,2},{2,3},{3,0},{4,5},{5,6},{6,7},{7,4},{8,9},{9,10},{10,1... | collective-permute-start | bytes 1966088 | tf_op jit(solution)/shard_map/ppermute | solution.py:302
  5.1 32.3 %collective-permute-start.1 = (f32[640,256]{1,0:T(8,128)}, f32[640,256]{1,0:T(8,128)S(1)}, u32[]{:S(2)}, u32[]{:S(2)}) collective-permute-start(f32[640,256]{1,0:T(8,128)} %get-tuple-element.90), channel_id=1, source_target_pairs={{0,2},{1,3},{2,0},{3,1},{4,6},{5,7},{6,4},{7,5},{8,10},{9,11},{10,... | collective-permute-start | bytes 1966088 | tf_op jit(solution)/shard_map/ppermute | solution.py:302
  8.7 29.6 %collective-permute-start.2 = (f32[640,256]{1,0:T(8,128)}, f32[640,256]{1,0:T(8,128)}, u32[]{:S(2)}, u32[]{:S(2)}) collective-permute-start(f32[640,256]{1,0:T(8,128)} %get-tuple-element.89), channel_id=1, source_target_pairs={{0,3},{1,0},{2,1},{3,2},{4,7},{5,4},{6,5},{7,6},{8,11},{9,8},{10,9... | collective-permute-start | bytes 1966088 | tf_op jit(solution)/shard_map/ppermute | solution.py:302
  17.4 16.9 %all-to-all-start = ((f32[32,16,256]{2,1,0:T(8,128)}), f32[32,16,256]{2,1,0:T(8,128)S(1)}, u32[]{:S(2)}, u32[]{:S(2)}) async-start(f32[32,16,256]{2,1,0:T(8,128)} %bitcast.9), calls=%async_computation | async-start | bytes 1048576 | tf_op jit(solution)/shard_map/all_to_all | solution.py:321
  38.2 15.9 %copy-start.18 = (f32[192,256]{1,0:T(8,128)S(1)}, f32[192,256]{1,0:T(8,128)}, u32[]{:S(2)}) copy-start(f32[192,256]{1,0:T(8,128)} %get-tuple-element.87) | copy-start | bytes 589828
  38.2 16.7 %copy-start.17 = (f32[192,256]{1,0:T(8,128)S(1)}, f32[192,256]{1,0:T(8,128)}, u32[]{:S(2)}) copy-start(f32[192,256]{1,0:T(8,128)} %get-tuple-element.82) | copy-start | bytes 589828
  38.3 9.5 %collective-permute-start.3 = (f32[208,256]{1,0:T(8,128)S(1)}, f32[208,256]{1,0:T(8,128)S(1)}, u32[]{:S(2)}, u32[]{:S(2)}) collective-permute-start(f32[208,256]{1,0:T(8,128)S(1)} %get-tuple-element.95), channel_id=1, source_target_pairs={{0,1},{1,2},{2,3},{3,0},{4,5},{5,6},{6,7},{7,4},{8,9},{9,10},{10,1... | collective-permute-start | bytes 638984 | tf_op jit(solution)/shard_map/ppermute | solution.py:302
  38.8 12.1 %collective-permute-start.4 = (f32[208,256]{1,0:T(8,128)S(1)}, f32[208,256]{1,0:T(8,128)S(1)}, u32[]{:S(2)}, u32[]{:S(2)}) collective-permute-start(f32[208,256]{1,0:T(8,128)S(1)} %get-tuple-element.94), channel_id=1, source_target_pairs={{0,2},{1,3},{2,0},{3,1},{4,6},{5,7},{6,4},{7,5},{8,10},{9,11},{10,... | collective-permute-start | bytes 638984 | tf_op jit(solution)/shard_map/ppermute | solution.py:302
  41.1 9.7 %collective-permute-start.5 = (f32[208,256]{1,0:T(8,128)S(1)}, f32[208,256]{1,0:T(8,128)S(1)}, u32[]{:S(2)}, u32[]{:S(2)}) collective-permute-start(f32[208,256]{1,0:T(8,128)S(1)} %get-tuple-element.93), channel_id=1, source_target_pairs={{0,3},{1,0},{2,1},{3,2},{4,7},{5,4},{6,5},{7,6},{8,11},{9,8},{10,9... | collective-permute-start | bytes 638984 | tf_op jit(solution)/shard_map/ppermute | solution.py:302
  44.7 13.8 %copy-start.4 = (f32[192,256]{1,0:T(8,128)S(1)}, f32[192,256]{1,0:T(8,128)}, u32[]{:S(2)}) copy-start(f32[192,256]{1,0:T(8,128)} %get-tuple-element.62.a0) | copy-start | bytes 589828
  44.7 23.1 %copy-start.5 = (f32[192,256]{1,0:T(8,128)S(1)}, f32[192,256]{1,0:T(8,128)}, u32[]{:S(2)}) copy-start(f32[192,256]{1,0:T(8,128)} %get-tuple-element.88.a0) | copy-start | bytes 589828
  54.1 7.9 %collective-permute-start.6 = (f32[208,256]{1,0:T(8,128)S(1)}, f32[208,256]{1,0:T(8,128)S(1)}, u32[]{:S(2)}, u32[]{:S(2)}) collective-permute-start(f32[208,256]{1,0:T(8,128)S(1)} %pad_maximum_fusion.3), channel_id=1, source_target_pairs={{0,1},{1,2},{2,3},{3,0},{4,5},{5,6},{6,7},{7,4},{8,9},{9,10},{10,1... | collective-permute-start | bytes 638984 | tf_op jit(solution)/shard_map/ppermute | solution.py:302
  54.9 12.8 %collective-permute-start.7 = (f32[208,256]{1,0:T(8,128)S(1)}, f32[208,256]{1,0:T(8,128)S(1)}, u32[]{:S(2)}, u32[]{:S(2)}) collective-permute-start(f32[208,256]{1,0:T(8,128)S(1)} %pad_maximum_fusion.4), channel_id=1, source_target_pairs={{0,2},{1,3},{2,0},{3,1},{4,6},{5,7},{6,4},{7,5},{8,10},{9,11},{10,... | collective-permute-start | bytes 638984 | tf_op jit(solution)/shard_map/ppermute | solution.py:302
  58.4 9.4 %collective-permute-start.8 = (f32[208,256]{1,0:T(8,128)S(1)}, f32[208,256]{1,0:T(8,128)S(1)}, u32[]{:S(2)}, u32[]{:S(2)}) collective-permute-start(f32[208,256]{1,0:T(8,128)S(1)} %pad_maximum_fusion.5), channel_id=1, source_target_pairs={{0,3},{1,0},{2,1},{3,2},{4,7},{5,4},{6,5},{7,6},{8,11},{9,8},{10,9... | collective-permute-start | bytes 638984 | tf_op jit(solution)/shard_map/ppermute | solution.py:302
  67.7 63.6 %copy-start.16 = (f32[256]{0:T(256)S(1)}, f32[256]{0:T(256)}, u32[]{:S(2)}) copy-start(f32[256]{0:T(256)} %param.6) | copy-start | bytes 3076
  71.3 9.0 %collective-permute-start.9 = (f32[272,256]{1,0:T(8,128)S(1)}, f32[272,256]{1,0:T(8,128)S(1)}, u32[]{:S(2)}, u32[]{:S(2)}) collective-permute-start(f32[272,256]{1,0:T(8,128)S(1)} %get-tuple-element.68.m0), channel_id=1, source_target_pairs={{0,1},{1,2},{2,3},{3,0},{4,5},{5,6},{6,7},{7,4},{8,9},{9,10},{10,1... | collective-permute-start | bytes 835592 | tf_op jit(solution)/shard_map/ppermute | solution.py:302
  71.3 16.2 %collective-permute-start.10 = (f32[272,256]{1,0:T(8,128)S(1)}, f32[272,256]{1,0:T(8,128)S(1)}, u32[]{:S(2)}, u32[]{:S(2)}) collective-permute-start(f32[272,256]{1,0:T(8,128)S(1)} %get-tuple-element.68.m0), channel_id=1, source_target_pairs={{0,2},{1,3},{2,0},{3,1},{4,6},{5,7},{6,4},{7,5},{8,10},{9,11},{10,... | collective-permute-start | bytes 835592 | tf_op jit(solution)/shard_map/ppermute | solution.py:302
  75.0 12.5 %collective-permute-start.11 = (f32[272,256]{1,0:T(8,128)S(1)}, f32[272,256]{1,0:T(8,128)S(1)}, u32[]{:S(2)}, u32[]{:S(2)}) collective-permute-start(f32[272,256]{1,0:T(8,128)S(1)} %get-tuple-element.68.m0), channel_id=1, source_target_pairs={{0,3},{1,0},{2,1},{3,2},{4,7},{5,4},{6,5},{7,6},{8,11},{9,8},{10,9... | collective-permute-start | bytes 835592 | tf_op jit(solution)/shard_map/ppermute | solution.py:302
  89.8 1.9 %collective-permute-start.12 = (f32[272,256]{1,0:T(8,128)}, f32[272,256]{1,0:T(8,128)}, u32[]{:S(2)}, u32[]{:S(2)}) collective-permute-start(f32[272,256]{1,0:T(8,128)} %get-tuple-element.69.own), channel_id=1, source_target_pairs={{0,4},{4,0},{8,12},{12,8},{16,20},{20,16},{24,28},{28,24},{32,36},... | collective-permute-start | bytes 835592 | tf_op jit(solution)/shard_map/ppermute | solution.py:362
  95.4 11.6 %collective-permute-start.13 = (f32[272,256]{1,0:T(8,128)}, f32[272,256]{1,0:T(8,128)}, u32[]{:S(2)}, u32[]{:S(2)}) collective-permute-start(f32[272,256]{1,0:T(8,128)} %get-tuple-element.71.m0), channel_id=1, source_target_pairs={{0,8},{8,16},{16,24},{24,0},{32,40},{40,48},{48,56},{56,32},{64,72... | collective-permute-start | bytes 835592 | tf_op jit(solution)/shard_map/ppermute | solution.py:366
  98.9 10.7 %collective-permute-start.14 = (f32[272,256]{1,0:T(8,128)}, f32[272,256]{1,0:T(8,128)}, u32[]{:S(2)}, u32[]{:S(2)}) collective-permute-start(f32[272,256]{1,0:T(8,128)} %get-tuple-element.71.m0), channel_id=1, source_target_pairs={{0,16},{8,24},{16,0},{24,8},{32,48},{40,56},{48,32},{56,40},{64,80... | collective-permute-start | bytes 835592 | tf_op jit(solution)/shard_map/ppermute | solution.py:366
  103.7 8.8 %collective-permute-start.15 = (f32[272,256]{1,0:T(8,128)}, f32[272,256]{1,0:T(8,128)}, u32[]{:S(2)}, u32[]{:S(2)}) collective-permute-start(f32[272,256]{1,0:T(8,128)} %get-tuple-element.71.m0), channel_id=1, source_target_pairs={{0,24},{8,0},{16,8},{24,16},{32,56},{40,32},{48,40},{56,48},{64,88... | collective-permute-start | bytes 835592 | tf_op jit(solution)/shard_map/ppermute | solution.py:366
  116.0 8.7 %collective-permute-start.16 = (f32[272,256]{1,0:T(8,128)}, f32[272,256]{1,0:T(8,128)}, u32[]{:S(2)}, u32[]{:S(2)}) collective-permute-start(f32[272,256]{1,0:T(8,128)} %get-tuple-element.72.m0), channel_id=1, source_target_pairs={{0,32},{8,40},{16,48},{24,56},{32,64},{40,72},{48,80},{56,88},{64,... | collective-permute-start | bytes 835592 | tf_op jit(solution)/shard_map/ppermute | solution.py:371
  117.3 10.3 %collective-permute-start.17 = (f32[272,256]{1,0:T(8,128)}, f32[272,256]{1,0:T(8,128)}, u32[]{:S(2)}, u32[]{:S(2)}) collective-permute-start(f32[272,256]{1,0:T(8,128)} %get-tuple-element.72.m0), channel_id=1, source_target_pairs={{0,64},{8,72},{16,80},{24,88},{32,96},{40,104},{48,112},{56,120},{... | collective-permute-start | bytes 835592 | tf_op jit(solution)/shard_map/ppermute | solution.py:371
  118.6 12.8 %collective-permute-start.18 = (f32[272,256]{1,0:T(8,128)}, f32[272,256]{1,0:T(8,128)}, u32[]{:S(2)}, u32[]{:S(2)}) collective-permute-start(f32[272,256]{1,0:T(8,128)} %get-tuple-element.72.m0), channel_id=1, source_target_pairs={{0,96},{8,104},{16,112},{24,120},{1,97},{9,105},{17,113},{25,121},... | collective-permute-start | bytes 835592 | tf_op jit(solution)/shard_map/ppermute | solution.py:371
  134.3 2.2 %collective-permute-start.19 = (f32[16,256]{1,0:T(8,128)S(1)}, f32[16,256]{1,0:T(8,128)S(1)}, u32[]{:S(2)}, u32[]{:S(2)}) collective-permute-start(f32[16,256]{1,0:T(8,128)S(1)} %shard_map.72.mine), channel_id=1, source_target_pairs={{0,4},{8,12},{16,20},{24,28},{32,36},{40,44},{48,52},{56,60},{64,6... | collective-permute-start | bytes 49160 | tf_op jit(solution)/shard_map/ppermute | solution.py:383
  139.6 4.9 %collective-permute-start.20 = (f32[16,64]{1,0:T(8,128)S(1)}, f32[16,64]{1,0:T(8,128)S(1)}, u32[]{:S(2)}, u32[]{:S(2)}) collective-permute-start(f32[16,64]{1,0:T(8,128)S(1)} %get-tuple-element.78), channel_id=1, source_target_pairs={{0,1},{1,2},{2,3},{3,0},{4,5},{5,6},{6,7},{7,4},{8,9},{9,10},{10,1... | collective-permute-start | bytes 12296 | tf_op jit(solution)/shard_map/ppermute | solution.py:302
  139.7 5.5 %collective-permute-start.21 = (f32[16,64]{1,0:T(8,128)S(1)}, f32[16,64]{1,0:T(8,128)S(1)}, u32[]{:S(2)}, u32[]{:S(2)}) collective-permute-start(f32[16,64]{1,0:T(8,128)S(1)} %get-tuple-element.79), channel_id=1, source_target_pairs={{0,2},{1,3},{2,0},{3,1},{4,6},{5,7},{6,4},{7,5},{8,10},{9,11},{10,... | collective-permute-start | bytes 12296 | tf_op jit(solution)/shard_map/ppermute | solution.py:302
  143.5 3.7 %collective-permute-start.22 = (f32[16,64]{1,0:T(8,128)S(1)}, f32[16,64]{1,0:T(8,128)S(1)}, u32[]{:S(2)}, u32[]{:S(2)}) collective-permute-start(f32[16,64]{1,0:T(8,128)S(1)} %get-tuple-element.80), channel_id=1, source_target_pairs={{0,3},{1,0},{2,1},{3,2},{4,7},{5,4},{6,5},{7,6},{8,11},{9,8},{10,9... | collective-permute-start | bytes 12296 | tf_op jit(solution)/shard_map/ppermute | solution.py:302
  (13 other events, 20.3 us)

commit v4 on v3

--- a/solution.py
+++ b/solution.py
@@ -7,12 +7,14 @@
 
 F32 = jnp.float32
 BF16 = jnp.bfloat16
-PARAMS = pltpu.CompilerParams(vmem_limit_bytes=24 * 1024 * 1024)
+MIB = 1024 * 1024
 VM = pl.BlockSpec(memory_space=pltpu.VMEM)
 SM = pl.BlockSpec(memory_space=pltpu.SMEM)
 N = 256
 PAD = 16
 R = N + PAD
+Z, C, Y, X = range(4)
+HALF = R // 2
 ROWS = 4
 SUB = 16
 CHUNKS = ((5, 5), (3,), (3,))
@@ -55,20 +57,23 @@
     return jnp.where(r == c, 1.0, 0.0).astype(F32)
 
 
+FAR = pl.BlockSpec(memory_space=pltpu.HBM)
+
+
 def near(x):
     return pltpu.with_memory_space_constraint(x, pltpu.VMEM)
 
 
-def call(kernel, outs, scalars, args, scratch=(), far=()):
+def call(kernel, outs, idx, args, scratch=(), far=(), mib=8):
     outs = [o if isinstance(o[0], tuple) else (o, F32) for o in outs]
     return pl.pallas_call(
         kernel,
         out_shape=[pltpu.VMEM(s, t) for s, t in outs],
-        in_specs=[SM] * len(scalars) + [VM] * (len(far) + len(args)),
+        in_specs=[SM] + [FAR] * len(far) + [VM] * len(args),
         out_specs=[VM] * len(outs),
         scratch_shapes=list(scratch),
-        compiler_params=PARAMS,
-    )(*scalars, *far, *[near(a) for a in args])
+        compiler_params=pltpu.CompilerParams(vmem_limit_bytes=mib * MIB),
+    )(idx, *[pltpu.with_memory_space_constraint(f, pltpu.HBM) for f in far], *[near(a) for a in args])
 
 
 BIN_M = 256
@@ -116,16 +121,22 @@
         ],
         out_specs=pl.BlockSpec((n_bins // 4, N), lambda i: (0, 0)),
         scratch_shapes=[pltpu.VMEM((4 * width, obs_rows), BF16), pltpu.VMEM((n_bins, 128), F32)],
-        compiler_params=PARAMS,
+        compiler_params=pltpu.CompilerParams(vmem_limit_bytes=24 * MIB),
     )(rid, observed)
 
 
-def assemble(z, parts, ah, al):
-    for d, part in enumerate(parts):
+def own_copy(z, flat, own, start, sem):
+    return pltpu.make_async_copy(flat.at[pl.ds(pl.multiple_of(z * (SUB * 64) + start * 64, 64), own.shape[0])], own, sem)
+
+
+def assemble(z, parts, ah, al, own=None):
+    for d in (1, 2, 3, 0):
         slot = lax.rem(z - d + ROWS, ROWS)
         rows = pl.ds(pl.multiple_of(slot * 64, 64), 64)
+        if d == 0:
+            own.wait()
         for k in range(ah.shape[0]):
-            hi, lo = split(part[k * 64 : (k + 1) * 64, :])
+            hi, lo = split(parts[d][k * 64 : (k + 1) * 64, :])
             ah[k, rows, :] = hi
             al[k, rows, :] = lo
 
@@ -150,23 +161,34 @@
                 pref[k] = by_step(pref[k - 1], ah[k], al[k])
 
 
-def first_kernel(z_ref, a0, a1, a2, a3, pref, ah, al, both):
-    assemble(z_ref[0], (a0, a1, a2, a3), ah, al)
+def first_kernel(idx, flat, gains, a1, a2, a3, pref, ah, al, both, staged, own, sems):
+    z = idx[Z]
+    late = pltpu.make_async_copy(gains, staged, sems.at[1])
+    copy = own_copy(z, flat, own, 0, sems.at[0])
+    copy.start()
+    late.start()
+    assemble(z, (own, a1, a2, a3), ah, al, copy)
     chains(CHUNKS[0], ah, al, pref)
     both[...] = mm(pref[CHUNKS[0][0] - 1], pref[SIZES[0] - 1])
-
-
-def second_kernel(z_ref, a0, a1, a2, a3, both, pref, ah, al, three):
-    assemble(z_ref[0], (a0, a1, a2, a3), ah, al)
+    late.wait()
+
+
+def second_kernel(idx, flat, a1, a2, a3, both, pref, ah, al, three, own, sem):
+    z = idx[Z]
+    copy = own_copy(z, flat, own, SIZES[0], sem)
+    copy.start()
+    assemble(z, (own, a1, a2, a3), ah, al, copy)
     chains(CHUNKS[1], ah, al, pref)
     three[...] = mm(both[...], pref[SIZES[1] - 1])
 
 
 def third_kernel(
-    z_ref, a0, a1, a2, a3, b0, p01, ah01, al01, p2, ah2, al2, three, pref, shifts, whole, ah, al, b_s
+    idx, flat, a1, a2, a3, b0, p01, ah01, al01, p2, ah2, al2, three, pref, shifts, whole, ah, al, b_s, own, sem
 ):
-    z = z_ref[0]
-    assemble(z, (a0, a1, a2, a3), ah, al)
+    z = idx[Z]
+    copy = own_copy(z, flat, own, SIZES[0] + SIZES[1], sem)
+    copy.start()
+    assemble(z, (own, a1, a2, a3), ah, al, copy)
     b_s[z] = b0[...]
     for d, a in ((1, a1), (2, a2), (3, a3)):
         b_s[lax.rem(z - d + ROWS, ROWS)] = a[SIZES[2] * 64 :, :]
@@ -198,30 +220,54 @@
     whole[N:, :] = v
 
 
-def four_kernel(pos_ref, m0, m1, m2, m3, total, before, m_s):
-    pos = pos_ref[0]
+def combine(pos, m_s, before):
+    m01 = then(m_s[0], m_s[1])
+    m23 = then(m_s[2], m_s[3])
+    before[...] = eye_map()
+
+    @pl.when(pos == 1)
+    def _():
+        before[...] = m_s[0]
+
+    @pl.when(pos == 2)
+    def _():
+        before[...] = m01
+
+    @pl.when(pos == 3)
+    def _():
+        before[...] = then(m01, m_s[2])
+
+    return then(m01, m23)
+
+
+def four_kernel(idx, m0, m1, m2, m3, total, before, m_s):
+    pos = idx[Z]
     for d, m in enumerate((m0, m1, m2, m3)):
         m_s[lax.rem(pos - d + 4, 4)] = m[...]
-    m01 = then(m_s[0], m_s[1])
-    m23 = then(m_s[2], m_s[3])
-    total[...] = then(m01, m23)
-    before[...] = eye_map()
-
-    @pl.when(pos == 1)
-    def _():
-        before[...] = m_s[0]
-
-    @pl.when(pos == 2)
-    def _():
-        before[...] = m01
-
-    @pl.when(pos == 3)
-    def _():
-        before[...] = then(m01, m_s[2])
-
-
-def pair_kernel(c_ref, own, other, before_in, total, before):
-    c = c_ref[0]
+    total[...] = combine(pos, m_s, before)
+
+
+def half_rows(c):
+    return pl.ds(pl.multiple_of(c * HALF, 8), HALF)
+
+
+def join_halves(pos, c, mine, others, m_s):
+    for d, (m, o) in enumerate(zip(mine, others)):
+        slot = lax.rem(pos - d + 3, 4)
+        m_s[slot, half_rows(c), :] = m[...]
+        m_s[slot, half_rows(1 - c), :] = o[...]
+
+
+def halves_kernel(idx, own, h1, h2, h3, o1, o2, o3, half, before, m_s):
+    pos, c = idx[Y], idx[C]
+    m_s[pos] = own[...]
+    join_halves(pos, c, (h1, h2, h3), (o1, o2, o3), m_s)
+    m_s[4] = combine(pos, m_s, before)
+    half[...] = m_s[4, half_rows(c), :]
+
+
+def pair_kernel(idx, own, other, before_in, total, half, before):
+    c = idx[C]
     swap = c == 1
 
     @pl.when(swap)
@@ -234,26 +280,25 @@
         total[...] = then(own[...], other[...])
         before[...] = before_in[...]
 
-
-def top_kernel(pos_ref, prior, m0, m1, m2, m3, ybefore, out, m_s, s_s):
-    pos = pos_ref[0]
-    for d, m in enumerate((m0, m1, m2, m3)):
-        m_s[lax.rem(pos - d + 4, 4)] = m[...]
-    r = lax.broadcasted_iota(jnp.int32, (PAD, N), 0)
-    s_s[...] = jnp.where(r == 0, prior[...], 0.0)
+    half[...] = total[half_rows(c), :]
+
+
+def fold_kernel(idx, first, second, out):
+    out[...] = then(first[...], second[...])
+
+
+def states_kernel(
+    idx, prior, h1, h2, h3, g1, g2, g3, before, p01, p2, p3, shifts, o0, o1, o2, o3, st_s, m_s, s_s
+):
+    z, pos = idx[Z], idx[X]
+    join_halves(pos, idx[C], (h1, h2, h3), (g1, g2, g3), m_s)
+    s_s[...] = jnp.where(lax.broadcasted_iota(jnp.int32, (PAD, N), 0) == 0, prior[...], 0.0)
     for i in range(3):
 
         @pl.when(i < pos)
         def _(i=i):
             s_s[...] = apply(s_s[...], m_s[i])
 
-    out[...] = apply(s_s[...], ybefore[...])
-
-
-def states_kernel(z_ref, c_ref, mine, other, before, p01, p2, p3, shifts, o0, o1, o2, o3, st_s, s_s):
-    z = z_ref[0]
-    c = c_ref[0]
-    s_s[...] = jnp.where(c == 0, mine[...], other[...])
     s = apply(s_s[...], before[...])
     eye = lax.broadcasted_iota(jnp.int32, (N, N), 0) == lax.broadcasted_iota(jnp.int32, (N, N), 1)
     first = lax.broadcasted_iota(jnp.int32, (PAD, N), 0) == 0
@@ -273,8 +318,39 @@
         o[...] = st_s[lax.rem(z + d, ROWS)]
 
 
-def offset_kernel(z_ref, g, i0, r1, r2, r3, o0, o1, o2, o3, info_s, off_s):
-    z = z_ref[0]
+def send_copies(z, flat, outs, start, count, sems):
+    copies = []
+    for d, o in enumerate(outs, 1):
+        at = lax.rem(z + d, ROWS) * (SUB * 64) + start * 64
+        source = flat.at[pl.ds(pl.multiple_of(at, 64), count * 64)]
+        copies.append(pltpu.make_async_copy(source, o.at[pl.ds(0, count * 64)], sems.at[d - 1]))
+    for copy in copies:
+        copy.start()
+    return copies
+
+
+def send_a_kernel(idx, flat, o1, o2, o3, sems):
+    for copy in send_copies(idx[Z], flat, (o1, o2, o3), 0, SIZES[0], sems):
+        copy.wait()
+
+
+def send_b_kernel(idx, flat, sums, o1, o2, o3, info, sems):
+    copies = send_copies(idx[Z], flat, (o1, o2, o3), SIZES[0], SIZES[1], sems)
+    info[...] = jnp.sum(sums[...], axis=0)
+    for copy, o in zip(copies, (o1, o2, o3)):
+        copy.wait()
+        o[SIZES[1] * 64 :, :] = info[...]
+
+
+def send_c_kernel(idx, flat, t1, t2, t3, o1, o2, o3, sems):
+    copies = send_copies(idx[Z], flat, (o1, o2, o3), SIZES[0] + SIZES[1], SIZES[2], sems)
+    for copy, o, t in zip(copies, (o1, o2, o3), (t1, t2, t3)):
+        copy.wait()
+        o[SIZES[2] * 64 :, :] = t[...]
+
+
+def offset_kernel(idx, g, i0, r1, r2, r3, o0, o1, o2, o3, info_s, off_s):
+    z = idx[Z]
     info_s[z] = i0[...]
     for d, r in ((1, r1), (2, r2), (3, r3)):
         info_s[lax.rem(z - d + ROWS, ROWS)] = r[r.shape[0] - 16 :, :]
@@ -291,8 +367,8 @@
         o[:, 128:] = jnp.zeros((16, 128), F32)
 
 
-def place_kernel(z_ref, r0, r1, r2, r3, out):
-    z = z_ref[0]
+def place_kernel(idx, r0, r1, r2, r3, out):
+    z = idx[Z]
     for d, r in enumerate((r0, r1, r2, r3)):
         slot = lax.rem(z - d + ROWS, ROWS)
         out[pl.ds(pl.multiple_of(slot * SUB, SUB), SUB), :] = r[...]
@@ -305,98 +381,104 @@
 def shards(prior, dynamics, gains, observed, owner, step):
     tm = lax.axis_index("tm").astype(jnp.int32)
     z = lax.axis_index("row").astype(jnp.int32)
-    x, y, c = tm // 8, (tm // 2) % 4, tm % 2
-    z1 = z.reshape(1)
-
+    idx = jnp.stack([z, tm & 1, (tm >> 1) & 3, tm >> 3])
+    prior = prior.reshape(1, N)
     flat = dynamics.reshape(ROWS * SUB * 64, N)
-
-    def piece(d, start, count):
-        return lax.dynamic_slice_in_dim(flat, ((z + d) % ROWS) * (SUB * 64) + start * 64, count * 64, 0)
-
-    at_b, at_c = SIZES[0], SIZES[0] + SIZES[1]
-    part_a = [piece(0, 0, SIZES[0])] + [along_row(piece(d, 0, SIZES[0]), d) for d in (1, 2, 3)]
+    dma3 = pltpu.SemaphoreType.DMA((3,))
+
+    def along_rows(blocks):
+        return [along_row(b, d) for d, b in enumerate(blocks, 1)]
+
+    part_a = along_rows(call(send_a_kernel, [(SIZES[0] * 64, N)] * 3, idx, (), [dma3], far=(flat,)))
 
     rid = owner[:, 0] * 16 + step % 16 + 512 * (step // 16)
     partial = binned(rid.reshape(1, -1), observed.T)
-    sums = lax.all_to_all(partial, "tm", 0, 0, tiled=True)
-    info = jnp.sum(sums.reshape(32, 16, N), axis=0)
-    info, *part_a = lax.optimization_barrier((info, *part_a))
-
-    sent_b = [jnp.concatenate([piece(d, at_b, SIZES[1]), info], axis=0) for d in (1, 2, 3)]
-    part_b = [piece(0, at_b, SIZES[1])] + [along_row(sent_b[d - 1], d) for d in (1, 2, 3)]
-    p01, ah01, al01, both = call(
+    sums = lax.all_to_all(partial, "tm", 0, 0, tiled=True).reshape(32, 16, N)
+    sums, idx, prior, *part_a = lax.optimization_barrier((sums, idx, prior, *part_a))
+
+    *sent_b, info = call(
+        send_b_kernel, [(SIZES[1] * 64 + 16, N)] * 3 + [(16, N)], idx, (sums,), [dma3], far=(flat,)
+    )
+    part_b = along_rows(sent_b)
+    p01, ah01, al01, both, staged = call(
         first_kernel,
-        [(SIZES[0], N, N), ((SIZES[0], N, N), BF16), ((SIZES[0], N, N), BF16), (N, N)],
-        (z1,),
+        [(SIZES[0], N, N), ((SIZES[0], N, N), BF16), ((SIZES[0], N, N), BF16), (N, N), gains.shape],
+        idx,
         part_a,
-    )
-    p01, ah01, al01, both, *part_b = lax.optimization_barrier((p01, ah01, al01, both, *part_b))
+        [pltpu.VMEM((SIZES[0] * 64, N), F32), pltpu.SemaphoreType.DMA((2,))],
+        far=(flat, gains),
+    )
+    p01, ah01, al01, both, staged, *part_b = lax.optimization_barrier((p01, ah01, al01, both, staged, *part_b))
     offs = call(
         offset_kernel,
         [(16, N)] * 4,
-        (z1,),
-        (info, *part_b[1:]),
+        idx,
+        (staged, info, *part_b),
         [pltpu.VMEM((ROWS, 16, N), F32), pltpu.VMEM((ROWS, 16, 128), F32)],
-        far=(gains,),
-    )
-    sent_c = [jnp.concatenate([piece(d, at_c, SIZES[2]), offs[d]], axis=0) for d in (1, 2, 3)]
-    part_c = [piece(0, at_c, SIZES[2])] + [along_row(sent_c[d - 1], d) for d in (1, 2, 3)]
+    )
+    sent_c = call(send_c_kernel, [(SIZES[2] * 64 + 16, N)] * 3, idx, offs[1:], [dma3], far=(flat,))
+    part_c = along_rows(sent_c)
     p2, ah2, al2, three = call(
         second_kernel,
         [(SIZES[1], N, N), ((SIZES[1], N, N), BF16), ((SIZES[1], N, N), BF16), (N, N)],
-        (z1,),
+        idx,
         (*part_b, both),
+        [pltpu.VMEM((SIZES[1] * 64, N), F32), pltpu.SemaphoreType.DMA],
+        far=(flat,),
     )
     p3, shifts, whole = call(
         third_kernel,
         [(SIZES[2], N, N), (SUB, N), (R, N)],
-        (z1,),
+        idx,
         (*part_c, offs[0], p01, ah01, al01, p2, ah2, al2, three),
-        [pltpu.VMEM((SIZES[2], N, N), BF16)] * 2 + [pltpu.VMEM((ROWS, 16, N), F32)],
-    )
-
-    def four(pos, maps):
-        return call(four_kernel, [(R, N), (R, N)], (pos.reshape(1),), maps, [pltpu.VMEM((4, R, N), F32)])
-
-    block, before = four(z, [whole] + [along_row(whole, d) for d in (1, 2, 3)])
-    swapped = lax.ppermute(block, "tm", [(i, i ^ 1) for i in range(32)])
-    column, before = call(pair_kernel, [(R, N), (R, N)], (c.reshape(1),), (block, swapped, before))
-
-    def along_y(m, d):
-        return lax.ppermute(
-            m, "tm", [(8 * i + 2 * j, 8 * i + 2 * ((j + d) % 4)) for i in range(4) for j in range(4)]
-        )
-
-    def along_x(m, d):
-        return lax.ppermute(
-            m, "tm", [(8 * i + 2 * j, 8 * (i + d) + 2 * j) for i in range(4 - d) for j in range(4)]
-        )
-
-    plane, ybefore = four(y, [column] + [along_y(column, d) for d in (1, 2, 3)])
-    (entry,) = call(
-        top_kernel,
-        [(PAD, N)],
-        (x.reshape(1),),
-        (prior.reshape(1, N), plane, *[along_x(plane, d) for d in (1, 2, 3)], ybefore),
-        [pltpu.VMEM((4, R, N), F32), pltpu.VMEM((PAD, N), F32)],
-    )
-    handed = lax.ppermute(entry, "tm", [(2 * i, 2 * i + 1) for i in range(16)])
+        [pltpu.VMEM((SIZES[2], N, N), BF16)] * 2
+        + [pltpu.VMEM((ROWS, 16, N), F32), pltpu.VMEM((SIZES[2] * 64, N), F32), pltpu.SemaphoreType.DMA],
+        far=(flat,),
+    )
+
+    block, before = call(
+        four_kernel,
+        [(R, N), (R, N)],
+        idx,
+        (whole, *[along_row(whole, d) for d in (1, 2, 3)]),
+        [pltpu.VMEM((4, R, N), F32)],
+    )
+
+    def other_core(m):
+        return lax.ppermute(m, "tm", [(i, i ^ 1) for i in range(32)])
+
+    def along_tm(m, d, n, stride):
+        places = [(i, i - i % (n * stride) + (i + d * stride) % (n * stride)) for i in range(32)]
+        return lax.ppermute(m, "tm", places)
+
+    column, half, before = call(
+        pair_kernel, [(R, N), (HALF, N), (R, N)], idx, (block, other_core(block), before)
+    )
+    halves = [along_tm(half, d, 4, 2) for d in (1, 2, 3)]
+    half, ybefore = call(
+        halves_kernel,
+        [(HALF, N), (R, N)],
+        idx,
+        (column, *halves, *[other_core(h) for h in halves]),
+        [pltpu.VMEM((5, R, N), F32)],
+    )
+    halves = [along_tm(half, d, 4, 8) for d in (1, 2, 3)]
+    (before,) = call(fold_kernel, [(R, N)], idx, (ybefore, before))
     outs = call(
         states_kernel,
         [(SUB, 64)] * 4,
-        (z1, c.reshape(1)),
-        (entry, handed, before, p01, p2, p3, shifts),
-        [pltpu.VMEM((ROWS, SUB, 64), F32), pltpu.VMEM((PAD, N), F32)],
-    )
-    got = [outs[0]] + [along_row(outs[d], d) for d in (1, 2, 3)]
-    states = pl.pallas_call(
+        idx,
+        (prior, *halves, *[other_core(h) for h in halves], before, p01, p2, p3, shifts),
+        [pltpu.VMEM((ROWS, SUB, 64), F32), pltpu.VMEM((4, R, N), F32), pltpu.VMEM((PAD, N), F32)],
+    )
+    got = [outs[0], *along_rows(outs[1:])]
+    return pl.pallas_call(
         place_kernel,
         out_shape=jax.ShapeDtypeStruct((64, 64), F32),
         in_specs=[SM] + [VM] * 4,
         out_specs=VM,
-        compiler_params=PARAMS,
-    )(z1, *[near(g) for g in got])
-    return states
+        compiler_params=pltpu.CompilerParams(vmem_limit_bytes=4 * MIB),
+    )(idx, *[near(g) for g in got])
 
 
 def solution(mesh):

time: 148 us -> 130 us (0.88)
  local copies, waits for them, and re-layouts: 17.8 us -> 0.01 us
  blocking collectives: 0 us -> 16.7 us
  starting transfers between devices: 46.9 us -> 34 us
  waiting for transfers between devices: 56.7 us -> 46.6 us
  Pallas kernels: 25.8 us -> 31.8 us
    all_to_all x0 -> x1, blocking collectives: none -> 16.7 us  [shards(): sums = lax.all_to_all(partial, 'tm', 0, 0, tiled=True).reshape(32, 16, N)]
    unnamed x42 -> x8, local copies, waits for them, and re-layouts: 12.3 us -> 0.01 us
    all_to_all x1 -> x0, starting transfers between devices: 7.61 us -> none  [shards(): sums = lax.all_to_all(partial, 'tm', 0, 0, tiled=True)]
    ppermute x8 -> x13, starting transfers between devices: 16.7 us -> 9.64 us  [the longest x6 9.04 us: along_tm(): return lax.ppermute(m, 'tm', places)]
    all_to_all x1 -> x0, waiting for transfers between devices: 6.79 us -> none  [shards(): sums = lax.all_to_all(partial, 'tm', 0, 0, tiled=True)]
    pallas_call x9 -> x12, Pallas kernels: 17.5 us -> 23.7 us  [call(): pl.pallas_call(kernel, out_shape=[pltpu.VMEM(s, t) for s, t in outs], in_...]
    dynamic_slice x2 -> x0, local copies, waits for them, and re-layouts: 5.54 us -> none  [piece(): lax.dynamic_slice_in_dim(flat, (z + d) % ROWS * (SUB * 64) + start * 64,...]
    ppermute x8 -> x13, waiting for transfers between devices: 19.6 us -> 16.2 us  [the longest x6 13.1 us: along_tm(): return lax.ppermute(m, 'tm', places)]
  transfers between devices with their start and end apart: 24 -> 28, of which waited for: 17 -> 18; matrix products, arithmetic and copies ran while one was open for 2% -> 0% of each run, Pallas kernels for 8% -> 11%
where the time goes in v4:
time: 130 us; the launch traced here: 129 us
  waiting for transfers between devices  46.6 us (36%)
  starting transfers between devices  34 us (26%)
  Pallas kernels  31.8 us (24%)
  blocking collectives  16.7 us (13%)
    ppermute x15, waiting for transfers between devices, along_row(): return lax.ppermute(x, 'row', [(i, (i + d) % ROWS) for i in range(ROWS)])  30.4 us
    ppermute x15, starting transfers between devices, along_row(): return lax.ppermute(x, 'row', [(i, (i + d) % ROWS) for i in range(ROWS)])  24.3 us
    pallas_call x12, Pallas kernels, call(): pl.pallas_call(kernel, out_shape=[pltpu.VMEM(s, t) for s, t in outs], in_...  23.7 us
    all_to_all x1, blocking collectives, shards(): sums = lax.all_to_all(partial, 'tm', 0, 0, tiled=True).reshape(32, 16, N)  16.7 us
    ppermute x6, waiting for transfers between devices, along_tm(): return lax.ppermute(m, 'tm', places)  13.1 us
    ppermute x6, starting transfers between devices, along_tm(): return lax.ppermute(m, 'tm', places)  9.04 us
    pallas_call x1, Pallas kernels, binned(): pl.pallas_call(bin_kernel, out_shape=jax.ShapeDtypeStruct((n_bins // 4, N...  6.91 us
    ppermute x7, waiting for transfers between devices, other_core(): return lax.ppermute(m, 'tm', [(i, i ^ 1) for i in range(32)])  3.09 us
  transfers between devices with their start and end apart: 28, of which 18 were waited for; matrix products, arithmetic and copies ran while one was open for 0% of the time, Pallas kernels for 11%

profile of v4, /device:TPU:6, one launch (start us, length us, event | category | flops | bytes accessed | tf_op | source)
XLA Modules:
  0.0 129.4 jit_solution(14675430062515156518)
XLA Ops:
  0.1 2.1 %shard_map.65 = (f32[640,256]{1,0:T(8,128)S(1)}, f32[640,256]{1,0:T(8,128)S(1)}, f32[640,256]{1,0:T(8,128)S(1)}) custom-call(s32[4]{0:T(128)S(1)} %pad_add_fusion.idx, f32[4096,256]{1,0:T(8,128)} %bitcast.14), custom_call_target="tpu_custom_call" | custom-call | tf_op jit(solution)/shard_map/pallas_call | solution.py:69
  2.2 2.0 %collective-permute-start = (f32[640,256]{1,0:T(8,128)S(1)}, f32[640,256]{1,0:T(8,128)S(1)}, u32[]{:S(2)}, u32[]{:S(2)}) collective-permute-start(f32[640,256]{1,0:T(8,128)S(1)} %get-tuple-element.56), channel_id=1, source_target_pairs={{0,1},{1,2},{2,3},{3,0},{4,5},{5,6},{6,7},{7,4},{8,9},{9,10},{10,1... | collective-permute-start | bytes 1966088 | tf_op jit(solution)/shard_map/ppermute | solution.py:378
  4.1 3.6 %collective-permute-start.1 = (f32[640,256]{1,0:T(8,128)S(1)}, f32[640,256]{1,0:T(8,128)S(1)}, u32[]{:S(2)}, u32[]{:S(2)}) collective-permute-start(f32[640,256]{1,0:T(8,128)S(1)} %get-tuple-element.57), channel_id=1, source_target_pairs={{0,2},{1,3},{2,0},{3,1},{4,6},{5,7},{6,4},{7,5},{8,10},{9,11},{10,... | collective-permute-start | bytes 1966088 | tf_op jit(solution)/shard_map/ppermute | solution.py:378
  8.8 6.9 %shard_map.64 = f32[512,256]{1,0:T(8,128)S(1)} custom-call(s32[1,4096]{1,0:T(1,128)S(1)} %bitcast.12, f32[64,4096]{1,0:T(8,128)S(1)} %bitcast.11), custom_call_target="tpu_custom_call" | custom-call | tf_op jit(solution)/shard_map/pallas_call | solution.py:114
  15.7 16.7 %all_to_all.9.sums = f32[32,16,256]{2,1,0:T(8,128)S(1)} all-to-all(f32[32,16,256]{2,1,0:T(8,128)S(1)} %bitcast.10), channel_id=1, replica_groups=mesh['tm'=32,'row'=4] {'tm'}, dimensions={0} | all-to-all | bytes 1048576 | tf_op jit(solution)/shard_map/all_to_all | solution.py:396
  32.4 3.8 %collective-permute-done.1.a2 = f32[640,256]{1,0:T(8,128)S(1)} collective-permute-done((f32[640,256]{1,0:T(8,128)S(1)}, f32[640,256]{1,0:T(8,128)S(1)}, u32[]{:S(2)}, u32[]{:S(2)}) %collective-permute-start.1) | collective-permute-done | bytes 655392 | tf_op jit(solution)/shard_map/ppermute | solution.py:378
  36.2 1.7 %shard_map.67 = (f32[208,256]{1,0:T(8,128)S(1)}, f32[208,256]{1,0:T(8,128)S(1)}, f32[208,256]{1,0:T(8,128)S(1)}, f32[16,256]{1,0:T(8,128)S(1)}) custom-call(s32[4]{0:T(128)S(1)} %pad_add_fusion.idx, f32[4096,256]{1,0:T(8,128)} %bitcast.15, f32[32,16,256]{2,1,0:T(8,128)S(1)} %all_to_all.9.sums), custom_call_target="tpu_custom_call" | custom-call | tf_op jit(solution)/shard_map/pallas_call | solution.py:69
  39.2 2.4 %collective-permute-start.4 = (f32[208,256]{1,0:T(8,128)S(1)}, f32[208,256]{1,0:T(8,128)S(1)}, u32[]{:S(2)}, u32[]{:S(2)}) collective-permute-start(f32[208,256]{1,0:T(8,128)S(1)} %get-tuple-element.71), channel_id=1, source_target_pairs={{0,2},{1,3},{2,0},{3,1},{4,6},{5,7},{6,4},{7,5},{8,10},{9,11},{10,... | collective-permute-start | bytes 638984 | tf_op jit(solution)/shard_map/ppermute | solution.py:378
  42.9 3.4 %shard_map.66 = (f32[10,256,256]{2,1,0:T(8,128)S(1)}, bf16[10,256,256]{2,1,0:T(8,128)(2,1)S(1)}, bf16[10,256,256]{2,1,0:T(8,128)(2,1)S(1)}, f32[256,256]{1,0:T(8,128)S(1)}, f32[64,64,256]{2,1,0:T(8,128)S(1)}) custom-call(s32[4]{0:T(128)S(1)} %pad_add_fusion.idx, f32[4096,256]{1,0:T(8,128)} %bitcast.16, f32[64,64,256]{2,1,0:T(8,128)} %gains.1, ...), custom_call_target="tpu_custom_call" | custom-call | tf_op jit(solution)/shard_map/pallas_call | solution.py:69
  46.3 5.0 %collective-permute-done.4.r2.a2 = f32[208,256]{1,0:T(8,128)S(1)} collective-permute-done((f32[208,256]{1,0:T(8,128)S(1)}, f32[208,256]{1,0:T(8,128)S(1)}, u32[]{:S(2)}, u32[]{:S(2)}) %collective-permute-start.4) | collective-permute-done | bytes 213024 | tf_op jit(solution)/shard_map/ppermute | solution.py:378
  51.3 1.6 %shard_map.68 = (f32[16,256]{1,0:T(8,128)S(1)}, f32[16,256]{1,0:T(8,128)S(1)}, f32[16,256]{1,0:T(8,128)S(1)}, f32[16,256]{1,0:T(8,128)S(1)}) custom-call(s32[4]{0:T(128)S(1)} %pad_add_fusion.idx, f32[64,64,256]{2,1,0:T(8,128)S(1)} %get-tuple-element.73.g, f32[16,256]{1,0:T(8,128)S(1)} %get-tuple-element.74.i0, f32[208,256]{1,0:T(8,128)S(1)} %collective-permute-done.3.r1.a1, ...), custom_call_target="tpu_custom_call" | custom-call | tf_op jit(solution)/shard_map/pallas_call | solution.py:69
  52.9 1.7 %shard_map.69 = (f32[208,256]{1,0:T(8,128)S(1)}, f32[208,256]{1,0:T(8,128)S(1)}, f32[208,256]{1,0:T(8,128)S(1)}) custom-call(s32[4]{0:T(128)S(1)} %pad_add_fusion.idx, f32[4096,256]{1,0:T(8,128)} %bitcast.17, f32[16,256]{1,0:T(8,128)S(1)} %get-tuple-element.78.t1, f32[16,256]{1,0:T(8,128)S(1)} %get-tuple-element.79.t2, f32[16,256]{1,0:T(8,128)S(1)} %get-tuple-element.80.t3), custom_call_target="tpu_custom_call" | custom-call | tf_op jit(solution)/shard_map/pallas_call | solution.py:69
  55.5 2.8 %collective-permute-start.7 = (f32[208,256]{1,0:T(8,128)S(1)}, f32[208,256]{1,0:T(8,128)S(1)}, u32[]{:S(2)}, u32[]{:S(2)}) collective-permute-start(f32[208,256]{1,0:T(8,128)S(1)} %get-tuple-element.82), channel_id=1, source_target_pairs={{0,2},{1,3},{2,0},{3,1},{4,6},{5,7},{6,4},{7,5},{8,10},{9,11},{10,... | collective-permute-start | bytes 638984 | tf_op jit(solution)/shard_map/ppermute | solution.py:378
  58.8 2.6 %shard_map.70 = (f32[3,256,256]{2,1,0:T(8,128)S(1)}, bf16[3,256,256]{2,1,0:T(8,128)(2,1)S(1)}, bf16[3,256,256]{2,1,0:T(8,128)(2,1)S(1)}, f32[256,256]{1,0:T(8,128)S(1)}) custom-call(s32[4]{0:T(128)S(1)} %pad_add_fusion.idx, f32[4096,256]{1,0:T(8,128)} %bitcast.18, f32[208,256]{1,0:T(8,128)S(1)} %collective-permute-done.3.r1.a1, ...), custom_call_target="tpu_custom_call" | custom-call | tf_op jit(solution)/shard_map/pallas_call | solution.py:69
  62.7 5.0 %collective-permute-done.7.a2 = f32[208,256]{1,0:T(8,128)S(1)} collective-permute-done((f32[208,256]{1,0:T(8,128)S(1)}, f32[208,256]{1,0:T(8,128)S(1)}, u32[]{:S(2)}, u32[]{:S(2)}) %collective-permute-start.7) | collective-permute-done | bytes 213024 | tf_op jit(solution)/shard_map/ppermute | solution.py:378
  67.7 4.1 %shard_map.71 = (f32[3,256,256]{2,1,0:T(8,128)S(1)}, f32[16,256]{1,0:T(8,128)S(1)}, f32[272,256]{1,0:T(8,128)S(1)}) custom-call(s32[4]{0:T(128)S(1)} %pad_add_fusion.idx, f32[4096,256]{1,0:T(8,128)} %bitcast.19, f32[208,256]{1,0:T(8,128)S(1)} %collective-permute-done.6.a1, f32[208,256]{1,0:T(8,128)S(1)} %collective-permute-done.7.a2, ...), custom_call_target="tpu_custom_call" | custom-call | tf_op jit(solution)/shard_map/pallas_call | solution.py:69
  72.9 2.8 %collective-permute-start.10 = (f32[272,256]{1,0:T(8,128)S(1)}, f32[272,256]{1,0:T(8,128)S(1)}, u32[]{:S(2)}, u32[]{:S(2)}) collective-permute-start(f32[272,256]{1,0:T(8,128)S(1)} %get-tuple-element.93.m0), channel_id=1, source_target_pairs={{0,2},{1,3},{2,0},{3,1},{4,6},{5,7},{6,4},{7,5},{8,10},{9,11},{10,... | collective-permute-start | bytes 835592 | tf_op jit(solution)/shard_map/ppermute | solution.py:378
  76.2 4.8 %collective-permute-done.9.m1 = f32[272,256]{1,0:T(8,128)S(1)} collective-permute-done((f32[272,256]{1,0:T(8,128)S(1)}, f32[272,256]{1,0:T(8,128)S(1)}, u32[]{:S(2)}, u32[]{:S(2)}) %collective-permute-start.9) | collective-permute-done | bytes 278560 | tf_op jit(solution)/shard_map/ppermute | solution.py:378
  81.0 7.1 %collective-permute-done.10.m2 = f32[272,256]{1,0:T(8,128)S(1)} collective-permute-done((f32[272,256]{1,0:T(8,128)S(1)}, f32[272,256]{1,0:T(8,128)S(1)}, u32[]{:S(2)}, u32[]{:S(2)}) %collective-permute-start.10) | collective-permute-done | bytes 278560 | tf_op jit(solution)/shard_map/ppermute | solution.py:378
  88.2 1.3 %shard_map.72 = (f32[272,256]{1,0:T(8,128)S(1)}, f32[272,256]{1,0:T(8,128)S(1)}) custom-call(s32[4]{0:T(128)S(1)} %pad_add_fusion.idx, f32[272,256]{1,0:T(8,128)S(1)} %get-tuple-element.93.m0, f32[272,256]{1,0:T(8,128)S(1)} %collective-permute-done.9.m1, f32[272,256]{1,0:T(8,128)S(1)} %collective-permute-done.10.m2, f32[272,256]{1,0:T(8,128)S(1)} %collective-permute-done.11.m3), custom_call_target="tpu_custom_call" | custom-call | tf_op jit(solution)/shard_map/pallas_call | solution.py:69
  89.6 1.5 %collective-permute-done.12.other = f32[272,256]{1,0:T(8,128)S(1)} collective-permute-done((f32[272,256]{1,0:T(8,128)S(1)}, f32[272,256]{1,0:T(8,128)S(1)}, u32[]{:S(2)}, u32[]{:S(2)}) %collective-permute-start.12) | collective-permute-done | bytes 278560 | tf_op jit(solution)/shard_map/ppermute | solution.py:448
  92.0 1.8 %collective-permute-start.13 = (f32[136,256]{1,0:T(8,128)S(1)}, f32[136,256]{1,0:T(8,128)S(1)}, u32[]{:S(2)}, u32[]{:S(2)}) collective-permute-start(f32[136,256]{1,0:T(8,128)S(1)} %get-tuple-element.97), channel_id=1, source_target_pairs={{0,8},{4,12},{8,16},{12,20},{16,24},{20,28},{24,0},{28,4},{32,40},... | collective-permute-start | bytes 417800 | tf_op jit(solution)/shard_map/ppermute | solution.py:452
  93.8 2.9 %collective-permute-start.14 = (f32[136,256]{1,0:T(8,128)S(1)}, f32[136,256]{1,0:T(8,128)S(1)}, u32[]{:S(2)}, u32[]{:S(2)}) collective-permute-start(f32[136,256]{1,0:T(8,128)S(1)} %get-tuple-element.97), channel_id=1, source_target_pairs={{0,16},{4,20},{8,24},{12,28},{16,0},{20,4},{24,8},{28,12},{32,48},... | collective-permute-start | bytes 417800 | tf_op jit(solution)/shard_map/ppermute | solution.py:452
  96.7 1.3 %collective-permute-start.15 = (f32[136,256]{1,0:T(8,128)S(1)}, f32[136,256]{1,0:T(8,128)S(1)}, u32[]{:S(2)}, u32[]{:S(2)}) collective-permute-start(f32[136,256]{1,0:T(8,128)S(1)} %get-tuple-element.97), channel_id=1, source_target_pairs={{0,24},{4,28},{8,0},{12,4},{16,8},{20,12},{24,16},{28,20},{32,56},... | collective-permute-start | bytes 417800 | tf_op jit(solution)/shard_map/ppermute | solution.py:452
  99.4 4.2 %collective-permute-done.14.h2 = f32[136,256]{1,0:T(8,128)S(1)} collective-permute-done((f32[136,256]{1,0:T(8,128)S(1)}, f32[136,256]{1,0:T(8,128)S(1)}, u32[]{:S(2)}, u32[]{:S(2)}) %collective-permute-start.14) | collective-permute-done | bytes 139296 | tf_op jit(solution)/shard_map/ppermute | solution.py:452
  106.9 2.4 %collective-permute-start.20 = (f32[136,256]{1,0:T(8,128)S(1)}, f32[136,256]{1,0:T(8,128)S(1)}, u32[]{:S(2)}, u32[]{:S(2)}) collective-permute-start(f32[136,256]{1,0:T(8,128)S(1)} %get-tuple-element.98), channel_id=1, source_target_pairs={{0,64},{4,68},{8,72},{12,76},{16,80},{20,84},{24,88},{28,92},{32,9... | collective-permute-start | bytes 417800 | tf_op jit(solution)/shard_map/ppermute | solution.py:452
  109.3 3.6 %collective-permute-done.19.h1 = f32[136,256]{1,0:T(8,128)S(1)} collective-permute-done((f32[136,256]{1,0:T(8,128)S(1)}, f32[136,256]{1,0:T(8,128)S(1)}, u32[]{:S(2)}, u32[]{:S(2)}) %collective-permute-start.19) | collective-permute-done | bytes 139296 | tf_op jit(solution)/shard_map/ppermute | solution.py:452
  112.9 2.0 %collective-permute-done.20.h2 = f32[136,256]{1,0:T(8,128)S(1)} collective-permute-done((f32[136,256]{1,0:T(8,128)S(1)}, f32[136,256]{1,0:T(8,128)S(1)}, u32[]{:S(2)}, u32[]{:S(2)}) %collective-permute-start.20) | collective-permute-done | bytes 139296 | tf_op jit(solution)/shard_map/ppermute | solution.py:452
  115.0 2.1 %collective-permute-done.21.h3 = f32[136,256]{1,0:T(8,128)S(1)} collective-permute-done((f32[136,256]{1,0:T(8,128)S(1)}, f32[136,256]{1,0:T(8,128)S(1)}, u32[]{:S(2)}, u32[]{:S(2)}) %collective-permute-start.21) | collective-permute-done | bytes 139296 | tf_op jit(solution)/shard_map/ppermute | solution.py:452
  118.4 2.2 %shard_map.76 = (f32[16,64]{1,0:T(8,128)S(1)}, f32[16,64]{1,0:T(8,128)S(1)}, f32[16,64]{1,0:T(8,128)S(1)}, f32[16,64]{1,0:T(8,128)S(1)}) custom-call(s32[4]{0:T(128)S(1)} %pad_add_fusion.idx, f32[1,256]{1,0:T(1,128)S(1)} %bitcast.13, f32[136,256]{1,0:T(8,128)S(1)} %collective-permute-done.19.h1, f32[136,256]{1,0:T(8,128)S(1)} %collective-permute-done.20.h2, ...), custom_call_target="tpu_custom_call" | custom-call | tf_op jit(solution)/shard_map/pallas_call | solution.py:69
  121.6 3.0 %collective-permute-start.26 = (f32[16,64]{1,0:T(8,128)S(1)}, f32[16,64]{1,0:T(8,128)S(1)}, u32[]{:S(2)}, u32[]{:S(2)}) collective-permute-start(f32[16,64]{1,0:T(8,128)S(1)} %get-tuple-element.105), channel_id=1, source_target_pairs={{0,2},{1,3},{2,0},{3,1},{4,6},{5,7},{6,4},{7,5},{8,10},{9,11},{10,... | collective-permute-start | bytes 12296 | tf_op jit(solution)/shard_map/ppermute | solution.py:378
  126.7 1.5 %collective-permute-done.27.r3 = f32[16,64]{1,0:T(8,128)S(1)} collective-permute-done((f32[16,64]{1,0:T(8,128)S(1)}, f32[16,64]{1,0:T(8,128)S(1)}, u32[]{:S(2)}, u32[]{:S(2)}) %collective-permute-start.27) | collective-permute-done | bytes 4128 | tf_op jit(solution)/shard_map/ppermute | solution.py:378
  (50 shorter events, 19.2 us)
Async XLA Ops:
  0.0 8.7 %copy-start.3 = (s32[4096,1]{0,1:T(1,128)S(1)}, s32[4096,1]{0,1:T(1,128)}, u32[]{:S(2)}) copy-start(s32[4096,1]{0,1:T(1,128)} %param.10) | copy-start | bytes 49156
  0.0 8.8 %copy-start.2 = (s32[4096]{0:T(1024)S(1)}, s32[4096]{0:T(1024)}, u32[]{:S(2)}) copy-start(s32[4096]{0:T(1024)} %param.11) | copy-start | bytes 49156
  0.0 8.8 %copy-start = (f32[4096,64]{0,1:T(8,128)S(1)}, f32[4096,64]{0,1:T(8,128)}, u32[]{:S(2)}) copy-start(f32[4096,64]{0,1:T(8,128)} %param.9) | copy-start | bytes 3145732
  2.2 30.3 %collective-permute-start = (f32[640,256]{1,0:T(8,128)S(1)}, f32[640,256]{1,0:T(8,128)S(1)}, u32[]{:S(2)}, u32[]{:S(2)}) collective-permute-start(f32[640,256]{1,0:T(8,128)S(1)} %get-tuple-element.56), channel_id=1, source_target_pairs={{0,1},{1,2},{2,3},{3,0},{4,5},{5,6},{6,7},{7,4},{8,9},{9,10},{10,1... | collective-permute-start | bytes 1966088 | tf_op jit(solution)/shard_map/ppermute | solution.py:378
  4.1 32.1 %collective-permute-start.1 = (f32[640,256]{1,0:T(8,128)S(1)}, f32[640,256]{1,0:T(8,128)S(1)}, u32[]{:S(2)}, u32[]{:S(2)}) collective-permute-start(f32[640,256]{1,0:T(8,128)S(1)} %get-tuple-element.57), channel_id=1, source_target_pairs={{0,2},{1,3},{2,0},{3,1},{4,6},{5,7},{6,4},{7,5},{8,10},{9,11},{10,... | collective-permute-start | bytes 1966088 | tf_op jit(solution)/shard_map/ppermute | solution.py:378
  7.7 28.5 %collective-permute-start.2 = (f32[640,256]{1,0:T(8,128)S(1)}, f32[640,256]{1,0:T(8,128)S(1)}, u32[]{:S(2)}, u32[]{:S(2)}) collective-permute-start(f32[640,256]{1,0:T(8,128)S(1)} %get-tuple-element.58), channel_id=1, source_target_pairs={{0,3},{1,0},{2,1},{3,2},{4,7},{5,4},{6,5},{7,6},{8,11},{9,8},{10,9... | collective-permute-start | bytes 1966088 | tf_op jit(solution)/shard_map/ppermute | solution.py:378
  37.9 8.4 %collective-permute-start.3 = (f32[208,256]{1,0:T(8,128)S(1)}, f32[208,256]{1,0:T(8,128)S(1)}, u32[]{:S(2)}, u32[]{:S(2)}) collective-permute-start(f32[208,256]{1,0:T(8,128)S(1)} %get-tuple-element.70), channel_id=1, source_target_pairs={{0,1},{1,2},{2,3},{3,0},{4,5},{5,6},{6,7},{7,4},{8,9},{9,10},{10,1... | collective-permute-start | bytes 638984 | tf_op jit(solution)/shard_map/ppermute | solution.py:378
  39.2 12.1 %collective-permute-start.4 = (f32[208,256]{1,0:T(8,128)S(1)}, f32[208,256]{1,0:T(8,128)S(1)}, u32[]{:S(2)}, u32[]{:S(2)}) collective-permute-start(f32[208,256]{1,0:T(8,128)S(1)} %get-tuple-element.71), channel_id=1, source_target_pairs={{0,2},{1,3},{2,0},{3,1},{4,6},{5,7},{6,4},{7,5},{8,10},{9,11},{10,... | collective-permute-start | bytes 638984 | tf_op jit(solution)/shard_map/ppermute | solution.py:378
  41.6 9.7 %collective-permute-start.5 = (f32[208,256]{1,0:T(8,128)S(1)}, f32[208,256]{1,0:T(8,128)S(1)}, u32[]{:S(2)}, u32[]{:S(2)}) collective-permute-start(f32[208,256]{1,0:T(8,128)S(1)} %get-tuple-element.72), channel_id=1, source_target_pairs={{0,3},{1,0},{2,1},{3,2},{4,7},{5,4},{6,5},{7,6},{8,11},{9,8},{10,9... | collective-permute-start | bytes 638984 | tf_op jit(solution)/shard_map/ppermute | solution.py:378
  54.6 8.1 %collective-permute-start.6 = (f32[208,256]{1,0:T(8,128)S(1)}, f32[208,256]{1,0:T(8,128)S(1)}, u32[]{:S(2)}, u32[]{:S(2)}) collective-permute-start(f32[208,256]{1,0:T(8,128)S(1)} %get-tuple-element.81), channel_id=1, source_target_pairs={{0,1},{1,2},{2,3},{3,0},{4,5},{5,6},{6,7},{7,4},{8,9},{9,10},{10,1... | collective-permute-start | bytes 638984 | tf_op jit(solution)/shard_map/ppermute | solution.py:378
  55.5 12.2 %collective-permute-start.7 = (f32[208,256]{1,0:T(8,128)S(1)}, f32[208,256]{1,0:T(8,128)S(1)}, u32[]{:S(2)}, u32[]{:S(2)}) collective-permute-start(f32[208,256]{1,0:T(8,128)S(1)} %get-tuple-element.82), channel_id=1, source_target_pairs={{0,2},{1,3},{2,0},{3,1},{4,6},{5,7},{6,4},{7,5},{8,10},{9,11},{10,... | collective-permute-start | bytes 638984 | tf_op jit(solution)/shard_map/ppermute | solution.py:378
  58.3 9.4 %collective-permute-start.8 = (f32[208,256]{1,0:T(8,128)S(1)}, f32[208,256]{1,0:T(8,128)S(1)}, u32[]{:S(2)}, u32[]{:S(2)}) collective-permute-start(f32[208,256]{1,0:T(8,128)S(1)} %get-tuple-element.83), channel_id=1, source_target_pairs={{0,3},{1,0},{2,1},{3,2},{4,7},{5,4},{6,5},{7,6},{8,11},{9,8},{10,9... | collective-permute-start | bytes 638984 | tf_op jit(solution)/shard_map/ppermute | solution.py:378
  67.7 50.7 %copy-start.1 = (f32[256]{0:T(256)S(1)}, f32[256]{0:T(256)}, u32[]{:S(2)}) copy-start(f32[256]{0:T(256)} %param.6) | copy-start | bytes 3076
  71.8 9.3 %collective-permute-start.9 = (f32[272,256]{1,0:T(8,128)S(1)}, f32[272,256]{1,0:T(8,128)S(1)}, u32[]{:S(2)}, u32[]{:S(2)}) collective-permute-start(f32[272,256]{1,0:T(8,128)S(1)} %get-tuple-element.93.m0), channel_id=1, source_target_pairs={{0,1},{1,2},{2,3},{3,0},{4,5},{5,6},{6,7},{7,4},{8,9},{9,10},{10,1... | collective-permute-start | bytes 835592 | tf_op jit(solution)/shard_map/ppermute | solution.py:378
  72.9 15.3 %collective-permute-start.10 = (f32[272,256]{1,0:T(8,128)S(1)}, f32[272,256]{1,0:T(8,128)S(1)}, u32[]{:S(2)}, u32[]{:S(2)}) collective-permute-start(f32[272,256]{1,0:T(8,128)S(1)} %get-tuple-element.93.m0), channel_id=1, source_target_pairs={{0,2},{1,3},{2,0},{3,1},{4,6},{5,7},{6,4},{7,5},{8,10},{9,11},{10,... | collective-permute-start | bytes 835592 | tf_op jit(solution)/shard_map/ppermute | solution.py:378
  75.7 12.5 %collective-permute-start.11 = (f32[272,256]{1,0:T(8,128)S(1)}, f32[272,256]{1,0:T(8,128)S(1)}, u32[]{:S(2)}, u32[]{:S(2)}) collective-permute-start(f32[272,256]{1,0:T(8,128)S(1)} %get-tuple-element.93.m0), channel_id=1, source_target_pairs={{0,3},{1,0},{2,1},{3,2},{4,7},{5,4},{6,5},{7,6},{8,11},{9,8},{10,9... | collective-permute-start | bytes 835592 | tf_op jit(solution)/shard_map/ppermute | solution.py:378
  89.5 1.6 %collective-permute-start.12 = (f32[272,256]{1,0:T(8,128)S(1)}, f32[272,256]{1,0:T(8,128)S(1)}, u32[]{:S(2)}, u32[]{:S(2)}) collective-permute-start(f32[272,256]{1,0:T(8,128)S(1)} %get-tuple-element.94.own), channel_id=1, source_target_pairs={{0,4},{4,0},{8,12},{12,8},{16,20},{20,16},{24,28},{28,24},{32,36},... | collective-permute-start | bytes 835592 | tf_op jit(solution)/shard_map/ppermute | solution.py:448
  92.0 7.3 %collective-permute-start.13 = (f32[136,256]{1,0:T(8,128)S(1)}, f32[136,256]{1,0:T(8,128)S(1)}, u32[]{:S(2)}, u32[]{:S(2)}) collective-permute-start(f32[136,256]{1,0:T(8,128)S(1)} %get-tuple-element.97), channel_id=1, source_target_pairs={{0,8},{4,12},{8,16},{12,20},{16,24},{20,28},{24,0},{28,4},{32,40},... | collective-permute-start | bytes 417800 | tf_op jit(solution)/shard_map/ppermute | solution.py:452
  93.8 9.7 %collective-permute-start.14 = (f32[136,256]{1,0:T(8,128)S(1)}, f32[136,256]{1,0:T(8,128)S(1)}, u32[]{:S(2)}, u32[]{:S(2)}) collective-permute-start(f32[136,256]{1,0:T(8,128)S(1)} %get-tuple-element.97), channel_id=1, source_target_pairs={{0,16},{4,20},{8,24},{12,28},{16,0},{20,4},{24,8},{28,12},{32,48},... | collective-permute-start | bytes 417800 | tf_op jit(solution)/shard_map/ppermute | solution.py:452
  96.7 6.8 %collective-permute-start.15 = (f32[136,256]{1,0:T(8,128)S(1)}, f32[136,256]{1,0:T(8,128)S(1)}, u32[]{:S(2)}, u32[]{:S(2)}) collective-permute-start(f32[136,256]{1,0:T(8,128)S(1)} %get-tuple-element.97), channel_id=1, source_target_pairs={{0,24},{4,28},{8,0},{12,4},{16,8},{20,12},{24,16},{28,20},{32,56},... | collective-permute-start | bytes 417800 | tf_op jit(solution)/shard_map/ppermute | solution.py:452
  99.4 4.7 %collective-permute-start.16 = (f32[136,256]{1,0:T(8,128)S(1)}, f32[136,256]{1,0:T(8,128)S(1)}, u32[]{:S(2)}, u32[]{:S(2)}) collective-permute-start(f32[136,256]{1,0:T(8,128)S(1)} %collective-permute-done.13.h1), channel_id=1, source_target_pairs={{0,4},{4,0},{8,12},{12,8},{16,20},{20,16},{24,28},{28,24},{32,36},... | collective-permute-start | bytes 417800 | tf_op jit(solution)/shard_map/ppermute | solution.py:448
  103.5 1.4 %collective-permute-start.17 = (f32[136,256]{1,0:T(8,128)S(1)}, f32[136,256]{1,0:T(8,128)S(1)}, u32[]{:S(2)}, u32[]{:S(2)}) collective-permute-start(f32[136,256]{1,0:T(8,128)S(1)} %collective-permute-done.14.h2), channel_id=1, source_target_pairs={{0,4},{4,0},{8,12},{12,8},{16,20},{20,16},{24,28},{28,24},{32,36},... | collective-permute-start | bytes 417800 | tf_op jit(solution)/shard_map/ppermute | solution.py:448
  103.5 1.6 %collective-permute-start.18 = (f32[136,256]{1,0:T(8,128)S(1)}, f32[136,256]{1,0:T(8,128)S(1)}, u32[]{:S(2)}, u32[]{:S(2)}) collective-permute-start(f32[136,256]{1,0:T(8,128)S(1)} %collective-permute-done.15.h3), channel_id=1, source_target_pairs={{0,4},{4,0},{8,12},{12,8},{16,20},{20,16},{24,28},{28,24},{32,36},... | collective-permute-start | bytes 417800 | tf_op jit(solution)/shard_map/ppermute | solution.py:448
  106.4 6.6 %collective-permute-start.19 = (f32[136,256]{1,0:T(8,128)S(1)}, f32[136,256]{1,0:T(8,128)S(1)}, u32[]{:S(2)}, u32[]{:S(2)}) collective-permute-start(f32[136,256]{1,0:T(8,128)S(1)} %get-tuple-element.98), channel_id=1, source_target_pairs={{0,32},{4,36},{8,40},{12,44},{16,48},{20,52},{24,56},{28,60},{32,6... | collective-permute-start | bytes 417800 | tf_op jit(solution)/shard_map/ppermute | solution.py:452
  106.9 8.0 %collective-permute-start.20 = (f32[136,256]{1,0:T(8,128)S(1)}, f32[136,256]{1,0:T(8,128)S(1)}, u32[]{:S(2)}, u32[]{:S(2)}) collective-permute-start(f32[136,256]{1,0:T(8,128)S(1)} %get-tuple-element.98), channel_id=1, source_target_pairs={{0,64},{4,68},{8,72},{12,76},{16,80},{20,84},{24,88},{28,92},{32,9... | collective-permute-start | bytes 417800 | tf_op jit(solution)/shard_map/ppermute | solution.py:452
  109.3 7.7 %collective-permute-start.21 = (f32[136,256]{1,0:T(8,128)S(1)}, f32[136,256]{1,0:T(8,128)S(1)}, u32[]{:S(2)}, u32[]{:S(2)}) collective-permute-start(f32[136,256]{1,0:T(8,128)S(1)} %get-tuple-element.98), channel_id=1, source_target_pairs={{0,96},{4,100},{8,104},{12,108},{16,112},{20,116},{24,120},{28,124... | collective-permute-start | bytes 417800 | tf_op jit(solution)/shard_map/ppermute | solution.py:452
  112.9 4.9 %collective-permute-start.22 = (f32[136,256]{1,0:T(8,128)S(1)}, f32[136,256]{1,0:T(8,128)S(1)}, u32[]{:S(2)}, u32[]{:S(2)}) collective-permute-start(f32[136,256]{1,0:T(8,128)S(1)} %collective-permute-done.19.h1), channel_id=1, source_target_pairs={{0,4},{4,0},{8,12},{12,8},{16,20},{20,16},{24,28},{28,24},{32,36},... | collective-permute-start | bytes 417800 | tf_op jit(solution)/shard_map/ppermute | solution.py:448
  115.0 2.9 %collective-permute-start.23 = (f32[136,256]{1,0:T(8,128)S(1)}, f32[136,256]{1,0:T(8,128)S(1)}, u32[]{:S(2)}, u32[]{:S(2)}) collective-permute-start(f32[136,256]{1,0:T(8,128)S(1)} %collective-permute-done.20.h2), channel_id=1, source_target_pairs={{0,4},{4,0},{8,12},{12,8},{16,20},{20,16},{24,28},{28,24},{32,36},... | collective-permute-start | bytes 417800 | tf_op jit(solution)/shard_map/ppermute | solution.py:448
  117.0 1.4 %collective-permute-start.24 = (f32[136,256]{1,0:T(8,128)S(1)}, f32[136,256]{1,0:T(8,128)S(1)}, u32[]{:S(2)}, u32[]{:S(2)}) collective-permute-start(f32[136,256]{1,0:T(8,128)S(1)} %collective-permute-done.21.h3), channel_id=1, source_target_pairs={{0,4},{4,0},{8,12},{12,8},{16,20},{20,16},{24,28},{28,24},{32,36},... | collective-permute-start | bytes 417800 | tf_op jit(solution)/shard_map/ppermute | solution.py:448
  120.6 4.9 %collective-permute-start.25 = (f32[16,64]{1,0:T(8,128)S(1)}, f32[16,64]{1,0:T(8,128)S(1)}, u32[]{:S(2)}, u32[]{:S(2)}) collective-permute-start(f32[16,64]{1,0:T(8,128)S(1)} %get-tuple-element.104), channel_id=1, source_target_pairs={{0,1},{1,2},{2,3},{3,0},{4,5},{5,6},{6,7},{7,4},{8,9},{9,10},{10,1... | collective-permute-start | bytes 12296 | tf_op jit(solution)/shard_map/ppermute | solution.py:378
  121.6 5.2 %collective-permute-start.26 = (f32[16,64]{1,0:T(8,128)S(1)}, f32[16,64]{1,0:T(8,128)S(1)}, u32[]{:S(2)}, u32[]{:S(2)}) collective-permute-start(f32[16,64]{1,0:T(8,128)S(1)} %get-tuple-element.105), channel_id=1, source_target_pairs={{0,2},{1,3},{2,0},{3,1},{4,6},{5,7},{6,4},{7,5},{8,10},{9,11},{10,... | collective-permute-start | bytes 12296 | tf_op jit(solution)/shard_map/ppermute | solution.py:378
  124.6 3.7 %collective-permute-start.27 = (f32[16,64]{1,0:T(8,128)S(1)}, f32[16,64]{1,0:T(8,128)S(1)}, u32[]{:S(2)}, u32[]{:S(2)}) collective-permute-start(f32[16,64]{1,0:T(8,128)S(1)} %get-tuple-element.106), channel_id=1, source_target_pairs={{0,3},{1,0},{2,1},{3,2},{4,7},{5,4},{6,5},{7,6},{8,11},{9,8},{10,9... | collective-permute-start | bytes 12296 | tf_op jit(solution)/shard_map/ppermute | solution.py:378

commit v5 on v4

--- a/solution.py
+++ b/solution.py
@@ -17,7 +17,7 @@
 HALF = R // 2
 ROWS = 4
 SUB = 16
-CHUNKS = ((5, 5), (3,), (3,))
+CHUNKS = ((5, 5), (3, 3))
 SEGS = tuple(n for chunk in CHUNKS for n in chunk)
 SIZES = tuple(sum(chunk) for chunk in CHUNKS)
 ENDS = tuple(sum(SEGS[: i + 1]) for i in range(len(SEGS)))
@@ -173,33 +173,27 @@
     late.wait()
 
 
-def second_kernel(idx, flat, a1, a2, a3, both, pref, ah, al, three, own, sem):
+def second_kernel(idx, flat, a1, a2, a3, both, pref, ah, al, four, three, own, sem):
     z = idx[Z]
     copy = own_copy(z, flat, own, SIZES[0], sem)
     copy.start()
     assemble(z, (own, a1, a2, a3), ah, al, copy)
     chains(CHUNKS[1], ah, al, pref)
-    three[...] = mm(both[...], pref[SIZES[1] - 1])
-
-
-def third_kernel(
-    idx, flat, a1, a2, a3, b0, p01, ah01, al01, p2, ah2, al2, three, pref, shifts, whole, ah, al, b_s, own, sem
-):
+    three[...] = mm(both[...], pref[CHUNKS[1][0] - 1])
+    four[...] = mm(three[...], pref[SIZES[1] - 1])
+
+
+def third_kernel(idx, b0, b1, b2, b3, p01, ah01, al01, p23, ah23, al23, four, shifts, whole, b_s):
     z = idx[Z]
-    copy = own_copy(z, flat, own, SIZES[0] + SIZES[1], sem)
-    copy.start()
-    assemble(z, (own, a1, a2, a3), ah, al, copy)
-    b_s[z] = b0[...]
-    for d, a in ((1, a1), (2, a2), (3, a3)):
-        b_s[lax.rem(z - d + ROWS, ROWS)] = a[SIZES[2] * 64 :, :]
+    for d, b in enumerate((b0, b1, b2, b3)):
+        b_s[lax.rem(z - d + ROWS, ROWS)] = b[...]
     b = jnp.concatenate([b_s[i, :, :64] for i in range(ROWS)], axis=1)
     first = lax.broadcasted_iota(jnp.int32, (PAD, N), 0) == 0
 
     def row(k):
         return jnp.where(first, b[k : k + 1, :], 0.0)
 
-    mats = [(ah01, al01, i) for i in range(SIZES[0])] + [(ah2, al2, i) for i in range(SIZES[1])]
-    mats += [(ah, al, i) for i in range(SIZES[2])]
+    mats = [(ah01, al01, i) for i in range(SIZES[0])] + [(ah23, al23, i) for i in range(SIZES[1])]
     starts = [end - n for end, n in zip(ENDS, SEGS)]
     p = [row(k) for k in starts]
     for c, k in enumerate(starts):
@@ -212,11 +206,10 @@
             h, l, i = mats[k]
             p[c] = by_step(p[c], h[i], l[i]) + row(k)
             shifts[k : k + 1, :] = p[c][:1]
-    chains(CHUNKS[2], ah, al, pref)
     v = mm(p[0], p01[SIZES[0] - 1]) + p[1]
-    v = mm(v, p2[SIZES[1] - 1]) + p[2]
-    v = mm(v, pref[SIZES[2] - 1]) + p[3]
-    whole[:N, :] = mm(three[...], pref[SIZES[2] - 1])
+    v = mm(v, p23[CHUNKS[1][0] - 1]) + p[2]
+    v = mm(v, p23[SIZES[1] - 1]) + p[3]
+    whole[:N, :] = four[...]
     whole[N:, :] = v
 
 
@@ -288,7 +281,7 @@
 
 
 def states_kernel(
-    idx, prior, h1, h2, h3, g1, g2, g3, before, p01, p2, p3, shifts, o0, o1, o2, o3, st_s, m_s, s_s
+    idx, prior, h1, h2, h3, g1, g2, g3, before, p01, p23, shifts, o0, o1, o2, o3, st_s, m_s, s_s
 ):
     z, pos = idx[Z], idx[X]
     join_halves(pos, idx[C], (h1, h2, h3), (g1, g2, g3), m_s)
@@ -302,8 +295,7 @@
     s = apply(s_s[...], before[...])
     eye = lax.broadcasted_iota(jnp.int32, (N, N), 0) == lax.broadcasted_iota(jnp.int32, (N, N), 1)
     first = lax.broadcasted_iota(jnp.int32, (PAD, N), 0) == 0
-    prefs = [(p01, i) for i in range(SIZES[0])] + [(p2, i) for i in range(SIZES[1])]
-    prefs += [(p3, i) for i in range(SIZES[2])]
+    prefs = [(p01, i) for i in range(SIZES[0])] + [(p23, i) for i in range(SIZES[1])]
     for end, n in zip(ENDS, SEGS):
         col = jnp.sum(jnp.where(eye, s[0:1, :], 0.0), axis=1, keepdims=True)
         for k in range(end - n, end):
@@ -334,26 +326,20 @@
         copy.wait()
 
 
-def send_b_kernel(idx, flat, sums, o1, o2, o3, info, sems):
-    copies = send_copies(idx[Z], flat, (o1, o2, o3), SIZES[0], SIZES[1], sems)
+def sum_kernel(idx, sums, info):
     info[...] = jnp.sum(sums[...], axis=0)
-    for copy, o in zip(copies, (o1, o2, o3)):
+
+
+def send_b_kernel(idx, flat, o1, o2, o3, sems):
+    for copy in send_copies(idx[Z], flat, (o1, o2, o3), SIZES[0], SIZES[1], sems):
         copy.wait()
-        o[SIZES[1] * 64 :, :] = info[...]
-
-
-def send_c_kernel(idx, flat, t1, t2, t3, o1, o2, o3, sems):
-    copies = send_copies(idx[Z], flat, (o1, o2, o3), SIZES[0] + SIZES[1], SIZES[2], sems)
-    for copy, o, t in zip(copies, (o1, o2, o3), (t1, t2, t3)):
-        copy.wait()
-        o[SIZES[2] * 64 :, :] = t[...]
 
 
 def offset_kernel(idx, g, i0, r1, r2, r3, o0, o1, o2, o3, info_s, off_s):
     z = idx[Z]
     info_s[z] = i0[...]
     for d, r in ((1, r1), (2, r2), (3, r3)):
-        info_s[lax.rem(z - d + ROWS, ROWS)] = r[r.shape[0] - 16 :, :]
+        info_s[lax.rem(z - d + ROWS, ROWS)] = r[...]
     lane = lax.broadcasted_iota(jnp.int32, (64, 128), 1)
     for q in range(4):
         full = jnp.concatenate([info_s[i, :, q * 64 : (q + 1) * 64] for i in range(ROWS)], axis=1)
@@ -396,9 +382,10 @@
     sums = lax.all_to_all(partial, "tm", 0, 0, tiled=True).reshape(32, 16, N)
     sums, idx, prior, *part_a = lax.optimization_barrier((sums, idx, prior, *part_a))
 
-    *sent_b, info = call(
-        send_b_kernel, [(SIZES[1] * 64 + 16, N)] * 3 + [(16, N)], idx, (sums,), [dma3], far=(flat,)
-    )
+    (info,) = call(sum_kernel, [(16, N)], idx, (sums,))
+    infos = along_rows([info] * 3)
+    sent_b = call(send_b_kernel, [(SIZES[1] * 64, N)] * 3, idx, (), [dma3], far=(flat,))
+    infos, sent_b = lax.optimization_barrier((infos, sent_b))
     part_b = along_rows(sent_b)
     p01, ah01, al01, both, staged = call(
         first_kernel,
@@ -408,32 +395,28 @@
         [pltpu.VMEM((SIZES[0] * 64, N), F32), pltpu.SemaphoreType.DMA((2,))],
         far=(flat, gains),
     )
-    p01, ah01, al01, both, staged, *part_b = lax.optimization_barrier((p01, ah01, al01, both, staged, *part_b))
     offs = call(
         offset_kernel,
         [(16, N)] * 4,
         idx,
-        (staged, info, *part_b),
+        (staged, info, *infos),
         [pltpu.VMEM((ROWS, 16, N), F32), pltpu.VMEM((ROWS, 16, 128), F32)],
     )
-    sent_c = call(send_c_kernel, [(SIZES[2] * 64 + 16, N)] * 3, idx, offs[1:], [dma3], far=(flat,))
-    part_c = along_rows(sent_c)
-    p2, ah2, al2, three = call(
+    offs = [offs[0], *along_rows(offs[1:])]
+    p23, ah23, al23, four = call(
         second_kernel,
         [(SIZES[1], N, N), ((SIZES[1], N, N), BF16), ((SIZES[1], N, N), BF16), (N, N)],
         idx,
         (*part_b, both),
-        [pltpu.VMEM((SIZES[1] * 64, N), F32), pltpu.SemaphoreType.DMA],
+        [pltpu.VMEM((N, N), F32), pltpu.VMEM((SIZES[1] * 64, N), F32), pltpu.SemaphoreType.DMA],
         far=(flat,),
     )
-    p3, shifts, whole = call(
+    shifts, whole = call(
         third_kernel,
-        [(SIZES[2], N, N), (SUB, N), (R, N)],
-        idx,
-        (*part_c, offs[0], p01, ah01, al01, p2, ah2, al2, three),
-        [pltpu.VMEM((SIZES[2], N, N), BF16)] * 2
-        + [pltpu.VMEM((ROWS, 16, N), F32), pltpu.VMEM((SIZES[2] * 64, N), F32), pltpu.SemaphoreType.DMA],
-        far=(flat,),
+        [(SUB, N), (R, N)],
+        idx,
+        (*offs, p01, ah01, al01, p23, ah23, al23, four),
+        [pltpu.VMEM((ROWS, 16, N), F32)],
     )
 
     block, before = call(
@@ -468,7 +451,7 @@
         states_kernel,
         [(SUB, 64)] * 4,
         idx,
-        (prior, *halves, *[other_core(h) for h in halves], before, p01, p2, p3, shifts),
+        (prior, *halves, *[other_core(h) for h in halves], before, p01, p23, shifts),
         [pltpu.VMEM((ROWS, SUB, 64), F32), pltpu.VMEM((4, R, N), F32), pltpu.VMEM((PAD, N), F32)],
     )
     got = [outs[0], *along_rows(outs[1:])]

time: 130 us -> 128 us (0.985)
  Pallas kernels: 31.8 us -> 29.6 us
  starting transfers between devices: 34 us -> 35.6 us
    pallas_call x12, Pallas kernels: 23.7 us -> 21.5 us  [call(): pl.pallas_call(kernel, out_shape=[pltpu.VMEM(s, t) for s, t in outs], in_...]
    ppermute x15 -> x18, starting transfers between devices: 24.3 us -> 25.9 us  [along_row(): return lax.ppermute(x, 'row', [(i, (i + d) % ROWS) for i in range(ROWS)])]
    ppermute x15 -> x18, waiting for transfers between devices: 30.4 us -> 29.5 us  [along_row(): return lax.ppermute(x, 'row', [(i, (i + d) % ROWS) for i in range(ROWS)])]
  transfers between devices with their start and end apart: 28 -> 31, of which waited for: 18 -> 19; matrix products, arithmetic and copies ran while one was open for 0% -> 0% of each run, Pallas kernels for 11% -> 14%
where the time goes in v5:
time: 128 us
  waiting for transfers between devices  45.7 us (36%)
  starting transfers between devices  35.6 us (28%)
  Pallas kernels  29.6 us (23%)
  blocking collectives  16.7 us (13%)
    ppermute x18, waiting for transfers between devices, along_row(): return lax.ppermute(x, 'row', [(i, (i + d) % ROWS) for i in range(ROWS)])  29.5 us
    ppermute x18, starting transfers between devices, along_row(): return lax.ppermute(x, 'row', [(i, (i + d) % ROWS) for i in range(ROWS)])  25.9 us
    pallas_call x12, Pallas kernels, call(): pl.pallas_call(kernel, out_shape=[pltpu.VMEM(s, t) for s, t in outs], in_...  21.5 us
    all_to_all x1, blocking collectives, shards(): sums = lax.all_to_all(partial, 'tm', 0, 0, tiled=True).reshape(32, 16, N)  16.7 us
    ppermute x6, waiting for transfers between devices, along_tm(): return lax.ppermute(m, 'tm', places)  13.1 us
    ppermute x6, starting transfers between devices, along_tm(): return lax.ppermute(m, 'tm', places)  8.86 us
    pallas_call x1, Pallas kernels, binned(): pl.pallas_call(bin_kernel, out_shape=jax.ShapeDtypeStruct((n_bins // 4, N...  6.91 us
    ppermute x7, waiting for transfers between devices, other_core(): return lax.ppermute(m, 'tm', [(i, i ^ 1) for i in range(32)])  3.09 us
  transfers between devices with their start and end apart: 31, of which 19 were waited for; matrix products, arithmetic and copies ran while one was open for 0% of the time, Pallas kernels for 14%

profile of v5, /device:TPU:6, one launch (start us, length us, event | category | flops | bytes accessed | tf_op | source)
XLA Modules:
  0.0 127.8 jit_solution(8315123801942751934)
XLA Ops:
  0.1 2.1 %shard_map.65 = (f32[640,256]{1,0:T(8,128)S(1)}, f32[640,256]{1,0:T(8,128)S(1)}, f32[640,256]{1,0:T(8,128)S(1)}) custom-call(s32[4]{0:T(128)S(1)} %pad_add_fusion.idx, f32[4096,256]{1,0:T(8,128)} %bitcast.14), custom_call_target="tpu_custom_call" | custom-call | tf_op jit(solution)/shard_map/pallas_call | solution.py:69
  2.2 2.0 %collective-permute-start = (f32[640,256]{1,0:T(8,128)S(1)}, f32[640,256]{1,0:T(8,128)S(1)}, u32[]{:S(2)}, u32[]{:S(2)}) collective-permute-start(f32[640,256]{1,0:T(8,128)S(1)} %get-tuple-element.49), channel_id=1, source_target_pairs={{0,1},{1,2},{2,3},{3,0},{4,5},{5,6},{6,7},{7,4},{8,9},{9,10},{10,1... | collective-permute-start | bytes 1966088 | tf_op jit(solution)/shard_map/ppermute | solution.py:364
  4.1 3.6 %collective-permute-start.1 = (f32[640,256]{1,0:T(8,128)S(1)}, f32[640,256]{1,0:T(8,128)S(1)}, u32[]{:S(2)}, u32[]{:S(2)}) collective-permute-start(f32[640,256]{1,0:T(8,128)S(1)} %get-tuple-element.50), channel_id=1, source_target_pairs={{0,2},{1,3},{2,0},{3,1},{4,6},{5,7},{6,4},{7,5},{8,10},{9,11},{10,... | collective-permute-start | bytes 1966088 | tf_op jit(solution)/shard_map/ppermute | solution.py:364
  8.8 6.9 %shard_map.64 = f32[512,256]{1,0:T(8,128)S(1)} custom-call(s32[1,4096]{1,0:T(1,128)S(1)} %bitcast.12, f32[64,4096]{1,0:T(8,128)S(1)} %bitcast.11), custom_call_target="tpu_custom_call" | custom-call | tf_op jit(solution)/shard_map/pallas_call | solution.py:114
  15.7 16.7 %all_to_all.9.sums = f32[32,16,256]{2,1,0:T(8,128)S(1)} all-to-all(f32[32,16,256]{2,1,0:T(8,128)S(1)} %bitcast.10), channel_id=1, replica_groups=mesh['tm'=32,'row'=4] {'tm'}, dimensions={0} | all-to-all | bytes 1048576 | tf_op jit(solution)/shard_map/all_to_all | solution.py:382
  32.4 3.8 %collective-permute-done.1.a2 = f32[640,256]{1,0:T(8,128)S(1)} collective-permute-done((f32[640,256]{1,0:T(8,128)S(1)}, f32[640,256]{1,0:T(8,128)S(1)}, u32[]{:S(2)}, u32[]{:S(2)}) %collective-permute-start.1) | collective-permute-done | bytes 655392 | tf_op jit(solution)/shard_map/ppermute | solution.py:364
  38.1 2.4 %collective-permute-start.4 = (f32[16,256]{1,0:T(8,128)S(1)}, f32[16,256]{1,0:T(8,128)S(1)}, u32[]{:S(2)}, u32[]{:S(2)}) collective-permute-start(f32[16,256]{1,0:T(8,128)S(1)} %shard_map.67.i0), channel_id=1, source_target_pairs={{0,2},{1,3},{2,0},{3,1},{4,6},{5,7},{6,4},{7,5},{8,10},{9,11},{10,... | collective-permute-start | bytes 49160 | tf_op jit(solution)/shard_map/ppermute | solution.py:364
  41.7 1.8 %shard_map.68 = (f32[384,256]{1,0:T(8,128)S(1)}, f32[384,256]{1,0:T(8,128)S(1)}, f32[384,256]{1,0:T(8,128)S(1)}) custom-call(s32[4]{0:T(128)S(1)} %pad_add_fusion.idx, f32[4096,256]{1,0:T(8,128)} %bitcast.15), custom_call_target="tpu_custom_call" | custom-call | tf_op jit(solution)/shard_map/pallas_call | solution.py:69
  44.7 3.4 %collective-permute-start.10 = (f32[384,256]{1,0:T(8,128)S(1)}, f32[384,256]{1,0:T(8,128)S(1)}, u32[]{:S(2)}, u32[]{:S(2)}) collective-permute-start(f32[384,256]{1,0:T(8,128)S(1)} %get-tuple-element.73), channel_id=1, source_target_pairs={{0,2},{1,3},{2,0},{3,1},{4,6},{5,7},{6,4},{7,5},{8,10},{9,11},{10,... | collective-permute-start | bytes 1179656 | tf_op jit(solution)/shard_map/ppermute | solution.py:364
  48.4 3.5 %shard_map.66 = (f32[10,256,256]{2,1,0:T(8,128)S(1)}, bf16[10,256,256]{2,1,0:T(8,128)(2,1)S(1)}, bf16[10,256,256]{2,1,0:T(8,128)(2,1)S(1)}, f32[256,256]{1,0:T(8,128)S(1)}, f32[64,64,256]{2,1,0:T(8,128)S(1)}) custom-call(s32[4]{0:T(128)S(1)} %pad_add_fusion.idx, f32[4096,256]{1,0:T(8,128)} %bitcast.16, f32[64,64,256]{2,1,0:T(8,128)} %gains.1, ...), custom_call_target="tpu_custom_call" | custom-call | tf_op jit(solution)/shard_map/pallas_call | solution.py:69
  51.8 1.6 %shard_map.69 = (f32[16,256]{1,0:T(8,128)S(1)}, f32[16,256]{1,0:T(8,128)S(1)}, f32[16,256]{1,0:T(8,128)S(1)}, f32[16,256]{1,0:T(8,128)S(1)}) custom-call(s32[4]{0:T(128)S(1)} %pad_add_fusion.idx, f32[64,64,256]{2,1,0:T(8,128)S(1)} %get-tuple-element.57.g, f32[16,256]{1,0:T(8,128)S(1)} %shard_map.67.i0, f32[16,256]{1,0:T(8,128)S(1)} %collective-permute-done.3.r1, ...), custom_call_target="tpu_custom_call" | custom-call | tf_op jit(solution)/shard_map/pallas_call | solution.py:69
  53.4 1.8 %collective-permute-start.6 = (f32[16,256]{1,0:T(8,128)S(1)}, f32[16,256]{1,0:T(8,128)S(1)}, u32[]{:S(2)}, u32[]{:S(2)}) collective-permute-start(f32[16,256]{1,0:T(8,128)S(1)} %get-tuple-element.66), channel_id=1, source_target_pairs={{0,1},{1,2},{2,3},{3,0},{4,5},{5,6},{6,7},{7,4},{8,9},{9,10},{10,1... | collective-permute-start | bytes 49160 | tf_op jit(solution)/shard_map/ppermute | solution.py:364
  55.5 8.6 %collective-permute-done.9.a1 = f32[384,256]{1,0:T(8,128)S(1)} collective-permute-done((f32[384,256]{1,0:T(8,128)S(1)}, f32[384,256]{1,0:T(8,128)S(1)}, u32[]{:S(2)}, u32[]{:S(2)}) %collective-permute-start.9) | collective-permute-done | bytes 393248 | tf_op jit(solution)/shard_map/ppermute | solution.py:364
  64.6 3.1 %shard_map.70 = (f32[6,256,256]{2,1,0:T(8,128)S(1)}, bf16[6,256,256]{2,1,0:T(8,128)(2,1)S(1)}, bf16[6,256,256]{2,1,0:T(8,128)(2,1)S(1)}, f32[256,256]{1,0:T(8,128)S(1)}) custom-call(s32[4]{0:T(128)S(1)} %pad_add_fusion.idx, f32[4096,256]{1,0:T(8,128)} %bitcast.17, f32[384,256]{1,0:T(8,128)S(1)} %collective-permute-done.9.a1, ...), custom_call_target="tpu_custom_call" | custom-call | tf_op jit(solution)/shard_map/pallas_call | solution.py:69
  67.9 2.4 %shard_map.71 = (f32[16,256]{1,0:T(8,128)S(1)}, f32[272,256]{1,0:T(8,128)S(1)}) custom-call(s32[4]{0:T(128)S(1)} %pad_add_fusion.idx, f32[16,256]{1,0:T(8,128)S(1)} %get-tuple-element.65.b0, f32[16,256]{1,0:T(8,128)S(1)} %collective-permute-done.6.b1, f32[16,256]{1,0:T(8,128)S(1)} %collective-permute-done.7.b2, f32[16,256]{1,0:T(8,128)S(1)} %collective-permute-done.8.b3, ...), custom_call_target="tpu_custom_call" | custom-call | tf_op jit(solution)/shard_map/pallas_call | solution.py:69
  70.4 1.4 %collective-permute-start.12 = (f32[272,256]{1,0:T(8,128)S(1)}, f32[272,256]{1,0:T(8,128)S(1)}, u32[]{:S(2)}, u32[]{:S(2)}) collective-permute-start(f32[272,256]{1,0:T(8,128)S(1)} %get-tuple-element.80.m0), channel_id=1, source_target_pairs={{0,1},{1,2},{2,3},{3,0},{4,5},{5,6},{6,7},{7,4},{8,9},{9,10},{10,1... | collective-permute-start | bytes 835592 | tf_op jit(solution)/shard_map/ppermute | solution.py:364
  71.8 2.4 %collective-permute-start.13 = (f32[272,256]{1,0:T(8,128)S(1)}, f32[272,256]{1,0:T(8,128)S(1)}, u32[]{:S(2)}, u32[]{:S(2)}) collective-permute-start(f32[272,256]{1,0:T(8,128)S(1)} %get-tuple-element.80.m0), channel_id=1, source_target_pairs={{0,2},{1,3},{2,0},{3,1},{4,6},{5,7},{6,4},{7,5},{8,10},{9,11},{10,... | collective-permute-start | bytes 835592 | tf_op jit(solution)/shard_map/ppermute | solution.py:364
  74.5 4.9 %collective-permute-done.12.m1 = f32[272,256]{1,0:T(8,128)S(1)} collective-permute-done((f32[272,256]{1,0:T(8,128)S(1)}, f32[272,256]{1,0:T(8,128)S(1)}, u32[]{:S(2)}, u32[]{:S(2)}) %collective-permute-start.12) | collective-permute-done | bytes 278560 | tf_op jit(solution)/shard_map/ppermute | solution.py:364
  79.5 7.1 %collective-permute-done.13.m2 = f32[272,256]{1,0:T(8,128)S(1)} collective-permute-done((f32[272,256]{1,0:T(8,128)S(1)}, f32[272,256]{1,0:T(8,128)S(1)}, u32[]{:S(2)}, u32[]{:S(2)}) %collective-permute-start.13) | collective-permute-done | bytes 278560 | tf_op jit(solution)/shard_map/ppermute | solution.py:364
  86.6 1.3 %shard_map.72 = (f32[272,256]{1,0:T(8,128)S(1)}, f32[272,256]{1,0:T(8,128)S(1)}) custom-call(s32[4]{0:T(128)S(1)} %pad_add_fusion.idx, f32[272,256]{1,0:T(8,128)S(1)} %get-tuple-element.80.m0, f32[272,256]{1,0:T(8,128)S(1)} %collective-permute-done.12.m1, f32[272,256]{1,0:T(8,128)S(1)} %collective-permute-done.13.m2, f32[272,256]{1,0:T(8,128)S(1)} %collective-permute-done.14.m3), custom_call_target="tpu_custom_call" | custom-call | tf_op jit(solution)/shard_map/pallas_call | solution.py:69
  88.2 1.5 %collective-permute-done.15.other = f32[272,256]{1,0:T(8,128)S(1)} collective-permute-done((f32[272,256]{1,0:T(8,128)S(1)}, f32[272,256]{1,0:T(8,128)S(1)}, u32[]{:S(2)}, u32[]{:S(2)}) %collective-permute-start.15) | collective-permute-done | bytes 278560 | tf_op jit(solution)/shard_map/ppermute | solution.py:431
  90.6 1.6 %collective-permute-start.16 = (f32[136,256]{1,0:T(8,128)S(1)}, f32[136,256]{1,0:T(8,128)S(1)}, u32[]{:S(2)}, u32[]{:S(2)}) collective-permute-start(f32[136,256]{1,0:T(8,128)S(1)} %get-tuple-element.84), channel_id=1, source_target_pairs={{0,8},{4,12},{8,16},{12,20},{16,24},{20,28},{24,0},{28,4},{32,40},... | collective-permute-start | bytes 417800 | tf_op jit(solution)/shard_map/ppermute | solution.py:435
  92.3 2.9 %collective-permute-start.17 = (f32[136,256]{1,0:T(8,128)S(1)}, f32[136,256]{1,0:T(8,128)S(1)}, u32[]{:S(2)}, u32[]{:S(2)}) collective-permute-start(f32[136,256]{1,0:T(8,128)S(1)} %get-tuple-element.84), channel_id=1, source_target_pairs={{0,16},{4,20},{8,24},{12,28},{16,0},{20,4},{24,8},{28,12},{32,48},... | collective-permute-start | bytes 417800 | tf_op jit(solution)/shard_map/ppermute | solution.py:435
  95.2 1.3 %collective-permute-start.18 = (f32[136,256]{1,0:T(8,128)S(1)}, f32[136,256]{1,0:T(8,128)S(1)}, u32[]{:S(2)}, u32[]{:S(2)}) collective-permute-start(f32[136,256]{1,0:T(8,128)S(1)} %get-tuple-element.84), channel_id=1, source_target_pairs={{0,24},{4,28},{8,0},{12,4},{16,8},{20,12},{24,16},{28,20},{32,56},... | collective-permute-start | bytes 417800 | tf_op jit(solution)/shard_map/ppermute | solution.py:435
  97.8 4.2 %collective-permute-done.17.h2 = f32[136,256]{1,0:T(8,128)S(1)} collective-permute-done((f32[136,256]{1,0:T(8,128)S(1)}, f32[136,256]{1,0:T(8,128)S(1)}, u32[]{:S(2)}, u32[]{:S(2)}) %collective-permute-start.17) | collective-permute-done | bytes 139296 | tf_op jit(solution)/shard_map/ppermute | solution.py:435
  105.4 2.4 %collective-permute-start.23 = (f32[136,256]{1,0:T(8,128)S(1)}, f32[136,256]{1,0:T(8,128)S(1)}, u32[]{:S(2)}, u32[]{:S(2)}) collective-permute-start(f32[136,256]{1,0:T(8,128)S(1)} %get-tuple-element.85), channel_id=1, source_target_pairs={{0,64},{4,68},{8,72},{12,76},{16,80},{20,84},{24,88},{28,92},{32,9... | collective-permute-start | bytes 417800 | tf_op jit(solution)/shard_map/ppermute | solution.py:435
  107.8 3.6 %collective-permute-done.22.h1 = f32[136,256]{1,0:T(8,128)S(1)} collective-permute-done((f32[136,256]{1,0:T(8,128)S(1)}, f32[136,256]{1,0:T(8,128)S(1)}, u32[]{:S(2)}, u32[]{:S(2)}) %collective-permute-start.22) | collective-permute-done | bytes 139296 | tf_op jit(solution)/shard_map/ppermute | solution.py:435
  111.4 2.0 %collective-permute-done.23.h2 = f32[136,256]{1,0:T(8,128)S(1)} collective-permute-done((f32[136,256]{1,0:T(8,128)S(1)}, f32[136,256]{1,0:T(8,128)S(1)}, u32[]{:S(2)}, u32[]{:S(2)}) %collective-permute-start.23) | collective-permute-done | bytes 139296 | tf_op jit(solution)/shard_map/ppermute | solution.py:435
  113.4 2.1 %collective-permute-done.24.h3 = f32[136,256]{1,0:T(8,128)S(1)} collective-permute-done((f32[136,256]{1,0:T(8,128)S(1)}, f32[136,256]{1,0:T(8,128)S(1)}, u32[]{:S(2)}, u32[]{:S(2)}) %collective-permute-start.24) | collective-permute-done | bytes 139296 | tf_op jit(solution)/shard_map/ppermute | solution.py:435
  116.9 2.2 %shard_map.76 = (f32[16,64]{1,0:T(8,128)S(1)}, f32[16,64]{1,0:T(8,128)S(1)}, f32[16,64]{1,0:T(8,128)S(1)}, f32[16,64]{1,0:T(8,128)S(1)}) custom-call(s32[4]{0:T(128)S(1)} %pad_add_fusion.idx, f32[1,256]{1,0:T(1,128)S(1)} %bitcast.13, f32[136,256]{1,0:T(8,128)S(1)} %collective-permute-done.22.h1, f32[136,256]{1,0:T(8,128)S(1)} %collective-permute-done.23.h2, ...), custom_call_target="tpu_custom_call" | custom-call | tf_op jit(solution)/shard_map/pallas_call | solution.py:69
  119.4 3.6 %collective-permute-start.29 = (f32[16,64]{1,0:T(8,128)S(1)}, f32[16,64]{1,0:T(8,128)S(1)}, u32[]{:S(2)}, u32[]{:S(2)}) collective-permute-start(f32[16,64]{1,0:T(8,128)S(1)} %get-tuple-element.91), channel_id=1, source_target_pairs={{0,2},{1,3},{2,0},{3,1},{4,6},{5,7},{6,4},{7,5},{8,10},{9,11},{10,... | collective-permute-start | bytes 12296 | tf_op jit(solution)/shard_map/ppermute | solution.py:364
  124.7 1.9 %collective-permute-done.30.r3 = f32[16,64]{1,0:T(8,128)S(1)} collective-permute-done((f32[16,64]{1,0:T(8,128)S(1)}, f32[16,64]{1,0:T(8,128)S(1)}, u32[]{:S(2)}, u32[]{:S(2)}) %collective-permute-start.30) | collective-permute-done | bytes 4128 | tf_op jit(solution)/shard_map/ppermute | solution.py:364
  (56 shorter events, 17.2 us)
Async XLA Ops:
  2.2 30.3 %collective-permute-start = (f32[640,256]{1,0:T(8,128)S(1)}, f32[640,256]{1,0:T(8,128)S(1)}, u32[]{:S(2)}, u32[]{:S(2)}) collective-permute-start(f32[640,256]{1,0:T(8,128)S(1)} %get-tuple-element.49), channel_id=1, source_target_pairs={{0,1},{1,2},{2,3},{3,0},{4,5},{5,6},{6,7},{7,4},{8,9},{9,10},{10,1... | collective-permute-start | bytes 1966088 | tf_op jit(solution)/shard_map/ppermute | solution.py:364
  4.1 32.1 %collective-permute-start.1 = (f32[640,256]{1,0:T(8,128)S(1)}, f32[640,256]{1,0:T(8,128)S(1)}, u32[]{:S(2)}, u32[]{:S(2)}) collective-permute-start(f32[640,256]{1,0:T(8,128)S(1)} %get-tuple-element.50), channel_id=1, source_target_pairs={{0,2},{1,3},{2,0},{3,1},{4,6},{5,7},{6,4},{7,5},{8,10},{9,11},{10,... | collective-permute-start | bytes 1966088 | tf_op jit(solution)/shard_map/ppermute | solution.py:364
  7.7 28.5 %collective-permute-start.2 = (f32[640,256]{1,0:T(8,128)S(1)}, f32[640,256]{1,0:T(8,128)S(1)}, u32[]{:S(2)}, u32[]{:S(2)}) collective-permute-start(f32[640,256]{1,0:T(8,128)S(1)} %get-tuple-element.51), channel_id=1, source_target_pairs={{0,3},{1,0},{2,1},{3,2},{4,7},{5,4},{6,5},{7,6},{8,11},{9,8},{10,9... | collective-permute-start | bytes 1966088 | tf_op jit(solution)/shard_map/ppermute | solution.py:364
  36.8 6.8 %collective-permute-start.3 = (f32[16,256]{1,0:T(8,128)S(1)}, f32[16,256]{1,0:T(8,128)S(1)}, u32[]{:S(2)}, u32[]{:S(2)}) collective-permute-start(f32[16,256]{1,0:T(8,128)S(1)} %shard_map.67.i0), channel_id=1, source_target_pairs={{0,1},{1,2},{2,3},{3,0},{4,5},{5,6},{6,7},{7,4},{8,9},{9,10},{10,1... | collective-permute-start | bytes 49160 | tf_op jit(solution)/shard_map/ppermute | solution.py:364
  38.1 5.5 %collective-permute-start.4 = (f32[16,256]{1,0:T(8,128)S(1)}, f32[16,256]{1,0:T(8,128)S(1)}, u32[]{:S(2)}, u32[]{:S(2)}) collective-permute-start(f32[16,256]{1,0:T(8,128)S(1)} %shard_map.67.i0), channel_id=1, source_target_pairs={{0,2},{1,3},{2,0},{3,1},{4,6},{5,7},{6,4},{7,5},{8,10},{9,11},{10,... | collective-permute-start | bytes 49160 | tf_op jit(solution)/shard_map/ppermute | solution.py:364
  40.5 3.7 %collective-permute-start.5 = (f32[16,256]{1,0:T(8,128)S(1)}, f32[16,256]{1,0:T(8,128)S(1)}, u32[]{:S(2)}, u32[]{:S(2)}) collective-permute-start(f32[16,256]{1,0:T(8,128)S(1)} %shard_map.67.i0), channel_id=1, source_target_pairs={{0,3},{1,0},{2,1},{3,2},{4,7},{5,4},{6,5},{7,6},{8,11},{9,8},{10,9... | collective-permute-start | bytes 49160 | tf_op jit(solution)/shard_map/ppermute | solution.py:364
  44.2 19.9 %collective-permute-start.9 = (f32[384,256]{1,0:T(8,128)S(1)}, f32[384,256]{1,0:T(8,128)S(1)}, u32[]{:S(2)}, u32[]{:S(2)}) collective-permute-start(f32[384,256]{1,0:T(8,128)S(1)} %get-tuple-element.72), channel_id=1, source_target_pairs={{0,1},{1,2},{2,3},{3,0},{4,5},{5,6},{6,7},{7,4},{8,9},{9,10},{10,1... | collective-permute-start | bytes 1179656 | tf_op jit(solution)/shard_map/ppermute | solution.py:364
  44.7 19.5 %collective-permute-start.10 = (f32[384,256]{1,0:T(8,128)S(1)}, f32[384,256]{1,0:T(8,128)S(1)}, u32[]{:S(2)}, u32[]{:S(2)}) collective-permute-start(f32[384,256]{1,0:T(8,128)S(1)} %get-tuple-element.73), channel_id=1, source_target_pairs={{0,2},{1,3},{2,0},{3,1},{4,6},{5,7},{6,4},{7,5},{8,10},{9,11},{10,... | collective-permute-start | bytes 1179656 | tf_op jit(solution)/shard_map/ppermute | solution.py:364
  48.2 16.4 %collective-permute-start.11 = (f32[384,256]{1,0:T(8,128)S(1)}, f32[384,256]{1,0:T(8,128)S(1)}, u32[]{:S(2)}, u32[]{:S(2)}) collective-permute-start(f32[384,256]{1,0:T(8,128)S(1)} %get-tuple-element.74), channel_id=1, source_target_pairs={{0,3},{1,0},{2,1},{3,2},{4,7},{5,4},{6,5},{7,6},{8,11},{9,8},{10,9... | collective-permute-start | bytes 1179656 | tf_op jit(solution)/shard_map/ppermute | solution.py:364
  53.4 14.3 %collective-permute-start.6 = (f32[16,256]{1,0:T(8,128)S(1)}, f32[16,256]{1,0:T(8,128)S(1)}, u32[]{:S(2)}, u32[]{:S(2)}) collective-permute-start(f32[16,256]{1,0:T(8,128)S(1)} %get-tuple-element.66), channel_id=1, source_target_pairs={{0,1},{1,2},{2,3},{3,0},{4,5},{5,6},{6,7},{7,4},{8,9},{9,10},{10,1... | collective-permute-start | bytes 49160 | tf_op jit(solution)/shard_map/ppermute | solution.py:364
  55.2 12.5 %collective-permute-start.7 = (f32[16,256]{1,0:T(8,128)S(1)}, f32[16,256]{1,0:T(8,128)S(1)}, u32[]{:S(2)}, u32[]{:S(2)}) collective-permute-start(f32[16,256]{1,0:T(8,128)S(1)} %get-tuple-element.67), channel_id=1, source_target_pairs={{0,2},{1,3},{2,0},{3,1},{4,6},{5,7},{6,4},{7,5},{8,10},{9,11},{10,... | collective-permute-start | bytes 49160 | tf_op jit(solution)/shard_map/ppermute | solution.py:364
  64.2 3.7 %collective-permute-start.8 = (f32[16,256]{1,0:T(8,128)S(1)}, f32[16,256]{1,0:T(8,128)S(1)}, u32[]{:S(2)}, u32[]{:S(2)}) collective-permute-start(f32[16,256]{1,0:T(8,128)S(1)} %get-tuple-element.68), channel_id=1, source_target_pairs={{0,3},{1,0},{2,1},{3,2},{4,7},{5,4},{6,5},{7,6},{8,11},{9,8},{10,9... | collective-permute-start | bytes 49160 | tf_op jit(solution)/shard_map/ppermute | solution.py:364
  70.4 46.5 %copy-start.1 = (f32[256]{0:T(256)S(1)}, f32[256]{0:T(256)}, u32[]{:S(2)}) copy-start(f32[256]{0:T(256)} %param.6) | copy-start | bytes 3076
  70.4 9.1 %collective-permute-start.12 = (f32[272,256]{1,0:T(8,128)S(1)}, f32[272,256]{1,0:T(8,128)S(1)}, u32[]{:S(2)}, u32[]{:S(2)}) collective-permute-start(f32[272,256]{1,0:T(8,128)S(1)} %get-tuple-element.80.m0), channel_id=1, source_target_pairs={{0,1},{1,2},{2,3},{3,0},{4,5},{5,6},{6,7},{7,4},{8,9},{9,10},{10,1... | collective-permute-start | bytes 835592 | tf_op jit(solution)/shard_map/ppermute | solution.py:364
  71.8 14.8 %collective-permute-start.13 = (f32[272,256]{1,0:T(8,128)S(1)}, f32[272,256]{1,0:T(8,128)S(1)}, u32[]{:S(2)}, u32[]{:S(2)}) collective-permute-start(f32[272,256]{1,0:T(8,128)S(1)} %get-tuple-element.80.m0), channel_id=1, source_target_pairs={{0,2},{1,3},{2,0},{3,1},{4,6},{5,7},{6,4},{7,5},{8,10},{9,11},{10,... | collective-permute-start | bytes 835592 | tf_op jit(solution)/shard_map/ppermute | solution.py:364
  74.2 12.4 %collective-permute-start.14 = (f32[272,256]{1,0:T(8,128)S(1)}, f32[272,256]{1,0:T(8,128)S(1)}, u32[]{:S(2)}, u32[]{:S(2)}) collective-permute-start(f32[272,256]{1,0:T(8,128)S(1)} %get-tuple-element.80.m0), channel_id=1, source_target_pairs={{0,3},{1,0},{2,1},{3,2},{4,7},{5,4},{6,5},{7,6},{8,11},{9,8},{10,9... | collective-permute-start | bytes 835592 | tf_op jit(solution)/shard_map/ppermute | solution.py:364
  88.0 1.8 %collective-permute-start.15 = (f32[272,256]{1,0:T(8,128)S(1)}, f32[272,256]{1,0:T(8,128)S(1)}, u32[]{:S(2)}, u32[]{:S(2)}) collective-permute-start(f32[272,256]{1,0:T(8,128)S(1)} %get-tuple-element.81.own), channel_id=1, source_target_pairs={{0,4},{4,0},{8,12},{12,8},{16,20},{20,16},{24,28},{28,24},{32,36},... | collective-permute-start | bytes 835592 | tf_op jit(solution)/shard_map/ppermute | solution.py:431
  90.6 7.2 %collective-permute-start.16 = (f32[136,256]{1,0:T(8,128)S(1)}, f32[136,256]{1,0:T(8,128)S(1)}, u32[]{:S(2)}, u32[]{:S(2)}) collective-permute-start(f32[136,256]{1,0:T(8,128)S(1)} %get-tuple-element.84), channel_id=1, source_target_pairs={{0,8},{4,12},{8,16},{12,20},{16,24},{20,28},{24,0},{28,4},{32,40},... | collective-permute-start | bytes 417800 | tf_op jit(solution)/shard_map/ppermute | solution.py:435
  92.3 9.7 %collective-permute-start.17 = (f32[136,256]{1,0:T(8,128)S(1)}, f32[136,256]{1,0:T(8,128)S(1)}, u32[]{:S(2)}, u32[]{:S(2)}) collective-permute-start(f32[136,256]{1,0:T(8,128)S(1)} %get-tuple-element.84), channel_id=1, source_target_pairs={{0,16},{4,20},{8,24},{12,28},{16,0},{20,4},{24,8},{28,12},{32,48},... | collective-permute-start | bytes 417800 | tf_op jit(solution)/shard_map/ppermute | solution.py:435
  95.2 6.8 %collective-permute-start.18 = (f32[136,256]{1,0:T(8,128)S(1)}, f32[136,256]{1,0:T(8,128)S(1)}, u32[]{:S(2)}, u32[]{:S(2)}) collective-permute-start(f32[136,256]{1,0:T(8,128)S(1)} %get-tuple-element.84), channel_id=1, source_target_pairs={{0,24},{4,28},{8,0},{12,4},{16,8},{20,12},{24,16},{28,20},{32,56},... | collective-permute-start | bytes 417800 | tf_op jit(solution)/shard_map/ppermute | solution.py:435
  97.8 4.7 %collective-permute-start.19 = (f32[136,256]{1,0:T(8,128)S(1)}, f32[136,256]{1,0:T(8,128)S(1)}, u32[]{:S(2)}, u32[]{:S(2)}) collective-permute-start(f32[136,256]{1,0:T(8,128)S(1)} %collective-permute-done.16.h1), channel_id=1, source_target_pairs={{0,4},{4,0},{8,12},{12,8},{16,20},{20,16},{24,28},{28,24},{32,36},... | collective-permute-start | bytes 417800 | tf_op jit(solution)/shard_map/ppermute | solution.py:431
  102.0 1.4 %collective-permute-start.20 = (f32[136,256]{1,0:T(8,128)S(1)}, f32[136,256]{1,0:T(8,128)S(1)}, u32[]{:S(2)}, u32[]{:S(2)}) collective-permute-start(f32[136,256]{1,0:T(8,128)S(1)} %collective-permute-done.17.h2), channel_id=1, source_target_pairs={{0,4},{4,0},{8,12},{12,8},{16,20},{20,16},{24,28},{28,24},{32,36},... | collective-permute-start | bytes 417800 | tf_op jit(solution)/shard_map/ppermute | solution.py:431
  102.0 1.6 %collective-permute-start.21 = (f32[136,256]{1,0:T(8,128)S(1)}, f32[136,256]{1,0:T(8,128)S(1)}, u32[]{:S(2)}, u32[]{:S(2)}) collective-permute-start(f32[136,256]{1,0:T(8,128)S(1)} %collective-permute-done.18.h3), channel_id=1, source_target_pairs={{0,4},{4,0},{8,12},{12,8},{16,20},{20,16},{24,28},{28,24},{32,36},... | collective-permute-start | bytes 417800 | tf_op jit(solution)/shard_map/ppermute | solution.py:431
  104.8 6.6 %collective-permute-start.22 = (f32[136,256]{1,0:T(8,128)S(1)}, f32[136,256]{1,0:T(8,128)S(1)}, u32[]{:S(2)}, u32[]{:S(2)}) collective-permute-start(f32[136,256]{1,0:T(8,128)S(1)} %get-tuple-element.85), channel_id=1, source_target_pairs={{0,32},{4,36},{8,40},{12,44},{16,48},{20,52},{24,56},{28,60},{32,6... | collective-permute-start | bytes 417800 | tf_op jit(solution)/shard_map/ppermute | solution.py:435
  105.4 8.0 %collective-permute-start.23 = (f32[136,256]{1,0:T(8,128)S(1)}, f32[136,256]{1,0:T(8,128)S(1)}, u32[]{:S(2)}, u32[]{:S(2)}) collective-permute-start(f32[136,256]{1,0:T(8,128)S(1)} %get-tuple-element.85), channel_id=1, source_target_pairs={{0,64},{4,68},{8,72},{12,76},{16,80},{20,84},{24,88},{28,92},{32,9... | collective-permute-start | bytes 417800 | tf_op jit(solution)/shard_map/ppermute | solution.py:435
  107.8 7.7 %collective-permute-start.24 = (f32[136,256]{1,0:T(8,128)S(1)}, f32[136,256]{1,0:T(8,128)S(1)}, u32[]{:S(2)}, u32[]{:S(2)}) collective-permute-start(f32[136,256]{1,0:T(8,128)S(1)} %get-tuple-element.85), channel_id=1, source_target_pairs={{0,96},{4,100},{8,104},{12,108},{16,112},{20,116},{24,120},{28,124... | collective-permute-start | bytes 417800 | tf_op jit(solution)/shard_map/ppermute | solution.py:435
  111.4 4.9 %collective-permute-start.25 = (f32[136,256]{1,0:T(8,128)S(1)}, f32[136,256]{1,0:T(8,128)S(1)}, u32[]{:S(2)}, u32[]{:S(2)}) collective-permute-start(f32[136,256]{1,0:T(8,128)S(1)} %collective-permute-done.22.h1), channel_id=1, source_target_pairs={{0,4},{4,0},{8,12},{12,8},{16,20},{20,16},{24,28},{28,24},{32,36},... | collective-permute-start | bytes 417800 | tf_op jit(solution)/shard_map/ppermute | solution.py:431
  113.4 2.9 %collective-permute-start.26 = (f32[136,256]{1,0:T(8,128)S(1)}, f32[136,256]{1,0:T(8,128)S(1)}, u32[]{:S(2)}, u32[]{:S(2)}) collective-permute-start(f32[136,256]{1,0:T(8,128)S(1)} %collective-permute-done.23.h2), channel_id=1, source_target_pairs={{0,4},{4,0},{8,12},{12,8},{16,20},{20,16},{24,28},{28,24},{32,36},... | collective-permute-start | bytes 417800 | tf_op jit(solution)/shard_map/ppermute | solution.py:431
  115.5 1.4 %collective-permute-start.27 = (f32[136,256]{1,0:T(8,128)S(1)}, f32[136,256]{1,0:T(8,128)S(1)}, u32[]{:S(2)}, u32[]{:S(2)}) collective-permute-start(f32[136,256]{1,0:T(8,128)S(1)} %collective-permute-done.24.h3), channel_id=1, source_target_pairs={{0,4},{4,0},{8,12},{12,8},{16,20},{20,16},{24,28},{28,24},{32,36},... | collective-permute-start | bytes 417800 | tf_op jit(solution)/shard_map/ppermute | solution.py:431
  119.1 4.9 %collective-permute-start.28 = (f32[16,64]{1,0:T(8,128)S(1)}, f32[16,64]{1,0:T(8,128)S(1)}, u32[]{:S(2)}, u32[]{:S(2)}) collective-permute-start(f32[16,64]{1,0:T(8,128)S(1)} %get-tuple-element.90), channel_id=1, source_target_pairs={{0,1},{1,2},{2,3},{3,0},{4,5},{5,6},{6,7},{7,4},{8,9},{9,10},{10,1... | collective-permute-start | bytes 12296 | tf_op jit(solution)/shard_map/ppermute | solution.py:364
  119.4 5.4 %collective-permute-start.29 = (f32[16,64]{1,0:T(8,128)S(1)}, f32[16,64]{1,0:T(8,128)S(1)}, u32[]{:S(2)}, u32[]{:S(2)}) collective-permute-start(f32[16,64]{1,0:T(8,128)S(1)} %get-tuple-element.91), channel_id=1, source_target_pairs={{0,2},{1,3},{2,0},{3,1},{4,6},{5,7},{6,4},{7,5},{8,10},{9,11},{10,... | collective-permute-start | bytes 12296 | tf_op jit(solution)/shard_map/ppermute | solution.py:364
  123.0 3.7 %collective-permute-start.30 = (f32[16,64]{1,0:T(8,128)S(1)}, f32[16,64]{1,0:T(8,128)S(1)}, u32[]{:S(2)}, u32[]{:S(2)}) collective-permute-start(f32[16,64]{1,0:T(8,128)S(1)} %get-tuple-element.92), channel_id=1, source_target_pairs={{0,3},{1,0},{2,1},{3,2},{4,7},{5,4},{6,5},{7,6},{8,11},{9,8},{10,9... | collective-permute-start | bytes 12296 | tf_op jit(solution)/shard_map/ppermute | solution.py:364
  (3 other events, 26.3 us)

commit v6 on v5

--- a/solution.py
+++ b/solution.py
@@ -17,7 +17,7 @@
 HALF = R // 2
 ROWS = 4
 SUB = 16
-CHUNKS = ((5, 5), (3, 3))
+CHUNKS = ((4, 4, 4), (2, 2))
 SEGS = tuple(n for chunk in CHUNKS for n in chunk)
 SIZES = tuple(sum(chunk) for chunk in CHUNKS)
 ENDS = tuple(sum(SEGS[: i + 1]) for i in range(len(SEGS)))
@@ -161,7 +161,7 @@
                 pref[k] = by_step(pref[k - 1], ah[k], al[k])
 
 
-def first_kernel(idx, flat, gains, a1, a2, a3, pref, ah, al, both, staged, own, sems):
+def first_kernel(idx, flat, gains, a1, a2, a3, pref, ah, al, tail, staged, own, sems):
     z = idx[Z]
     late = pltpu.make_async_copy(gains, staged, sems.at[1])
     copy = own_copy(z, flat, own, 0, sems.at[0])
@@ -169,21 +169,22 @@
     late.start()
     assemble(z, (own, a1, a2, a3), ah, al, copy)
     chains(CHUNKS[0], ah, al, pref)
-    both[...] = mm(pref[CHUNKS[0][0] - 1], pref[SIZES[0] - 1])
+    tail[0] = mm(pref[ENDS[1] - 1], pref[ENDS[2] - 1])
+    tail[1] = mm(pref[ENDS[0] - 1], tail[0])
     late.wait()
 
 
-def second_kernel(idx, flat, a1, a2, a3, both, pref, ah, al, four, three, own, sem):
+def second_kernel(idx, flat, a1, a2, a3, tail, pref, ah, al, last, own, sem):
     z = idx[Z]
     copy = own_copy(z, flat, own, SIZES[0], sem)
     copy.start()
     assemble(z, (own, a1, a2, a3), ah, al, copy)
     chains(CHUNKS[1], ah, al, pref)
-    three[...] = mm(both[...], pref[CHUNKS[1][0] - 1])
-    four[...] = mm(three[...], pref[SIZES[1] - 1])
-
-
-def third_kernel(idx, b0, b1, b2, b3, p01, ah01, al01, p23, ah23, al23, four, shifts, whole, b_s):
+    last[0] = mm(pref[CHUNKS[1][0] - 1], pref[SIZES[1] - 1])
+    last[1] = mm(tail[1], last[0])
+
+
+def third_kernel(idx, b0, b1, b2, b3, p01, ah01, al01, tail, p23, ah23, al23, last, shifts, whole, b_s):
     z = idx[Z]
     for d, b in enumerate((b0, b1, b2, b3)):
         b_s[lax.rem(z - d + ROWS, ROWS)] = b[...]
@@ -206,10 +207,9 @@
             h, l, i = mats[k]
             p[c] = by_step(p[c], h[i], l[i]) + row(k)
             shifts[k : k + 1, :] = p[c][:1]
-    v = mm(p[0], p01[SIZES[0] - 1]) + p[1]
-    v = mm(v, p23[CHUNKS[1][0] - 1]) + p[2]
-    v = mm(v, p23[SIZES[1] - 1]) + p[3]
-    whole[:N, :] = four[...]
+    v = mm(p[0], tail[0]) + mm(p[1], p01[SIZES[0] - 1]) + p[2]
+    v = mm(v, last[0]) + (mm(p[3], p23[SIZES[1] - 1]) + p[4])
+    whole[:N, :] = last[1]
     whole[N:, :] = v
 
 
@@ -380,16 +380,14 @@
     rid = owner[:, 0] * 16 + step % 16 + 512 * (step // 16)
     partial = binned(rid.reshape(1, -1), observed.T)
     sums = lax.all_to_all(partial, "tm", 0, 0, tiled=True).reshape(32, 16, N)
-    sums, idx, prior, *part_a = lax.optimization_barrier((sums, idx, prior, *part_a))
-
     (info,) = call(sum_kernel, [(16, N)], idx, (sums,))
     infos = along_rows([info] * 3)
     sent_b = call(send_b_kernel, [(SIZES[1] * 64, N)] * 3, idx, (), [dma3], far=(flat,))
-    infos, sent_b = lax.optimization_barrier((infos, sent_b))
+    infos, sent_b, part_a, idx, prior = lax.optimization_barrier((infos, sent_b, part_a, idx, prior))
     part_b = along_rows(sent_b)
-    p01, ah01, al01, both, staged = call(
+    p01, ah01, al01, tail, staged = call(
         first_kernel,
-        [(SIZES[0], N, N), ((SIZES[0], N, N), BF16), ((SIZES[0], N, N), BF16), (N, N), gains.shape],
+        [(SIZES[0], N, N), ((SIZES[0], N, N), BF16), ((SIZES[0], N, N), BF16), (2, N, N), gains.shape],
         idx,
         part_a,
         [pltpu.VMEM((SIZES[0] * 64, N), F32), pltpu.SemaphoreType.DMA((2,))],
@@ -403,19 +401,19 @@
         [pltpu.VMEM((ROWS, 16, N), F32), pltpu.VMEM((ROWS, 16, 128), F32)],
     )
     offs = [offs[0], *along_rows(offs[1:])]
-    p23, ah23, al23, four = call(
+    p23, ah23, al23, last = call(
         second_kernel,
-        [(SIZES[1], N, N), ((SIZES[1], N, N), BF16), ((SIZES[1], N, N), BF16), (N, N)],
-        idx,
-        (*part_b, both),
-        [pltpu.VMEM((N, N), F32), pltpu.VMEM((SIZES[1] * 64, N), F32), pltpu.SemaphoreType.DMA],
+        [(SIZES[1], N, N), ((SIZES[1], N, N), BF16), ((SIZES[1], N, N), BF16), (2, N, N)],
+        idx,
+        (*part_b, tail),
+        [pltpu.VMEM((SIZES[1] * 64, N), F32), pltpu.SemaphoreType.DMA],
         far=(flat,),
     )
     shifts, whole = call(
         third_kernel,
         [(SUB, N), (R, N)],
         idx,
-        (*offs, p01, ah01, al01, p23, ah23, al23, four),
+        (*offs, p01, ah01, al01, tail, p23, ah23, al23, last),
         [pltpu.VMEM((ROWS, 16, N), F32)],
     )
 

time: 128 us -> 128 us (level); the launches traced: 128 us -> 126 us
  waiting for transfers between devices: 45.7 us -> 42.3 us
  starting transfers between devices: 35.6 us -> 37 us
    ppermute x18, waiting for transfers between devices: 29.5 us -> 24.5 us  [along_row(): return lax.ppermute(x, 'row', [(i, (i + d) % ROWS) for i in range(ROWS)])]
    ppermute x18, starting transfers between devices: 25.9 us -> 27.6 us  [along_row(): return lax.ppermute(x, 'row', [(i, (i + d) % ROWS) for i in range(ROWS)])]
  transfers between devices with their start and end apart: 31 -> 31, of which waited for: 19 -> 17; matrix products, arithmetic and copies ran while one was open for 0% -> 0% of each run, Pallas kernels for 14% -> 14%
where the time goes in v6:
time: 128 us; the launch traced here: 126 us
  waiting for transfers between devices  42.3 us (33%)
  starting transfers between devices  37 us (29%)
  Pallas kernels  29.8 us (23%)
  blocking collectives  16.7 us (13%)
    ppermute x18, starting transfers between devices, along_row(): return lax.ppermute(x, 'row', [(i, (i + d) % ROWS) for i in range(ROWS)])  27.6 us
    ppermute x18, waiting for transfers between devices, along_row(): return lax.ppermute(x, 'row', [(i, (i + d) % ROWS) for i in range(ROWS)])  24.5 us
    pallas_call x12, Pallas kernels, call(): pl.pallas_call(kernel, out_shape=[pltpu.VMEM(s, t) for s, t in outs], in_...  21.7 us
    all_to_all x1, blocking collectives, shards(): sums = lax.all_to_all(partial, 'tm', 0, 0, tiled=True).reshape(32, 16, N)  16.7 us
    ppermute x6, waiting for transfers between devices, along_tm(): return lax.ppermute(m, 'tm', places)  14.4 us
    ppermute x6, starting transfers between devices, along_tm(): return lax.ppermute(m, 'tm', places)  8.79 us
    pallas_call x1, Pallas kernels, binned(): pl.pallas_call(bin_kernel, out_shape=jax.ShapeDtypeStruct((n_bins // 4, N...  6.91 us
    ppermute x7, waiting for transfers between devices, other_core(): return lax.ppermute(m, 'tm', [(i, i ^ 1) for i in range(32)])  3.39 us
  transfers between devices with their start and end apart: 31, of which 17 were waited for; matrix products, arithmetic and copies ran while one was open for 0% of the time, Pallas kernels for 14%

profile of v6, /device:TPU:6, one launch (start us, length us, event | category | flops | bytes accessed | tf_op | source)
XLA Modules:
  0.0 126.0 jit_solution(9267884119236978506)
XLA Ops:
  0.1 2.2 %shard_map.67 = (f32[768,256]{1,0:T(8,128)S(1)}, f32[768,256]{1,0:T(8,128)S(1)}, f32[768,256]{1,0:T(8,128)S(1)}) custom-call(s32[4]{0:T(128)S(1)} %pad_add_fusion.idx, f32[4096,256]{1,0:T(8,128)} %bitcast.14), custom_call_target="tpu_custom_call" | custom-call | tf_op jit(solution)/shard_map/pallas_call | solution.py:69
  2.3 2.0 %collective-permute-start.3 = (f32[768,256]{1,0:T(8,128)S(1)}, f32[768,256]{1,0:T(8,128)S(1)}, u32[]{:S(2)}, u32[]{:S(2)}) collective-permute-start(f32[768,256]{1,0:T(8,128)S(1)} %get-tuple-element.51), channel_id=1, source_target_pairs={{0,1},{1,2},{2,3},{3,0},{4,5},{5,6},{6,7},{7,4},{8,9},{9,10},{10,1... | collective-permute-start | bytes 2359304 | tf_op jit(solution)/shard_map/ppermute | solution.py:364
  4.3 3.6 %collective-permute-start.4 = (f32[768,256]{1,0:T(8,128)S(1)}, f32[768,256]{1,0:T(8,128)S(1)}, u32[]{:S(2)}, u32[]{:S(2)}) collective-permute-start(f32[768,256]{1,0:T(8,128)S(1)} %get-tuple-element.52), channel_id=1, source_target_pairs={{0,2},{1,3},{2,0},{3,1},{4,6},{5,7},{6,4},{7,5},{8,10},{9,11},{10,... | collective-permute-start | bytes 2359304 | tf_op jit(solution)/shard_map/ppermute | solution.py:364
  8.9 6.9 %shard_map.64 = f32[512,256]{1,0:T(8,128)S(1)} custom-call(s32[1,4096]{1,0:T(1,128)S(1)} %bitcast.12, f32[64,4096]{1,0:T(8,128)S(1)} %bitcast.11), custom_call_target="tpu_custom_call" | custom-call | tf_op jit(solution)/shard_map/pallas_call | solution.py:114
  15.8 16.7 %all_to_all.9.sums = f32[32,16,256]{2,1,0:T(8,128)S(1)} all-to-all(f32[32,16,256]{2,1,0:T(8,128)S(1)} %bitcast.10), channel_id=1, replica_groups=mesh['tm'=32,'row'=4] {'tm'}, dimensions={0} | all-to-all | bytes 1048576 | tf_op jit(solution)/shard_map/all_to_all | solution.py:382
  33.2 3.1 %collective-permute-start.1 = (f32[16,256]{1,0:T(8,128)S(1)}, f32[16,256]{1,0:T(8,128)S(1)}, u32[]{:S(2)}, u32[]{:S(2)}) collective-permute-start(f32[16,256]{1,0:T(8,128)S(1)} %shard_map.65.i0), channel_id=1, source_target_pairs={{0,2},{1,3},{2,0},{3,1},{4,6},{5,7},{6,4},{7,5},{8,10},{9,11},{10,... | collective-permute-start | bytes 49160 | tf_op jit(solution)/shard_map/ppermute | solution.py:364
  36.3 5.7 %collective-permute-done.2.r3 = f32[16,256]{1,0:T(8,128)S(1)} collective-permute-done((f32[16,256]{1,0:T(8,128)S(1)}, f32[16,256]{1,0:T(8,128)S(1)}, u32[]{:S(2)}, u32[]{:S(2)}) %collective-permute-start.2) | collective-permute-done | bytes 16416 | tf_op jit(solution)/shard_map/ppermute | solution.py:364
  42.0 1.7 %collective-permute-start = (f32[16,256]{1,0:T(8,128)S(1)}, f32[16,256]{1,0:T(8,128)S(1)}, u32[]{:S(2)}, u32[]{:S(2)}) collective-permute-start(f32[16,256]{1,0:T(8,128)S(1)} %shard_map.65.i0), channel_id=1, source_target_pairs={{0,1},{1,2},{2,3},{3,0},{4,5},{5,6},{6,7},{7,4},{8,9},{9,10},{10,1... | collective-permute-start | bytes 49160 | tf_op jit(solution)/shard_map/ppermute | solution.py:364
  43.7 1.7 %shard_map.66 = (f32[256,256]{1,0:T(8,128)S(1)}, f32[256,256]{1,0:T(8,128)S(1)}, f32[256,256]{1,0:T(8,128)S(1)}) custom-call(s32[4]{0:T(128)S(1)} %pad_add_fusion.idx, f32[4096,256]{1,0:T(8,128)} %bitcast.15), custom_call_target="tpu_custom_call" | custom-call | tf_op jit(solution)/shard_map/pallas_call | solution.py:69
  45.4 1.5 %collective-permute-done.r1 = f32[16,256]{1,0:T(8,128)S(1)} collective-permute-done((f32[16,256]{1,0:T(8,128)S(1)}, f32[16,256]{1,0:T(8,128)S(1)}, u32[]{:S(2)}, u32[]{:S(2)}) %collective-permute-start) | collective-permute-done | bytes 16416 | tf_op jit(solution)/shard_map/ppermute | solution.py:364
  47.5 2.4 %collective-permute-start.10 = (f32[256,256]{1,0:T(8,128)S(1)}, f32[256,256]{1,0:T(8,128)S(1)}, u32[]{:S(2)}, u32[]{:S(2)}) collective-permute-start(f32[256,256]{1,0:T(8,128)S(1)} %get-tuple-element.72), channel_id=1, source_target_pairs={{0,2},{1,3},{2,0},{3,1},{4,6},{5,7},{6,4},{7,5},{8,10},{9,11},{10,... | collective-permute-start | bytes 786440 | tf_op jit(solution)/shard_map/ppermute | solution.py:364
  51.2 3.8 %shard_map.68 = (f32[12,256,256]{2,1,0:T(8,128)S(1)}, bf16[12,256,256]{2,1,0:T(8,128)(2,1)S(1)}, bf16[12,256,256]{2,1,0:T(8,128)(2,1)S(1)}, f32[2,256,256]{2,1,0:T(8,128)S(1)}, f32[64,64,256]{2,1,0:T(8,128)S(1)}) custom-call(s32[4]{0:T(128)S(1)} %pad_add_fusion.idx, f32[4096,256]{1,0:T(8,128)} %bitcast.16, f32[64,64,256]{2,1,0:T(8,128)} %gains.1, ...), custom_call_target="tpu_custom_call" | custom-call | tf_op jit(solution)/shard_map/pallas_call | solution.py:69
  55.0 1.6 %shard_map.69 = (f32[16,256]{1,0:T(8,128)S(1)}, f32[16,256]{1,0:T(8,128)S(1)}, f32[16,256]{1,0:T(8,128)S(1)}, f32[16,256]{1,0:T(8,128)S(1)}) custom-call(s32[4]{0:T(128)S(1)} %pad_add_fusion.idx, f32[64,64,256]{2,1,0:T(8,128)S(1)} %get-tuple-element.59.g, f32[16,256]{1,0:T(8,128)S(1)} %shard_map.65.i0, f32[16,256]{1,0:T(8,128)S(1)} %collective-permute-done.r1, ...), custom_call_target="tpu_custom_call" | custom-call | tf_op jit(solution)/shard_map/pallas_call | solution.py:69
  57.4 1.4 %collective-permute-start.7 = (f32[16,256]{1,0:T(8,128)S(1)}, f32[16,256]{1,0:T(8,128)S(1)}, u32[]{:S(2)}, u32[]{:S(2)}) collective-permute-start(f32[16,256]{1,0:T(8,128)S(1)} %get-tuple-element.65), channel_id=1, source_target_pairs={{0,2},{1,3},{2,0},{3,1},{4,6},{5,7},{6,4},{7,5},{8,10},{9,11},{10,... | collective-permute-start | bytes 49160 | tf_op jit(solution)/shard_map/ppermute | solution.py:364
  58.8 2.5 %collective-permute-start.8 = (f32[16,256]{1,0:T(8,128)S(1)}, f32[16,256]{1,0:T(8,128)S(1)}, u32[]{:S(2)}, u32[]{:S(2)}) collective-permute-start(f32[16,256]{1,0:T(8,128)S(1)} %get-tuple-element.66), channel_id=1, source_target_pairs={{0,3},{1,0},{2,1},{3,2},{4,7},{5,4},{6,5},{7,6},{8,11},{9,8},{10,9... | collective-permute-start | bytes 49160 | tf_op jit(solution)/shard_map/ppermute | solution.py:364
  61.6 2.8 %shard_map.70 = (f32[4,256,256]{2,1,0:T(8,128)S(1)}, bf16[4,256,256]{2,1,0:T(8,128)(2,1)S(1)}, bf16[4,256,256]{2,1,0:T(8,128)(2,1)S(1)}, f32[2,256,256]{2,1,0:T(8,128)S(1)}) custom-call(s32[4]{0:T(128)S(1)} %pad_add_fusion.idx, f32[4096,256]{1,0:T(8,128)} %bitcast.17, f32[256,256]{1,0:T(8,128)S(1)} %collective-permute-done.9.a1, ...), custom_call_target="tpu_custom_call" | custom-call | tf_op jit(solution)/shard_map/pallas_call | solution.py:69
  64.5 2.2 %shard_map.71 = (f32[16,256]{1,0:T(8,128)S(1)}, f32[272,256]{1,0:T(8,128)S(1)}) custom-call(s32[4]{0:T(128)S(1)} %pad_add_fusion.idx, f32[16,256]{1,0:T(8,128)S(1)} %get-tuple-element.63.b0, f32[16,256]{1,0:T(8,128)S(1)} %collective-permute-done.6.b1, f32[16,256]{1,0:T(8,128)S(1)} %collective-permute-done.7.b2, f32[16,256]{1,0:T(8,128)S(1)} %collective-permute-done.8.b3, ...), custom_call_target="tpu_custom_call" | custom-call | tf_op jit(solution)/shard_map/pallas_call | solution.py:69
  66.7 2.6 %collective-permute-start.14 = (f32[272,256]{1,0:T(8,128)S(1)}, f32[272,256]{1,0:T(8,128)S(1)}, u32[]{:S(2)}, u32[]{:S(2)}) collective-permute-start(f32[272,256]{1,0:T(8,128)S(1)} %get-tuple-element.78.m0), channel_id=1, source_target_pairs={{0,3},{1,0},{2,1},{3,2},{4,7},{5,4},{6,5},{7,6},{8,11},{9,8},{10,9... | collective-permute-start | bytes 835592 | tf_op jit(solution)/shard_map/ppermute | solution.py:364
  70.2 10.8 %collective-permute-done.14.m3 = f32[272,256]{1,0:T(8,128)S(1)} collective-permute-done((f32[272,256]{1,0:T(8,128)S(1)}, f32[272,256]{1,0:T(8,128)S(1)}, u32[]{:S(2)}, u32[]{:S(2)}) %collective-permute-start.14) | collective-permute-done | bytes 278560 | tf_op jit(solution)/shard_map/ppermute | solution.py:364
  81.1 3.7 %collective-permute-done.12.m1 = f32[272,256]{1,0:T(8,128)S(1)} collective-permute-done((f32[272,256]{1,0:T(8,128)S(1)}, f32[272,256]{1,0:T(8,128)S(1)}, u32[]{:S(2)}, u32[]{:S(2)}) %collective-permute-start.12) | collective-permute-done | bytes 278560 | tf_op jit(solution)/shard_map/ppermute | solution.py:364
  84.8 1.5 %shard_map.72 = (f32[272,256]{1,0:T(8,128)S(1)}, f32[272,256]{1,0:T(8,128)S(1)}) custom-call(s32[4]{0:T(128)S(1)} %pad_add_fusion.idx, f32[272,256]{1,0:T(8,128)S(1)} %get-tuple-element.78.m0, f32[272,256]{1,0:T(8,128)S(1)} %collective-permute-done.12.m1, f32[272,256]{1,0:T(8,128)S(1)} %collective-permute-done.13.m2, f32[272,256]{1,0:T(8,128)S(1)} %collective-permute-done.14.m3), custom_call_target="tpu_custom_call" | custom-call | tf_op jit(solution)/shard_map/pallas_call | solution.py:69
  86.4 1.5 %collective-permute-done.15.other = f32[272,256]{1,0:T(8,128)S(1)} collective-permute-done((f32[272,256]{1,0:T(8,128)S(1)}, f32[272,256]{1,0:T(8,128)S(1)}, u32[]{:S(2)}, u32[]{:S(2)}) %collective-permute-start.15) | collective-permute-done | bytes 278560 | tf_op jit(solution)/shard_map/ppermute | solution.py:429
  88.8 3.1 %collective-permute-start.18 = (f32[136,256]{1,0:T(8,128)S(1)}, f32[136,256]{1,0:T(8,128)S(1)}, u32[]{:S(2)}, u32[]{:S(2)}) collective-permute-start(f32[136,256]{1,0:T(8,128)S(1)} %get-tuple-element.82), channel_id=1, source_target_pairs={{0,24},{4,28},{8,0},{12,4},{16,8},{20,12},{24,16},{28,20},{32,56},... | collective-permute-start | bytes 417800 | tf_op jit(solution)/shard_map/ppermute | solution.py:433
  93.4 4.7 %collective-permute-done.18.h3 = f32[136,256]{1,0:T(8,128)S(1)} collective-permute-done((f32[136,256]{1,0:T(8,128)S(1)}, f32[136,256]{1,0:T(8,128)S(1)}, u32[]{:S(2)}, u32[]{:S(2)}) %collective-permute-start.18) | collective-permute-done | bytes 139296 | tf_op jit(solution)/shard_map/ppermute | solution.py:433
  98.2 1.8 %collective-permute-done.17.h2 = f32[136,256]{1,0:T(8,128)S(1)} collective-permute-done((f32[136,256]{1,0:T(8,128)S(1)}, f32[136,256]{1,0:T(8,128)S(1)}, u32[]{:S(2)}, u32[]{:S(2)}) %collective-permute-start.17) | collective-permute-done | bytes 139296 | tf_op jit(solution)/shard_map/ppermute | solution.py:433
  99.9 1.9 %collective-permute-done.16.h1 = f32[136,256]{1,0:T(8,128)S(1)} collective-permute-done((f32[136,256]{1,0:T(8,128)S(1)}, f32[136,256]{1,0:T(8,128)S(1)}, u32[]{:S(2)}, u32[]{:S(2)}) %collective-permute-start.16) | collective-permute-done | bytes 139296 | tf_op jit(solution)/shard_map/ppermute | solution.py:433
  101.9 1.3 %collective-permute-done.19.o1 = f32[136,256]{1,0:T(8,128)S(1)} collective-permute-done((f32[136,256]{1,0:T(8,128)S(1)}, f32[136,256]{1,0:T(8,128)S(1)}, u32[]{:S(2)}, u32[]{:S(2)}) %collective-permute-start.19) | collective-permute-done | bytes 139296 | tf_op jit(solution)/shard_map/ppermute | solution.py:429
  103.2 1.3 %shard_map.74 = (f32[136,256]{1,0:T(8,128)S(1)}, f32[272,256]{1,0:T(8,128)S(1)}) custom-call(s32[4]{0:T(128)S(1)} %pad_add_fusion.idx, f32[272,256]{1,0:T(8,128)S(1)} %get-tuple-element.81.own, f32[136,256]{1,0:T(8,128)S(1)} %collective-permute-done.16.h1, f32[136,256]{1,0:T(8,128)S(1)} %collective-permute-done.17.h2, ...), custom_call_target="tpu_custom_call" | custom-call | tf_op jit(solution)/shard_map/pallas_call | solution.py:69
  106.6 2.1 %collective-permute-start.22 = (f32[136,256]{1,0:T(8,128)S(1)}, f32[136,256]{1,0:T(8,128)S(1)}, u32[]{:S(2)}, u32[]{:S(2)}) collective-permute-start(f32[136,256]{1,0:T(8,128)S(1)} %get-tuple-element.83), channel_id=1, source_target_pairs={{0,32},{4,36},{8,40},{12,44},{16,48},{20,52},{24,56},{28,60},{32,6... | collective-permute-start | bytes 417800 | tf_op jit(solution)/shard_map/ppermute | solution.py:433
  108.7 5.9 %collective-permute-done.24.h3 = f32[136,256]{1,0:T(8,128)S(1)} collective-permute-done((f32[136,256]{1,0:T(8,128)S(1)}, f32[136,256]{1,0:T(8,128)S(1)}, u32[]{:S(2)}, u32[]{:S(2)}) %collective-permute-start.24) | collective-permute-done | bytes 139296 | tf_op jit(solution)/shard_map/ppermute | solution.py:433
  116.5 2.3 %shard_map.76 = (f32[16,64]{1,0:T(8,128)S(1)}, f32[16,64]{1,0:T(8,128)S(1)}, f32[16,64]{1,0:T(8,128)S(1)}, f32[16,64]{1,0:T(8,128)S(1)}) custom-call(s32[4]{0:T(128)S(1)} %pad_add_fusion.idx, f32[1,256]{1,0:T(1,128)S(1)} %bitcast.13, f32[136,256]{1,0:T(8,128)S(1)} %collective-permute-done.22.h1, f32[136,256]{1,0:T(8,128)S(1)} %collective-permute-done.23.h2, ...), custom_call_target="tpu_custom_call" | custom-call | tf_op jit(solution)/shard_map/pallas_call | solution.py:69
  118.9 2.3 %collective-permute-start.29 = (f32[16,64]{1,0:T(8,128)S(1)}, f32[16,64]{1,0:T(8,128)S(1)}, u32[]{:S(2)}, u32[]{:S(2)}) collective-permute-start(f32[16,64]{1,0:T(8,128)S(1)} %get-tuple-element.89), channel_id=1, source_target_pairs={{0,2},{1,3},{2,0},{3,1},{4,6},{5,7},{6,4},{7,5},{8,10},{9,11},{10,... | collective-permute-start | bytes 12296 | tf_op jit(solution)/shard_map/ppermute | solution.py:364
  (56 shorter events, 17.1 us)
Async XLA Ops:
  2.3 44.7 %collective-permute-start.3 = (f32[768,256]{1,0:T(8,128)S(1)}, f32[768,256]{1,0:T(8,128)S(1)}, u32[]{:S(2)}, u32[]{:S(2)}) collective-permute-start(f32[768,256]{1,0:T(8,128)S(1)} %get-tuple-element.51), channel_id=1, source_target_pairs={{0,1},{1,2},{2,3},{3,0},{4,5},{5,6},{6,7},{7,4},{8,9},{9,10},{10,1... | collective-permute-start | bytes 2359304 | tf_op jit(solution)/shard_map/ppermute | solution.py:364
  4.3 42.7 %collective-permute-start.4 = (f32[768,256]{1,0:T(8,128)S(1)}, f32[768,256]{1,0:T(8,128)S(1)}, u32[]{:S(2)}, u32[]{:S(2)}) collective-permute-start(f32[768,256]{1,0:T(8,128)S(1)} %get-tuple-element.52), channel_id=1, source_target_pairs={{0,2},{1,3},{2,0},{3,1},{4,6},{5,7},{6,4},{7,5},{8,10},{9,11},{10,... | collective-permute-start | bytes 2359304 | tf_op jit(solution)/shard_map/ppermute | solution.py:364
  7.9 39.1 %collective-permute-start.5 = (f32[768,256]{1,0:T(8,128)S(1)}, f32[768,256]{1,0:T(8,128)S(1)}, u32[]{:S(2)}, u32[]{:S(2)}) collective-permute-start(f32[768,256]{1,0:T(8,128)S(1)} %get-tuple-element.53), channel_id=1, source_target_pairs={{0,3},{1,0},{2,1},{3,2},{4,7},{5,4},{6,5},{7,6},{8,11},{9,8},{10,9... | collective-permute-start | bytes 2359304 | tf_op jit(solution)/shard_map/ppermute | solution.py:364
  33.1 8.9 %collective-permute-start.2 = (f32[16,256]{1,0:T(8,128)S(1)}, f32[16,256]{1,0:T(8,128)S(1)}, u32[]{:S(2)}, u32[]{:S(2)}) collective-permute-start(f32[16,256]{1,0:T(8,128)S(1)} %shard_map.65.i0), channel_id=1, source_target_pairs={{0,3},{1,0},{2,1},{3,2},{4,7},{5,4},{6,5},{7,6},{8,11},{9,8},{10,9... | collective-permute-start | bytes 49160 | tf_op jit(solution)/shard_map/ppermute | solution.py:364
  33.2 12.2 %collective-permute-start.1 = (f32[16,256]{1,0:T(8,128)S(1)}, f32[16,256]{1,0:T(8,128)S(1)}, u32[]{:S(2)}, u32[]{:S(2)}) collective-permute-start(f32[16,256]{1,0:T(8,128)S(1)} %shard_map.65.i0), channel_id=1, source_target_pairs={{0,2},{1,3},{2,0},{3,1},{4,6},{5,7},{6,4},{7,5},{8,10},{9,11},{10,... | collective-permute-start | bytes 49160 | tf_op jit(solution)/shard_map/ppermute | solution.py:364
  42.0 4.9 %collective-permute-start = (f32[16,256]{1,0:T(8,128)S(1)}, f32[16,256]{1,0:T(8,128)S(1)}, u32[]{:S(2)}, u32[]{:S(2)}) collective-permute-start(f32[16,256]{1,0:T(8,128)S(1)} %shard_map.65.i0), channel_id=1, source_target_pairs={{0,1},{1,2},{2,3},{3,0},{4,5},{5,6},{6,7},{7,4},{8,9},{9,10},{10,1... | collective-permute-start | bytes 49160 | tf_op jit(solution)/shard_map/ppermute | solution.py:364
  47.0 11.8 %collective-permute-start.9 = (f32[256,256]{1,0:T(8,128)S(1)}, f32[256,256]{1,0:T(8,128)S(1)}, u32[]{:S(2)}, u32[]{:S(2)}) collective-permute-start(f32[256,256]{1,0:T(8,128)S(1)} %get-tuple-element.71), channel_id=1, source_target_pairs={{0,1},{1,2},{2,3},{3,0},{4,5},{5,6},{6,7},{7,4},{8,9},{9,10},{10,1... | collective-permute-start | bytes 786440 | tf_op jit(solution)/shard_map/ppermute | solution.py:364
  47.5 13.8 %collective-permute-start.10 = (f32[256,256]{1,0:T(8,128)S(1)}, f32[256,256]{1,0:T(8,128)S(1)}, u32[]{:S(2)}, u32[]{:S(2)}) collective-permute-start(f32[256,256]{1,0:T(8,128)S(1)} %get-tuple-element.72), channel_id=1, source_target_pairs={{0,2},{1,3},{2,0},{3,1},{4,6},{5,7},{6,4},{7,5},{8,10},{9,11},{10,... | collective-permute-start | bytes 786440 | tf_op jit(solution)/shard_map/ppermute | solution.py:364
  49.9 11.7 %collective-permute-start.11 = (f32[256,256]{1,0:T(8,128)S(1)}, f32[256,256]{1,0:T(8,128)S(1)}, u32[]{:S(2)}, u32[]{:S(2)}) collective-permute-start(f32[256,256]{1,0:T(8,128)S(1)} %get-tuple-element.73), channel_id=1, source_target_pairs={{0,3},{1,0},{2,1},{3,2},{4,7},{5,4},{6,5},{7,6},{8,11},{9,8},{10,9... | collective-permute-start | bytes 786440 | tf_op jit(solution)/shard_map/ppermute | solution.py:364
  56.6 7.8 %collective-permute-start.6 = (f32[16,256]{1,0:T(8,128)S(1)}, f32[16,256]{1,0:T(8,128)S(1)}, u32[]{:S(2)}, u32[]{:S(2)}) collective-permute-start(f32[16,256]{1,0:T(8,128)S(1)} %get-tuple-element.64), channel_id=1, source_target_pairs={{0,1},{1,2},{2,3},{3,0},{4,5},{5,6},{6,7},{7,4},{8,9},{9,10},{10,1... | collective-permute-start | bytes 49160 | tf_op jit(solution)/shard_map/ppermute | solution.py:364
  57.4 7.0 %collective-permute-start.7 = (f32[16,256]{1,0:T(8,128)S(1)}, f32[16,256]{1,0:T(8,128)S(1)}, u32[]{:S(2)}, u32[]{:S(2)}) collective-permute-start(f32[16,256]{1,0:T(8,128)S(1)} %get-tuple-element.65), channel_id=1, source_target_pairs={{0,2},{1,3},{2,0},{3,1},{4,6},{5,7},{6,4},{7,5},{8,10},{9,11},{10,... | collective-permute-start | bytes 49160 | tf_op jit(solution)/shard_map/ppermute | solution.py:364
  58.8 5.7 %collective-permute-start.8 = (f32[16,256]{1,0:T(8,128)S(1)}, f32[16,256]{1,0:T(8,128)S(1)}, u32[]{:S(2)}, u32[]{:S(2)}) collective-permute-start(f32[16,256]{1,0:T(8,128)S(1)} %get-tuple-element.66), channel_id=1, source_target_pairs={{0,3},{1,0},{2,1},{3,2},{4,7},{5,4},{6,5},{7,6},{8,11},{9,8},{10,9... | collective-permute-start | bytes 49160 | tf_op jit(solution)/shard_map/ppermute | solution.py:364
  64.5 52.0 %copy-start.1 = (f32[256]{0:T(256)S(1)}, f32[256]{0:T(256)}, u32[]{:S(2)}) copy-start(f32[256]{0:T(256)} %param.6) | copy-start | bytes 3076
  66.7 14.4 %collective-permute-start.14 = (f32[272,256]{1,0:T(8,128)S(1)}, f32[272,256]{1,0:T(8,128)S(1)}, u32[]{:S(2)}, u32[]{:S(2)}) collective-permute-start(f32[272,256]{1,0:T(8,128)S(1)} %get-tuple-element.78.m0), channel_id=1, source_target_pairs={{0,3},{1,0},{2,1},{3,2},{4,7},{5,4},{6,5},{7,6},{8,11},{9,8},{10,9... | collective-permute-start | bytes 835592 | tf_op jit(solution)/shard_map/ppermute | solution.py:364
  69.3 11.8 %collective-permute-start.13 = (f32[272,256]{1,0:T(8,128)S(1)}, f32[272,256]{1,0:T(8,128)S(1)}, u32[]{:S(2)}, u32[]{:S(2)}) collective-permute-start(f32[272,256]{1,0:T(8,128)S(1)} %get-tuple-element.78.m0), channel_id=1, source_target_pairs={{0,2},{1,3},{2,0},{3,1},{4,6},{5,7},{6,4},{7,5},{8,10},{9,11},{10,... | collective-permute-start | bytes 835592 | tf_op jit(solution)/shard_map/ppermute | solution.py:364
  70.1 14.7 %collective-permute-start.12 = (f32[272,256]{1,0:T(8,128)S(1)}, f32[272,256]{1,0:T(8,128)S(1)}, u32[]{:S(2)}, u32[]{:S(2)}) collective-permute-start(f32[272,256]{1,0:T(8,128)S(1)} %get-tuple-element.78.m0), channel_id=1, source_target_pairs={{0,1},{1,2},{2,3},{3,0},{4,5},{5,6},{6,7},{7,4},{8,9},{9,10},{10,1... | collective-permute-start | bytes 835592 | tf_op jit(solution)/shard_map/ppermute | solution.py:364
  86.3 1.6 %collective-permute-start.15 = (f32[272,256]{1,0:T(8,128)S(1)}, f32[272,256]{1,0:T(8,128)S(1)}, u32[]{:S(2)}, u32[]{:S(2)}) collective-permute-start(f32[272,256]{1,0:T(8,128)S(1)} %get-tuple-element.79.own), channel_id=1, source_target_pairs={{0,4},{4,0},{8,12},{12,8},{16,20},{20,16},{24,28},{28,24},{32,36},... | collective-permute-start | bytes 835592 | tf_op jit(solution)/shard_map/ppermute | solution.py:429
  88.8 9.4 %collective-permute-start.18 = (f32[136,256]{1,0:T(8,128)S(1)}, f32[136,256]{1,0:T(8,128)S(1)}, u32[]{:S(2)}, u32[]{:S(2)}) collective-permute-start(f32[136,256]{1,0:T(8,128)S(1)} %get-tuple-element.82), channel_id=1, source_target_pairs={{0,24},{4,28},{8,0},{12,4},{16,8},{20,12},{24,16},{28,20},{32,56},... | collective-permute-start | bytes 417800 | tf_op jit(solution)/shard_map/ppermute | solution.py:433
  91.8 8.1 %collective-permute-start.17 = (f32[136,256]{1,0:T(8,128)S(1)}, f32[136,256]{1,0:T(8,128)S(1)}, u32[]{:S(2)}, u32[]{:S(2)}) collective-permute-start(f32[136,256]{1,0:T(8,128)S(1)} %get-tuple-element.82), channel_id=1, source_target_pairs={{0,16},{4,20},{8,24},{12,28},{16,0},{20,4},{24,8},{28,12},{32,48},... | collective-permute-start | bytes 417800 | tf_op jit(solution)/shard_map/ppermute | solution.py:433
  92.5 9.4 %collective-permute-start.16 = (f32[136,256]{1,0:T(8,128)S(1)}, f32[136,256]{1,0:T(8,128)S(1)}, u32[]{:S(2)}, u32[]{:S(2)}) collective-permute-start(f32[136,256]{1,0:T(8,128)S(1)} %get-tuple-element.82), channel_id=1, source_target_pairs={{0,8},{4,12},{8,16},{12,20},{16,24},{20,28},{24,0},{28,4},{32,40},... | collective-permute-start | bytes 417800 | tf_op jit(solution)/shard_map/ppermute | solution.py:433
  98.2 3.7 %collective-permute-start.21 = (f32[136,256]{1,0:T(8,128)S(1)}, f32[136,256]{1,0:T(8,128)S(1)}, u32[]{:S(2)}, u32[]{:S(2)}) collective-permute-start(f32[136,256]{1,0:T(8,128)S(1)} %collective-permute-done.18.h3), channel_id=1, source_target_pairs={{0,4},{4,0},{8,12},{12,8},{16,20},{20,16},{24,28},{28,24},{32,36},... | collective-permute-start | bytes 417800 | tf_op jit(solution)/shard_map/ppermute | solution.py:429
  99.9 2.0 %collective-permute-start.20 = (f32[136,256]{1,0:T(8,128)S(1)}, f32[136,256]{1,0:T(8,128)S(1)}, u32[]{:S(2)}, u32[]{:S(2)}) collective-permute-start(f32[136,256]{1,0:T(8,128)S(1)} %collective-permute-done.17.h2), channel_id=1, source_target_pairs={{0,4},{4,0},{8,12},{12,8},{16,20},{20,16},{24,28},{28,24},{32,36},... | collective-permute-start | bytes 417800 | tf_op jit(solution)/shard_map/ppermute | solution.py:429
  101.9 1.4 %collective-permute-start.19 = (f32[136,256]{1,0:T(8,128)S(1)}, f32[136,256]{1,0:T(8,128)S(1)}, u32[]{:S(2)}, u32[]{:S(2)}) collective-permute-start(f32[136,256]{1,0:T(8,128)S(1)} %collective-permute-done.16.h1), channel_id=1, source_target_pairs={{0,4},{4,0},{8,12},{12,8},{16,20},{20,16},{24,28},{28,24},{32,36},... | collective-permute-start | bytes 417800 | tf_op jit(solution)/shard_map/ppermute | solution.py:429
  104.5 10.0 %collective-permute-start.24 = (f32[136,256]{1,0:T(8,128)S(1)}, f32[136,256]{1,0:T(8,128)S(1)}, u32[]{:S(2)}, u32[]{:S(2)}) collective-permute-start(f32[136,256]{1,0:T(8,128)S(1)} %get-tuple-element.83), channel_id=1, source_target_pairs={{0,96},{4,100},{8,104},{12,108},{16,112},{20,116},{24,120},{28,124... | collective-permute-start | bytes 417800 | tf_op jit(solution)/shard_map/ppermute | solution.py:433
  105.4 9.1 %collective-permute-start.23 = (f32[136,256]{1,0:T(8,128)S(1)}, f32[136,256]{1,0:T(8,128)S(1)}, u32[]{:S(2)}, u32[]{:S(2)}) collective-permute-start(f32[136,256]{1,0:T(8,128)S(1)} %get-tuple-element.83), channel_id=1, source_target_pairs={{0,64},{4,68},{8,72},{12,76},{16,80},{20,84},{24,88},{28,92},{32,9... | collective-permute-start | bytes 417800 | tf_op jit(solution)/shard_map/ppermute | solution.py:433
  106.6 8.6 %collective-permute-start.22 = (f32[136,256]{1,0:T(8,128)S(1)}, f32[136,256]{1,0:T(8,128)S(1)}, u32[]{:S(2)}, u32[]{:S(2)}) collective-permute-start(f32[136,256]{1,0:T(8,128)S(1)} %get-tuple-element.83), channel_id=1, source_target_pairs={{0,32},{4,36},{8,40},{12,44},{16,48},{20,52},{24,56},{28,60},{32,6... | collective-permute-start | bytes 417800 | tf_op jit(solution)/shard_map/ppermute | solution.py:433
  114.5 1.4 %collective-permute-start.27 = (f32[136,256]{1,0:T(8,128)S(1)}, f32[136,256]{1,0:T(8,128)S(1)}, u32[]{:S(2)}, u32[]{:S(2)}) collective-permute-start(f32[136,256]{1,0:T(8,128)S(1)} %collective-permute-done.24.h3), channel_id=1, source_target_pairs={{0,4},{4,0},{8,12},{12,8},{16,20},{20,16},{24,28},{28,24},{32,36},... | collective-permute-start | bytes 417800 | tf_op jit(solution)/shard_map/ppermute | solution.py:429
  114.5 1.6 %collective-permute-start.26 = (f32[136,256]{1,0:T(8,128)S(1)}, f32[136,256]{1,0:T(8,128)S(1)}, u32[]{:S(2)}, u32[]{:S(2)}) collective-permute-start(f32[136,256]{1,0:T(8,128)S(1)} %collective-permute-done.23.h2), channel_id=1, source_target_pairs={{0,4},{4,0},{8,12},{12,8},{16,20},{20,16},{24,28},{28,24},{32,36},... | collective-permute-start | bytes 417800 | tf_op jit(solution)/shard_map/ppermute | solution.py:429
  115.1 1.4 %collective-permute-start.25 = (f32[136,256]{1,0:T(8,128)S(1)}, f32[136,256]{1,0:T(8,128)S(1)}, u32[]{:S(2)}, u32[]{:S(2)}) collective-permute-start(f32[136,256]{1,0:T(8,128)S(1)} %collective-permute-done.22.h1), channel_id=1, source_target_pairs={{0,4},{4,0},{8,12},{12,8},{16,20},{20,16},{24,28},{28,24},{32,36},... | collective-permute-start | bytes 417800 | tf_op jit(solution)/shard_map/ppermute | solution.py:429
  118.8 4.9 %collective-permute-start.28 = (f32[16,64]{1,0:T(8,128)S(1)}, f32[16,64]{1,0:T(8,128)S(1)}, u32[]{:S(2)}, u32[]{:S(2)}) collective-permute-start(f32[16,64]{1,0:T(8,128)S(1)} %get-tuple-element.88), channel_id=1, source_target_pairs={{0,1},{1,2},{2,3},{3,0},{4,5},{5,6},{6,7},{7,4},{8,9},{9,10},{10,1... | collective-permute-start | bytes 12296 | tf_op jit(solution)/shard_map/ppermute | solution.py:364
  118.9 5.2 %collective-permute-start.29 = (f32[16,64]{1,0:T(8,128)S(1)}, f32[16,64]{1,0:T(8,128)S(1)}, u32[]{:S(2)}, u32[]{:S(2)}) collective-permute-start(f32[16,64]{1,0:T(8,128)S(1)} %get-tuple-element.89), channel_id=1, source_target_pairs={{0,2},{1,3},{2,0},{3,1},{4,6},{5,7},{6,4},{7,5},{8,10},{9,11},{10,... | collective-permute-start | bytes 12296 | tf_op jit(solution)/shard_map/ppermute | solution.py:364
  121.2 3.7 %collective-permute-start.30 = (f32[16,64]{1,0:T(8,128)S(1)}, f32[16,64]{1,0:T(8,128)S(1)}, u32[]{:S(2)}, u32[]{:S(2)}) collective-permute-start(f32[16,64]{1,0:T(8,128)S(1)} %get-tuple-element.90), channel_id=1, source_target_pairs={{0,3},{1,0},{2,1},{3,2},{4,7},{5,4},{6,5},{7,6},{8,11},{9,8},{10,9... | collective-permute-start | bytes 12296 | tf_op jit(solution)/shard_map/ppermute | solution.py:364
  (3 other events, 26.7 us)

commit v7 on v6

--- a/solution.py
+++ b/solution.py
@@ -17,7 +17,7 @@
 HALF = R // 2
 ROWS = 4
 SUB = 16
-CHUNKS = ((4, 4, 4), (2, 2))
+CHUNKS = ((5, 5, 4), (2,))
 SEGS = tuple(n for chunk in CHUNKS for n in chunk)
 SIZES = tuple(sum(chunk) for chunk in CHUNKS)
 ENDS = tuple(sum(SEGS[: i + 1]) for i in range(len(SEGS)))
@@ -179,9 +179,11 @@
     copy = own_copy(z, flat, own, SIZES[0], sem)
     copy.start()
     assemble(z, (own, a1, a2, a3), ah, al, copy)
+    total = tail[1]
+    for k in range(SIZES[1]):
+        total = by_step(total, ah[k], al[k])
+    last[...] = total
     chains(CHUNKS[1], ah, al, pref)
-    last[0] = mm(pref[CHUNKS[1][0] - 1], pref[SIZES[1] - 1])
-    last[1] = mm(tail[1], last[0])
 
 
 def third_kernel(idx, b0, b1, b2, b3, p01, ah01, al01, tail, p23, ah23, al23, last, shifts, whole, b_s):
@@ -208,8 +210,8 @@
             p[c] = by_step(p[c], h[i], l[i]) + row(k)
             shifts[k : k + 1, :] = p[c][:1]
     v = mm(p[0], tail[0]) + mm(p[1], p01[SIZES[0] - 1]) + p[2]
-    v = mm(v, last[0]) + (mm(p[3], p23[SIZES[1] - 1]) + p[4])
-    whole[:N, :] = last[1]
+    v = mm(v, p23[SIZES[1] - 1]) + p[3]
+    whole[:N, :] = last[...]
     whole[N:, :] = v
 
 
@@ -244,19 +246,19 @@
     return pl.ds(pl.multiple_of(c * HALF, 8), HALF)
 
 
-def join_halves(pos, c, mine, others, m_s):
-    for d, (m, o) in enumerate(zip(mine, others)):
-        slot = lax.rem(pos - d + 3, 4)
-        m_s[slot, half_rows(c), :] = m[...]
-        m_s[slot, half_rows(1 - c), :] = o[...]
-
-
-def halves_kernel(idx, own, h1, h2, h3, o1, o2, o3, half, before, m_s):
+def join(pos, c, near_map, near_other, far_half, far_other, m_s):
+    m_s[lax.rem(pos + 3 + 2 * c, 4)] = near_map[...]
+    m_s[lax.rem(pos + 5 - 2 * c, 4)] = near_other[...]
+    m_s[lax.rem(pos + 2, 4), half_rows(c), :] = far_half[...]
+    m_s[lax.rem(pos + 2, 4), half_rows(1 - c), :] = far_other[...]
+
+
+def plane_kernel(idx, own, n, no, f, fo, total, half, before, m_s):
     pos, c = idx[Y], idx[C]
     m_s[pos] = own[...]
-    join_halves(pos, c, (h1, h2, h3), (o1, o2, o3), m_s)
-    m_s[4] = combine(pos, m_s, before)
-    half[...] = m_s[4, half_rows(c), :]
+    join(pos, c, n, no, f, fo, m_s)
+    total[...] = combine(pos, m_s, before)
+    half[...] = total[half_rows(c), :]
 
 
 def pair_kernel(idx, own, other, before_in, total, half, before):
@@ -281,10 +283,10 @@
 
 
 def states_kernel(
-    idx, prior, h1, h2, h3, g1, g2, g3, before, p01, p23, shifts, o0, o1, o2, o3, st_s, m_s, s_s
+    idx, prior, n, no, f, fo, before, p01, p23, shifts, o0, o1, o2, o3, st_s, m_s, s_s
 ):
     z, pos = idx[Z], idx[X]
-    join_halves(pos, idx[C], (h1, h2, h3), (g1, g2, g3), m_s)
+    join(pos, idx[C], n, no, f, fo, m_s)
     s_s[...] = jnp.where(lax.broadcasted_iota(jnp.int32, (PAD, N), 0) == 0, prior[...], 0.0)
     for i in range(3):
 
@@ -403,7 +405,7 @@
     offs = [offs[0], *along_rows(offs[1:])]
     p23, ah23, al23, last = call(
         second_kernel,
-        [(SIZES[1], N, N), ((SIZES[1], N, N), BF16), ((SIZES[1], N, N), BF16), (2, N, N)],
+        [(SIZES[1], N, N), ((SIZES[1], N, N), BF16), ((SIZES[1], N, N), BF16), (N, N)],
         idx,
         (*part_b, tail),
         [pltpu.VMEM((SIZES[1] * 64, N), F32), pltpu.SemaphoreType.DMA],
@@ -428,28 +430,30 @@
     def other_core(m):
         return lax.ppermute(m, "tm", [(i, i ^ 1) for i in range(32)])
 
-    def along_tm(m, d, n, stride):
-        places = [(i, i - i % (n * stride) + (i + d * stride) % (n * stride)) for i in range(32)]
-        return lax.ppermute(m, "tm", places)
+    def along_tm(m, stride, moves):
+        n = 4 * stride
+        return lax.ppermute(m, "tm", [(i, i - i % n + (i + moves[i % 2] * stride) % n) for i in range(32)])
+
+    def gathered(m, half, stride):
+        far, near_map = along_tm(half, stride, (2, 2)), along_tm(m, stride, (1, 3))
+        return near_map, other_core(near_map), far, other_core(far)
 
     column, half, before = call(
         pair_kernel, [(R, N), (HALF, N), (R, N)], idx, (block, other_core(block), before)
     )
-    halves = [along_tm(half, d, 4, 2) for d in (1, 2, 3)]
-    half, ybefore = call(
-        halves_kernel,
-        [(HALF, N), (R, N)],
-        idx,
-        (column, *halves, *[other_core(h) for h in halves]),
-        [pltpu.VMEM((5, R, N), F32)],
-    )
-    halves = [along_tm(half, d, 4, 8) for d in (1, 2, 3)]
+    plane, half, ybefore = call(
+        plane_kernel,
+        [(R, N), (HALF, N), (R, N)],
+        idx,
+        (column, *gathered(column, half, 2)),
+        [pltpu.VMEM((4, R, N), F32)],
+    )
     (before,) = call(fold_kernel, [(R, N)], idx, (ybefore, before))
     outs = call(
         states_kernel,
         [(SUB, 64)] * 4,
         idx,
-        (prior, *halves, *[other_core(h) for h in halves], before, p01, p23, shifts),
+        (prior, *gathered(plane, half, 8), before, p01, p23, shifts),
         [pltpu.VMEM((ROWS, SUB, 64), F32), pltpu.VMEM((4, R, N), F32), pltpu.VMEM((PAD, N), F32)],
     )
     got = [outs[0], *along_rows(outs[1:])]

time: 128 us -> 127 us (level)
    ppermute x6 -> x4, waiting for transfers between devices: 14.4 us -> 11.6 us  [along_tm(): lax.ppermute(m, 'tm', [(i, i - i % n + (i + moves[i % 2] * stride) % n) f...]
    ppermute x7 -> x5, starting transfers between devices: 0.63 us -> 2.79 us  [other_core(): return lax.ppermute(m, 'tm', [(i, i ^ 1) for i in range(32)])]
    ppermute x18, waiting for transfers between devices: 24.5 us -> 26.2 us  [along_row(): return lax.ppermute(x, 'row', [(i, (i + d) % ROWS) for i in range(ROWS)])]
    ppermute x6 -> x4, starting transfers between devices: 8.79 us -> 7.51 us  [along_tm(): lax.ppermute(m, 'tm', [(i, i - i % n + (i + moves[i % 2] * stride) % n) f...]
    ppermute x7 -> x5, waiting for transfers between devices: 3.39 us -> 3.45 us  [other_core(): return lax.ppermute(m, 'tm', [(i, i ^ 1) for i in range(32)])]
  transfers between devices with their start and end apart: 31 -> 27, of which waited for: 17 -> 14; matrix products, arithmetic and copies ran while one was open for 0% -> 0% of each run, Pallas kernels for 14% -> 14%
where the time goes in v7:
time: 127 us; the launch traced here: 126 us
  waiting for transfers between devices  41.3 us (33%)
  starting transfers between devices  37.9 us (30%)
  Pallas kernels  29.5 us (23%)
  blocking collectives  16.7 us (13%)
    ppermute x18, starting transfers between devices, along_row(): return lax.ppermute(x, 'row', [(i, (i + d) % ROWS) for i in range(ROWS)])  27.6 us
    ppermute x18, waiting for transfers between devices, along_row(): return lax.ppermute(x, 'row', [(i, (i + d) % ROWS) for i in range(ROWS)])  26.2 us
    pallas_call x12, Pallas kernels, call(): pl.pallas_call(kernel, out_shape=[pltpu.VMEM(s, t) for s, t in outs], in_...  21.4 us
    all_to_all x1, blocking collectives, shards(): sums = lax.all_to_all(partial, 'tm', 0, 0, tiled=True).reshape(32, 16, N)  16.7 us
    ppermute x4, waiting for transfers between devices, along_tm(): lax.ppermute(m, 'tm', [(i, i - i % n + (i + moves[i % 2] * stride) % n) f...  11.6 us
    ppermute x4, starting transfers between devices, along_tm(): lax.ppermute(m, 'tm', [(i, i - i % n + (i + moves[i % 2] * stride) % n) f...  7.51 us
    pallas_call x1, Pallas kernels, binned(): pl.pallas_call(bin_kernel, out_shape=jax.ShapeDtypeStruct((n_bins // 4, N...  6.91 us
    ppermute x5, waiting for transfers between devices, other_core(): return lax.ppermute(m, 'tm', [(i, i ^ 1) for i in range(32)])  3.45 us
  transfers between devices with their start and end apart: 27, of which 14 were waited for; matrix products, arithmetic and copies ran while one was open for 0% of the time, Pallas kernels for 14%

profile of v7, /device:TPU:6, one launch (start us, length us, event | category | flops | bytes accessed | tf_op | source)
XLA Modules:
  0.0 125.7 jit_solution(2601152345885881695)
XLA Ops:
  0.1 2.3 %shard_map.67 = (f32[896,256]{1,0:T(8,128)S(1)}, f32[896,256]{1,0:T(8,128)S(1)}, f32[896,256]{1,0:T(8,128)S(1)}) custom-call(s32[4]{0:T(128)S(1)} %pad_add_fusion.idx, f32[4096,256]{1,0:T(8,128)} %bitcast.14), custom_call_target="tpu_custom_call" | custom-call | tf_op jit(solution)/shard_map/pallas_call | solution.py:69
  2.4 2.0 %collective-permute-start.3 = (f32[896,256]{1,0:T(8,128)S(1)}, f32[896,256]{1,0:T(8,128)S(1)}, u32[]{:S(2)}, u32[]{:S(2)}) collective-permute-start(f32[896,256]{1,0:T(8,128)S(1)} %get-tuple-element.52), channel_id=1, source_target_pairs={{0,1},{1,2},{2,3},{3,0},{4,5},{5,6},{6,7},{7,4},{8,9},{9,10},{10,1... | collective-permute-start | bytes 2752520 | tf_op jit(solution)/shard_map/ppermute | solution.py:366
  4.4 3.6 %collective-permute-start.4 = (f32[896,256]{1,0:T(8,128)S(1)}, f32[896,256]{1,0:T(8,128)S(1)}, u32[]{:S(2)}, u32[]{:S(2)}) collective-permute-start(f32[896,256]{1,0:T(8,128)S(1)} %get-tuple-element.53), channel_id=1, source_target_pairs={{0,2},{1,3},{2,0},{3,1},{4,6},{5,7},{6,4},{7,5},{8,10},{9,11},{10,... | collective-permute-start | bytes 2752520 | tf_op jit(solution)/shard_map/ppermute | solution.py:366
  9.1 6.9 %shard_map.64 = f32[512,256]{1,0:T(8,128)S(1)} custom-call(s32[1,4096]{1,0:T(1,128)S(1)} %bitcast.12, f32[64,4096]{1,0:T(8,128)S(1)} %bitcast.11), custom_call_target="tpu_custom_call" | custom-call | tf_op jit(solution)/shard_map/pallas_call | solution.py:114
  16.0 16.7 %all_to_all.9.sums = f32[32,16,256]{2,1,0:T(8,128)S(1)} all-to-all(f32[32,16,256]{2,1,0:T(8,128)S(1)} %bitcast.10), channel_id=1, replica_groups=mesh['tm'=32,'row'=4] {'tm'}, dimensions={0} | all-to-all | bytes 1048576 | tf_op jit(solution)/shard_map/all_to_all | solution.py:384
  33.3 3.1 %collective-permute-start.1 = (f32[16,256]{1,0:T(8,128)S(1)}, f32[16,256]{1,0:T(8,128)S(1)}, u32[]{:S(2)}, u32[]{:S(2)}) collective-permute-start(f32[16,256]{1,0:T(8,128)S(1)} %shard_map.65.i0), channel_id=1, source_target_pairs={{0,2},{1,3},{2,0},{3,1},{4,6},{5,7},{6,4},{7,5},{8,10},{9,11},{10,... | collective-permute-start | bytes 49160 | tf_op jit(solution)/shard_map/ppermute | solution.py:366
  36.4 11.4 %collective-permute-done.2.r3 = f32[16,256]{1,0:T(8,128)S(1)} collective-permute-done((f32[16,256]{1,0:T(8,128)S(1)}, f32[16,256]{1,0:T(8,128)S(1)}, u32[]{:S(2)}, u32[]{:S(2)}) %collective-permute-start.2) | collective-permute-done | bytes 16416 | tf_op jit(solution)/shard_map/ppermute | solution.py:366
  47.8 1.7 %collective-permute-start = (f32[16,256]{1,0:T(8,128)S(1)}, f32[16,256]{1,0:T(8,128)S(1)}, u32[]{:S(2)}, u32[]{:S(2)}) collective-permute-start(f32[16,256]{1,0:T(8,128)S(1)} %shard_map.65.i0), channel_id=1, source_target_pairs={{0,1},{1,2},{2,3},{3,0},{4,5},{5,6},{6,7},{7,4},{8,9},{9,10},{10,1... | collective-permute-start | bytes 49160 | tf_op jit(solution)/shard_map/ppermute | solution.py:366
  49.5 1.6 %shard_map.66 = (f32[128,256]{1,0:T(8,128)S(1)}, f32[128,256]{1,0:T(8,128)S(1)}, f32[128,256]{1,0:T(8,128)S(1)}) custom-call(s32[4]{0:T(128)S(1)} %pad_add_fusion.idx, f32[4096,256]{1,0:T(8,128)} %bitcast.15), custom_call_target="tpu_custom_call" | custom-call | tf_op jit(solution)/shard_map/pallas_call | solution.py:69
  51.1 1.6 %collective-permute-done.r1 = f32[16,256]{1,0:T(8,128)S(1)} collective-permute-done((f32[16,256]{1,0:T(8,128)S(1)}, f32[16,256]{1,0:T(8,128)S(1)}, u32[]{:S(2)}, u32[]{:S(2)}) %collective-permute-start) | collective-permute-done | bytes 16416 | tf_op jit(solution)/shard_map/ppermute | solution.py:366
  53.3 2.4 %collective-permute-start.10 = (f32[128,256]{1,0:T(8,128)S(1)}, f32[128,256]{1,0:T(8,128)S(1)}, u32[]{:S(2)}, u32[]{:S(2)}) collective-permute-start(f32[128,256]{1,0:T(8,128)S(1)} %get-tuple-element.73), channel_id=1, source_target_pairs={{0,2},{1,3},{2,0},{3,1},{4,6},{5,7},{6,4},{7,5},{8,10},{9,11},{10,... | collective-permute-start | bytes 393224 | tf_op jit(solution)/shard_map/ppermute | solution.py:366
  56.9 4.0 %shard_map.68 = (f32[14,256,256]{2,1,0:T(8,128)S(1)}, bf16[14,256,256]{2,1,0:T(8,128)(2,1)S(1)}, bf16[14,256,256]{2,1,0:T(8,128)(2,1)S(1)}, f32[2,256,256]{2,1,0:T(8,128)S(1)}, f32[64,64,256]{2,1,0:T(8,128)S(1)}) custom-call(s32[4]{0:T(128)S(1)} %pad_add_fusion.idx, f32[4096,256]{1,0:T(8,128)} %bitcast.16, f32[64,64,256]{2,1,0:T(8,128)} %gains.1, ...), custom_call_target="tpu_custom_call" | custom-call | tf_op jit(solution)/shard_map/pallas_call | solution.py:69
  61.0 1.6 %shard_map.69 = (f32[16,256]{1,0:T(8,128)S(1)}, f32[16,256]{1,0:T(8,128)S(1)}, f32[16,256]{1,0:T(8,128)S(1)}, f32[16,256]{1,0:T(8,128)S(1)}) custom-call(s32[4]{0:T(128)S(1)} %pad_add_fusion.idx, f32[64,64,256]{2,1,0:T(8,128)S(1)} %get-tuple-element.60.g, f32[16,256]{1,0:T(8,128)S(1)} %shard_map.65.i0, f32[16,256]{1,0:T(8,128)S(1)} %collective-permute-done.r1, ...), custom_call_target="tpu_custom_call" | custom-call | tf_op jit(solution)/shard_map/pallas_call | solution.py:69
  63.3 1.4 %collective-permute-start.7 = (f32[16,256]{1,0:T(8,128)S(1)}, f32[16,256]{1,0:T(8,128)S(1)}, u32[]{:S(2)}, u32[]{:S(2)}) collective-permute-start(f32[16,256]{1,0:T(8,128)S(1)} %get-tuple-element.66), channel_id=1, source_target_pairs={{0,2},{1,3},{2,0},{3,1},{4,6},{5,7},{6,4},{7,5},{8,10},{9,11},{10,... | collective-permute-start | bytes 49160 | tf_op jit(solution)/shard_map/ppermute | solution.py:366
  64.7 2.5 %collective-permute-start.8 = (f32[16,256]{1,0:T(8,128)S(1)}, f32[16,256]{1,0:T(8,128)S(1)}, u32[]{:S(2)}, u32[]{:S(2)}) collective-permute-start(f32[16,256]{1,0:T(8,128)S(1)} %get-tuple-element.67), channel_id=1, source_target_pairs={{0,3},{1,0},{2,1},{3,2},{4,7},{5,4},{6,5},{7,6},{8,11},{9,8},{10,9... | collective-permute-start | bytes 49160 | tf_op jit(solution)/shard_map/ppermute | solution.py:366
  67.2 2.3 %shard_map.70 = (f32[2,256,256]{2,1,0:T(8,128)S(1)}, bf16[2,256,256]{2,1,0:T(8,128)(2,1)S(1)}, bf16[2,256,256]{2,1,0:T(8,128)(2,1)S(1)}, f32[256,256]{1,0:T(8,128)S(1)}) custom-call(s32[4]{0:T(128)S(1)} %pad_add_fusion.idx, f32[4096,256]{1,0:T(8,128)} %bitcast.17, f32[128,256]{1,0:T(8,128)S(1)} %collective-permute-done.9.a1, ...), custom_call_target="tpu_custom_call" | custom-call | tf_op jit(solution)/shard_map/pallas_call | solution.py:69
  69.6 2.4 %shard_map.71 = (f32[16,256]{1,0:T(8,128)S(1)}, f32[272,256]{1,0:T(8,128)S(1)}) custom-call(s32[4]{0:T(128)S(1)} %pad_add_fusion.idx, f32[16,256]{1,0:T(8,128)S(1)} %get-tuple-element.64.b0, f32[16,256]{1,0:T(8,128)S(1)} %collective-permute-done.6.b1, f32[16,256]{1,0:T(8,128)S(1)} %collective-permute-done.7.b2, f32[16,256]{1,0:T(8,128)S(1)} %collective-permute-done.8.b3, ...), custom_call_target="tpu_custom_call" | custom-call | tf_op jit(solution)/shard_map/pallas_call | solution.py:69
  71.9 2.6 %collective-permute-start.14 = (f32[272,256]{1,0:T(8,128)S(1)}, f32[272,256]{1,0:T(8,128)S(1)}, u32[]{:S(2)}, u32[]{:S(2)}) collective-permute-start(f32[272,256]{1,0:T(8,128)S(1)} %get-tuple-element.79.m0), channel_id=1, source_target_pairs={{0,3},{1,0},{2,1},{3,2},{4,7},{5,4},{6,5},{7,6},{8,11},{9,8},{10,9... | collective-permute-start | bytes 835592 | tf_op jit(solution)/shard_map/ppermute | solution.py:366
  75.4 7.5 %collective-permute-done.14.m3 = f32[272,256]{1,0:T(8,128)S(1)} collective-permute-done((f32[272,256]{1,0:T(8,128)S(1)}, f32[272,256]{1,0:T(8,128)S(1)}, u32[]{:S(2)}, u32[]{:S(2)}) %collective-permute-start.14) | collective-permute-done | bytes 278560 | tf_op jit(solution)/shard_map/ppermute | solution.py:366
  83.4 2.8 %collective-permute-done.12.m1 = f32[272,256]{1,0:T(8,128)S(1)} collective-permute-done((f32[272,256]{1,0:T(8,128)S(1)}, f32[272,256]{1,0:T(8,128)S(1)}, u32[]{:S(2)}, u32[]{:S(2)}) %collective-permute-start.12) | collective-permute-done | bytes 278560 | tf_op jit(solution)/shard_map/ppermute | solution.py:366
  86.3 1.5 %shard_map.72 = (f32[272,256]{1,0:T(8,128)S(1)}, f32[272,256]{1,0:T(8,128)S(1)}) custom-call(s32[4]{0:T(128)S(1)} %pad_add_fusion.idx, f32[272,256]{1,0:T(8,128)S(1)} %get-tuple-element.79.m0, f32[272,256]{1,0:T(8,128)S(1)} %collective-permute-done.12.m1, f32[272,256]{1,0:T(8,128)S(1)} %collective-permute-done.13.m2, f32[272,256]{1,0:T(8,128)S(1)} %collective-permute-done.14.m3), custom_call_target="tpu_custom_call" | custom-call | tf_op jit(solution)/shard_map/pallas_call | solution.py:69
  87.9 1.5 %collective-permute-done.15.other = f32[272,256]{1,0:T(8,128)S(1)} collective-permute-done((f32[272,256]{1,0:T(8,128)S(1)}, f32[272,256]{1,0:T(8,128)S(1)}, u32[]{:S(2)}, u32[]{:S(2)}) %collective-permute-start.15) | collective-permute-done | bytes 278560 | tf_op jit(solution)/shard_map/ppermute | solution.py:431
  90.3 1.6 %collective-permute-start.16 = (f32[272,256]{1,0:T(8,128)S(1)}, f32[272,256]{1,0:T(8,128)S(1)}, u32[]{:S(2)}, u32[]{:S(2)}) collective-permute-start(f32[272,256]{1,0:T(8,128)S(1)} %get-tuple-element.82.own), channel_id=1, source_target_pairs={{0,8},{4,28},{8,16},{12,4},{16,24},{20,12},{24,0},{28,20},{32,40},... | collective-permute-start | bytes 835592 | tf_op jit(solution)/shard_map/ppermute | solution.py:435
  91.9 2.9 %collective-permute-start.18 = (f32[136,256]{1,0:T(8,128)S(1)}, f32[136,256]{1,0:T(8,128)S(1)}, u32[]{:S(2)}, u32[]{:S(2)}) collective-permute-start(f32[136,256]{1,0:T(8,128)S(1)} %get-tuple-element.83), channel_id=1, source_target_pairs={{0,16},{4,20},{8,24},{12,28},{16,0},{20,4},{24,8},{28,12},{32,48},... | collective-permute-start | bytes 417800 | tf_op jit(solution)/shard_map/ppermute | solution.py:435
  94.8 4.0 %collective-permute-done.16.n = f32[272,256]{1,0:T(8,128)S(1)} collective-permute-done((f32[272,256]{1,0:T(8,128)S(1)}, f32[272,256]{1,0:T(8,128)S(1)}, u32[]{:S(2)}, u32[]{:S(2)}) %collective-permute-start.16) | collective-permute-done | bytes 278560 | tf_op jit(solution)/shard_map/ppermute | solution.py:435
  99.8 2.5 %collective-permute-done.18.f = f32[136,256]{1,0:T(8,128)S(1)} collective-permute-done((f32[136,256]{1,0:T(8,128)S(1)}, f32[136,256]{1,0:T(8,128)S(1)}, u32[]{:S(2)}, u32[]{:S(2)}) %collective-permute-start.18) | collective-permute-done | bytes 139296 | tf_op jit(solution)/shard_map/ppermute | solution.py:435
  102.3 1.4 %collective-permute-done.19.fo = f32[136,256]{1,0:T(8,128)S(1)} collective-permute-done((f32[136,256]{1,0:T(8,128)S(1)}, f32[136,256]{1,0:T(8,128)S(1)}, u32[]{:S(2)}, u32[]{:S(2)}) %collective-permute-start.19) | collective-permute-done | bytes 139296 | tf_op jit(solution)/shard_map/ppermute | solution.py:431
  105.5 2.4 %collective-permute-start.22 = (f32[136,256]{1,0:T(8,128)S(1)}, f32[136,256]{1,0:T(8,128)S(1)}, u32[]{:S(2)}, u32[]{:S(2)}) collective-permute-start(f32[136,256]{1,0:T(8,128)S(1)} %get-tuple-element.85), channel_id=1, source_target_pairs={{0,64},{4,68},{8,72},{12,76},{16,80},{20,84},{24,88},{28,92},{32,9... | collective-permute-start | bytes 417800 | tf_op jit(solution)/shard_map/ppermute | solution.py:435
  108.0 5.1 %collective-permute-done.20.n = f32[272,256]{1,0:T(8,128)S(1)} collective-permute-done((f32[272,256]{1,0:T(8,128)S(1)}, f32[272,256]{1,0:T(8,128)S(1)}, u32[]{:S(2)}, u32[]{:S(2)}) %collective-permute-start.20) | collective-permute-done | bytes 278560 | tf_op jit(solution)/shard_map/ppermute | solution.py:435
  113.1 1.7 %collective-permute-start.21 = (f32[272,256]{1,0:T(8,128)S(1)}, f32[272,256]{1,0:T(8,128)S(1)}, u32[]{:S(2)}, u32[]{:S(2)}) collective-permute-start(f32[272,256]{1,0:T(8,128)S(1)} %collective-permute-done.20.n), channel_id=1, source_target_pairs={{0,4},{4,0},{8,12},{12,8},{16,20},{20,16},{24,28},{28,24},{32,36},... | collective-permute-start | bytes 835592 | tf_op jit(solution)/shard_map/ppermute | solution.py:431
  116.2 2.2 %shard_map.76 = (f32[16,64]{1,0:T(8,128)S(1)}, f32[16,64]{1,0:T(8,128)S(1)}, f32[16,64]{1,0:T(8,128)S(1)}, f32[16,64]{1,0:T(8,128)S(1)}) custom-call(s32[4]{0:T(128)S(1)} %pad_add_fusion.idx, f32[1,256]{1,0:T(1,128)S(1)} %bitcast.13, f32[272,256]{1,0:T(8,128)S(1)} %collective-permute-done.20.n, f32[272,256]{1,0:T(8,128)S(1)} %collective-permute-done.21.no, ...), custom_call_target="tpu_custom_call" | custom-call | tf_op jit(solution)/shard_map/pallas_call | solution.py:69
  118.5 2.4 %collective-permute-start.25 = (f32[16,64]{1,0:T(8,128)S(1)}, f32[16,64]{1,0:T(8,128)S(1)}, u32[]{:S(2)}, u32[]{:S(2)}) collective-permute-start(f32[16,64]{1,0:T(8,128)S(1)} %get-tuple-element.91), channel_id=1, source_target_pairs={{0,2},{1,3},{2,0},{3,1},{4,6},{5,7},{6,4},{7,5},{8,10},{9,11},{10,... | collective-permute-start | bytes 12296 | tf_op jit(solution)/shard_map/ppermute | solution.py:366
  (48 shorter events, 15.9 us)
Async XLA Ops:
  0.0 9.0 %copy-start.3 = (s32[4096,1]{0,1:T(1,128)S(1)}, s32[4096,1]{0,1:T(1,128)}, u32[]{:S(2)}) copy-start(s32[4096,1]{0,1:T(1,128)} %param.10) | copy-start | bytes 49156
  0.0 9.0 %copy-start.2 = (s32[4096]{0:T(1024)S(1)}, s32[4096]{0:T(1024)}, u32[]{:S(2)}) copy-start(s32[4096]{0:T(1024)} %param.11) | copy-start | bytes 49156
  0.0 9.0 %copy-start = (f32[4096,64]{0,1:T(8,128)S(1)}, f32[4096,64]{0,1:T(8,128)}, u32[]{:S(2)}) copy-start(f32[4096,64]{0,1:T(8,128)} %param.9) | copy-start | bytes 3145732
  2.4 50.3 %collective-permute-start.3 = (f32[896,256]{1,0:T(8,128)S(1)}, f32[896,256]{1,0:T(8,128)S(1)}, u32[]{:S(2)}, u32[]{:S(2)}) collective-permute-start(f32[896,256]{1,0:T(8,128)S(1)} %get-tuple-element.52), channel_id=1, source_target_pairs={{0,1},{1,2},{2,3},{3,0},{4,5},{5,6},{6,7},{7,4},{8,9},{9,10},{10,1... | collective-permute-start | bytes 2752520 | tf_op jit(solution)/shard_map/ppermute | solution.py:366
  4.4 48.3 %collective-permute-start.4 = (f32[896,256]{1,0:T(8,128)S(1)}, f32[896,256]{1,0:T(8,128)S(1)}, u32[]{:S(2)}, u32[]{:S(2)}) collective-permute-start(f32[896,256]{1,0:T(8,128)S(1)} %get-tuple-element.53), channel_id=1, source_target_pairs={{0,2},{1,3},{2,0},{3,1},{4,6},{5,7},{6,4},{7,5},{8,10},{9,11},{10,... | collective-permute-start | bytes 2752520 | tf_op jit(solution)/shard_map/ppermute | solution.py:366
  8.0 44.7 %collective-permute-start.5 = (f32[896,256]{1,0:T(8,128)S(1)}, f32[896,256]{1,0:T(8,128)S(1)}, u32[]{:S(2)}, u32[]{:S(2)}) collective-permute-start(f32[896,256]{1,0:T(8,128)S(1)} %get-tuple-element.54), channel_id=1, source_target_pairs={{0,3},{1,0},{2,1},{3,2},{4,7},{5,4},{6,5},{7,6},{8,11},{9,8},{10,9... | collective-permute-start | bytes 2752520 | tf_op jit(solution)/shard_map/ppermute | solution.py:366
  33.3 14.5 %collective-permute-start.2 = (f32[16,256]{1,0:T(8,128)S(1)}, f32[16,256]{1,0:T(8,128)S(1)}, u32[]{:S(2)}, u32[]{:S(2)}) collective-permute-start(f32[16,256]{1,0:T(8,128)S(1)} %shard_map.65.i0), channel_id=1, source_target_pairs={{0,3},{1,0},{2,1},{3,2},{4,7},{5,4},{6,5},{7,6},{8,11},{9,8},{10,9... | collective-permute-start | bytes 49160 | tf_op jit(solution)/shard_map/ppermute | solution.py:366
  33.3 17.7 %collective-permute-start.1 = (f32[16,256]{1,0:T(8,128)S(1)}, f32[16,256]{1,0:T(8,128)S(1)}, u32[]{:S(2)}, u32[]{:S(2)}) collective-permute-start(f32[16,256]{1,0:T(8,128)S(1)} %shard_map.65.i0), channel_id=1, source_target_pairs={{0,2},{1,3},{2,0},{3,1},{4,6},{5,7},{6,4},{7,5},{8,10},{9,11},{10,... | collective-permute-start | bytes 49160 | tf_op jit(solution)/shard_map/ppermute | solution.py:366
  47.8 4.9 %collective-permute-start = (f32[16,256]{1,0:T(8,128)S(1)}, f32[16,256]{1,0:T(8,128)S(1)}, u32[]{:S(2)}, u32[]{:S(2)}) collective-permute-start(f32[16,256]{1,0:T(8,128)S(1)} %shard_map.65.i0), channel_id=1, source_target_pairs={{0,1},{1,2},{2,3},{3,0},{4,5},{5,6},{6,7},{7,4},{8,9},{9,10},{10,1... | collective-permute-start | bytes 49160 | tf_op jit(solution)/shard_map/ppermute | solution.py:366
  52.7 11.9 %collective-permute-start.9 = (f32[128,256]{1,0:T(8,128)S(1)}, f32[128,256]{1,0:T(8,128)S(1)}, u32[]{:S(2)}, u32[]{:S(2)}) collective-permute-start(f32[128,256]{1,0:T(8,128)S(1)} %get-tuple-element.72), channel_id=1, source_target_pairs={{0,1},{1,2},{2,3},{3,0},{4,5},{5,6},{6,7},{7,4},{8,9},{9,10},{10,1... | collective-permute-start | bytes 393224 | tf_op jit(solution)/shard_map/ppermute | solution.py:366
  53.3 13.9 %collective-permute-start.10 = (f32[128,256]{1,0:T(8,128)S(1)}, f32[128,256]{1,0:T(8,128)S(1)}, u32[]{:S(2)}, u32[]{:S(2)}) collective-permute-start(f32[128,256]{1,0:T(8,128)S(1)} %get-tuple-element.73), channel_id=1, source_target_pairs={{0,2},{1,3},{2,0},{3,1},{4,6},{5,7},{6,4},{7,5},{8,10},{9,11},{10,... | collective-permute-start | bytes 393224 | tf_op jit(solution)/shard_map/ppermute | solution.py:366
  55.7 11.5 %collective-permute-start.11 = (f32[128,256]{1,0:T(8,128)S(1)}, f32[128,256]{1,0:T(8,128)S(1)}, u32[]{:S(2)}, u32[]{:S(2)}) collective-permute-start(f32[128,256]{1,0:T(8,128)S(1)} %get-tuple-element.74), channel_id=1, source_target_pairs={{0,3},{1,0},{2,1},{3,2},{4,7},{5,4},{6,5},{7,6},{8,11},{9,8},{10,9... | collective-permute-start | bytes 393224 | tf_op jit(solution)/shard_map/ppermute | solution.py:366
  62.5 7.0 %collective-permute-start.6 = (f32[16,256]{1,0:T(8,128)S(1)}, f32[16,256]{1,0:T(8,128)S(1)}, u32[]{:S(2)}, u32[]{:S(2)}) collective-permute-start(f32[16,256]{1,0:T(8,128)S(1)} %get-tuple-element.65), channel_id=1, source_target_pairs={{0,1},{1,2},{2,3},{3,0},{4,5},{5,6},{6,7},{7,4},{8,9},{9,10},{10,1... | collective-permute-start | bytes 49160 | tf_op jit(solution)/shard_map/ppermute | solution.py:366
  63.3 6.2 %collective-permute-start.7 = (f32[16,256]{1,0:T(8,128)S(1)}, f32[16,256]{1,0:T(8,128)S(1)}, u32[]{:S(2)}, u32[]{:S(2)}) collective-permute-start(f32[16,256]{1,0:T(8,128)S(1)} %get-tuple-element.66), channel_id=1, source_target_pairs={{0,2},{1,3},{2,0},{3,1},{4,6},{5,7},{6,4},{7,5},{8,10},{9,11},{10,... | collective-permute-start | bytes 49160 | tf_op jit(solution)/shard_map/ppermute | solution.py:366
  64.7 4.9 %collective-permute-start.8 = (f32[16,256]{1,0:T(8,128)S(1)}, f32[16,256]{1,0:T(8,128)S(1)}, u32[]{:S(2)}, u32[]{:S(2)}) collective-permute-start(f32[16,256]{1,0:T(8,128)S(1)} %get-tuple-element.67), channel_id=1, source_target_pairs={{0,3},{1,0},{2,1},{3,2},{4,7},{5,4},{6,5},{7,6},{8,11},{9,8},{10,9... | collective-permute-start | bytes 49160 | tf_op jit(solution)/shard_map/ppermute | solution.py:366
  69.6 46.6 %copy-start.1 = (f32[256]{0:T(256)S(1)}, f32[256]{0:T(256)}, u32[]{:S(2)}) copy-start(f32[256]{0:T(256)} %param.6) | copy-start | bytes 3076
  71.9 11.0 %collective-permute-start.14 = (f32[272,256]{1,0:T(8,128)S(1)}, f32[272,256]{1,0:T(8,128)S(1)}, u32[]{:S(2)}, u32[]{:S(2)}) collective-permute-start(f32[272,256]{1,0:T(8,128)S(1)} %get-tuple-element.79.m0), channel_id=1, source_target_pairs={{0,3},{1,0},{2,1},{3,2},{4,7},{5,4},{6,5},{7,6},{8,11},{9,8},{10,9... | collective-permute-start | bytes 835592 | tf_op jit(solution)/shard_map/ppermute | solution.py:366
  74.5 8.9 %collective-permute-start.13 = (f32[272,256]{1,0:T(8,128)S(1)}, f32[272,256]{1,0:T(8,128)S(1)}, u32[]{:S(2)}, u32[]{:S(2)}) collective-permute-start(f32[272,256]{1,0:T(8,128)S(1)} %get-tuple-element.79.m0), channel_id=1, source_target_pairs={{0,2},{1,3},{2,0},{3,1},{4,6},{5,7},{6,4},{7,5},{8,10},{9,11},{10,... | collective-permute-start | bytes 835592 | tf_op jit(solution)/shard_map/ppermute | solution.py:366
  74.8 11.5 %collective-permute-start.12 = (f32[272,256]{1,0:T(8,128)S(1)}, f32[272,256]{1,0:T(8,128)S(1)}, u32[]{:S(2)}, u32[]{:S(2)}) collective-permute-start(f32[272,256]{1,0:T(8,128)S(1)} %get-tuple-element.79.m0), channel_id=1, source_target_pairs={{0,1},{1,2},{2,3},{3,0},{4,5},{5,6},{6,7},{7,4},{8,9},{9,10},{10,1... | collective-permute-start | bytes 835592 | tf_op jit(solution)/shard_map/ppermute | solution.py:366
  87.8 1.6 %collective-permute-start.15 = (f32[272,256]{1,0:T(8,128)S(1)}, f32[272,256]{1,0:T(8,128)S(1)}, u32[]{:S(2)}, u32[]{:S(2)}) collective-permute-start(f32[272,256]{1,0:T(8,128)S(1)} %get-tuple-element.80.own), channel_id=1, source_target_pairs={{0,4},{4,0},{8,12},{12,8},{16,20},{20,16},{24,28},{28,24},{32,36},... | collective-permute-start | bytes 835592 | tf_op jit(solution)/shard_map/ppermute | solution.py:431
  90.3 8.5 %collective-permute-start.16 = (f32[272,256]{1,0:T(8,128)S(1)}, f32[272,256]{1,0:T(8,128)S(1)}, u32[]{:S(2)}, u32[]{:S(2)}) collective-permute-start(f32[272,256]{1,0:T(8,128)S(1)} %get-tuple-element.82.own), channel_id=1, source_target_pairs={{0,8},{4,28},{8,16},{12,4},{16,24},{20,12},{24,0},{28,20},{32,40},... | collective-permute-start | bytes 835592 | tf_op jit(solution)/shard_map/ppermute | solution.py:435
  91.9 10.4 %collective-permute-start.18 = (f32[136,256]{1,0:T(8,128)S(1)}, f32[136,256]{1,0:T(8,128)S(1)}, u32[]{:S(2)}, u32[]{:S(2)}) collective-permute-start(f32[136,256]{1,0:T(8,128)S(1)} %get-tuple-element.83), channel_id=1, source_target_pairs={{0,16},{4,20},{8,24},{12,28},{16,0},{20,4},{24,8},{28,12},{32,48},... | collective-permute-start | bytes 417800 | tf_op jit(solution)/shard_map/ppermute | solution.py:435
  98.8 4.9 %collective-permute-start.17 = (f32[272,256]{1,0:T(8,128)S(1)}, f32[272,256]{1,0:T(8,128)S(1)}, u32[]{:S(2)}, u32[]{:S(2)}) collective-permute-start(f32[272,256]{1,0:T(8,128)S(1)} %collective-permute-done.16.n), channel_id=1, source_target_pairs={{0,4},{4,0},{8,12},{12,8},{16,20},{20,16},{24,28},{28,24},{32,36},... | collective-permute-start | bytes 835592 | tf_op jit(solution)/shard_map/ppermute | solution.py:431
  102.3 1.4 %collective-permute-start.19 = (f32[136,256]{1,0:T(8,128)S(1)}, f32[136,256]{1,0:T(8,128)S(1)}, u32[]{:S(2)}, u32[]{:S(2)}) collective-permute-start(f32[136,256]{1,0:T(8,128)S(1)} %collective-permute-done.18.f), channel_id=1, source_target_pairs={{0,4},{4,0},{8,12},{12,8},{16,20},{20,16},{24,28},{28,24},{32,36},... | collective-permute-start | bytes 417800 | tf_op jit(solution)/shard_map/ppermute | solution.py:431
  105.0 8.1 %collective-permute-start.20 = (f32[272,256]{1,0:T(8,128)S(1)}, f32[272,256]{1,0:T(8,128)S(1)}, u32[]{:S(2)}, u32[]{:S(2)}) collective-permute-start(f32[272,256]{1,0:T(8,128)S(1)} %get-tuple-element.84), channel_id=1, source_target_pairs={{0,32},{4,100},{8,40},{12,108},{16,48},{20,116},{24,56},{28,124},{... | collective-permute-start | bytes 835592 | tf_op jit(solution)/shard_map/ppermute | solution.py:435
  105.5 9.3 %collective-permute-start.22 = (f32[136,256]{1,0:T(8,128)S(1)}, f32[136,256]{1,0:T(8,128)S(1)}, u32[]{:S(2)}, u32[]{:S(2)}) collective-permute-start(f32[136,256]{1,0:T(8,128)S(1)} %get-tuple-element.85), channel_id=1, source_target_pairs={{0,64},{4,68},{8,72},{12,76},{16,80},{20,84},{24,88},{28,92},{32,9... | collective-permute-start | bytes 417800 | tf_op jit(solution)/shard_map/ppermute | solution.py:435
  113.1 3.1 %collective-permute-start.21 = (f32[272,256]{1,0:T(8,128)S(1)}, f32[272,256]{1,0:T(8,128)S(1)}, u32[]{:S(2)}, u32[]{:S(2)}) collective-permute-start(f32[272,256]{1,0:T(8,128)S(1)} %collective-permute-done.20.n), channel_id=1, source_target_pairs={{0,4},{4,0},{8,12},{12,8},{16,20},{20,16},{24,28},{28,24},{32,36},... | collective-permute-start | bytes 835592 | tf_op jit(solution)/shard_map/ppermute | solution.py:431
  114.8 1.4 %collective-permute-start.23 = (f32[136,256]{1,0:T(8,128)S(1)}, f32[136,256]{1,0:T(8,128)S(1)}, u32[]{:S(2)}, u32[]{:S(2)}) collective-permute-start(f32[136,256]{1,0:T(8,128)S(1)} %collective-permute-done.22.f), channel_id=1, source_target_pairs={{0,4},{4,0},{8,12},{12,8},{16,20},{20,16},{24,28},{28,24},{32,36},... | collective-permute-start | bytes 417800 | tf_op jit(solution)/shard_map/ppermute | solution.py:431
  118.4 4.9 %collective-permute-start.24 = (f32[16,64]{1,0:T(8,128)S(1)}, f32[16,64]{1,0:T(8,128)S(1)}, u32[]{:S(2)}, u32[]{:S(2)}) collective-permute-start(f32[16,64]{1,0:T(8,128)S(1)} %get-tuple-element.90), channel_id=1, source_target_pairs={{0,1},{1,2},{2,3},{3,0},{4,5},{5,6},{6,7},{7,4},{8,9},{9,10},{10,1... | collective-permute-start | bytes 12296 | tf_op jit(solution)/shard_map/ppermute | solution.py:366
  118.5 5.2 %collective-permute-start.25 = (f32[16,64]{1,0:T(8,128)S(1)}, f32[16,64]{1,0:T(8,128)S(1)}, u32[]{:S(2)}, u32[]{:S(2)}) collective-permute-start(f32[16,64]{1,0:T(8,128)S(1)} %get-tuple-element.91), channel_id=1, source_target_pairs={{0,2},{1,3},{2,0},{3,1},{4,6},{5,7},{6,4},{7,5},{8,10},{9,11},{10,... | collective-permute-start | bytes 12296 | tf_op jit(solution)/shard_map/ppermute | solution.py:366
  120.9 3.7 %collective-permute-start.26 = (f32[16,64]{1,0:T(8,128)S(1)}, f32[16,64]{1,0:T(8,128)S(1)}, u32[]{:S(2)}, u32[]{:S(2)}) collective-permute-start(f32[16,64]{1,0:T(8,128)S(1)} %get-tuple-element.92), channel_id=1, source_target_pairs={{0,3},{1,0},{2,1},{3,2},{4,7},{5,4},{6,5},{7,6},{8,11},{9,8},{10,9... | collective-permute-start | bytes 12296 | tf_op jit(solution)/shard_map/ppermute | solution.py:366

commit v8 on v6

--- a/solution.py
+++ b/solution.py
@@ -17,7 +17,7 @@
 HALF = R // 2
 ROWS = 4
 SUB = 16
-CHUNKS = ((4, 4, 4), (2, 2))
+CHUNKS = ((5, 5), (3, 3))
 SEGS = tuple(n for chunk in CHUNKS for n in chunk)
 SIZES = tuple(sum(chunk) for chunk in CHUNKS)
 ENDS = tuple(sum(SEGS[: i + 1]) for i in range(len(SEGS)))
@@ -129,14 +129,21 @@
     return pltpu.make_async_copy(flat.at[pl.ds(pl.multiple_of(z * (SUB * 64) + start * 64, 64), own.shape[0])], own, sem)
 
 
-def assemble(z, parts, ah, al, own=None):
-    for d in (1, 2, 3, 0):
+def assemble(z, first, prev, after, opposite, own, copy, ah, al):
+    n = ah.shape[0]
+    for d in (1, 3, 2, 0):
         slot = lax.rem(z - d + ROWS, ROWS)
         rows = pl.ds(pl.multiple_of(slot * 64, 64), 64)
         if d == 0:
-            own.wait()
-        for k in range(ah.shape[0]):
-            hi, lo = split(parts[d][k * 64 : (k + 1) * 64, :])
+            copy.wait()
+        for k in range(n):
+            ref, at = {
+                0: (own, k),
+                1: (prev, first + k),
+                2: (opposite[2 * k // n], k % (n // 2)),
+                3: (after, first + k),
+            }[d]
+            hi, lo = split(ref[at * 64 : (at + 1) * 64, :])
             ah[k, rows, :] = hi
             al[k, rows, :] = lo
 
@@ -161,30 +168,26 @@
                 pref[k] = by_step(pref[k - 1], ah[k], al[k])
 
 
-def first_kernel(idx, flat, gains, a1, a2, a3, pref, ah, al, tail, staged, own, sems):
+def first_kernel(idx, flat, prev, after, q1, q2, pref, ah, al, tail, own, sem):
     z = idx[Z]
-    late = pltpu.make_async_copy(gains, staged, sems.at[1])
-    copy = own_copy(z, flat, own, 0, sems.at[0])
+    copy = own_copy(z, flat, own, 0, sem)
     copy.start()
-    late.start()
-    assemble(z, (own, a1, a2, a3), ah, al, copy)
+    assemble(z, 0, prev, after, (q1, q2), own, copy, ah, al)
     chains(CHUNKS[0], ah, al, pref)
-    tail[0] = mm(pref[ENDS[1] - 1], pref[ENDS[2] - 1])
-    tail[1] = mm(pref[ENDS[0] - 1], tail[0])
-    late.wait()
-
-
-def second_kernel(idx, flat, a1, a2, a3, tail, pref, ah, al, last, own, sem):
+    tail[...] = mm(pref[ENDS[0] - 1], pref[ENDS[1] - 1])
+
+
+def second_kernel(idx, flat, prev, after, q1, q2, tail, pref, ah, al, last, own, sem):
     z = idx[Z]
     copy = own_copy(z, flat, own, SIZES[0], sem)
     copy.start()
-    assemble(z, (own, a1, a2, a3), ah, al, copy)
+    assemble(z, SIZES[0], prev, after, (q1, q2), own, copy, ah, al)
     chains(CHUNKS[1], ah, al, pref)
     last[0] = mm(pref[CHUNKS[1][0] - 1], pref[SIZES[1] - 1])
-    last[1] = mm(tail[1], last[0])
-
-
-def third_kernel(idx, b0, b1, b2, b3, p01, ah01, al01, tail, p23, ah23, al23, last, shifts, whole, b_s):
+    last[1] = mm(tail[...], last[0])
+
+
+def third_kernel(idx, b0, b1, b2, b3, p01, ah01, al01, p23, ah23, al23, last, shifts, whole, b_s):
     z = idx[Z]
     for d, b in enumerate((b0, b1, b2, b3)):
         b_s[lax.rem(z - d + ROWS, ROWS)] = b[...]
@@ -207,8 +210,8 @@
             h, l, i = mats[k]
             p[c] = by_step(p[c], h[i], l[i]) + row(k)
             shifts[k : k + 1, :] = p[c][:1]
-    v = mm(p[0], tail[0]) + mm(p[1], p01[SIZES[0] - 1]) + p[2]
-    v = mm(v, last[0]) + (mm(p[3], p23[SIZES[1] - 1]) + p[4])
+    v = mm(p[0], p01[SIZES[0] - 1]) + p[1]
+    v = mm(v, last[0]) + (mm(p[2], p23[SIZES[1] - 1]) + p[3])
     whole[:N, :] = last[1]
     whole[N:, :] = v
 
@@ -244,22 +247,31 @@
     return pl.ds(pl.multiple_of(c * HALF, 8), HALF)
 
 
-def join_halves(pos, c, mine, others, m_s):
-    for d, (m, o) in enumerate(zip(mine, others)):
-        slot = lax.rem(pos - d + 3, 4)
-        m_s[slot, half_rows(c), :] = m[...]
-        m_s[slot, half_rows(1 - c), :] = o[...]
-
-
-def halves_kernel(idx, own, h1, h2, h3, o1, o2, o3, half, before, m_s):
+def join(pos, c, mine, rest, far, o_mine, o_rest, o_far, m_s):
+    mine_at, other_at = half_rows(c), half_rows(1 - c)
+    near_slot, other_slot, far_slot = lax.rem(pos + 3 + 2 * c, 4), lax.rem(pos + 5 - 2 * c, 4), lax.rem(pos + 2, 4)
+    m_s[near_slot, mine_at, :] = mine[...]
+    m_s[near_slot, other_at, :] = rest[...]
+    m_s[other_slot, other_at, :] = o_mine[...]
+    m_s[other_slot, mine_at, :] = o_rest[...]
+    m_s[far_slot, mine_at, :] = far[...]
+    m_s[far_slot, other_at, :] = o_far[...]
+
+
+def halve(c, whole, mine, rest):
+    mine[...] = whole[half_rows(c), :]
+    rest[...] = whole[half_rows(1 - c), :]
+
+
+def plane_kernel(idx, own, n0, n1, n2, o0, o1, o2, mine, rest, before, m_s, all_s):
     pos, c = idx[Y], idx[C]
     m_s[pos] = own[...]
-    join_halves(pos, c, (h1, h2, h3), (o1, o2, o3), m_s)
-    m_s[4] = combine(pos, m_s, before)
-    half[...] = m_s[4, half_rows(c), :]
-
-
-def pair_kernel(idx, own, other, before_in, total, half, before):
+    join(pos, c, n0, n1, n2, o0, o1, o2, m_s)
+    all_s[...] = combine(pos, m_s, before)
+    halve(c, all_s, mine, rest)
+
+
+def pair_kernel(idx, own, other, before_in, total, mine, rest, before):
     c = idx[C]
     swap = c == 1
 
@@ -273,7 +285,7 @@
         total[...] = then(own[...], other[...])
         before[...] = before_in[...]
 
-    half[...] = total[half_rows(c), :]
+    halve(c, total, mine, rest)
 
 
 def fold_kernel(idx, first, second, out):
@@ -281,10 +293,10 @@
 
 
 def states_kernel(
-    idx, prior, h1, h2, h3, g1, g2, g3, before, p01, p23, shifts, o0, o1, o2, o3, st_s, m_s, s_s
+    idx, prior, n0, n1, n2, g0, g1, g2, before, p01, p23, shifts, o0, o1, o2, o3, st_s, m_s, s_s
 ):
     z, pos = idx[Z], idx[X]
-    join_halves(pos, idx[C], (h1, h2, h3), (g1, g2, g3), m_s)
+    join(pos, idx[C], n0, n1, n2, g0, g1, g2, m_s)
     s_s[...] = jnp.where(lax.broadcasted_iota(jnp.int32, (PAD, N), 0) == 0, prior[...], 0.0)
     for i in range(3):
 
@@ -310,29 +322,49 @@
         o[...] = st_s[lax.rem(z + d, ROWS)]
 
 
-def send_copies(z, flat, outs, start, count, sems):
+RELAYED = tuple(
+    [(sum(SIZES[:i]) + w * n // 2, n // 2) for i, n in enumerate(SIZES)] for w in range(2)
+)
+SENT = SUB + SUB // 2
+
+
+def send_kernel(idx, flat, ahead, back, sems):
+    z = idx[Z]
     copies = []
-    for d, o in enumerate(outs, 1):
-        at = lax.rem(z + d, ROWS) * (SUB * 64) + start * 64
-        source = flat.at[pl.ds(pl.multiple_of(at, 64), count * 64)]
-        copies.append(pltpu.make_async_copy(source, o.at[pl.ds(0, count * 64)], sems.at[d - 1]))
+    for way, out in enumerate((ahead, back)):
+        at = 0
+        for d, first, count in [((1, 3)[way], 0, SUB)] + [(2, *r) for r in RELAYED[way]]:
+            source = lax.rem(z + d, ROWS) * (SUB * 64) + first * 64
+            copies.append(
+                pltpu.make_async_copy(
+                    flat.at[pl.ds(pl.multiple_of(source, 64), count * 64)],
+                    out.at[pl.ds(at * 64, count * 64)],
+                    sems.at[len(copies)],
+                )
+            )
+            at += count
     for copy in copies:
         copy.start()
-    return copies
-
-
-def send_a_kernel(idx, flat, o1, o2, o3, sems):
-    for copy in send_copies(idx[Z], flat, (o1, o2, o3), 0, SIZES[0], sems):
+    for copy in copies:
         copy.wait()
+
+
+def relay_kernel(idx, prev, after, p1, a1, p2, a2):
+    cut = SUB + RELAYED[0][0][1]
+    p1[...] = prev[SUB * 64 : cut * 64, :]
+    a1[...] = after[SUB * 64 : cut * 64, :]
+    p2[...] = prev[cut * 64 :, :]
+    a2[...] = after[cut * 64 :, :]
+
+
+def stage_kernel(idx, gains, info, staged, sem):
+    copy = pltpu.make_async_copy(gains, staged, sem)
+    copy.start()
+    copy.wait()
 
 
 def sum_kernel(idx, sums, info):
     info[...] = jnp.sum(sums[...], axis=0)
-
-
-def send_b_kernel(idx, flat, o1, o2, o3, sems):
-    for copy in send_copies(idx[Z], flat, (o1, o2, o3), SIZES[0], SIZES[1], sems):
-        copy.wait()
 
 
 def offset_kernel(idx, g, i0, r1, r2, r3, o0, o1, o2, o3, info_s, off_s):
@@ -370,28 +402,32 @@
     idx = jnp.stack([z, tm & 1, (tm >> 1) & 3, tm >> 3])
     prior = prior.reshape(1, N)
     flat = dynamics.reshape(ROWS * SUB * 64, N)
-    dma3 = pltpu.SemaphoreType.DMA((3,))
 
     def along_rows(blocks):
         return [along_row(b, d) for d, b in enumerate(blocks, 1)]
 
-    part_a = along_rows(call(send_a_kernel, [(SIZES[0] * 64, N)] * 3, idx, (), [dma3], far=(flat,)))
+    ahead, back = call(
+        send_kernel, [(SENT * 64, N)] * 2, idx, (), [pltpu.SemaphoreType.DMA((6,))], far=(flat,)
+    )
+    prev, after = along_row(ahead, 1), along_row(back, 3)
 
     rid = owner[:, 0] * 16 + step % 16 + 512 * (step // 16)
     partial = binned(rid.reshape(1, -1), observed.T)
     sums = lax.all_to_all(partial, "tm", 0, 0, tiled=True).reshape(32, 16, N)
     (info,) = call(sum_kernel, [(16, N)], idx, (sums,))
     infos = along_rows([info] * 3)
-    sent_b = call(send_b_kernel, [(SIZES[1] * 64, N)] * 3, idx, (), [dma3], far=(flat,))
-    infos, sent_b, part_a, idx, prior = lax.optimization_barrier((infos, sent_b, part_a, idx, prior))
-    part_b = along_rows(sent_b)
-    p01, ah01, al01, tail, staged = call(
+    (staged,) = call(stage_kernel, [gains.shape], idx, (info,), [pltpu.SemaphoreType.DMA], far=(gains,))
+    infos, staged, prev, after, idx, prior = lax.optimization_barrier((infos, staged, prev, after, idx, prior))
+    pieces = call(relay_kernel, [(n * 64, N) for n in (5, 5, 3, 3)], idx, (prev, after))
+    pieces, infos = lax.optimization_barrier((pieces, infos))
+    relayed = [along_row(p, d) for p, d in zip(pieces, (1, 3, 1, 3))]
+    p01, ah01, al01, tail = call(
         first_kernel,
-        [(SIZES[0], N, N), ((SIZES[0], N, N), BF16), ((SIZES[0], N, N), BF16), (2, N, N), gains.shape],
-        idx,
-        part_a,
-        [pltpu.VMEM((SIZES[0] * 64, N), F32), pltpu.SemaphoreType.DMA((2,))],
-        far=(flat, gains),
+        [(SIZES[0], N, N), ((SIZES[0], N, N), BF16), ((SIZES[0], N, N), BF16), (N, N)],
+        idx,
+        (prev, after, *relayed[:2]),
+        [pltpu.VMEM((SIZES[0] * 64, N), F32), pltpu.SemaphoreType.DMA],
+        far=(flat,),
     )
     offs = call(
         offset_kernel,
@@ -405,7 +441,7 @@
         second_kernel,
         [(SIZES[1], N, N), ((SIZES[1], N, N), BF16), ((SIZES[1], N, N), BF16), (2, N, N)],
         idx,
-        (*part_b, tail),
+        (prev, after, *relayed[2:], tail),
         [pltpu.VMEM((SIZES[1] * 64, N), F32), pltpu.SemaphoreType.DMA],
         far=(flat,),
     )
@@ -413,7 +449,7 @@
         third_kernel,
         [(SUB, N), (R, N)],
         idx,
-        (*offs, p01, ah01, al01, tail, p23, ah23, al23, last),
+        (*offs, p01, ah01, al01, p23, ah23, al23, last),
         [pltpu.VMEM((ROWS, 16, N), F32)],
     )
 
@@ -428,28 +464,31 @@
     def other_core(m):
         return lax.ppermute(m, "tm", [(i, i ^ 1) for i in range(32)])
 
-    def along_tm(m, d, n, stride):
-        places = [(i, i - i % (n * stride) + (i + d * stride) % (n * stride)) for i in range(32)]
-        return lax.ppermute(m, "tm", places)
-
-    column, half, before = call(
-        pair_kernel, [(R, N), (HALF, N), (R, N)], idx, (block, other_core(block), before)
-    )
-    halves = [along_tm(half, d, 4, 2) for d in (1, 2, 3)]
-    half, ybefore = call(
-        halves_kernel,
-        [(HALF, N), (R, N)],
-        idx,
-        (column, *halves, *[other_core(h) for h in halves]),
-        [pltpu.VMEM((5, R, N), F32)],
-    )
-    halves = [along_tm(half, d, 4, 8) for d in (1, 2, 3)]
+    def along_tm(m, stride, moves):
+        n = 4 * stride
+        return lax.ppermute(m, "tm", [(i, i - i % n + (i + moves[i % 2] * stride) % n) for i in range(32)])
+
+    def gathered(mine, rest, stride):
+        near_mine = along_tm(mine, stride, (1, 3))
+        got = near_mine, along_tm(rest, stride, (1, 3)), along_tm(near_mine, stride, (1, 3))
+        return *got, *[other_core(g) for g in got]
+
+    column, *halves, before = call(
+        pair_kernel, [(R, N), (HALF, N), (HALF, N), (R, N)], idx, (block, other_core(block), before)
+    )
+    *halves, ybefore = call(
+        plane_kernel,
+        [(HALF, N), (HALF, N), (R, N)],
+        idx,
+        (column, *gathered(*halves, 2)),
+        [pltpu.VMEM((4, R, N), F32), pltpu.VMEM((R, N), F32)],
+    )
     (before,) = call(fold_kernel, [(R, N)], idx, (ybefore, before))
     outs = call(
         states_kernel,
         [(SUB, 64)] * 4,
         idx,
-        (prior, *halves, *[other_core(h) for h in halves], before, p01, p23, shifts),
+        (prior, *gathered(*halves, 8), before, p01, p23, shifts),
         [pltpu.VMEM((ROWS, SUB, 64), F32), pltpu.VMEM((4, R, N), F32), pltpu.VMEM((PAD, N), F32)],
     )
     got = [outs[0], *along_rows(outs[1:])]

time: 128 us -> 122 us (0.953)
  starting transfers between devices: 37 us -> 32.5 us
  waiting for transfers between devices: 42.3 us -> 38.3 us
  Pallas kernels: 29.8 us -> 31.5 us
    ppermute x18, starting transfers between devices: 27.6 us -> 22.8 us  [along_row(): return lax.ppermute(x, 'row', [(i, (i + d) % ROWS) for i in range(ROWS)])]
    ppermute x18, waiting for transfers between devices: 24.5 us -> 21.7 us  [along_row(): return lax.ppermute(x, 'row', [(i, (i + d) % ROWS) for i in range(ROWS)])]
    pallas_call x12 -> x13, Pallas kernels: 21.7 us -> 23.5 us  [call(): pl.pallas_call(kernel, out_shape=[pltpu.VMEM(s, t) for s, t in outs], in_...]
    ppermute x7, starting transfers between devices: 0.63 us -> 2.35 us  [other_core(): return lax.ppermute(m, 'tm', [(i, i ^ 1) for i in range(32)])]
    ppermute x6, starting transfers between devices: 8.79 us -> 7.37 us  [along_tm(): lax.ppermute(m, 'tm', [(i, i - i % n + (i + moves[i % 2] * stride) % n) f...]
  transfers between devices with their start and end apart: 31 -> 31, of which waited for: 17 -> 16; matrix products, arithmetic and copies ran while one was open for 0% -> 0% of each run, Pallas kernels for 14% -> 16%
where the time goes in v8:
time: 122 us; the launch traced here: 119 us
  waiting for transfers between devices  38.3 us (31%)
  starting transfers between devices  32.5 us (27%)
  Pallas kernels  31.5 us (26%)
  blocking collectives  16.7 us (14%)
    pallas_call x13, Pallas kernels, call(): pl.pallas_call(kernel, out_shape=[pltpu.VMEM(s, t) for s, t in outs], in_...  23.5 us
    ppermute x18, starting transfers between devices, along_row(): return lax.ppermute(x, 'row', [(i, (i + d) % ROWS) for i in range(ROWS)])  22.8 us
    ppermute x18, waiting for transfers between devices, along_row(): return lax.ppermute(x, 'row', [(i, (i + d) % ROWS) for i in range(ROWS)])  21.7 us
    all_to_all x1, blocking collectives, shards(): sums = lax.all_to_all(partial, 'tm', 0, 0, tiled=True).reshape(32, 16, N)  16.7 us
    ppermute x6, waiting for transfers between devices, along_tm(): lax.ppermute(m, 'tm', [(i, i - i % n + (i + moves[i % 2] * stride) % n) f...  13.4 us
    ppermute x6, starting transfers between devices, along_tm(): lax.ppermute(m, 'tm', [(i, i - i % n + (i + moves[i % 2] * stride) % n) f...  7.37 us
    pallas_call x1, Pallas kernels, binned(): pl.pallas_call(bin_kernel, out_shape=jax.ShapeDtypeStruct((n_bins // 4, N...  6.9 us
    ppermute x7, waiting for transfers between devices, other_core(): return lax.ppermute(m, 'tm', [(i, i ^ 1) for i in range(32)])  3.14 us
  transfers between devices with their start and end apart: 31, of which 16 were waited for; matrix products, arithmetic and copies ran while one was open for 0% of the time, Pallas kernels for 16%

profile of v8, /device:TPU:6, one launch (start us, length us, event | category | flops | bytes accessed | tf_op | source)
XLA Modules:
  0.0 119.4 jit_solution(17934145548882131858)
XLA Ops:
  0.1 2.4 %shard_map.67 = (f32[1536,256]{1,0:T(8,128)S(1)}, f32[1536,256]{1,0:T(8,128)S(1)}) custom-call(s32[4]{0:T(128)S(1)} %pad_add_fusion.idx, f32[4096,256]{1,0:T(8,128)} %bitcast.14), custom_call_target="tpu_custom_call" | custom-call | tf_op jit(solution)/shard_map/pallas_call | solution.py:69
  2.5 2.0 %collective-permute-start.3 = (f32[1536,256]{1,0:T(8,128)S(1)}, f32[1536,256]{1,0:T(8,128)S(1)}, u32[]{:S(2)}, u32[]{:S(2)}) collective-permute-start(f32[1536,256]{1,0:T(8,128)S(1)} %get-tuple-element.53), channel_id=1, source_target_pairs={{0,1},{1,2},{2,3},{3,0},{4,5},{5,6},{6,7},{7,4},{8,9},{9,10},{10,1... | collective-permute-start | bytes 4718600 | tf_op jit(solution)/shard_map/ppermute | solution.py:396
  4.5 2.2 %collective-permute-start.4 = (f32[1536,256]{1,0:T(8,128)S(1)}, f32[1536,256]{1,0:T(8,128)S(1)}, u32[]{:S(2)}, u32[]{:S(2)}) collective-permute-start(f32[1536,256]{1,0:T(8,128)S(1)} %get-tuple-element.54), channel_id=1, source_target_pairs={{0,3},{1,0},{2,1},{3,2},{4,7},{5,4},{6,5},{7,6},{8,11},{9,8},{10,9... | collective-permute-start | bytes 4718600 | tf_op jit(solution)/shard_map/ppermute | solution.py:396
  6.8 6.9 %shard_map.64 = f32[512,256]{1,0:T(8,128)S(1)} custom-call(s32[1,4096]{1,0:T(1,128)S(1)} %bitcast.12, f32[64,4096]{1,0:T(8,128)S(1)} %bitcast.11), custom_call_target="tpu_custom_call" | custom-call | tf_op jit(solution)/shard_map/pallas_call | solution.py:114
  13.7 16.7 %all_to_all.9.sums = f32[32,16,256]{2,1,0:T(8,128)S(1)} all-to-all(f32[32,16,256]{2,1,0:T(8,128)S(1)} %bitcast.10), channel_id=1, replica_groups=mesh['tm'=32,'row'=4] {'tm'}, dimensions={0} | all-to-all | bytes 1048576 | tf_op jit(solution)/shard_map/all_to_all | solution.py:416
  31.0 2.0 %collective-permute-start.2 = (f32[16,256]{1,0:T(8,128)S(1)}, f32[16,256]{1,0:T(8,128)S(1)}, u32[]{:S(2)}, u32[]{:S(2)}) collective-permute-start(f32[16,256]{1,0:T(8,128)S(1)} %shard_map.65.info.i0), channel_id=1, source_target_pairs={{0,3},{1,0},{2,1},{3,2},{4,7},{5,4},{6,5},{7,6},{8,11},{9,8},{10,9... | collective-permute-start | bytes 49160 | tf_op jit(solution)/shard_map/ppermute | solution.py:396
  34.2 2.7 %shard_map.66.g = f32[64,64,256]{2,1,0:T(8,128)S(1)} custom-call(s32[4]{0:T(128)S(1)} %pad_add_fusion.idx, f32[64,64,256]{2,1,0:T(8,128)} %gains.1, f32[16,256]{1,0:T(8,128)S(1)} %shard_map.65.info.i0), custom_call_target="tpu_custom_call" | custom-call | tf_op jit(solution)/shard_map/pallas_call | solution.py:69
  37.0 4.1 %collective-permute-done.2.r3 = f32[16,256]{1,0:T(8,128)S(1)} collective-permute-done((f32[16,256]{1,0:T(8,128)S(1)}, f32[16,256]{1,0:T(8,128)S(1)}, u32[]{:S(2)}, u32[]{:S(2)}) %collective-permute-start.2) | collective-permute-done | bytes 16416 | tf_op jit(solution)/shard_map/ppermute | solution.py:396
  41.1 1.6 %collective-permute-done.1.r2 = f32[16,256]{1,0:T(8,128)S(1)} collective-permute-done((f32[16,256]{1,0:T(8,128)S(1)}, f32[16,256]{1,0:T(8,128)S(1)}, u32[]{:S(2)}, u32[]{:S(2)}) %collective-permute-start.1) | collective-permute-done | bytes 16416 | tf_op jit(solution)/shard_map/ppermute | solution.py:396
  44.7 1.9 %collective-permute-start.9 = (f32[320,256]{1,0:T(8,128)S(1)}, f32[320,256]{1,0:T(8,128)S(1)}, u32[]{:S(2)}, u32[]{:S(2)}) collective-permute-start(f32[320,256]{1,0:T(8,128)S(1)} %get-tuple-element.75), channel_id=1, source_target_pairs={{0,3},{1,0},{2,1},{3,2},{4,7},{5,4},{6,5},{7,6},{8,11},{9,8},{10,9... | collective-permute-start | bytes 983048 | tf_op jit(solution)/shard_map/ppermute | solution.py:396
  46.8 3.1 %collective-permute-start.11 = (f32[192,256]{1,0:T(8,128)S(1)}, f32[192,256]{1,0:T(8,128)S(1)}, u32[]{:S(2)}, u32[]{:S(2)}) collective-permute-start(f32[192,256]{1,0:T(8,128)S(1)} %get-tuple-element.80), channel_id=1, source_target_pairs={{0,3},{1,0},{2,1},{3,2},{4,7},{5,4},{6,5},{7,6},{8,11},{9,8},{10,9... | collective-permute-start | bytes 589832 | tf_op jit(solution)/shard_map/ppermute | solution.py:396
  49.9 1.6 %shard_map.69 = (f32[16,256]{1,0:T(8,128)S(1)}, f32[16,256]{1,0:T(8,128)S(1)}, f32[16,256]{1,0:T(8,128)S(1)}, f32[16,256]{1,0:T(8,128)S(1)}) custom-call(s32[4]{0:T(128)S(1)} %pad_add_fusion.idx, f32[64,64,256]{2,1,0:T(8,128)S(1)} %shard_map.66.g, f32[16,256]{1,0:T(8,128)S(1)} %shard_map.65.info.i0, f32[16,256]{1,0:T(8,128)S(1)} %collective-permute-done.r1, ...), custom_call_target="tpu_custom_call" | custom-call | tf_op jit(solution)/shard_map/pallas_call | solution.py:69
  51.5 3.5 %collective-permute-done.8.q1 = f32[320,256]{1,0:T(8,128)S(1)} collective-permute-done((f32[320,256]{1,0:T(8,128)S(1)}, f32[320,256]{1,0:T(8,128)S(1)}, u32[]{:S(2)}, u32[]{:S(2)}) %collective-permute-start.8) | collective-permute-done | bytes 327712 | tf_op jit(solution)/shard_map/ppermute | solution.py:396
  55.5 2.6 %collective-permute-start.7 = (f32[16,256]{1,0:T(8,128)S(1)}, f32[16,256]{1,0:T(8,128)S(1)}, u32[]{:S(2)}, u32[]{:S(2)}) collective-permute-start(f32[16,256]{1,0:T(8,128)S(1)} %get-tuple-element.73), channel_id=1, source_target_pairs={{0,3},{1,0},{2,1},{3,2},{4,7},{5,4},{6,5},{7,6},{8,11},{9,8},{10,9... | collective-permute-start | bytes 49160 | tf_op jit(solution)/shard_map/ppermute | solution.py:396
  58.1 3.4 %shard_map.70 = (f32[10,256,256]{2,1,0:T(8,128)S(1)}, bf16[10,256,256]{2,1,0:T(8,128)(2,1)S(1)}, bf16[10,256,256]{2,1,0:T(8,128)(2,1)S(1)}, f32[256,256]{1,0:T(8,128)S(1)}) custom-call(s32[4]{0:T(128)S(1)} %pad_add_fusion.idx, f32[4096,256]{1,0:T(8,128)} %bitcast.15, f32[1536,256]{1,0:T(8,128)S(1)} %collective-permute-done.3.prev, ...), custom_call_target="tpu_custom_call" | custom-call | tf_op jit(solution)/shard_map/pallas_call | solution.py:69
  61.6 3.1 %shard_map.71 = (f32[6,256,256]{2,1,0:T(8,128)S(1)}, bf16[6,256,256]{2,1,0:T(8,128)(2,1)S(1)}, bf16[6,256,256]{2,1,0:T(8,128)(2,1)S(1)}, f32[2,256,256]{2,1,0:T(8,128)S(1)}) custom-call(s32[4]{0:T(128)S(1)} %pad_add_fusion.idx, f32[4096,256]{1,0:T(8,128)} %bitcast.16, f32[1536,256]{1,0:T(8,128)S(1)} %collective-permute-done.3.prev, ...), custom_call_target="tpu_custom_call" | custom-call | tf_op jit(solution)/shard_map/pallas_call | solution.py:69
  64.8 2.3 %shard_map.72 = (f32[16,256]{1,0:T(8,128)S(1)}, f32[272,256]{1,0:T(8,128)S(1)}) custom-call(s32[4]{0:T(128)S(1)} %pad_add_fusion.idx, f32[16,256]{1,0:T(8,128)S(1)} %get-tuple-element.70.b0, f32[16,256]{1,0:T(8,128)S(1)} %collective-permute-done.5.b1, f32[16,256]{1,0:T(8,128)S(1)} %collective-permute-done.6.b2, f32[16,256]{1,0:T(8,128)S(1)} %collective-permute-done.7.b3, ...), custom_call_target="tpu_custom_call" | custom-call | tf_op jit(solution)/shard_map/pallas_call | solution.py:69
  69.4 4.2 %collective-permute-done.14.m3 = f32[272,256]{1,0:T(8,128)S(1)} collective-permute-done((f32[272,256]{1,0:T(8,128)S(1)}, f32[272,256]{1,0:T(8,128)S(1)}, u32[]{:S(2)}, u32[]{:S(2)}) %collective-permute-start.14) | collective-permute-done | bytes 278560 | tf_op jit(solution)/shard_map/ppermute | solution.py:396
  73.6 2.6 %collective-permute-done.13.m2 = f32[272,256]{1,0:T(8,128)S(1)} collective-permute-done((f32[272,256]{1,0:T(8,128)S(1)}, f32[272,256]{1,0:T(8,128)S(1)}, u32[]{:S(2)}, u32[]{:S(2)}) %collective-permute-start.13) | collective-permute-done | bytes 278560 | tf_op jit(solution)/shard_map/ppermute | solution.py:396
  76.2 2.9 %collective-permute-done.12.m1 = f32[272,256]{1,0:T(8,128)S(1)} collective-permute-done((f32[272,256]{1,0:T(8,128)S(1)}, f32[272,256]{1,0:T(8,128)S(1)}, u32[]{:S(2)}, u32[]{:S(2)}) %collective-permute-start.12) | collective-permute-done | bytes 278560 | tf_op jit(solution)/shard_map/ppermute | solution.py:396
  79.1 1.5 %shard_map.73 = (f32[272,256]{1,0:T(8,128)S(1)}, f32[272,256]{1,0:T(8,128)S(1)}) custom-call(s32[4]{0:T(128)S(1)} %pad_add_fusion.idx, f32[272,256]{1,0:T(8,128)S(1)} %get-tuple-element.86.m0, f32[272,256]{1,0:T(8,128)S(1)} %collective-permute-done.12.m1, f32[272,256]{1,0:T(8,128)S(1)} %collective-permute-done.13.m2, f32[272,256]{1,0:T(8,128)S(1)} %collective-permute-done.14.m3), custom_call_target="tpu_custom_call" | custom-call | tf_op jit(solution)/shard_map/pallas_call | solution.py:69
  80.7 1.5 %collective-permute-done.15.other = f32[272,256]{1,0:T(8,128)S(1)} collective-permute-done((f32[272,256]{1,0:T(8,128)S(1)}, f32[272,256]{1,0:T(8,128)S(1)}, u32[]{:S(2)}, u32[]{:S(2)}) %collective-permute-start.15) | collective-permute-done | bytes 278560 | tf_op jit(solution)/shard_map/ppermute | solution.py:465
  83.1 1.6 %collective-permute-start.16 = (f32[136,256]{1,0:T(8,128)S(1)}, f32[136,256]{1,0:T(8,128)S(1)}, u32[]{:S(2)}, u32[]{:S(2)}) collective-permute-start(f32[136,256]{1,0:T(8,128)S(1)} %get-tuple-element.90), channel_id=1, source_target_pairs={{0,8},{4,28},{8,16},{12,4},{16,24},{20,12},{24,0},{28,20},{32,40},... | collective-permute-start | bytes 417800 | tf_op jit(solution)/shard_map/ppermute | solution.py:469
  84.7 1.6 %collective-permute-start.17 = (f32[136,256]{1,0:T(8,128)S(1)}, f32[136,256]{1,0:T(8,128)S(1)}, u32[]{:S(2)}, u32[]{:S(2)}) collective-permute-start(f32[136,256]{1,0:T(8,128)S(1)} %get-tuple-element.91), channel_id=1, source_target_pairs={{0,8},{4,28},{8,16},{12,4},{16,24},{20,12},{24,0},{28,20},{32,40},... | collective-permute-start | bytes 417800 | tf_op jit(solution)/shard_map/ppermute | solution.py:469
  86.3 3.1 %collective-permute-done.16.n0 = f32[136,256]{1,0:T(8,128)S(1)} collective-permute-done((f32[136,256]{1,0:T(8,128)S(1)}, f32[136,256]{1,0:T(8,128)S(1)}, u32[]{:S(2)}, u32[]{:S(2)}) %collective-permute-start.16) | collective-permute-done | bytes 139296 | tf_op jit(solution)/shard_map/ppermute | solution.py:469
  91.3 4.4 %collective-permute-done.18.n2 = f32[136,256]{1,0:T(8,128)S(1)} collective-permute-done((f32[136,256]{1,0:T(8,128)S(1)}, f32[136,256]{1,0:T(8,128)S(1)}, u32[]{:S(2)}, u32[]{:S(2)}) %collective-permute-start.18) | collective-permute-done | bytes 139296 | tf_op jit(solution)/shard_map/ppermute | solution.py:469
  100.4 3.1 %collective-permute-done.22.n0 = f32[136,256]{1,0:T(8,128)S(1)} collective-permute-done((f32[136,256]{1,0:T(8,128)S(1)}, f32[136,256]{1,0:T(8,128)S(1)}, u32[]{:S(2)}, u32[]{:S(2)}) %collective-permute-start.22) | collective-permute-done | bytes 139296 | tf_op jit(solution)/shard_map/ppermute | solution.py:469
  103.5 1.7 %collective-permute-start.24 = (f32[136,256]{1,0:T(8,128)S(1)}, f32[136,256]{1,0:T(8,128)S(1)}, u32[]{:S(2)}, u32[]{:S(2)}) collective-permute-start(f32[136,256]{1,0:T(8,128)S(1)} %collective-permute-done.22.n0), channel_id=1, source_target_pairs={{0,32},{4,100},{8,40},{12,108},{16,48},{20,116},{24,56},{28,124},{... | collective-permute-start | bytes 417800 | tf_op jit(solution)/shard_map/ppermute | solution.py:469
  105.7 2.8 %collective-permute-done.24.n2 = f32[136,256]{1,0:T(8,128)S(1)} collective-permute-done((f32[136,256]{1,0:T(8,128)S(1)}, f32[136,256]{1,0:T(8,128)S(1)}, u32[]{:S(2)}, u32[]{:S(2)}) %collective-permute-start.24) | collective-permute-done | bytes 139296 | tf_op jit(solution)/shard_map/ppermute | solution.py:469
  109.9 2.2 %shard_map.77 = (f32[16,64]{1,0:T(8,128)S(1)}, f32[16,64]{1,0:T(8,128)S(1)}, f32[16,64]{1,0:T(8,128)S(1)}, f32[16,64]{1,0:T(8,128)S(1)}) custom-call(s32[4]{0:T(128)S(1)} %pad_add_fusion.idx, f32[1,256]{1,0:T(1,128)S(1)} %bitcast.13, f32[136,256]{1,0:T(8,128)S(1)} %collective-permute-done.22.n0, f32[136,256]{1,0:T(8,128)S(1)} %collective-permute-done.23.n1, ...), custom_call_target="tpu_custom_call" | custom-call | tf_op jit(solution)/shard_map/pallas_call | solution.py:69
  112.2 2.3 %collective-permute-start.29 = (f32[16,64]{1,0:T(8,128)S(1)}, f32[16,64]{1,0:T(8,128)S(1)}, u32[]{:S(2)}, u32[]{:S(2)}) collective-permute-start(f32[16,64]{1,0:T(8,128)S(1)} %get-tuple-element.99), channel_id=1, source_target_pairs={{0,2},{1,3},{2,0},{3,1},{4,6},{5,7},{6,4},{7,5},{8,10},{9,11},{10,... | collective-permute-start | bytes 12296 | tf_op jit(solution)/shard_map/ppermute | solution.py:396
  115.4 1.6 %collective-permute-done.28.r1 = f32[16,64]{1,0:T(8,128)S(1)} collective-permute-done((f32[16,64]{1,0:T(8,128)S(1)}, f32[16,64]{1,0:T(8,128)S(1)}, u32[]{:S(2)}, u32[]{:S(2)}) %collective-permute-start.28) | collective-permute-done | bytes 4128 | tf_op jit(solution)/shard_map/ppermute | solution.py:396
  (57 shorter events, 19.6 us)
Async XLA Ops:
  2.5 40.2 %collective-permute-start.3 = (f32[1536,256]{1,0:T(8,128)S(1)}, f32[1536,256]{1,0:T(8,128)S(1)}, u32[]{:S(2)}, u32[]{:S(2)}) collective-permute-start(f32[1536,256]{1,0:T(8,128)S(1)} %get-tuple-element.53), channel_id=1, source_target_pairs={{0,1},{1,2},{2,3},{3,0},{4,5},{5,6},{6,7},{7,4},{8,9},{9,10},{10,1... | collective-permute-start | bytes 4718600 | tf_op jit(solution)/shard_map/ppermute | solution.py:396
  4.5 38.2 %collective-permute-start.4 = (f32[1536,256]{1,0:T(8,128)S(1)}, f32[1536,256]{1,0:T(8,128)S(1)}, u32[]{:S(2)}, u32[]{:S(2)}) collective-permute-start(f32[1536,256]{1,0:T(8,128)S(1)} %get-tuple-element.54), channel_id=1, source_target_pairs={{0,3},{1,0},{2,1},{3,2},{4,7},{5,4},{6,5},{7,6},{8,11},{9,8},{10,9... | collective-permute-start | bytes 4718600 | tf_op jit(solution)/shard_map/ppermute | solution.py:396
  31.0 10.1 %collective-permute-start.2 = (f32[16,256]{1,0:T(8,128)S(1)}, f32[16,256]{1,0:T(8,128)S(1)}, u32[]{:S(2)}, u32[]{:S(2)}) collective-permute-start(f32[16,256]{1,0:T(8,128)S(1)} %shard_map.65.info.i0), channel_id=1, source_target_pairs={{0,3},{1,0},{2,1},{3,2},{4,7},{5,4},{6,5},{7,6},{8,11},{9,8},{10,9... | collective-permute-start | bytes 49160 | tf_op jit(solution)/shard_map/ppermute | solution.py:396
  33.0 9.7 %collective-permute-start.1 = (f32[16,256]{1,0:T(8,128)S(1)}, f32[16,256]{1,0:T(8,128)S(1)}, u32[]{:S(2)}, u32[]{:S(2)}) collective-permute-start(f32[16,256]{1,0:T(8,128)S(1)} %shard_map.65.info.i0), channel_id=1, source_target_pairs={{0,2},{1,3},{2,0},{3,1},{4,6},{5,7},{6,4},{7,5},{8,10},{9,11},{10,... | collective-permute-start | bytes 49160 | tf_op jit(solution)/shard_map/ppermute | solution.py:396
  33.0 9.7 %collective-permute-start = (f32[16,256]{1,0:T(8,128)S(1)}, f32[16,256]{1,0:T(8,128)S(1)}, u32[]{:S(2)}, u32[]{:S(2)}) collective-permute-start(f32[16,256]{1,0:T(8,128)S(1)} %shard_map.65.info.i0), channel_id=1, source_target_pairs={{0,1},{1,2},{2,3},{3,0},{4,5},{5,6},{6,7},{7,4},{8,9},{9,10},{10,1... | collective-permute-start | bytes 49160 | tf_op jit(solution)/shard_map/ppermute | solution.py:396
  43.3 11.7 %collective-permute-start.8 = (f32[320,256]{1,0:T(8,128)S(1)}, f32[320,256]{1,0:T(8,128)S(1)}, u32[]{:S(2)}, u32[]{:S(2)}) collective-permute-start(f32[320,256]{1,0:T(8,128)S(1)} %get-tuple-element.74), channel_id=1, source_target_pairs={{0,1},{1,2},{2,3},{3,0},{4,5},{5,6},{6,7},{7,4},{8,9},{9,10},{10,1... | collective-permute-start | bytes 983048 | tf_op jit(solution)/shard_map/ppermute | solution.py:396
  44.7 10.8 %collective-permute-start.9 = (f32[320,256]{1,0:T(8,128)S(1)}, f32[320,256]{1,0:T(8,128)S(1)}, u32[]{:S(2)}, u32[]{:S(2)}) collective-permute-start(f32[320,256]{1,0:T(8,128)S(1)} %get-tuple-element.75), channel_id=1, source_target_pairs={{0,3},{1,0},{2,1},{3,2},{4,7},{5,4},{6,5},{7,6},{8,11},{9,8},{10,9... | collective-permute-start | bytes 983048 | tf_op jit(solution)/shard_map/ppermute | solution.py:396
  46.6 15.0 %collective-permute-start.10 = (f32[192,256]{1,0:T(8,128)S(1)}, f32[192,256]{1,0:T(8,128)S(1)}, u32[]{:S(2)}, u32[]{:S(2)}) collective-permute-start(f32[192,256]{1,0:T(8,128)S(1)} %get-tuple-element.79), channel_id=1, source_target_pairs={{0,1},{1,2},{2,3},{3,0},{4,5},{5,6},{6,7},{7,4},{8,9},{9,10},{10,1... | collective-permute-start | bytes 589832 | tf_op jit(solution)/shard_map/ppermute | solution.py:396
  46.8 14.9 %collective-permute-start.11 = (f32[192,256]{1,0:T(8,128)S(1)}, f32[192,256]{1,0:T(8,128)S(1)}, u32[]{:S(2)}, u32[]{:S(2)}) collective-permute-start(f32[192,256]{1,0:T(8,128)S(1)} %get-tuple-element.80), channel_id=1, source_target_pairs={{0,3},{1,0},{2,1},{3,2},{4,7},{5,4},{6,5},{7,6},{8,11},{9,8},{10,9... | collective-permute-start | bytes 589832 | tf_op jit(solution)/shard_map/ppermute | solution.py:396
  51.4 13.3 %collective-permute-start.5 = (f32[16,256]{1,0:T(8,128)S(1)}, f32[16,256]{1,0:T(8,128)S(1)}, u32[]{:S(2)}, u32[]{:S(2)}) collective-permute-start(f32[16,256]{1,0:T(8,128)S(1)} %get-tuple-element.71), channel_id=1, source_target_pairs={{0,1},{1,2},{2,3},{3,0},{4,5},{5,6},{6,7},{7,4},{8,9},{9,10},{10,1... | collective-permute-start | bytes 49160 | tf_op jit(solution)/shard_map/ppermute | solution.py:396
  55.0 9.8 %collective-permute-start.6 = (f32[16,256]{1,0:T(8,128)S(1)}, f32[16,256]{1,0:T(8,128)S(1)}, u32[]{:S(2)}, u32[]{:S(2)}) collective-permute-start(f32[16,256]{1,0:T(8,128)S(1)} %get-tuple-element.72), channel_id=1, source_target_pairs={{0,2},{1,3},{2,0},{3,1},{4,6},{5,7},{6,4},{7,5},{8,10},{9,11},{10,... | collective-permute-start | bytes 49160 | tf_op jit(solution)/shard_map/ppermute | solution.py:396
  55.5 9.3 %collective-permute-start.7 = (f32[16,256]{1,0:T(8,128)S(1)}, f32[16,256]{1,0:T(8,128)S(1)}, u32[]{:S(2)}, u32[]{:S(2)}) collective-permute-start(f32[16,256]{1,0:T(8,128)S(1)} %get-tuple-element.73), channel_id=1, source_target_pairs={{0,3},{1,0},{2,1},{3,2},{4,7},{5,4},{6,5},{7,6},{8,11},{9,8},{10,9... | collective-permute-start | bytes 49160 | tf_op jit(solution)/shard_map/ppermute | solution.py:396
  67.1 6.6 %collective-permute-start.14 = (f32[272,256]{1,0:T(8,128)S(1)}, f32[272,256]{1,0:T(8,128)S(1)}, u32[]{:S(2)}, u32[]{:S(2)}) collective-permute-start(f32[272,256]{1,0:T(8,128)S(1)} %get-tuple-element.86.m0), channel_id=1, source_target_pairs={{0,3},{1,0},{2,1},{3,2},{4,7},{5,4},{6,5},{7,6},{8,11},{9,8},{10,9... | collective-permute-start | bytes 835592 | tf_op jit(solution)/shard_map/ppermute | solution.py:396
  68.0 8.2 %collective-permute-start.13 = (f32[272,256]{1,0:T(8,128)S(1)}, f32[272,256]{1,0:T(8,128)S(1)}, u32[]{:S(2)}, u32[]{:S(2)}) collective-permute-start(f32[272,256]{1,0:T(8,128)S(1)} %get-tuple-element.86.m0), channel_id=1, source_target_pairs={{0,2},{1,3},{2,0},{3,1},{4,6},{5,7},{6,4},{7,5},{8,10},{9,11},{10,... | collective-permute-start | bytes 835592 | tf_op jit(solution)/shard_map/ppermute | solution.py:396
  68.6 10.5 %collective-permute-start.12 = (f32[272,256]{1,0:T(8,128)S(1)}, f32[272,256]{1,0:T(8,128)S(1)}, u32[]{:S(2)}, u32[]{:S(2)}) collective-permute-start(f32[272,256]{1,0:T(8,128)S(1)} %get-tuple-element.86.m0), channel_id=1, source_target_pairs={{0,1},{1,2},{2,3},{3,0},{4,5},{5,6},{6,7},{7,4},{8,9},{9,10},{10,1... | collective-permute-start | bytes 835592 | tf_op jit(solution)/shard_map/ppermute | solution.py:396
  80.6 29.3 %copy-start.1 = (f32[256]{0:T(256)S(1)}, f32[256]{0:T(256)}, u32[]{:S(2)}) copy-start(f32[256]{0:T(256)} %param.6) | copy-start | bytes 3076
  80.6 1.6 %collective-permute-start.15 = (f32[272,256]{1,0:T(8,128)S(1)}, f32[272,256]{1,0:T(8,128)S(1)}, u32[]{:S(2)}, u32[]{:S(2)}) collective-permute-start(f32[272,256]{1,0:T(8,128)S(1)} %get-tuple-element.87.own), channel_id=1, source_target_pairs={{0,4},{4,0},{8,12},{12,8},{16,20},{20,16},{24,28},{28,24},{32,36},... | collective-permute-start | bytes 835592 | tf_op jit(solution)/shard_map/ppermute | solution.py:465
  83.1 6.3 %collective-permute-start.16 = (f32[136,256]{1,0:T(8,128)S(1)}, f32[136,256]{1,0:T(8,128)S(1)}, u32[]{:S(2)}, u32[]{:S(2)}) collective-permute-start(f32[136,256]{1,0:T(8,128)S(1)} %get-tuple-element.90), channel_id=1, source_target_pairs={{0,8},{4,28},{8,16},{12,4},{16,24},{20,12},{24,0},{28,20},{32,40},... | collective-permute-start | bytes 417800 | tf_op jit(solution)/shard_map/ppermute | solution.py:469
  84.7 6.5 %collective-permute-start.17 = (f32[136,256]{1,0:T(8,128)S(1)}, f32[136,256]{1,0:T(8,128)S(1)}, u32[]{:S(2)}, u32[]{:S(2)}) collective-permute-start(f32[136,256]{1,0:T(8,128)S(1)} %get-tuple-element.91), channel_id=1, source_target_pairs={{0,8},{4,28},{8,16},{12,4},{16,24},{20,12},{24,0},{28,20},{32,40},... | collective-permute-start | bytes 417800 | tf_op jit(solution)/shard_map/ppermute | solution.py:469
  89.4 6.3 %collective-permute-start.18 = (f32[136,256]{1,0:T(8,128)S(1)}, f32[136,256]{1,0:T(8,128)S(1)}, u32[]{:S(2)}, u32[]{:S(2)}) collective-permute-start(f32[136,256]{1,0:T(8,128)S(1)} %collective-permute-done.16.n0), channel_id=1, source_target_pairs={{0,8},{4,28},{8,16},{12,4},{16,24},{20,12},{24,0},{28,20},{32,40},... | collective-permute-start | bytes 417800 | tf_op jit(solution)/shard_map/ppermute | solution.py:469
  89.8 5.9 %collective-permute-start.19 = (f32[136,256]{1,0:T(8,128)S(1)}, f32[136,256]{1,0:T(8,128)S(1)}, u32[]{:S(2)}, u32[]{:S(2)}) collective-permute-start(f32[136,256]{1,0:T(8,128)S(1)} %collective-permute-done.16.n0), channel_id=1, source_target_pairs={{0,4},{4,0},{8,12},{12,8},{16,20},{20,16},{24,28},{28,24},{32,36},... | collective-permute-start | bytes 417800 | tf_op jit(solution)/shard_map/ppermute | solution.py:465
  91.3 4.4 %collective-permute-start.20 = (f32[136,256]{1,0:T(8,128)S(1)}, f32[136,256]{1,0:T(8,128)S(1)}, u32[]{:S(2)}, u32[]{:S(2)}) collective-permute-start(f32[136,256]{1,0:T(8,128)S(1)} %collective-permute-done.17.n1), channel_id=1, source_target_pairs={{0,4},{4,0},{8,12},{12,8},{16,20},{20,16},{24,28},{28,24},{32,36},... | collective-permute-start | bytes 417800 | tf_op jit(solution)/shard_map/ppermute | solution.py:465
  95.7 1.4 %collective-permute-start.21 = (f32[136,256]{1,0:T(8,128)S(1)}, f32[136,256]{1,0:T(8,128)S(1)}, u32[]{:S(2)}, u32[]{:S(2)}) collective-permute-start(f32[136,256]{1,0:T(8,128)S(1)} %collective-permute-done.18.n2), channel_id=1, source_target_pairs={{0,4},{4,0},{8,12},{12,8},{16,20},{20,16},{24,28},{28,24},{32,36},... | collective-permute-start | bytes 417800 | tf_op jit(solution)/shard_map/ppermute | solution.py:465
  98.4 5.1 %collective-permute-start.22 = (f32[136,256]{1,0:T(8,128)S(1)}, f32[136,256]{1,0:T(8,128)S(1)}, u32[]{:S(2)}, u32[]{:S(2)}) collective-permute-start(f32[136,256]{1,0:T(8,128)S(1)} %get-tuple-element.92), channel_id=1, source_target_pairs={{0,32},{4,100},{8,40},{12,108},{16,48},{20,116},{24,56},{28,124},{... | collective-permute-start | bytes 417800 | tf_op jit(solution)/shard_map/ppermute | solution.py:469
  98.9 6.3 %collective-permute-start.23 = (f32[136,256]{1,0:T(8,128)S(1)}, f32[136,256]{1,0:T(8,128)S(1)}, u32[]{:S(2)}, u32[]{:S(2)}) collective-permute-start(f32[136,256]{1,0:T(8,128)S(1)} %get-tuple-element.93), channel_id=1, source_target_pairs={{0,32},{4,100},{8,40},{12,108},{16,48},{20,116},{24,56},{28,124},{... | collective-permute-start | bytes 417800 | tf_op jit(solution)/shard_map/ppermute | solution.py:469
  103.5 5.1 %collective-permute-start.24 = (f32[136,256]{1,0:T(8,128)S(1)}, f32[136,256]{1,0:T(8,128)S(1)}, u32[]{:S(2)}, u32[]{:S(2)}) collective-permute-start(f32[136,256]{1,0:T(8,128)S(1)} %collective-permute-done.22.n0), channel_id=1, source_target_pairs={{0,32},{4,100},{8,40},{12,108},{16,48},{20,116},{24,56},{28,124},{... | collective-permute-start | bytes 417800 | tf_op jit(solution)/shard_map/ppermute | solution.py:469
  105.2 4.5 %collective-permute-start.25 = (f32[136,256]{1,0:T(8,128)S(1)}, f32[136,256]{1,0:T(8,128)S(1)}, u32[]{:S(2)}, u32[]{:S(2)}) collective-permute-start(f32[136,256]{1,0:T(8,128)S(1)} %collective-permute-done.22.n0), channel_id=1, source_target_pairs={{0,4},{4,0},{8,12},{12,8},{16,20},{20,16},{24,28},{28,24},{32,36},... | collective-permute-start | bytes 417800 | tf_op jit(solution)/shard_map/ppermute | solution.py:465
  105.2 4.5 %collective-permute-start.26 = (f32[136,256]{1,0:T(8,128)S(1)}, f32[136,256]{1,0:T(8,128)S(1)}, u32[]{:S(2)}, u32[]{:S(2)}) collective-permute-start(f32[136,256]{1,0:T(8,128)S(1)} %collective-permute-done.23.n1), channel_id=1, source_target_pairs={{0,4},{4,0},{8,12},{12,8},{16,20},{20,16},{24,28},{28,24},{32,36},... | collective-permute-start | bytes 417800 | tf_op jit(solution)/shard_map/ppermute | solution.py:465
  108.6 1.4 %collective-permute-start.27 = (f32[136,256]{1,0:T(8,128)S(1)}, f32[136,256]{1,0:T(8,128)S(1)}, u32[]{:S(2)}, u32[]{:S(2)}) collective-permute-start(f32[136,256]{1,0:T(8,128)S(1)} %collective-permute-done.24.n2), channel_id=1, source_target_pairs={{0,4},{4,0},{8,12},{12,8},{16,20},{20,16},{24,28},{28,24},{32,36},... | collective-permute-start | bytes 417800 | tf_op jit(solution)/shard_map/ppermute | solution.py:465
  112.1 4.9 %collective-permute-start.28 = (f32[16,64]{1,0:T(8,128)S(1)}, f32[16,64]{1,0:T(8,128)S(1)}, u32[]{:S(2)}, u32[]{:S(2)}) collective-permute-start(f32[16,64]{1,0:T(8,128)S(1)} %get-tuple-element.98), channel_id=1, source_target_pairs={{0,1},{1,2},{2,3},{3,0},{4,5},{5,6},{6,7},{7,4},{8,9},{9,10},{10,1... | collective-permute-start | bytes 12296 | tf_op jit(solution)/shard_map/ppermute | solution.py:396
  112.2 5.2 %collective-permute-start.29 = (f32[16,64]{1,0:T(8,128)S(1)}, f32[16,64]{1,0:T(8,128)S(1)}, u32[]{:S(2)}, u32[]{:S(2)}) collective-permute-start(f32[16,64]{1,0:T(8,128)S(1)} %get-tuple-element.99), channel_id=1, source_target_pairs={{0,2},{1,3},{2,0},{3,1},{4,6},{5,7},{6,4},{7,5},{8,10},{9,11},{10,... | collective-permute-start | bytes 12296 | tf_op jit(solution)/shard_map/ppermute | solution.py:396
  114.5 3.7 %collective-permute-start.30 = (f32[16,64]{1,0:T(8,128)S(1)}, f32[16,64]{1,0:T(8,128)S(1)}, u32[]{:S(2)}, u32[]{:S(2)}) collective-permute-start(f32[16,64]{1,0:T(8,128)S(1)} %get-tuple-element.100), channel_id=1, source_target_pairs={{0,3},{1,0},{2,1},{3,2},{4,7},{5,4},{6,5},{7,6},{8,11},{9,8},{10,9... | collective-permute-start | bytes 12296 | tf_op jit(solution)/shard_map/ppermute | solution.py:396
  (3 other events, 19.9 us)

commit v9 on v5

--- a/solution.py
+++ b/solution.py
@@ -13,6 +13,12 @@
 N = 256
 PAD = 16
 R = N + PAD
+Z, C, Y, X = range(4)
+HALF = R // 2
+ROWS = 4
+SUB = 16
+SEG = 4
+HALF_SUB = SUB // 2
 Z, C, Y, X = range(4)
 HALF = R // 2
 ROWS = 4
@@ -125,92 +131,41 @@
     )(rid, observed)
 
 
-def own_copy(z, flat, own, start, sem):
-    return pltpu.make_async_copy(flat.at[pl.ds(pl.multiple_of(z * (SUB * 64) + start * 64, 64), own.shape[0])], own, sem)
-
-
-def assemble(z, parts, ah, al, own=None):
-    for d in (1, 2, 3, 0):
+def assemble(z, own, prev, after, opposite, ah, al):
+    for d in range(ROWS):
         slot = lax.rem(z - d + ROWS, ROWS)
         rows = pl.ds(pl.multiple_of(slot * 64, 64), 64)
-        if d == 0:
-            own.wait()
-        for k in range(ah.shape[0]):
-            hi, lo = split(parts[d][k * 64 : (k + 1) * 64, :])
+        for k in range(SUB):
+            ref, at = ((own, k), (prev, k), (opposite[k // HALF_SUB], k % HALF_SUB), (after, k))[d]
+            hi, lo = split(ref[at * 64 : (at + 1) * 64, :])
             ah[k, rows, :] = hi
             al[k, rows, :] = lo
 
 
-def by_step(x, ah, al):
-    xh, xl = split(x)
-    return dot_nt(xh, ah) + dot_nt(xl, ah) + dot_nt(xh, al)
-
-
-def chains(lengths, ah, al, pref):
-    eye = jnp.where(
-        lax.broadcasted_iota(jnp.int32, (N, N), 0) == lax.broadcasted_iota(jnp.int32, (N, N), 1), 1.0, 0.0
-    ).astype(BF16)
-    for t in range(max(lengths)):
-        for c, length in enumerate(lengths):
-            if t >= length:
-                continue
-            k = sum(lengths[:c]) + t
-            if t == 0:
-                pref[k] = dot_nt(eye, ah[k]) + dot_nt(eye, al[k])
-            else:
-                pref[k] = by_step(pref[k - 1], ah[k], al[k])
-
-
-def first_kernel(idx, flat, gains, a1, a2, a3, pref, ah, al, both, staged, own, sems):
+def compose_kernel(idx, own, prev, after, q1, q2, b0, b1, b2, b3, pref, whole, ah, al, b_s):
     z = idx[Z]
-    late = pltpu.make_async_copy(gains, staged, sems.at[1])
-    copy = own_copy(z, flat, own, 0, sems.at[0])
-    copy.start()
-    late.start()
-    assemble(z, (own, a1, a2, a3), ah, al, copy)
-    chains(CHUNKS[0], ah, al, pref)
-    both[...] = mm(pref[CHUNKS[0][0] - 1], pref[SIZES[0] - 1])
-    late.wait()
-
-
-def second_kernel(idx, flat, a1, a2, a3, both, pref, ah, al, four, three, own, sem):
-    z = idx[Z]
-    copy = own_copy(z, flat, own, SIZES[0], sem)
-    copy.start()
-    assemble(z, (own, a1, a2, a3), ah, al, copy)
-    chains(CHUNKS[1], ah, al, pref)
-    three[...] = mm(both[...], pref[CHUNKS[1][0] - 1])
-    four[...] = mm(three[...], pref[SIZES[1] - 1])
-
-
-def third_kernel(idx, b0, b1, b2, b3, p01, ah01, al01, p23, ah23, al23, four, shifts, whole, b_s):
-    z = idx[Z]
+    assemble(z, own, prev, after, (q1, q2), ah, al)
     for d, b in enumerate((b0, b1, b2, b3)):
         b_s[lax.rem(z - d + ROWS, ROWS)] = b[...]
     b = jnp.concatenate([b_s[i, :, :64] for i in range(ROWS)], axis=1)
     first = lax.broadcasted_iota(jnp.int32, (PAD, N), 0) == 0
-
-    def row(k):
-        return jnp.where(first, b[k : k + 1, :], 0.0)
-
-    mats = [(ah01, al01, i) for i in range(SIZES[0])] + [(ah23, al23, i) for i in range(SIZES[1])]
-    starts = [end - n for end, n in zip(ENDS, SEGS)]
-    p = [row(k) for k in starts]
-    for c, k in enumerate(starts):
-        shifts[k : k + 1, :] = p[c][:1]
-    for t in range(1, max(SEGS)):
-        for c, start in enumerate(starts):
-            if t >= SEGS[c]:
-                continue
-            k = start + t
-            h, l, i = mats[k]
-            p[c] = by_step(p[c], h[i], l[i]) + row(k)
-            shifts[k : k + 1, :] = p[c][:1]
-    v = mm(p[0], p01[SIZES[0] - 1]) + p[1]
-    v = mm(v, p23[CHUNKS[1][0] - 1]) + p[2]
-    v = mm(v, p23[SIZES[1] - 1]) + p[3]
-    whole[:N, :] = four[...]
-    whole[N:, :] = v
+    eye = lax.broadcasted_iota(jnp.int32, (N, N), 0) == lax.broadcasted_iota(jnp.int32, (N, N), 1)
+    eye = jnp.where(eye, 1.0, 0.0).astype(BF16)
+    chains = range(SUB // SEG)
+    for t in range(SEG):
+        for c in chains:
+            k = c * SEG + t
+            shift = jnp.where(first, b[k : k + 1, :], 0.0)
+            if t == 0:
+                pref[k, :N, :] = dot_nt(eye, ah[k]) + dot_nt(eye, al[k])
+                pref[k, N:, :] = shift
+            else:
+                hi, lo = split(pref[k - 1])
+                out = dot_nt(hi, ah[k]) + dot_nt(lo, ah[k]) + dot_nt(hi, al[k])
+                pref[k, :N, :] = out[:N]
+                pref[k, N:, :] = out[N:] + shift
+    ends = [pref[c * SEG + SEG - 1] for c in chains]
+    whole[...] = then(then(ends[0], ends[1]), then(ends[2], ends[3]))
 
 
 def combine(pos, m_s, before):
@@ -244,19 +199,19 @@
     return pl.ds(pl.multiple_of(c * HALF, 8), HALF)
 
 
-def join_halves(pos, c, mine, others, m_s):
-    for d, (m, o) in enumerate(zip(mine, others)):
-        slot = lax.rem(pos - d + 3, 4)
+def join(pos, c, mine, others, m_s):
+    for d, (m, o) in enumerate(zip(mine, others), 1):
+        slot = lax.rem(pos - d + 4, 4)
         m_s[slot, half_rows(c), :] = m[...]
         m_s[slot, half_rows(1 - c), :] = o[...]
 
 
-def halves_kernel(idx, own, h1, h2, h3, o1, o2, o3, half, before, m_s):
+def plane_kernel(idx, own, h1, h2, h3, o1, o2, o3, half, before, m_s, all_s):
     pos, c = idx[Y], idx[C]
     m_s[pos] = own[...]
-    join_halves(pos, c, (h1, h2, h3), (o1, o2, o3), m_s)
-    m_s[4] = combine(pos, m_s, before)
-    half[...] = m_s[4, half_rows(c), :]
+    join(pos, c, (h1, h2, h3), (o1, o2, o3), m_s)
+    all_s[...] = combine(pos, m_s, before)
+    half[...] = all_s[half_rows(c), :]
 
 
 def pair_kernel(idx, own, other, before_in, total, half, before):
@@ -280,11 +235,9 @@
     out[...] = then(first[...], second[...])
 
 
-def states_kernel(
-    idx, prior, h1, h2, h3, g1, g2, g3, before, p01, p23, shifts, o0, o1, o2, o3, st_s, m_s, s_s
-):
+def states_kernel(idx, prior, h1, h2, h3, g1, g2, g3, before, pref, o0, o1, o2, o3, st_s, m_s, s_s):
     z, pos = idx[Z], idx[X]
-    join_halves(pos, idx[C], (h1, h2, h3), (g1, g2, g3), m_s)
+    join(pos, idx[C], (h1, h2, h3), (g1, g2, g3), m_s)
     s_s[...] = jnp.where(lax.broadcasted_iota(jnp.int32, (PAD, N), 0) == 0, prior[...], 0.0)
     for i in range(3):
 
@@ -294,45 +247,60 @@
 
     s = apply(s_s[...], before[...])
     eye = lax.broadcasted_iota(jnp.int32, (N, N), 0) == lax.broadcasted_iota(jnp.int32, (N, N), 1)
-    first = lax.broadcasted_iota(jnp.int32, (PAD, N), 0) == 0
-    prefs = [(p01, i) for i in range(SIZES[0])] + [(p23, i) for i in range(SIZES[1])]
-    for end, n in zip(ENDS, SEGS):
+    for end in range(SEG, SUB + 1, SEG):
         col = jnp.sum(jnp.where(eye, s[0:1, :], 0.0), axis=1, keepdims=True)
-        for k in range(end - n, end):
-            m, i = prefs[k]
-            row = jnp.sum(m[i] * col, axis=0, keepdims=True) + shifts[k : k + 1, :]
+        for k in range(end - SEG, end):
+            row = jnp.sum(pref[k, :N, :] * col, axis=0, keepdims=True) + pref[k, N : N + 1, :]
             for j in range(ROWS):
                 st_s[j, k : k + 1, :] = row[:, j * 64 : (j + 1) * 64]
         if end < SUB:
-            m, i = prefs[end - 1]
-            s = mm(s, m[i]) + jnp.where(first, shifts[end - 1 : end, :], 0.0)
+            s = apply(s, pref[end - 1])
     for d, o in enumerate((o0, o1, o2, o3)):
         o[...] = st_s[lax.rem(z + d, ROWS)]
 
 
-def send_copies(z, flat, outs, start, count, sems):
+SENT = SUB + HALF_SUB
+COPIED = 4
+
+
+def send_kernel(idx, flat, ahead, back, sems):
+    z = idx[Z]
     copies = []
-    for d, o in enumerate(outs, 1):
-        at = lax.rem(z + d, ROWS) * (SUB * 64) + start * 64
-        source = flat.at[pl.ds(pl.multiple_of(at, 64), count * 64)]
-        copies.append(pltpu.make_async_copy(source, o.at[pl.ds(0, count * 64)], sems.at[d - 1]))
+    for way, out in enumerate((ahead, back)):
+        for at in range(0, SENT, COPIED):
+            d, first = ((1, 3)[way], at) if at < SUB else (2, at - SUB + way * HALF_SUB)
+            source = lax.rem(z + d, ROWS) * (SUB * 64) + first * 64
+            copies.append(
+                pltpu.make_async_copy(
+                    flat.at[pl.ds(pl.multiple_of(source, 64), COPIED * 64)],
+                    out.at[pl.ds(at * 64, COPIED * 64)],
+                    sems.at[len(copies)],
+                )
+            )
     for copy in copies:
         copy.start()
-    return copies
-
-
-def send_a_kernel(idx, flat, o1, o2, o3, sems):
-    for copy in send_copies(idx[Z], flat, (o1, o2, o3), 0, SIZES[0], sems):
+    for copy in copies:
+        copy.wait()
+
+
+def relay_kernel(idx, prev, after, p, a):
+    p[...] = prev[SUB * 64 :, :]
+    a[...] = after[SUB * 64 :, :]
+
+
+def stage_kernel(idx, gains, flat, info, staged, own, sems):
+    copies = [
+        pltpu.make_async_copy(gains, staged, sems.at[0]),
+        pltpu.make_async_copy(flat.at[pl.ds(pl.multiple_of(idx[Z] * (SUB * 64), 64), SUB * 64)], own, sems.at[1]),
+    ]
+    for copy in copies:
+        copy.start()
+    for copy in copies:
         copy.wait()
 
 
 def sum_kernel(idx, sums, info):
     info[...] = jnp.sum(sums[...], axis=0)
-
-
-def send_b_kernel(idx, flat, o1, o2, o3, sems):
-    for copy in send_copies(idx[Z], flat, (o1, o2, o3), SIZES[0], SIZES[1], sems):
-        copy.wait()
 
 
 def offset_kernel(idx, g, i0, r1, r2, r3, o0, o1, o2, o3, info_s, off_s):
@@ -370,31 +338,34 @@
     idx = jnp.stack([z, tm & 1, (tm >> 1) & 3, tm >> 3])
     prior = prior.reshape(1, N)
     flat = dynamics.reshape(ROWS * SUB * 64, N)
-    dma3 = pltpu.SemaphoreType.DMA((3,))
 
     def along_rows(blocks):
         return [along_row(b, d) for d, b in enumerate(blocks, 1)]
 
-    part_a = along_rows(call(send_a_kernel, [(SIZES[0] * 64, N)] * 3, idx, (), [dma3], far=(flat,)))
+    ahead, back = call(
+        send_kernel, [(SENT * 64, N)] * 2, idx, (), [pltpu.SemaphoreType.DMA((2 * SENT // COPIED,))], far=(flat,)
+    )
+    prev, after = along_row(ahead, 1), along_row(back, 3)
 
     rid = owner[:, 0] * 16 + step % 16 + 512 * (step // 16)
     partial = binned(rid.reshape(1, -1), observed.T)
     sums = lax.all_to_all(partial, "tm", 0, 0, tiled=True).reshape(32, 16, N)
-    sums, idx, prior, *part_a = lax.optimization_barrier((sums, idx, prior, *part_a))
-
     (info,) = call(sum_kernel, [(16, N)], idx, (sums,))
     infos = along_rows([info] * 3)
-    sent_b = call(send_b_kernel, [(SIZES[1] * 64, N)] * 3, idx, (), [dma3], far=(flat,))
-    infos, sent_b = lax.optimization_barrier((infos, sent_b))
-    part_b = along_rows(sent_b)
-    p01, ah01, al01, both, staged = call(
-        first_kernel,
-        [(SIZES[0], N, N), ((SIZES[0], N, N), BF16), ((SIZES[0], N, N), BF16), (N, N), gains.shape],
-        idx,
-        part_a,
-        [pltpu.VMEM((SIZES[0] * 64, N), F32), pltpu.SemaphoreType.DMA((2,))],
-        far=(flat, gains),
-    )
+    staged, own = call(
+        stage_kernel,
+        [gains.shape, (SUB * 64, N)],
+        idx,
+        (info,),
+        [pltpu.SemaphoreType.DMA((2,))],
+        far=(gains, flat),
+    )
+    infos, staged, own, prev, after, idx, prior = lax.optimization_barrier(
+        (infos, staged, own, prev, after, idx, prior)
+    )
+    pieces = call(relay_kernel, [(HALF_SUB * 64, N)] * 2, idx, (prev, after))
+    pieces, infos = lax.optimization_barrier((pieces, infos))
+    relayed = [along_row(p, d) for p, d in zip(pieces, (1, 3))]
     offs = call(
         offset_kernel,
         [(16, N)] * 4,
@@ -403,20 +374,13 @@
         [pltpu.VMEM((ROWS, 16, N), F32), pltpu.VMEM((ROWS, 16, 128), F32)],
     )
     offs = [offs[0], *along_rows(offs[1:])]
-    p23, ah23, al23, four = call(
-        second_kernel,
-        [(SIZES[1], N, N), ((SIZES[1], N, N), BF16), ((SIZES[1], N, N), BF16), (N, N)],
-        idx,
-        (*part_b, both),
-        [pltpu.VMEM((N, N), F32), pltpu.VMEM((SIZES[1] * 64, N), F32), pltpu.SemaphoreType.DMA],
-        far=(flat,),
-    )
-    shifts, whole = call(
-        third_kernel,
-        [(SUB, N), (R, N)],
-        idx,
-        (*offs, p01, ah01, al01, p23, ah23, al23, four),
-        [pltpu.VMEM((ROWS, 16, N), F32)],
+    pref, whole = call(
+        compose_kernel,
+        [(SUB, R, N), (R, N)],
+        idx,
+        (own, prev, after, *relayed, *offs),
+        [pltpu.VMEM((SUB, N, N), BF16)] * 2 + [pltpu.VMEM((ROWS, 16, N), F32)],
+        mib=16,
     )
 
     block, before = call(
@@ -430,28 +394,29 @@
     def other_core(m):
         return lax.ppermute(m, "tm", [(i, i ^ 1) for i in range(32)])
 
-    def along_tm(m, d, n, stride):
-        places = [(i, i - i % (n * stride) + (i + d * stride) % (n * stride)) for i in range(32)]
-        return lax.ppermute(m, "tm", places)
+    def gathered(half, stride):
+        n = 4 * stride
+        got = [
+            lax.ppermute(half, "tm", [(i, i - i % n + (i + d * stride) % n) for i in range(32)]) for d in (1, 2, 3)
+        ]
+        return *got, *[other_core(g) for g in got]
 
     column, half, before = call(
         pair_kernel, [(R, N), (HALF, N), (R, N)], idx, (block, other_core(block), before)
     )
-    halves = [along_tm(half, d, 4, 2) for d in (1, 2, 3)]
     half, ybefore = call(
-        halves_kernel,
+        plane_kernel,
         [(HALF, N), (R, N)],
         idx,
-        (column, *halves, *[other_core(h) for h in halves]),
-        [pltpu.VMEM((5, R, N), F32)],
-    )
-    halves = [along_tm(half, d, 4, 8) for d in (1, 2, 3)]
+        (column, *gathered(half, 2)),
+        [pltpu.VMEM((4, R, N), F32), pltpu.VMEM((R, N), F32)],
+    )
     (before,) = call(fold_kernel, [(R, N)], idx, (ybefore, before))
     outs = call(
         states_kernel,
         [(SUB, 64)] * 4,
         idx,
-        (prior, *halves, *[other_core(h) for h in halves], before, p01, p23, shifts),
+        (prior, *gathered(half, 8), before, pref),
         [pltpu.VMEM((ROWS, SUB, 64), F32), pltpu.VMEM((4, R, N), F32), pltpu.VMEM((PAD, N), F32)],
     )
     got = [outs[0], *along_rows(outs[1:])]

time: 128 us -> 120 us (0.938); the launches traced: 128 us -> 118 us
  starting transfers between devices: 35.6 us -> 30.2 us
  Pallas kernels: 29.6 us -> 26.6 us
    ppermute x18 -> x16, starting transfers between devices: 25.9 us -> 20.8 us  [along_row(): return lax.ppermute(x, 'row', [(i, (i + d) % ROWS) for i in range(ROWS)])]
    pallas_call x12 -> x11, Pallas kernels: 21.5 us -> 18.5 us  [call(): pl.pallas_call(kernel, out_shape=[pltpu.VMEM(s, t) for s, t in outs], in_...]
    ppermute x18 -> x16, waiting for transfers between devices: 29.5 us -> 26.8 us  [along_row(): return lax.ppermute(x, 'row', [(i, (i + d) % ROWS) for i in range(ROWS)])]
  transfers between devices with their start and end apart: 31 -> 29, of which waited for: 19 -> 19; matrix products, arithmetic and copies ran while one was open for 0% -> 0% of each run, Pallas kernels for 14% -> 11%
where the time goes in v9:
time: 120 us; the launch traced here: 118 us
  waiting for transfers between devices  44.6 us (37%)
  starting transfers between devices  30.2 us (25%)
  Pallas kernels  26.6 us (22%)
  blocking collectives  16.7 us (14%)
    ppermute x16, waiting for transfers between devices, along_row(): return lax.ppermute(x, 'row', [(i, (i + d) % ROWS) for i in range(ROWS)])  26.8 us
    ppermute x16, starting transfers between devices, along_row(): return lax.ppermute(x, 'row', [(i, (i + d) % ROWS) for i in range(ROWS)])  20.8 us
    pallas_call x11, Pallas kernels, call(): pl.pallas_call(kernel, out_shape=[pltpu.VMEM(s, t) for s, t in outs], in_...  18.5 us
    all_to_all x1, blocking collectives, shards(): sums = lax.all_to_all(partial, 'tm', 0, 0, tiled=True).reshape(32, 16, N)  16.7 us
    ppermute x6, waiting for transfers between devices, gathered(): lax.ppermute(half, 'tm', [(i, i - i % n + (i + d * stride) % n) for i in...  14.4 us
    ppermute x6, starting transfers between devices, gathered(): lax.ppermute(half, 'tm', [(i, i - i % n + (i + d * stride) % n) for i in...  8.78 us
    pallas_call x1, Pallas kernels, binned(): pl.pallas_call(bin_kernel, out_shape=jax.ShapeDtypeStruct((n_bins // 4, N...  6.9 us
    ppermute x7, waiting for transfers between devices, other_core(): return lax.ppermute(m, 'tm', [(i, i ^ 1) for i in range(32)])  3.39 us
  transfers between devices with their start and end apart: 29, of which 19 were waited for; matrix products, arithmetic and copies ran while one was open for 0% of the time, Pallas kernels for 11%

profile of v9, /device:TPU:6, one launch (start us, length us, event | category | flops | bytes accessed | tf_op | source)
XLA Modules:
  0.0 118.4 jit_solution(2654052955832014152)
XLA Ops:
  0.1 2.5 %shard_map.67 = (f32[1536,256]{1,0:T(8,128)S(1)}, f32[1536,256]{1,0:T(8,128)S(1)}) custom-call(s32[4]{0:T(128)S(1)} %pad_add_fusion.idx, f32[4096,256]{1,0:T(8,128)} %bitcast.14), custom_call_target="tpu_custom_call" | custom-call | tf_op jit(solution)/shard_map/pallas_call | solution.py:75
  2.6 2.0 %collective-permute-start.3 = (f32[1536,256]{1,0:T(8,128)S(1)}, f32[1536,256]{1,0:T(8,128)S(1)}, u32[]{:S(2)}, u32[]{:S(2)}) collective-permute-start(f32[1536,256]{1,0:T(8,128)S(1)} %get-tuple-element.44), channel_id=1, source_target_pairs={{0,1},{1,2},{2,3},{3,0},{4,5},{5,6},{6,7},{7,4},{8,9},{9,10},{10,1... | collective-permute-start | bytes 4718600 | tf_op jit(solution)/shard_map/ppermute | solution.py:332
  4.6 2.2 %collective-permute-start.4 = (f32[1536,256]{1,0:T(8,128)S(1)}, f32[1536,256]{1,0:T(8,128)S(1)}, u32[]{:S(2)}, u32[]{:S(2)}) collective-permute-start(f32[1536,256]{1,0:T(8,128)S(1)} %get-tuple-element.45), channel_id=1, source_target_pairs={{0,3},{1,0},{2,1},{3,2},{4,7},{5,4},{6,5},{7,6},{8,11},{9,8},{10,9... | collective-permute-start | bytes 4718600 | tf_op jit(solution)/shard_map/ppermute | solution.py:332
  6.8 6.9 %shard_map.64 = f32[512,256]{1,0:T(8,128)S(1)} custom-call(s32[1,4096]{1,0:T(1,128)S(1)} %bitcast.12, f32[64,4096]{1,0:T(8,128)S(1)} %bitcast.11), custom_call_target="tpu_custom_call" | custom-call | tf_op jit(solution)/shard_map/pallas_call | solution.py:120
  13.7 16.7 %all_to_all.9.sums = f32[32,16,256]{2,1,0:T(8,128)S(1)} all-to-all(f32[32,16,256]{2,1,0:T(8,128)S(1)} %bitcast.10), channel_id=1, replica_groups=mesh['tm'=32,'row'=4] {'tm'}, dimensions={0} | all-to-all | bytes 1048576 | tf_op jit(solution)/shard_map/all_to_all | solution.py:352
  31.0 2.0 %collective-permute-start.2 = (f32[16,256]{1,0:T(8,128)S(1)}, f32[16,256]{1,0:T(8,128)S(1)}, u32[]{:S(2)}, u32[]{:S(2)}) collective-permute-start(f32[16,256]{1,0:T(8,128)S(1)} %shard_map.65.info.i0), channel_id=1, source_target_pairs={{0,3},{1,0},{2,1},{3,2},{4,7},{5,4},{6,5},{7,6},{8,11},{9,8},{10,9... | collective-permute-start | bytes 49160 | tf_op jit(solution)/shard_map/ppermute | solution.py:332
  33.0 1.3 %collective-permute-start = (f32[16,256]{1,0:T(8,128)S(1)}, f32[16,256]{1,0:T(8,128)S(1)}, u32[]{:S(2)}, u32[]{:S(2)}) collective-permute-start(f32[16,256]{1,0:T(8,128)S(1)} %shard_map.65.info.i0), channel_id=1, source_target_pairs={{0,1},{1,2},{2,3},{3,0},{4,5},{5,6},{6,7},{7,4},{8,9},{9,10},{10,1... | collective-permute-start | bytes 49160 | tf_op jit(solution)/shard_map/ppermute | solution.py:332
  34.3 3.0 %shard_map.66 = (f32[64,64,256]{2,1,0:T(8,128)S(1)}, f32[1024,256]{1,0:T(8,128)S(1)}) custom-call(s32[4]{0:T(128)S(1)} %pad_add_fusion.idx, f32[64,64,256]{2,1,0:T(8,128)} %gains.1, f32[4096,256]{1,0:T(8,128)} %bitcast.15, f32[16,256]{1,0:T(8,128)S(1)} %shard_map.65.info.i0), custom_call_target="tpu_custom_call" | custom-call | tf_op jit(solution)/shard_map/pallas_call | solution.py:75
  37.4 3.8 %collective-permute-done.2.r3 = f32[16,256]{1,0:T(8,128)S(1)} collective-permute-done((f32[16,256]{1,0:T(8,128)S(1)}, f32[16,256]{1,0:T(8,128)S(1)}, u32[]{:S(2)}, u32[]{:S(2)}) %collective-permute-start.2) | collective-permute-done | bytes 16416 | tf_op jit(solution)/shard_map/ppermute | solution.py:332
  41.2 1.6 %collective-permute-done.1.r2 = f32[16,256]{1,0:T(8,128)S(1)} collective-permute-done((f32[16,256]{1,0:T(8,128)S(1)}, f32[16,256]{1,0:T(8,128)S(1)}, u32[]{:S(2)}, u32[]{:S(2)}) %collective-permute-start.1) | collective-permute-done | bytes 16416 | tf_op jit(solution)/shard_map/ppermute | solution.py:332
  43.4 1.4 %collective-permute-start.5 = (f32[512,256]{1,0:T(8,128)S(1)}, f32[512,256]{1,0:T(8,128)S(1)}, u32[]{:S(2)}, u32[]{:S(2)}) collective-permute-start(f32[512,256]{1,0:T(8,128)S(1)} %get-tuple-element.56), channel_id=1, source_target_pairs={{0,1},{1,2},{2,3},{3,0},{4,5},{5,6},{6,7},{7,4},{8,9},{9,10},{10,1... | collective-permute-start | bytes 1572872 | tf_op jit(solution)/shard_map/ppermute | solution.py:332
  44.8 1.9 %collective-permute-start.6 = (f32[512,256]{1,0:T(8,128)S(1)}, f32[512,256]{1,0:T(8,128)S(1)}, u32[]{:S(2)}, u32[]{:S(2)}) collective-permute-start(f32[512,256]{1,0:T(8,128)S(1)} %get-tuple-element.57), channel_id=1, source_target_pairs={{0,3},{1,0},{2,1},{3,2},{4,7},{5,4},{6,5},{7,6},{8,11},{9,8},{10,9... | collective-permute-start | bytes 1572872 | tf_op jit(solution)/shard_map/ppermute | solution.py:332
  46.7 1.6 %shard_map.69 = (f32[16,256]{1,0:T(8,128)S(1)}, f32[16,256]{1,0:T(8,128)S(1)}, f32[16,256]{1,0:T(8,128)S(1)}, f32[16,256]{1,0:T(8,128)S(1)}) custom-call(s32[4]{0:T(128)S(1)} %pad_add_fusion.idx, f32[64,64,256]{2,1,0:T(8,128)S(1)} %get-tuple-element.58.g, f32[16,256]{1,0:T(8,128)S(1)} %shard_map.65.info.i0, f32[16,256]{1,0:T(8,128)S(1)} %collective-permute-done.r1, ...), custom_call_target="tpu_custom_call" | custom-call | tf_op jit(solution)/shard_map/pallas_call | solution.py:75
  48.4 2.2 %collective-permute-start.8 = (f32[16,256]{1,0:T(8,128)S(1)}, f32[16,256]{1,0:T(8,128)S(1)}, u32[]{:S(2)}, u32[]{:S(2)}) collective-permute-start(f32[16,256]{1,0:T(8,128)S(1)} %get-tuple-element.64), channel_id=1, source_target_pairs={{0,2},{1,3},{2,0},{3,1},{4,6},{5,7},{6,4},{7,5},{8,10},{9,11},{10,... | collective-permute-start | bytes 49160 | tf_op jit(solution)/shard_map/ppermute | solution.py:332
  51.5 6.0 %collective-permute-done.7.b1 = f32[16,256]{1,0:T(8,128)S(1)} collective-permute-done((f32[16,256]{1,0:T(8,128)S(1)}, f32[16,256]{1,0:T(8,128)S(1)}, u32[]{:S(2)}, u32[]{:S(2)}) %collective-permute-start.7) | collective-permute-done | bytes 16416 | tf_op jit(solution)/shard_map/ppermute | solution.py:332
  58.3 3.7 %shard_map.70 = (f32[16,272,256]{2,1,0:T(8,128)S(1)}, f32[272,256]{1,0:T(8,128)S(1)}) custom-call(s32[4]{0:T(128)S(1)} %pad_add_fusion.idx, f32[1024,256]{1,0:T(8,128)S(1)} %get-tuple-element.48.own, f32[1536,256]{1,0:T(8,128)S(1)} %collective-permute-done.3.prev, f32[1536,256]{1,0:T(8,128)S(1)} %collective-permute-done.4.after, ...), custom_call_target="tpu_custom_call" | custom-call | tf_op jit(solution)/shard_map/pallas_call | solution.py:75
  62.0 2.4 %collective-permute-start.12 = (f32[272,256]{1,0:T(8,128)S(1)}, f32[272,256]{1,0:T(8,128)S(1)}, u32[]{:S(2)}, u32[]{:S(2)}) collective-permute-start(f32[272,256]{1,0:T(8,128)S(1)} %get-tuple-element.66.m0), channel_id=1, source_target_pairs={{0,3},{1,0},{2,1},{3,2},{4,7},{5,4},{6,5},{7,6},{8,11},{9,8},{10,9... | collective-permute-start | bytes 835592 | tf_op jit(solution)/shard_map/ppermute | solution.py:332
  65.4 8.2 %collective-permute-done.12.m3 = f32[272,256]{1,0:T(8,128)S(1)} collective-permute-done((f32[272,256]{1,0:T(8,128)S(1)}, f32[272,256]{1,0:T(8,128)S(1)}, u32[]{:S(2)}, u32[]{:S(2)}) %collective-permute-start.12) | collective-permute-done | bytes 278560 | tf_op jit(solution)/shard_map/ppermute | solution.py:332
  74.5 2.8 %collective-permute-done.10.m1 = f32[272,256]{1,0:T(8,128)S(1)} collective-permute-done((f32[272,256]{1,0:T(8,128)S(1)}, f32[272,256]{1,0:T(8,128)S(1)}, u32[]{:S(2)}, u32[]{:S(2)}) %collective-permute-start.10) | collective-permute-done | bytes 278560 | tf_op jit(solution)/shard_map/ppermute | solution.py:332
  77.3 1.3 %shard_map.71 = (f32[272,256]{1,0:T(8,128)S(1)}, f32[272,256]{1,0:T(8,128)S(1)}) custom-call(s32[4]{0:T(128)S(1)} %pad_add_fusion.idx, f32[272,256]{1,0:T(8,128)S(1)} %get-tuple-element.66.m0, f32[272,256]{1,0:T(8,128)S(1)} %collective-permute-done.10.m1, f32[272,256]{1,0:T(8,128)S(1)} %collective-permute-done.11.m2, f32[272,256]{1,0:T(8,128)S(1)} %collective-permute-done.12.m3), custom_call_target="tpu_custom_call" | custom-call | tf_op jit(solution)/shard_map/pallas_call | solution.py:75
  78.8 1.5 %collective-permute-done.13.other = f32[272,256]{1,0:T(8,128)S(1)} collective-permute-done((f32[272,256]{1,0:T(8,128)S(1)}, f32[272,256]{1,0:T(8,128)S(1)}, u32[]{:S(2)}, u32[]{:S(2)}) %collective-permute-start.13) | collective-permute-done | bytes 278560 | tf_op jit(solution)/shard_map/ppermute | solution.py:395
  81.2 3.1 %collective-permute-start.16 = (f32[136,256]{1,0:T(8,128)S(1)}, f32[136,256]{1,0:T(8,128)S(1)}, u32[]{:S(2)}, u32[]{:S(2)}) collective-permute-start(f32[136,256]{1,0:T(8,128)S(1)} %get-tuple-element.70), channel_id=1, source_target_pairs={{0,24},{4,28},{8,0},{12,4},{16,8},{20,12},{24,16},{28,20},{32,56},... | collective-permute-start | bytes 417800 | tf_op jit(solution)/shard_map/ppermute | solution.py:400
  85.8 4.7 %collective-permute-done.16.h3 = f32[136,256]{1,0:T(8,128)S(1)} collective-permute-done((f32[136,256]{1,0:T(8,128)S(1)}, f32[136,256]{1,0:T(8,128)S(1)}, u32[]{:S(2)}, u32[]{:S(2)}) %collective-permute-start.16) | collective-permute-done | bytes 139296 | tf_op jit(solution)/shard_map/ppermute | solution.py:400
  90.6 1.8 %collective-permute-done.15.h2 = f32[136,256]{1,0:T(8,128)S(1)} collective-permute-done((f32[136,256]{1,0:T(8,128)S(1)}, f32[136,256]{1,0:T(8,128)S(1)}, u32[]{:S(2)}, u32[]{:S(2)}) %collective-permute-start.15) | collective-permute-done | bytes 139296 | tf_op jit(solution)/shard_map/ppermute | solution.py:400
  92.3 1.9 %collective-permute-done.14.h1 = f32[136,256]{1,0:T(8,128)S(1)} collective-permute-done((f32[136,256]{1,0:T(8,128)S(1)}, f32[136,256]{1,0:T(8,128)S(1)}, u32[]{:S(2)}, u32[]{:S(2)}) %collective-permute-start.14) | collective-permute-done | bytes 139296 | tf_op jit(solution)/shard_map/ppermute | solution.py:400
  94.3 1.3 %collective-permute-done.17.o1 = f32[136,256]{1,0:T(8,128)S(1)} collective-permute-done((f32[136,256]{1,0:T(8,128)S(1)}, f32[136,256]{1,0:T(8,128)S(1)}, u32[]{:S(2)}, u32[]{:S(2)}) %collective-permute-start.17) | collective-permute-done | bytes 139296 | tf_op jit(solution)/shard_map/ppermute | solution.py:395
  95.6 1.3 %shard_map.73 = (f32[136,256]{1,0:T(8,128)S(1)}, f32[272,256]{1,0:T(8,128)S(1)}) custom-call(s32[4]{0:T(128)S(1)} %pad_add_fusion.idx, f32[272,256]{1,0:T(8,128)S(1)} %get-tuple-element.69.own, f32[136,256]{1,0:T(8,128)S(1)} %collective-permute-done.14.h1, f32[136,256]{1,0:T(8,128)S(1)} %collective-permute-done.15.h2, ...), custom_call_target="tpu_custom_call" | custom-call | tf_op jit(solution)/shard_map/pallas_call | solution.py:75
  98.9 2.1 %collective-permute-start.20 = (f32[136,256]{1,0:T(8,128)S(1)}, f32[136,256]{1,0:T(8,128)S(1)}, u32[]{:S(2)}, u32[]{:S(2)}) collective-permute-start(f32[136,256]{1,0:T(8,128)S(1)} %get-tuple-element.71), channel_id=1, source_target_pairs={{0,32},{4,36},{8,40},{12,44},{16,48},{20,52},{24,56},{28,60},{32,6... | collective-permute-start | bytes 417800 | tf_op jit(solution)/shard_map/ppermute | solution.py:400
  101.0 5.9 %collective-permute-done.22.h3 = f32[136,256]{1,0:T(8,128)S(1)} collective-permute-done((f32[136,256]{1,0:T(8,128)S(1)}, f32[136,256]{1,0:T(8,128)S(1)}, u32[]{:S(2)}, u32[]{:S(2)}) %collective-permute-start.22) | collective-permute-done | bytes 139296 | tf_op jit(solution)/shard_map/ppermute | solution.py:400
  108.9 2.2 %shard_map.75 = (f32[16,64]{1,0:T(8,128)S(1)}, f32[16,64]{1,0:T(8,128)S(1)}, f32[16,64]{1,0:T(8,128)S(1)}, f32[16,64]{1,0:T(8,128)S(1)}) custom-call(s32[4]{0:T(128)S(1)} %pad_add_fusion.idx, f32[1,256]{1,0:T(1,128)S(1)} %bitcast.13, f32[136,256]{1,0:T(8,128)S(1)} %collective-permute-done.20.h1, f32[136,256]{1,0:T(8,128)S(1)} %collective-permute-done.21.h2, ...), custom_call_target="tpu_custom_call" | custom-call | tf_op jit(solution)/shard_map/pallas_call | solution.py:75
  111.2 2.4 %collective-permute-start.27 = (f32[16,64]{1,0:T(8,128)S(1)}, f32[16,64]{1,0:T(8,128)S(1)}, u32[]{:S(2)}, u32[]{:S(2)}) collective-permute-start(f32[16,64]{1,0:T(8,128)S(1)} %get-tuple-element.77), channel_id=1, source_target_pairs={{0,2},{1,3},{2,0},{3,1},{4,6},{5,7},{6,4},{7,5},{8,10},{9,11},{10,... | collective-permute-start | bytes 12296 | tf_op jit(solution)/shard_map/ppermute | solution.py:332
  114.5 1.6 %collective-permute-done.26.r1 = f32[16,64]{1,0:T(8,128)S(1)} collective-permute-done((f32[16,64]{1,0:T(8,128)S(1)}, f32[16,64]{1,0:T(8,128)S(1)}, u32[]{:S(2)}, u32[]{:S(2)}) %collective-permute-start.26) | collective-permute-done | bytes 4128 | tf_op jit(solution)/shard_map/ppermute | solution.py:332
  (51 shorter events, 14.8 us)
Async XLA Ops:
  0.0 6.8 %copy-start.2 = (s32[4096]{0:T(1024)S(1)}, s32[4096]{0:T(1024)}, u32[]{:S(2)}) copy-start(s32[4096]{0:T(1024)} %param.11) | copy-start | bytes 49156
  0.0 6.8 %copy-start = (f32[4096,64]{0,1:T(8,128)S(1)}, f32[4096,64]{0,1:T(8,128)}, u32[]{:S(2)}) copy-start(f32[4096,64]{0,1:T(8,128)} %param.9) | copy-start | bytes 3145732
  2.6 40.2 %collective-permute-start.3 = (f32[1536,256]{1,0:T(8,128)S(1)}, f32[1536,256]{1,0:T(8,128)S(1)}, u32[]{:S(2)}, u32[]{:S(2)}) collective-permute-start(f32[1536,256]{1,0:T(8,128)S(1)} %get-tuple-element.44), channel_id=1, source_target_pairs={{0,1},{1,2},{2,3},{3,0},{4,5},{5,6},{6,7},{7,4},{8,9},{9,10},{10,1... | collective-permute-start | bytes 4718600 | tf_op jit(solution)/shard_map/ppermute | solution.py:332
  4.6 38.2 %collective-permute-start.4 = (f32[1536,256]{1,0:T(8,128)S(1)}, f32[1536,256]{1,0:T(8,128)S(1)}, u32[]{:S(2)}, u32[]{:S(2)}) collective-permute-start(f32[1536,256]{1,0:T(8,128)S(1)} %get-tuple-element.45), channel_id=1, source_target_pairs={{0,3},{1,0},{2,1},{3,2},{4,7},{5,4},{6,5},{7,6},{8,11},{9,8},{10,9... | collective-permute-start | bytes 4718600 | tf_op jit(solution)/shard_map/ppermute | solution.py:332
  31.0 10.1 %collective-permute-start.2 = (f32[16,256]{1,0:T(8,128)S(1)}, f32[16,256]{1,0:T(8,128)S(1)}, u32[]{:S(2)}, u32[]{:S(2)}) collective-permute-start(f32[16,256]{1,0:T(8,128)S(1)} %shard_map.65.info.i0), channel_id=1, source_target_pairs={{0,3},{1,0},{2,1},{3,2},{4,7},{5,4},{6,5},{7,6},{8,11},{9,8},{10,9... | collective-permute-start | bytes 49160 | tf_op jit(solution)/shard_map/ppermute | solution.py:332
  33.0 9.7 %collective-permute-start.1 = (f32[16,256]{1,0:T(8,128)S(1)}, f32[16,256]{1,0:T(8,128)S(1)}, u32[]{:S(2)}, u32[]{:S(2)}) collective-permute-start(f32[16,256]{1,0:T(8,128)S(1)} %shard_map.65.info.i0), channel_id=1, source_target_pairs={{0,2},{1,3},{2,0},{3,1},{4,6},{5,7},{6,4},{7,5},{8,10},{9,11},{10,... | collective-permute-start | bytes 49160 | tf_op jit(solution)/shard_map/ppermute | solution.py:332
  33.0 9.7 %collective-permute-start = (f32[16,256]{1,0:T(8,128)S(1)}, f32[16,256]{1,0:T(8,128)S(1)}, u32[]{:S(2)}, u32[]{:S(2)}) collective-permute-start(f32[16,256]{1,0:T(8,128)S(1)} %shard_map.65.info.i0), channel_id=1, source_target_pairs={{0,1},{1,2},{2,3},{3,0},{4,5},{5,6},{6,7},{7,4},{8,9},{9,10},{10,1... | collective-permute-start | bytes 49160 | tf_op jit(solution)/shard_map/ppermute | solution.py:332
  43.4 14.9 %collective-permute-start.5 = (f32[512,256]{1,0:T(8,128)S(1)}, f32[512,256]{1,0:T(8,128)S(1)}, u32[]{:S(2)}, u32[]{:S(2)}) collective-permute-start(f32[512,256]{1,0:T(8,128)S(1)} %get-tuple-element.56), channel_id=1, source_target_pairs={{0,1},{1,2},{2,3},{3,0},{4,5},{5,6},{6,7},{7,4},{8,9},{9,10},{10,1... | collective-permute-start | bytes 1572872 | tf_op jit(solution)/shard_map/ppermute | solution.py:332
  44.8 13.5 %collective-permute-start.6 = (f32[512,256]{1,0:T(8,128)S(1)}, f32[512,256]{1,0:T(8,128)S(1)}, u32[]{:S(2)}, u32[]{:S(2)}) collective-permute-start(f32[512,256]{1,0:T(8,128)S(1)} %get-tuple-element.57), channel_id=1, source_target_pairs={{0,3},{1,0},{2,1},{3,2},{4,7},{5,4},{6,5},{7,6},{8,11},{9,8},{10,9... | collective-permute-start | bytes 1572872 | tf_op jit(solution)/shard_map/ppermute | solution.py:332
  48.3 9.3 %collective-permute-start.7 = (f32[16,256]{1,0:T(8,128)S(1)}, f32[16,256]{1,0:T(8,128)S(1)}, u32[]{:S(2)}, u32[]{:S(2)}) collective-permute-start(f32[16,256]{1,0:T(8,128)S(1)} %get-tuple-element.63), channel_id=1, source_target_pairs={{0,1},{1,2},{2,3},{3,0},{4,5},{5,6},{6,7},{7,4},{8,9},{9,10},{10,1... | collective-permute-start | bytes 49160 | tf_op jit(solution)/shard_map/ppermute | solution.py:332
  48.4 9.9 %collective-permute-start.8 = (f32[16,256]{1,0:T(8,128)S(1)}, f32[16,256]{1,0:T(8,128)S(1)}, u32[]{:S(2)}, u32[]{:S(2)}) collective-permute-start(f32[16,256]{1,0:T(8,128)S(1)} %get-tuple-element.64), channel_id=1, source_target_pairs={{0,2},{1,3},{2,0},{3,1},{4,6},{5,7},{6,4},{7,5},{8,10},{9,11},{10,... | collective-permute-start | bytes 49160 | tf_op jit(solution)/shard_map/ppermute | solution.py:332
  50.6 7.7 %collective-permute-start.9 = (f32[16,256]{1,0:T(8,128)S(1)}, f32[16,256]{1,0:T(8,128)S(1)}, u32[]{:S(2)}, u32[]{:S(2)}) collective-permute-start(f32[16,256]{1,0:T(8,128)S(1)} %get-tuple-element.65), channel_id=1, source_target_pairs={{0,3},{1,0},{2,1},{3,2},{4,7},{5,4},{6,5},{7,6},{8,11},{9,8},{10,9... | collective-permute-start | bytes 49160 | tf_op jit(solution)/shard_map/ppermute | solution.py:332
  58.3 50.6 %copy-start.1 = (f32[256]{0:T(256)S(1)}, f32[256]{0:T(256)}, u32[]{:S(2)}) copy-start(f32[256]{0:T(256)} %param.6) | copy-start | bytes 3076
  62.0 11.6 %collective-permute-start.12 = (f32[272,256]{1,0:T(8,128)S(1)}, f32[272,256]{1,0:T(8,128)S(1)}, u32[]{:S(2)}, u32[]{:S(2)}) collective-permute-start(f32[272,256]{1,0:T(8,128)S(1)} %get-tuple-element.66.m0), channel_id=1, source_target_pairs={{0,3},{1,0},{2,1},{3,2},{4,7},{5,4},{6,5},{7,6},{8,11},{9,8},{10,9... | collective-permute-start | bytes 835592 | tf_op jit(solution)/shard_map/ppermute | solution.py:332
  64.5 10.0 %collective-permute-start.11 = (f32[272,256]{1,0:T(8,128)S(1)}, f32[272,256]{1,0:T(8,128)S(1)}, u32[]{:S(2)}, u32[]{:S(2)}) collective-permute-start(f32[272,256]{1,0:T(8,128)S(1)} %get-tuple-element.66.m0), channel_id=1, source_target_pairs={{0,2},{1,3},{2,0},{3,1},{4,6},{5,7},{6,4},{7,5},{8,10},{9,11},{10,... | collective-permute-start | bytes 835592 | tf_op jit(solution)/shard_map/ppermute | solution.py:332
  65.1 12.2 %collective-permute-start.10 = (f32[272,256]{1,0:T(8,128)S(1)}, f32[272,256]{1,0:T(8,128)S(1)}, u32[]{:S(2)}, u32[]{:S(2)}) collective-permute-start(f32[272,256]{1,0:T(8,128)S(1)} %get-tuple-element.66.m0), channel_id=1, source_target_pairs={{0,1},{1,2},{2,3},{3,0},{4,5},{5,6},{6,7},{7,4},{8,9},{9,10},{10,1... | collective-permute-start | bytes 835592 | tf_op jit(solution)/shard_map/ppermute | solution.py:332
  78.7 1.6 %collective-permute-start.13 = (f32[272,256]{1,0:T(8,128)S(1)}, f32[272,256]{1,0:T(8,128)S(1)}, u32[]{:S(2)}, u32[]{:S(2)}) collective-permute-start(f32[272,256]{1,0:T(8,128)S(1)} %get-tuple-element.67.own), channel_id=1, source_target_pairs={{0,4},{4,0},{8,12},{12,8},{16,20},{20,16},{24,28},{28,24},{32,36},... | collective-permute-start | bytes 835592 | tf_op jit(solution)/shard_map/ppermute | solution.py:395
  81.2 9.4 %collective-permute-start.16 = (f32[136,256]{1,0:T(8,128)S(1)}, f32[136,256]{1,0:T(8,128)S(1)}, u32[]{:S(2)}, u32[]{:S(2)}) collective-permute-start(f32[136,256]{1,0:T(8,128)S(1)} %get-tuple-element.70), channel_id=1, source_target_pairs={{0,24},{4,28},{8,0},{12,4},{16,8},{20,12},{24,16},{28,20},{32,56},... | collective-permute-start | bytes 417800 | tf_op jit(solution)/shard_map/ppermute | solution.py:400
  84.2 8.1 %collective-permute-start.15 = (f32[136,256]{1,0:T(8,128)S(1)}, f32[136,256]{1,0:T(8,128)S(1)}, u32[]{:S(2)}, u32[]{:S(2)}) collective-permute-start(f32[136,256]{1,0:T(8,128)S(1)} %get-tuple-element.70), channel_id=1, source_target_pairs={{0,16},{4,20},{8,24},{12,28},{16,0},{20,4},{24,8},{28,12},{32,48},... | collective-permute-start | bytes 417800 | tf_op jit(solution)/shard_map/ppermute | solution.py:400
  84.9 9.4 %collective-permute-start.14 = (f32[136,256]{1,0:T(8,128)S(1)}, f32[136,256]{1,0:T(8,128)S(1)}, u32[]{:S(2)}, u32[]{:S(2)}) collective-permute-start(f32[136,256]{1,0:T(8,128)S(1)} %get-tuple-element.70), channel_id=1, source_target_pairs={{0,8},{4,12},{8,16},{12,20},{16,24},{20,28},{24,0},{28,4},{32,40},... | collective-permute-start | bytes 417800 | tf_op jit(solution)/shard_map/ppermute | solution.py:400
  90.6 3.7 %collective-permute-start.19 = (f32[136,256]{1,0:T(8,128)S(1)}, f32[136,256]{1,0:T(8,128)S(1)}, u32[]{:S(2)}, u32[]{:S(2)}) collective-permute-start(f32[136,256]{1,0:T(8,128)S(1)} %collective-permute-done.16.h3), channel_id=1, source_target_pairs={{0,4},{4,0},{8,12},{12,8},{16,20},{20,16},{24,28},{28,24},{32,36},... | collective-permute-start | bytes 417800 | tf_op jit(solution)/shard_map/ppermute | solution.py:395
  92.3 2.0 %collective-permute-start.18 = (f32[136,256]{1,0:T(8,128)S(1)}, f32[136,256]{1,0:T(8,128)S(1)}, u32[]{:S(2)}, u32[]{:S(2)}) collective-permute-start(f32[136,256]{1,0:T(8,128)S(1)} %collective-permute-done.15.h2), channel_id=1, source_target_pairs={{0,4},{4,0},{8,12},{12,8},{16,20},{20,16},{24,28},{28,24},{32,36},... | collective-permute-start | bytes 417800 | tf_op jit(solution)/shard_map/ppermute | solution.py:395
  94.3 1.4 %collective-permute-start.17 = (f32[136,256]{1,0:T(8,128)S(1)}, f32[136,256]{1,0:T(8,128)S(1)}, u32[]{:S(2)}, u32[]{:S(2)}) collective-permute-start(f32[136,256]{1,0:T(8,128)S(1)} %collective-permute-done.14.h1), channel_id=1, source_target_pairs={{0,4},{4,0},{8,12},{12,8},{16,20},{20,16},{24,28},{28,24},{32,36},... | collective-permute-start | bytes 417800 | tf_op jit(solution)/shard_map/ppermute | solution.py:395
  96.9 10.0 %collective-permute-start.22 = (f32[136,256]{1,0:T(8,128)S(1)}, f32[136,256]{1,0:T(8,128)S(1)}, u32[]{:S(2)}, u32[]{:S(2)}) collective-permute-start(f32[136,256]{1,0:T(8,128)S(1)} %get-tuple-element.71), channel_id=1, source_target_pairs={{0,96},{4,100},{8,104},{12,108},{16,112},{20,116},{24,120},{28,124... | collective-permute-start | bytes 417800 | tf_op jit(solution)/shard_map/ppermute | solution.py:400
  97.8 9.1 %collective-permute-start.21 = (f32[136,256]{1,0:T(8,128)S(1)}, f32[136,256]{1,0:T(8,128)S(1)}, u32[]{:S(2)}, u32[]{:S(2)}) collective-permute-start(f32[136,256]{1,0:T(8,128)S(1)} %get-tuple-element.71), channel_id=1, source_target_pairs={{0,64},{4,68},{8,72},{12,76},{16,80},{20,84},{24,88},{28,92},{32,9... | collective-permute-start | bytes 417800 | tf_op jit(solution)/shard_map/ppermute | solution.py:400
  98.9 8.6 %collective-permute-start.20 = (f32[136,256]{1,0:T(8,128)S(1)}, f32[136,256]{1,0:T(8,128)S(1)}, u32[]{:S(2)}, u32[]{:S(2)}) collective-permute-start(f32[136,256]{1,0:T(8,128)S(1)} %get-tuple-element.71), channel_id=1, source_target_pairs={{0,32},{4,36},{8,40},{12,44},{16,48},{20,52},{24,56},{28,60},{32,6... | collective-permute-start | bytes 417800 | tf_op jit(solution)/shard_map/ppermute | solution.py:400
  106.9 1.4 %collective-permute-start.25 = (f32[136,256]{1,0:T(8,128)S(1)}, f32[136,256]{1,0:T(8,128)S(1)}, u32[]{:S(2)}, u32[]{:S(2)}) collective-permute-start(f32[136,256]{1,0:T(8,128)S(1)} %collective-permute-done.22.h3), channel_id=1, source_target_pairs={{0,4},{4,0},{8,12},{12,8},{16,20},{20,16},{24,28},{28,24},{32,36},... | collective-permute-start | bytes 417800 | tf_op jit(solution)/shard_map/ppermute | solution.py:395
  106.9 1.6 %collective-permute-start.24 = (f32[136,256]{1,0:T(8,128)S(1)}, f32[136,256]{1,0:T(8,128)S(1)}, u32[]{:S(2)}, u32[]{:S(2)}) collective-permute-start(f32[136,256]{1,0:T(8,128)S(1)} %collective-permute-done.21.h2), channel_id=1, source_target_pairs={{0,4},{4,0},{8,12},{12,8},{16,20},{20,16},{24,28},{28,24},{32,36},... | collective-permute-start | bytes 417800 | tf_op jit(solution)/shard_map/ppermute | solution.py:395
  107.5 1.4 %collective-permute-start.23 = (f32[136,256]{1,0:T(8,128)S(1)}, f32[136,256]{1,0:T(8,128)S(1)}, u32[]{:S(2)}, u32[]{:S(2)}) collective-permute-start(f32[136,256]{1,0:T(8,128)S(1)} %collective-permute-done.20.h1), channel_id=1, source_target_pairs={{0,4},{4,0},{8,12},{12,8},{16,20},{20,16},{24,28},{28,24},{32,36},... | collective-permute-start | bytes 417800 | tf_op jit(solution)/shard_map/ppermute | solution.py:395
  111.1 4.9 %collective-permute-start.26 = (f32[16,64]{1,0:T(8,128)S(1)}, f32[16,64]{1,0:T(8,128)S(1)}, u32[]{:S(2)}, u32[]{:S(2)}) collective-permute-start(f32[16,64]{1,0:T(8,128)S(1)} %get-tuple-element.76), channel_id=1, source_target_pairs={{0,1},{1,2},{2,3},{3,0},{4,5},{5,6},{6,7},{7,4},{8,9},{9,10},{10,1... | collective-permute-start | bytes 12296 | tf_op jit(solution)/shard_map/ppermute | solution.py:332
  111.2 5.2 %collective-permute-start.27 = (f32[16,64]{1,0:T(8,128)S(1)}, f32[16,64]{1,0:T(8,128)S(1)}, u32[]{:S(2)}, u32[]{:S(2)}) collective-permute-start(f32[16,64]{1,0:T(8,128)S(1)} %get-tuple-element.77), channel_id=1, source_target_pairs={{0,2},{1,3},{2,0},{3,1},{4,6},{5,7},{6,4},{7,5},{8,10},{9,11},{10,... | collective-permute-start | bytes 12296 | tf_op jit(solution)/shard_map/ppermute | solution.py:332
  113.6 3.7 %collective-permute-start.28 = (f32[16,64]{1,0:T(8,128)S(1)}, f32[16,64]{1,0:T(8,128)S(1)}, u32[]{:S(2)}, u32[]{:S(2)}) collective-permute-start(f32[16,64]{1,0:T(8,128)S(1)} %get-tuple-element.78), channel_id=1, source_target_pairs={{0,3},{1,0},{2,1},{3,2},{4,7},{5,4},{6,5},{7,6},{8,11},{9,8},{10,9... | collective-permute-start | bytes 12296 | tf_op jit(solution)/shard_map/ppermute | solution.py:332
  (1 other events, 6.8 us)

commit v10 on v9

--- a/solution.py
+++ b/solution.py
@@ -142,7 +142,7 @@
             al[k, rows, :] = lo
 
 
-def compose_kernel(idx, own, prev, after, q1, q2, b0, b1, b2, b3, pref, whole, ah, al, b_s):
+def compose_kernel(idx, own, prev, after, q1, q2, b0, b1, b2, b3, pref, top, low, ah, al, b_s):
     z = idx[Z]
     assemble(z, own, prev, after, (q1, q2), ah, al)
     for d, b in enumerate((b0, b1, b2, b3)):
@@ -165,7 +165,9 @@
                 pref[k, :N, :] = out[:N]
                 pref[k, N:, :] = out[N:] + shift
     ends = [pref[c * SEG + SEG - 1] for c in chains]
-    whole[...] = then(then(ends[0], ends[1]), then(ends[2], ends[3]))
+    whole = then(then(ends[0], ends[1]), then(ends[2], ends[3]))
+    top[...] = whole[:HALF]
+    low[...] = whole[HALF:]
 
 
 def combine(pos, m_s, before):
@@ -188,10 +190,12 @@
     return then(m01, m23)
 
 
-def four_kernel(idx, m0, m1, m2, m3, total, before, m_s):
+def four_kernel(idx, t0, l0, t1, l1, t2, l2, t3, l3, total, before, m_s):
     pos = idx[Z]
-    for d, m in enumerate((m0, m1, m2, m3)):
-        m_s[lax.rem(pos - d + 4, 4)] = m[...]
+    for d, (t, l) in enumerate(((t0, l0), (t1, l1), (t2, l2), (t3, l3))):
+        slot = lax.rem(pos - d + 4, 4)
+        m_s[slot, :HALF, :] = t[...]
+        m_s[slot, HALF:, :] = l[...]
     total[...] = combine(pos, m_s, before)
 
 
@@ -200,7 +204,7 @@
 
 
 def join(pos, c, mine, others, m_s):
-    for d, (m, o) in enumerate(zip(mine, others), 1):
+    for d, m, o in zip((3, 2, 1), mine, others):
         slot = lax.rem(pos - d + 4, 4)
         m_s[slot, half_rows(c), :] = m[...]
         m_s[slot, half_rows(1 - c), :] = o[...]
@@ -360,8 +364,8 @@
         [pltpu.SemaphoreType.DMA((2,))],
         far=(gains, flat),
     )
-    infos, staged, own, prev, after, idx, prior = lax.optimization_barrier(
-        (infos, staged, own, prev, after, idx, prior)
+    infos[0], infos[2], staged, own, prev, after, idx, prior = lax.optimization_barrier(
+        (infos[0], infos[2], staged, own, prev, after, idx, prior)
     )
     pieces = call(relay_kernel, [(HALF_SUB * 64, N)] * 2, idx, (prev, after))
     pieces, infos = lax.optimization_barrier((pieces, infos))
@@ -374,20 +378,22 @@
         [pltpu.VMEM((ROWS, 16, N), F32), pltpu.VMEM((ROWS, 16, 128), F32)],
     )
     offs = [offs[0], *along_rows(offs[1:])]
-    pref, whole = call(
+    pref, top, low = call(
         compose_kernel,
-        [(SUB, R, N), (R, N)],
+        [(SUB, R, N), (HALF, N), (HALF, N)],
         idx,
         (own, prev, after, *relayed, *offs),
         [pltpu.VMEM((SUB, N, N), BF16)] * 2 + [pltpu.VMEM((ROWS, 16, N), F32)],
         mib=16,
     )
 
+    prev_top, after_low = along_row(top, 1), along_row(low, 3)
+    prev_low, after_top = along_row(low, 1), along_row(top, 3)
     block, before = call(
         four_kernel,
         [(R, N), (R, N)],
         idx,
-        (whole, *[along_row(whole, d) for d in (1, 2, 3)]),
+        (top, low, prev_top, prev_low, along_row(prev_top, 1), along_row(after_low, 3), after_top, after_low),
         [pltpu.VMEM((4, R, N), F32)],
     )
 
@@ -397,7 +403,7 @@
     def gathered(half, stride):
         n = 4 * stride
         got = [
-            lax.ppermute(half, "tm", [(i, i - i % n + (i + d * stride) % n) for i in range(32)]) for d in (1, 2, 3)
+            lax.ppermute(half, "tm", [(i, i - i % n + (i + d * stride) % n) for i in range(32)]) for d in (3, 2, 1)
         ]
         return *got, *[other_core(g) for g in got]
 

time: 120 us -> 119 us (level)
  waiting for transfers between devices: 44.6 us -> 36.5 us
  starting transfers between devices: 30.2 us -> 38.1 us
    ppermute x16 -> x19, starting transfers between devices: 20.8 us -> 28.6 us  [along_row(): return lax.ppermute(x, 'row', [(i, (i + d) % ROWS) for i in range(ROWS)])]
    ppermute x16 -> x19, waiting for transfers between devices: 26.8 us -> 20.3 us  [along_row(): return lax.ppermute(x, 'row', [(i, (i + d) % ROWS) for i in range(ROWS)])]
    ppermute x6, waiting for transfers between devices: 14.4 us -> 13.1 us  [gathered(): lax.ppermute(half, 'tm', [(i, i - i % n + (i + d * stride) % n) for i in...]
  transfers between devices with their start and end apart: 29 -> 32, of which waited for: 19 -> 19; matrix products, arithmetic and copies ran while one was open for 0% -> 0% of each run, Pallas kernels for 11% -> 11%
where the time goes in v10:
time: 119 us; the launch traced here: 118 us
  starting transfers between devices  38.1 us (32%)
  waiting for transfers between devices  36.5 us (31%)
  Pallas kernels  26.7 us (22%)
  blocking collectives  16.7 us (14%)
    ppermute x19, starting transfers between devices, along_row(): return lax.ppermute(x, 'row', [(i, (i + d) % ROWS) for i in range(ROWS)])  28.6 us
    ppermute x19, waiting for transfers between devices, along_row(): return lax.ppermute(x, 'row', [(i, (i + d) % ROWS) for i in range(ROWS)])  20.3 us
    pallas_call x11, Pallas kernels, call(): pl.pallas_call(kernel, out_shape=[pltpu.VMEM(s, t) for s, t in outs], in_...  18.7 us
    all_to_all x1, blocking collectives, shards(): sums = lax.all_to_all(partial, 'tm', 0, 0, tiled=True).reshape(32, 16, N)  16.7 us
    ppermute x6, waiting for transfers between devices, gathered(): lax.ppermute(half, 'tm', [(i, i - i % n + (i + d * stride) % n) for i in...  13.1 us
    ppermute x6, starting transfers between devices, gathered(): lax.ppermute(half, 'tm', [(i, i - i % n + (i + d * stride) % n) for i in...  8.87 us
    pallas_call x1, Pallas kernels, binned(): pl.pallas_call(bin_kernel, out_shape=jax.ShapeDtypeStruct((n_bins // 4, N...  6.9 us
    ppermute x7, waiting for transfers between devices, other_core(): return lax.ppermute(m, 'tm', [(i, i ^ 1) for i in range(32)])  3.09 us
  transfers between devices with their start and end apart: 32, of which 19 were waited for; matrix products, arithmetic and copies ran while one was open for 0% of the time, Pallas kernels for 11%

profile of v10, /device:TPU:6, one launch (start us, length us, event | category | flops | bytes accessed | tf_op | source)
XLA Modules:
  0.0 118.3 jit_solution(962145681514569063)
XLA Ops:
  0.1 2.5 %shard_map.67 = (f32[1536,256]{1,0:T(8,128)S(1)}, f32[1536,256]{1,0:T(8,128)S(1)}) custom-call(s32[4]{0:T(128)S(1)} %pad_add_fusion.idx, f32[4096,256]{1,0:T(8,128)} %bitcast.14), custom_call_target="tpu_custom_call" | custom-call | tf_op jit(solution)/shard_map/pallas_call | solution.py:75
  2.6 2.0 %collective-permute-start.2 = (f32[1536,256]{1,0:T(8,128)S(1)}, f32[1536,256]{1,0:T(8,128)S(1)}, u32[]{:S(2)}, u32[]{:S(2)}) collective-permute-start(f32[1536,256]{1,0:T(8,128)S(1)} %get-tuple-element.44), channel_id=1, source_target_pairs={{0,1},{1,2},{2,3},{3,0},{4,5},{5,6},{6,7},{7,4},{8,9},{9,10},{10,1... | collective-permute-start | bytes 4718600 | tf_op jit(solution)/shard_map/ppermute | solution.py:336
  4.6 2.2 %collective-permute-start.3 = (f32[1536,256]{1,0:T(8,128)S(1)}, f32[1536,256]{1,0:T(8,128)S(1)}, u32[]{:S(2)}, u32[]{:S(2)}) collective-permute-start(f32[1536,256]{1,0:T(8,128)S(1)} %get-tuple-element.45), channel_id=1, source_target_pairs={{0,3},{1,0},{2,1},{3,2},{4,7},{5,4},{6,5},{7,6},{8,11},{9,8},{10,9... | collective-permute-start | bytes 4718600 | tf_op jit(solution)/shard_map/ppermute | solution.py:336
  6.8 6.9 %shard_map.64 = f32[512,256]{1,0:T(8,128)S(1)} custom-call(s32[1,4096]{1,0:T(1,128)S(1)} %bitcast.12, f32[64,4096]{1,0:T(8,128)S(1)} %bitcast.11), custom_call_target="tpu_custom_call" | custom-call | tf_op jit(solution)/shard_map/pallas_call | solution.py:120
  13.7 16.7 %all_to_all.9.sums = f32[32,16,256]{2,1,0:T(8,128)S(1)} all-to-all(f32[32,16,256]{2,1,0:T(8,128)S(1)} %bitcast.10), channel_id=1, replica_groups=mesh['tm'=32,'row'=4] {'tm'}, dimensions={0} | all-to-all | bytes 1048576 | tf_op jit(solution)/shard_map/all_to_all | solution.py:356
  31.0 2.0 %collective-permute-start.1 = (f32[16,256]{1,0:T(8,128)S(1)}, f32[16,256]{1,0:T(8,128)S(1)}, u32[]{:S(2)}, u32[]{:S(2)}) collective-permute-start(f32[16,256]{1,0:T(8,128)S(1)} %shard_map.65.info.i0), channel_id=1, source_target_pairs={{0,3},{1,0},{2,1},{3,2},{4,7},{5,4},{6,5},{7,6},{8,11},{9,8},{10,9... | collective-permute-start | bytes 49160 | tf_op jit(solution)/shard_map/ppermute | solution.py:336
  33.1 1.8 %collective-permute-start.4 = (f32[16,256]{1,0:T(8,128)S(1)}, f32[16,256]{1,0:T(8,128)S(1)}, u32[]{:S(2)}, u32[]{:S(2)}) collective-permute-start(f32[16,256]{1,0:T(8,128)S(1)} %shard_map.65.info.i0), channel_id=1, source_target_pairs={{0,2},{1,3},{2,0},{3,1},{4,6},{5,7},{6,4},{7,5},{8,10},{9,11},{10,... | collective-permute-start | bytes 49160 | tf_op jit(solution)/shard_map/ppermute | solution.py:336
  34.9 3.0 %shard_map.66 = (f32[64,64,256]{2,1,0:T(8,128)S(1)}, f32[1024,256]{1,0:T(8,128)S(1)}) custom-call(s32[4]{0:T(128)S(1)} %pad_add_fusion.idx, f32[64,64,256]{2,1,0:T(8,128)} %gains.1, f32[4096,256]{1,0:T(8,128)} %bitcast.15, f32[16,256]{1,0:T(8,128)S(1)} %shard_map.65.info.i0), custom_call_target="tpu_custom_call" | custom-call | tf_op jit(solution)/shard_map/pallas_call | solution.py:75
  38.0 3.2 %collective-permute-done.1.r3 = f32[16,256]{1,0:T(8,128)S(1)} collective-permute-done((f32[16,256]{1,0:T(8,128)S(1)}, f32[16,256]{1,0:T(8,128)S(1)}, u32[]{:S(2)}, u32[]{:S(2)}) %collective-permute-start.1) | collective-permute-done | bytes 16416 | tf_op jit(solution)/shard_map/ppermute | solution.py:336
  44.1 2.1 %collective-permute-start.6 = (f32[512,256]{1,0:T(8,128)S(1)}, f32[512,256]{1,0:T(8,128)S(1)}, u32[]{:S(2)}, u32[]{:S(2)}) collective-permute-start(f32[512,256]{1,0:T(8,128)S(1)} %get-tuple-element.56), channel_id=1, source_target_pairs={{0,3},{1,0},{2,1},{3,2},{4,7},{5,4},{6,5},{7,6},{8,11},{9,8},{10,9... | collective-permute-start | bytes 1572872 | tf_op jit(solution)/shard_map/ppermute | solution.py:336
  46.2 1.6 %shard_map.69 = (f32[16,256]{1,0:T(8,128)S(1)}, f32[16,256]{1,0:T(8,128)S(1)}, f32[16,256]{1,0:T(8,128)S(1)}, f32[16,256]{1,0:T(8,128)S(1)}) custom-call(s32[4]{0:T(128)S(1)} %pad_add_fusion.idx, f32[64,64,256]{2,1,0:T(8,128)S(1)} %get-tuple-element.57.g, f32[16,256]{1,0:T(8,128)S(1)} %shard_map.65.info.i0, f32[16,256]{1,0:T(8,128)S(1)} %collective-permute-done.r1, ...), custom_call_target="tpu_custom_call" | custom-call | tf_op jit(solution)/shard_map/pallas_call | solution.py:75
  47.8 2.8 %collective-permute-start.8 = (f32[16,256]{1,0:T(8,128)S(1)}, f32[16,256]{1,0:T(8,128)S(1)}, u32[]{:S(2)}, u32[]{:S(2)}) collective-permute-start(f32[16,256]{1,0:T(8,128)S(1)} %get-tuple-element.63), channel_id=1, source_target_pairs={{0,2},{1,3},{2,0},{3,1},{4,6},{5,7},{6,4},{7,5},{8,10},{9,11},{10,... | collective-permute-start | bytes 49160 | tf_op jit(solution)/shard_map/ppermute | solution.py:336
  51.5 5.7 %collective-permute-done.7.b1 = f32[16,256]{1,0:T(8,128)S(1)} collective-permute-done((f32[16,256]{1,0:T(8,128)S(1)}, f32[16,256]{1,0:T(8,128)S(1)}, u32[]{:S(2)}, u32[]{:S(2)}) %collective-permute-start.7) | collective-permute-done | bytes 16416 | tf_op jit(solution)/shard_map/ppermute | solution.py:336
  58.3 3.7 %shard_map.70 = (f32[16,272,256]{2,1,0:T(8,128)S(1)}, f32[136,256]{1,0:T(8,128)S(1)}, f32[136,256]{1,0:T(8,128)S(1)}) custom-call(s32[4]{0:T(128)S(1)} %pad_add_fusion.idx, f32[1024,256]{1,0:T(8,128)S(1)} %get-tuple-element.48.own, f32[1536,256]{1,0:T(8,128)S(1)} %collective-permute-done.2.prev, f32[1536,256]{1,0:T(8,128)S(1)} %collective-permute-done.3.after, ...), custom_call_target="tpu_custom_call" | custom-call | tf_op jit(solution)/shard_map/pallas_call | solution.py:75
  63.0 2.3 %collective-permute-start.13 = (f32[136,256]{1,0:T(8,128)S(1)}, f32[136,256]{1,0:T(8,128)S(1)}, u32[]{:S(2)}, u32[]{:S(2)}) collective-permute-start(f32[136,256]{1,0:T(8,128)S(1)} %get-tuple-element.66.l0), channel_id=1, source_target_pairs={{0,3},{1,0},{2,1},{3,2},{4,7},{5,4},{6,5},{7,6},{8,11},{9,8},{10,9... | collective-permute-start | bytes 417800 | tf_op jit(solution)/shard_map/ppermute | solution.py:336
  67.3 2.4 %collective-permute-done.10.t1 = f32[136,256]{1,0:T(8,128)S(1)} collective-permute-done((f32[136,256]{1,0:T(8,128)S(1)}, f32[136,256]{1,0:T(8,128)S(1)}, u32[]{:S(2)}, u32[]{:S(2)}) %collective-permute-start.10) | collective-permute-done | bytes 139296 | tf_op jit(solution)/shard_map/ppermute | solution.py:336
  69.8 3.2 %collective-permute-start.14 = (f32[136,256]{1,0:T(8,128)S(1)}, f32[136,256]{1,0:T(8,128)S(1)}, u32[]{:S(2)}, u32[]{:S(2)}) collective-permute-start(f32[136,256]{1,0:T(8,128)S(1)} %collective-permute-done.13.l3), channel_id=1, source_target_pairs={{0,3},{1,0},{2,1},{3,2},{4,7},{5,4},{6,5},{7,6},{8,11},{9,8},{10,9... | collective-permute-start | bytes 417800 | tf_op jit(solution)/shard_map/ppermute | solution.py:336
  73.0 3.0 %collective-permute-done.12.t2 = f32[136,256]{1,0:T(8,128)S(1)} collective-permute-done((f32[136,256]{1,0:T(8,128)S(1)}, f32[136,256]{1,0:T(8,128)S(1)}, u32[]{:S(2)}, u32[]{:S(2)}) %collective-permute-start.12) | collective-permute-done | bytes 139296 | tf_op jit(solution)/shard_map/ppermute | solution.py:336
  76.0 1.5 %shard_map.71 = (f32[272,256]{1,0:T(8,128)S(1)}, f32[272,256]{1,0:T(8,128)S(1)}) custom-call(s32[4]{0:T(128)S(1)} %pad_add_fusion.idx, f32[136,256]{1,0:T(8,128)S(1)} %get-tuple-element.65.t0, f32[136,256]{1,0:T(8,128)S(1)} %get-tuple-element.66.l0, f32[136,256]{1,0:T(8,128)S(1)} %collective-permute-done.10.t1, f32[136,256]{1,0:T(8,128)S(1)} %collective-permute-done.11.l1, ...), custom_call_target="tpu_custom_call" | custom-call | tf_op jit(solution)/shard_map/pallas_call | solution.py:75
  77.6 1.5 %collective-permute-done.16.other = f32[272,256]{1,0:T(8,128)S(1)} collective-permute-done((f32[272,256]{1,0:T(8,128)S(1)}, f32[272,256]{1,0:T(8,128)S(1)}, u32[]{:S(2)}, u32[]{:S(2)}) %collective-permute-start.16) | collective-permute-done | bytes 278560 | tf_op jit(solution)/shard_map/ppermute | solution.py:401
  80.0 1.6 %collective-permute-start.19 = (f32[136,256]{1,0:T(8,128)S(1)}, f32[136,256]{1,0:T(8,128)S(1)}, u32[]{:S(2)}, u32[]{:S(2)}) collective-permute-start(f32[136,256]{1,0:T(8,128)S(1)} %get-tuple-element.70), channel_id=1, source_target_pairs={{0,8},{4,12},{8,16},{12,20},{16,24},{20,28},{24,0},{28,4},{32,40},... | collective-permute-start | bytes 417800 | tf_op jit(solution)/shard_map/ppermute | solution.py:406
  81.7 2.9 %collective-permute-start.18 = (f32[136,256]{1,0:T(8,128)S(1)}, f32[136,256]{1,0:T(8,128)S(1)}, u32[]{:S(2)}, u32[]{:S(2)}) collective-permute-start(f32[136,256]{1,0:T(8,128)S(1)} %get-tuple-element.70), channel_id=1, source_target_pairs={{0,16},{4,20},{8,24},{12,28},{16,0},{20,4},{24,8},{28,12},{32,48},... | collective-permute-start | bytes 417800 | tf_op jit(solution)/shard_map/ppermute | solution.py:406
  84.6 1.3 %collective-permute-start.17 = (f32[136,256]{1,0:T(8,128)S(1)}, f32[136,256]{1,0:T(8,128)S(1)}, u32[]{:S(2)}, u32[]{:S(2)}) collective-permute-start(f32[136,256]{1,0:T(8,128)S(1)} %get-tuple-element.70), channel_id=1, source_target_pairs={{0,24},{4,28},{8,0},{12,4},{16,8},{20,12},{24,16},{28,20},{32,56},... | collective-permute-start | bytes 417800 | tf_op jit(solution)/shard_map/ppermute | solution.py:406
  87.2 4.2 %collective-permute-done.18.h2 = f32[136,256]{1,0:T(8,128)S(1)} collective-permute-done((f32[136,256]{1,0:T(8,128)S(1)}, f32[136,256]{1,0:T(8,128)S(1)}, u32[]{:S(2)}, u32[]{:S(2)}) %collective-permute-start.18) | collective-permute-done | bytes 139296 | tf_op jit(solution)/shard_map/ppermute | solution.py:406
  94.8 2.4 %collective-permute-start.24 = (f32[136,256]{1,0:T(8,128)S(1)}, f32[136,256]{1,0:T(8,128)S(1)}, u32[]{:S(2)}, u32[]{:S(2)}) collective-permute-start(f32[136,256]{1,0:T(8,128)S(1)} %get-tuple-element.71), channel_id=1, source_target_pairs={{0,64},{4,68},{8,72},{12,76},{16,80},{20,84},{24,88},{28,92},{32,9... | collective-permute-start | bytes 417800 | tf_op jit(solution)/shard_map/ppermute | solution.py:406
  97.2 3.6 %collective-permute-done.25.h3 = f32[136,256]{1,0:T(8,128)S(1)} collective-permute-done((f32[136,256]{1,0:T(8,128)S(1)}, f32[136,256]{1,0:T(8,128)S(1)}, u32[]{:S(2)}, u32[]{:S(2)}) %collective-permute-start.25) | collective-permute-done | bytes 139296 | tf_op jit(solution)/shard_map/ppermute | solution.py:406
  100.8 2.0 %collective-permute-done.24.h2 = f32[136,256]{1,0:T(8,128)S(1)} collective-permute-done((f32[136,256]{1,0:T(8,128)S(1)}, f32[136,256]{1,0:T(8,128)S(1)}, u32[]{:S(2)}, u32[]{:S(2)}) %collective-permute-start.24) | collective-permute-done | bytes 139296 | tf_op jit(solution)/shard_map/ppermute | solution.py:406
  102.8 2.1 %collective-permute-done.23.h1 = f32[136,256]{1,0:T(8,128)S(1)} collective-permute-done((f32[136,256]{1,0:T(8,128)S(1)}, f32[136,256]{1,0:T(8,128)S(1)}, u32[]{:S(2)}, u32[]{:S(2)}) %collective-permute-start.23) | collective-permute-done | bytes 139296 | tf_op jit(solution)/shard_map/ppermute | solution.py:406
  106.2 2.2 %shard_map.75 = (f32[16,64]{1,0:T(8,128)S(1)}, f32[16,64]{1,0:T(8,128)S(1)}, f32[16,64]{1,0:T(8,128)S(1)}, f32[16,64]{1,0:T(8,128)S(1)}) custom-call(s32[4]{0:T(128)S(1)} %pad_add_fusion.idx, f32[1,256]{1,0:T(1,128)S(1)} %bitcast.13, f32[136,256]{1,0:T(8,128)S(1)} %collective-permute-done.23.h1, f32[136,256]{1,0:T(8,128)S(1)} %collective-permute-done.24.h2, ...), custom_call_target="tpu_custom_call" | custom-call | tf_op jit(solution)/shard_map/pallas_call | solution.py:75
  108.5 5.0 %collective-permute-start.30 = (f32[16,64]{1,0:T(8,128)S(1)}, f32[16,64]{1,0:T(8,128)S(1)}, u32[]{:S(2)}, u32[]{:S(2)}) collective-permute-start(f32[16,64]{1,0:T(8,128)S(1)} %get-tuple-element.77), channel_id=1, source_target_pairs={{0,2},{1,3},{2,0},{3,1},{4,6},{5,7},{6,4},{7,5},{8,10},{9,11},{10,... | collective-permute-start | bytes 12296 | tf_op jit(solution)/shard_map/ppermute | solution.py:336
  113.7 1.5 %collective-permute-done.30.r2 = f32[16,64]{1,0:T(8,128)S(1)} collective-permute-done((f32[16,64]{1,0:T(8,128)S(1)}, f32[16,64]{1,0:T(8,128)S(1)}, u32[]{:S(2)}, u32[]{:S(2)}) %collective-permute-start.30) | collective-permute-done | bytes 4128 | tf_op jit(solution)/shard_map/ppermute | solution.py:336
  115.2 1.9 %collective-permute-done.31.r3 = f32[16,64]{1,0:T(8,128)S(1)} collective-permute-done((f32[16,64]{1,0:T(8,128)S(1)}, f32[16,64]{1,0:T(8,128)S(1)}, u32[]{:S(2)}, u32[]{:S(2)}) %collective-permute-start.31) | collective-permute-done | bytes 4128 | tf_op jit(solution)/shard_map/ppermute | solution.py:336
  (57 shorter events, 17.2 us)
Async XLA Ops:
  2.6 38.9 %collective-permute-start.2 = (f32[1536,256]{1,0:T(8,128)S(1)}, f32[1536,256]{1,0:T(8,128)S(1)}, u32[]{:S(2)}, u32[]{:S(2)}) collective-permute-start(f32[1536,256]{1,0:T(8,128)S(1)} %get-tuple-element.44), channel_id=1, source_target_pairs={{0,1},{1,2},{2,3},{3,0},{4,5},{5,6},{6,7},{7,4},{8,9},{9,10},{10,1... | collective-permute-start | bytes 4718600 | tf_op jit(solution)/shard_map/ppermute | solution.py:336
  4.6 36.9 %collective-permute-start.3 = (f32[1536,256]{1,0:T(8,128)S(1)}, f32[1536,256]{1,0:T(8,128)S(1)}, u32[]{:S(2)}, u32[]{:S(2)}) collective-permute-start(f32[1536,256]{1,0:T(8,128)S(1)} %get-tuple-element.45), channel_id=1, source_target_pairs={{0,3},{1,0},{2,1},{3,2},{4,7},{5,4},{6,5},{7,6},{8,11},{9,8},{10,9... | collective-permute-start | bytes 4718600 | tf_op jit(solution)/shard_map/ppermute | solution.py:336
  31.0 10.1 %collective-permute-start.1 = (f32[16,256]{1,0:T(8,128)S(1)}, f32[16,256]{1,0:T(8,128)S(1)}, u32[]{:S(2)}, u32[]{:S(2)}) collective-permute-start(f32[16,256]{1,0:T(8,128)S(1)} %shard_map.65.info.i0), channel_id=1, source_target_pairs={{0,3},{1,0},{2,1},{3,2},{4,7},{5,4},{6,5},{7,6},{8,11},{9,8},{10,9... | collective-permute-start | bytes 49160 | tf_op jit(solution)/shard_map/ppermute | solution.py:336
  33.0 8.4 %collective-permute-start = (f32[16,256]{1,0:T(8,128)S(1)}, f32[16,256]{1,0:T(8,128)S(1)}, u32[]{:S(2)}, u32[]{:S(2)}) collective-permute-start(f32[16,256]{1,0:T(8,128)S(1)} %shard_map.65.info.i0), channel_id=1, source_target_pairs={{0,1},{1,2},{2,3},{3,0},{4,5},{5,6},{6,7},{7,4},{8,9},{9,10},{10,1... | collective-permute-start | bytes 49160 | tf_op jit(solution)/shard_map/ppermute | solution.py:336
  33.1 9.8 %collective-permute-start.4 = (f32[16,256]{1,0:T(8,128)S(1)}, f32[16,256]{1,0:T(8,128)S(1)}, u32[]{:S(2)}, u32[]{:S(2)}) collective-permute-start(f32[16,256]{1,0:T(8,128)S(1)} %shard_map.65.info.i0), channel_id=1, source_target_pairs={{0,2},{1,3},{2,0},{3,1},{4,6},{5,7},{6,4},{7,5},{8,10},{9,11},{10,... | collective-permute-start | bytes 49160 | tf_op jit(solution)/shard_map/ppermute | solution.py:336
  43.0 15.3 %collective-permute-start.5 = (f32[512,256]{1,0:T(8,128)S(1)}, f32[512,256]{1,0:T(8,128)S(1)}, u32[]{:S(2)}, u32[]{:S(2)}) collective-permute-start(f32[512,256]{1,0:T(8,128)S(1)} %get-tuple-element.55), channel_id=1, source_target_pairs={{0,1},{1,2},{2,3},{3,0},{4,5},{5,6},{6,7},{7,4},{8,9},{9,10},{10,1... | collective-permute-start | bytes 1572872 | tf_op jit(solution)/shard_map/ppermute | solution.py:336
  44.1 14.2 %collective-permute-start.6 = (f32[512,256]{1,0:T(8,128)S(1)}, f32[512,256]{1,0:T(8,128)S(1)}, u32[]{:S(2)}, u32[]{:S(2)}) collective-permute-start(f32[512,256]{1,0:T(8,128)S(1)} %get-tuple-element.56), channel_id=1, source_target_pairs={{0,3},{1,0},{2,1},{3,2},{4,7},{5,4},{6,5},{7,6},{8,11},{9,8},{10,9... | collective-permute-start | bytes 1572872 | tf_op jit(solution)/shard_map/ppermute | solution.py:336
  47.8 9.4 %collective-permute-start.7 = (f32[16,256]{1,0:T(8,128)S(1)}, f32[16,256]{1,0:T(8,128)S(1)}, u32[]{:S(2)}, u32[]{:S(2)}) collective-permute-start(f32[16,256]{1,0:T(8,128)S(1)} %get-tuple-element.62), channel_id=1, source_target_pairs={{0,1},{1,2},{2,3},{3,0},{4,5},{5,6},{6,7},{7,4},{8,9},{9,10},{10,1... | collective-permute-start | bytes 49160 | tf_op jit(solution)/shard_map/ppermute | solution.py:336
  47.8 10.5 %collective-permute-start.8 = (f32[16,256]{1,0:T(8,128)S(1)}, f32[16,256]{1,0:T(8,128)S(1)}, u32[]{:S(2)}, u32[]{:S(2)}) collective-permute-start(f32[16,256]{1,0:T(8,128)S(1)} %get-tuple-element.63), channel_id=1, source_target_pairs={{0,2},{1,3},{2,0},{3,1},{4,6},{5,7},{6,4},{7,5},{8,10},{9,11},{10,... | collective-permute-start | bytes 49160 | tf_op jit(solution)/shard_map/ppermute | solution.py:336
  50.6 7.7 %collective-permute-start.9 = (f32[16,256]{1,0:T(8,128)S(1)}, f32[16,256]{1,0:T(8,128)S(1)}, u32[]{:S(2)}, u32[]{:S(2)}) collective-permute-start(f32[16,256]{1,0:T(8,128)S(1)} %get-tuple-element.64), channel_id=1, source_target_pairs={{0,3},{1,0},{2,1},{3,2},{4,7},{5,4},{6,5},{7,6},{8,11},{9,8},{10,9... | collective-permute-start | bytes 49160 | tf_op jit(solution)/shard_map/ppermute | solution.py:336
  62.0 7.8 %collective-permute-start.10 = (f32[136,256]{1,0:T(8,128)S(1)}, f32[136,256]{1,0:T(8,128)S(1)}, u32[]{:S(2)}, u32[]{:S(2)}) collective-permute-start(f32[136,256]{1,0:T(8,128)S(1)} %get-tuple-element.65.t0), channel_id=1, source_target_pairs={{0,1},{1,2},{2,3},{3,0},{4,5},{5,6},{6,7},{7,4},{8,9},{9,10},{10,1... | collective-permute-start | bytes 417800 | tf_op jit(solution)/shard_map/ppermute | solution.py:336
  63.0 6.7 %collective-permute-start.13 = (f32[136,256]{1,0:T(8,128)S(1)}, f32[136,256]{1,0:T(8,128)S(1)}, u32[]{:S(2)}, u32[]{:S(2)}) collective-permute-start(f32[136,256]{1,0:T(8,128)S(1)} %get-tuple-element.66.l0), channel_id=1, source_target_pairs={{0,3},{1,0},{2,1},{3,2},{4,7},{5,4},{6,5},{7,6},{8,11},{9,8},{10,9... | collective-permute-start | bytes 417800 | tf_op jit(solution)/shard_map/ppermute | solution.py:336
  65.3 7.7 %collective-permute-start.15 = (f32[136,256]{1,0:T(8,128)S(1)}, f32[136,256]{1,0:T(8,128)S(1)}, u32[]{:S(2)}, u32[]{:S(2)}) collective-permute-start(f32[136,256]{1,0:T(8,128)S(1)} %get-tuple-element.65.t0), channel_id=1, source_target_pairs={{0,3},{1,0},{2,1},{3,2},{4,7},{5,4},{6,5},{7,6},{8,11},{9,8},{10,9... | collective-permute-start | bytes 417800 | tf_op jit(solution)/shard_map/ppermute | solution.py:336
  66.1 6.9 %collective-permute-start.11 = (f32[136,256]{1,0:T(8,128)S(1)}, f32[136,256]{1,0:T(8,128)S(1)}, u32[]{:S(2)}, u32[]{:S(2)}) collective-permute-start(f32[136,256]{1,0:T(8,128)S(1)} %get-tuple-element.66.l0), channel_id=1, source_target_pairs={{0,1},{1,2},{2,3},{3,0},{4,5},{5,6},{6,7},{7,4},{8,9},{9,10},{10,1... | collective-permute-start | bytes 417800 | tf_op jit(solution)/shard_map/ppermute | solution.py:336
  69.8 6.3 %collective-permute-start.12 = (f32[136,256]{1,0:T(8,128)S(1)}, f32[136,256]{1,0:T(8,128)S(1)}, u32[]{:S(2)}, u32[]{:S(2)}) collective-permute-start(f32[136,256]{1,0:T(8,128)S(1)} %collective-permute-done.10.t1), channel_id=1, source_target_pairs={{0,1},{1,2},{2,3},{3,0},{4,5},{5,6},{6,7},{7,4},{8,9},{9,10},{10,1... | collective-permute-start | bytes 417800 | tf_op jit(solution)/shard_map/ppermute | solution.py:336
  69.8 6.3 %collective-permute-start.14 = (f32[136,256]{1,0:T(8,128)S(1)}, f32[136,256]{1,0:T(8,128)S(1)}, u32[]{:S(2)}, u32[]{:S(2)}) collective-permute-start(f32[136,256]{1,0:T(8,128)S(1)} %collective-permute-done.13.l3), channel_id=1, source_target_pairs={{0,3},{1,0},{2,1},{3,2},{4,7},{5,4},{6,5},{7,6},{8,11},{9,8},{10,9... | collective-permute-start | bytes 417800 | tf_op jit(solution)/shard_map/ppermute | solution.py:336
  77.5 1.6 %collective-permute-start.16 = (f32[272,256]{1,0:T(8,128)S(1)}, f32[272,256]{1,0:T(8,128)S(1)}, u32[]{:S(2)}, u32[]{:S(2)}) collective-permute-start(f32[272,256]{1,0:T(8,128)S(1)} %get-tuple-element.67.own), channel_id=1, source_target_pairs={{0,4},{4,0},{8,12},{12,8},{16,20},{20,16},{24,28},{28,24},{32,36},... | collective-permute-start | bytes 835592 | tf_op jit(solution)/shard_map/ppermute | solution.py:401
  80.0 7.2 %collective-permute-start.19 = (f32[136,256]{1,0:T(8,128)S(1)}, f32[136,256]{1,0:T(8,128)S(1)}, u32[]{:S(2)}, u32[]{:S(2)}) collective-permute-start(f32[136,256]{1,0:T(8,128)S(1)} %get-tuple-element.70), channel_id=1, source_target_pairs={{0,8},{4,12},{8,16},{12,20},{16,24},{20,28},{24,0},{28,4},{32,40},... | collective-permute-start | bytes 417800 | tf_op jit(solution)/shard_map/ppermute | solution.py:406
  81.7 9.7 %collective-permute-start.18 = (f32[136,256]{1,0:T(8,128)S(1)}, f32[136,256]{1,0:T(8,128)S(1)}, u32[]{:S(2)}, u32[]{:S(2)}) collective-permute-start(f32[136,256]{1,0:T(8,128)S(1)} %get-tuple-element.70), channel_id=1, source_target_pairs={{0,16},{4,20},{8,24},{12,28},{16,0},{20,4},{24,8},{28,12},{32,48},... | collective-permute-start | bytes 417800 | tf_op jit(solution)/shard_map/ppermute | solution.py:406
  84.6 6.8 %collective-permute-start.17 = (f32[136,256]{1,0:T(8,128)S(1)}, f32[136,256]{1,0:T(8,128)S(1)}, u32[]{:S(2)}, u32[]{:S(2)}) collective-permute-start(f32[136,256]{1,0:T(8,128)S(1)} %get-tuple-element.70), channel_id=1, source_target_pairs={{0,24},{4,28},{8,0},{12,4},{16,8},{20,12},{24,16},{28,20},{32,56},... | collective-permute-start | bytes 417800 | tf_op jit(solution)/shard_map/ppermute | solution.py:406
  87.2 4.7 %collective-permute-start.22 = (f32[136,256]{1,0:T(8,128)S(1)}, f32[136,256]{1,0:T(8,128)S(1)}, u32[]{:S(2)}, u32[]{:S(2)}) collective-permute-start(f32[136,256]{1,0:T(8,128)S(1)} %collective-permute-done.19.h3), channel_id=1, source_target_pairs={{0,4},{4,0},{8,12},{12,8},{16,20},{20,16},{24,28},{28,24},{32,36},... | collective-permute-start | bytes 417800 | tf_op jit(solution)/shard_map/ppermute | solution.py:401
  91.4 1.4 %collective-permute-start.21 = (f32[136,256]{1,0:T(8,128)S(1)}, f32[136,256]{1,0:T(8,128)S(1)}, u32[]{:S(2)}, u32[]{:S(2)}) collective-permute-start(f32[136,256]{1,0:T(8,128)S(1)} %collective-permute-done.18.h2), channel_id=1, source_target_pairs={{0,4},{4,0},{8,12},{12,8},{16,20},{20,16},{24,28},{28,24},{32,36},... | collective-permute-start | bytes 417800 | tf_op jit(solution)/shard_map/ppermute | solution.py:401
  91.4 1.6 %collective-permute-start.20 = (f32[136,256]{1,0:T(8,128)S(1)}, f32[136,256]{1,0:T(8,128)S(1)}, u32[]{:S(2)}, u32[]{:S(2)}) collective-permute-start(f32[136,256]{1,0:T(8,128)S(1)} %collective-permute-done.17.h1), channel_id=1, source_target_pairs={{0,4},{4,0},{8,12},{12,8},{16,20},{20,16},{24,28},{28,24},{32,36},... | collective-permute-start | bytes 417800 | tf_op jit(solution)/shard_map/ppermute | solution.py:401
  94.2 6.6 %collective-permute-start.25 = (f32[136,256]{1,0:T(8,128)S(1)}, f32[136,256]{1,0:T(8,128)S(1)}, u32[]{:S(2)}, u32[]{:S(2)}) collective-permute-start(f32[136,256]{1,0:T(8,128)S(1)} %get-tuple-element.71), channel_id=1, source_target_pairs={{0,32},{4,36},{8,40},{12,44},{16,48},{20,52},{24,56},{28,60},{32,6... | collective-permute-start | bytes 417800 | tf_op jit(solution)/shard_map/ppermute | solution.py:406
  94.8 8.0 %collective-permute-start.24 = (f32[136,256]{1,0:T(8,128)S(1)}, f32[136,256]{1,0:T(8,128)S(1)}, u32[]{:S(2)}, u32[]{:S(2)}) collective-permute-start(f32[136,256]{1,0:T(8,128)S(1)} %get-tuple-element.71), channel_id=1, source_target_pairs={{0,64},{4,68},{8,72},{12,76},{16,80},{20,84},{24,88},{28,92},{32,9... | collective-permute-start | bytes 417800 | tf_op jit(solution)/shard_map/ppermute | solution.py:406
  97.2 7.7 %collective-permute-start.23 = (f32[136,256]{1,0:T(8,128)S(1)}, f32[136,256]{1,0:T(8,128)S(1)}, u32[]{:S(2)}, u32[]{:S(2)}) collective-permute-start(f32[136,256]{1,0:T(8,128)S(1)} %get-tuple-element.71), channel_id=1, source_target_pairs={{0,96},{4,100},{8,104},{12,108},{16,112},{20,116},{24,120},{28,124... | collective-permute-start | bytes 417800 | tf_op jit(solution)/shard_map/ppermute | solution.py:406
  100.8 4.9 %collective-permute-start.28 = (f32[136,256]{1,0:T(8,128)S(1)}, f32[136,256]{1,0:T(8,128)S(1)}, u32[]{:S(2)}, u32[]{:S(2)}) collective-permute-start(f32[136,256]{1,0:T(8,128)S(1)} %collective-permute-done.25.h3), channel_id=1, source_target_pairs={{0,4},{4,0},{8,12},{12,8},{16,20},{20,16},{24,28},{28,24},{32,36},... | collective-permute-start | bytes 417800 | tf_op jit(solution)/shard_map/ppermute | solution.py:401
  102.8 2.9 %collective-permute-start.27 = (f32[136,256]{1,0:T(8,128)S(1)}, f32[136,256]{1,0:T(8,128)S(1)}, u32[]{:S(2)}, u32[]{:S(2)}) collective-permute-start(f32[136,256]{1,0:T(8,128)S(1)} %collective-permute-done.24.h2), channel_id=1, source_target_pairs={{0,4},{4,0},{8,12},{12,8},{16,20},{20,16},{24,28},{28,24},{32,36},... | collective-permute-start | bytes 417800 | tf_op jit(solution)/shard_map/ppermute | solution.py:401
  104.9 1.4 %collective-permute-start.26 = (f32[136,256]{1,0:T(8,128)S(1)}, f32[136,256]{1,0:T(8,128)S(1)}, u32[]{:S(2)}, u32[]{:S(2)}) collective-permute-start(f32[136,256]{1,0:T(8,128)S(1)} %collective-permute-done.23.h1), channel_id=1, source_target_pairs={{0,4},{4,0},{8,12},{12,8},{16,20},{20,16},{24,28},{28,24},{32,36},... | collective-permute-start | bytes 417800 | tf_op jit(solution)/shard_map/ppermute | solution.py:401
  108.5 5.2 %collective-permute-start.29 = (f32[16,64]{1,0:T(8,128)S(1)}, f32[16,64]{1,0:T(8,128)S(1)}, u32[]{:S(2)}, u32[]{:S(2)}) collective-permute-start(f32[16,64]{1,0:T(8,128)S(1)} %get-tuple-element.76), channel_id=1, source_target_pairs={{0,1},{1,2},{2,3},{3,0},{4,5},{5,6},{6,7},{7,4},{8,9},{9,10},{10,1... | collective-permute-start | bytes 12296 | tf_op jit(solution)/shard_map/ppermute | solution.py:336
  108.5 6.7 %collective-permute-start.30 = (f32[16,64]{1,0:T(8,128)S(1)}, f32[16,64]{1,0:T(8,128)S(1)}, u32[]{:S(2)}, u32[]{:S(2)}) collective-permute-start(f32[16,64]{1,0:T(8,128)S(1)} %get-tuple-element.77), channel_id=1, source_target_pairs={{0,2},{1,3},{2,0},{3,1},{4,6},{5,7},{6,4},{7,5},{8,10},{9,11},{10,... | collective-permute-start | bytes 12296 | tf_op jit(solution)/shard_map/ppermute | solution.py:336
  113.5 3.7 %collective-permute-start.31 = (f32[16,64]{1,0:T(8,128)S(1)}, f32[16,64]{1,0:T(8,128)S(1)}, u32[]{:S(2)}, u32[]{:S(2)}) collective-permute-start(f32[16,64]{1,0:T(8,128)S(1)} %get-tuple-element.78), channel_id=1, source_target_pairs={{0,3},{1,0},{2,1},{3,2},{4,7},{5,4},{6,5},{7,6},{8,11},{9,8},{10,9... | collective-permute-start | bytes 12296 | tf_op jit(solution)/shard_map/ppermute | solution.py:336
  (4 other events, 68.3 us)

commit v11 on v10

--- a/solution.py
+++ b/solution.py
@@ -15,12 +15,14 @@
 R = N + PAD
 Z, C, Y, X = range(4)
 HALF = R // 2
+UPPER = 72
 ROWS = 4
 SUB = 16
 SEG = 4
 HALF_SUB = SUB // 2
 Z, C, Y, X = range(4)
 HALF = R // 2
+UPPER = 72
 ROWS = 4
 SUB = 16
 CHUNKS = ((5, 5), (3, 3))
@@ -199,26 +201,31 @@
     total[...] = combine(pos, m_s, before)
 
 
-def half_rows(c):
-    return pl.ds(pl.multiple_of(c * HALF, 8), HALF)
+def cut_half(c, whole, upper, lower):
+    at = pl.multiple_of(c * HALF, 8)
+    upper[...] = whole[pl.ds(at, UPPER), :]
+    lower[...] = whole[pl.ds(at + UPPER, HALF - UPPER), :]
 
 
 def join(pos, c, mine, others, m_s):
-    for d, m, o in zip((3, 2, 1), mine, others):
-        slot = lax.rem(pos - d + 4, 4)
-        m_s[slot, half_rows(c), :] = m[...]
-        m_s[slot, half_rows(1 - c), :] = o[...]
-
-
-def plane_kernel(idx, own, h1, h2, h3, o1, o2, o3, half, before, m_s, all_s):
+    for side, parts in ((c, mine), (1 - c, others)):
+        at = pl.multiple_of(side * HALF, 8)
+        for d, (u, l) in zip((1, 3, 2), zip(parts[::2], parts[1::2])):
+            slot = lax.rem(pos - d + 4, 4)
+            m_s[slot, pl.ds(at, UPPER), :] = u[...]
+            m_s[slot, pl.ds(at + UPPER, HALF - UPPER), :] = l[...]
+
+
+def plane_kernel(idx, own, *refs):
+    mine, others, (upper, lower, before, m_s, all_s) = refs[:6], refs[6:12], refs[12:]
     pos, c = idx[Y], idx[C]
     m_s[pos] = own[...]
-    join(pos, c, (h1, h2, h3), (o1, o2, o3), m_s)
+    join(pos, c, mine, others, m_s)
     all_s[...] = combine(pos, m_s, before)
-    half[...] = all_s[half_rows(c), :]
-
-
-def pair_kernel(idx, own, other, before_in, total, half, before):
+    cut_half(c, all_s, upper, lower)
+
+
+def pair_kernel(idx, own, other, before_in, total, upper, lower, before):
     c = idx[C]
     swap = c == 1
 
@@ -232,16 +239,17 @@
         total[...] = then(own[...], other[...])
         before[...] = before_in[...]
 
-    half[...] = total[half_rows(c), :]
+    cut_half(c, total, upper, lower)
 
 
 def fold_kernel(idx, first, second, out):
     out[...] = then(first[...], second[...])
 
 
-def states_kernel(idx, prior, h1, h2, h3, g1, g2, g3, before, pref, o0, o1, o2, o3, st_s, m_s, s_s):
+def states_kernel(idx, prior, *refs):
+    mine, others, (before, pref, o0, o1, o2, o3, st_s, m_s, s_s) = refs[:6], refs[6:12], refs[12:]
     z, pos = idx[Z], idx[X]
-    join(pos, idx[C], (h1, h2, h3), (g1, g2, g3), m_s)
+    join(pos, idx[C], mine, others, m_s)
     s_s[...] = jnp.where(lax.broadcasted_iota(jnp.int32, (PAD, N), 0) == 0, prior[...], 0.0)
     for i in range(3):
 
@@ -325,7 +333,7 @@
         o[:, 128:] = jnp.zeros((16, 128), F32)
 
 
-def place_kernel(idx, r0, r1, r2, r3, out):
+def place_kernel(idx, r0, r2, r1, r3, out):
     z = idx[Z]
     for d, r in enumerate((r0, r1, r2, r3)):
         slot = lax.rem(z - d + ROWS, ROWS)
@@ -400,21 +408,25 @@
     def other_core(m):
         return lax.ppermute(m, "tm", [(i, i ^ 1) for i in range(32)])
 
-    def gathered(half, stride):
+    def gathered(upper, lower, stride):
         n = 4 * stride
-        got = [
-            lax.ppermute(half, "tm", [(i, i - i % n + (i + d * stride) % n) for i in range(32)]) for d in (3, 2, 1)
-        ]
+
+        def along(m, d):
+            return lax.ppermute(m, "tm", [(i, i - i % n + (i + d * stride) % n) for i in range(32)])
+
+        prev_upper, after_lower = along(upper, 1), along(lower, 3)
+        got = prev_upper, along(lower, 1), along(upper, 3), after_lower, along(prev_upper, 1), along(after_lower, 3)
         return *got, *[other_core(g) for g in got]
 
-    column, half, before = call(
-        pair_kernel, [(R, N), (HALF, N), (R, N)], idx, (block, other_core(block), before)
-    )
-    half, ybefore = call(
+    quarters = [(UPPER, N), (HALF - UPPER, N)]
+    column, *cut, before = call(
+        pair_kernel, [(R, N), *quarters, (R, N)], idx, (block, other_core(block), before)
+    )
+    *cut, ybefore = call(
         plane_kernel,
-        [(HALF, N), (R, N)],
-        idx,
-        (column, *gathered(half, 2)),
+        [*quarters, (R, N)],
+        idx,
+        (column, *gathered(*cut, 2)),
         [pltpu.VMEM((4, R, N), F32), pltpu.VMEM((R, N), F32)],
     )
     (before,) = call(fold_kernel, [(R, N)], idx, (ybefore, before))
@@ -422,10 +434,10 @@
         states_kernel,
         [(SUB, 64)] * 4,
         idx,
-        (prior, *gathered(half, 8), before, pref),
+        (prior, *gathered(*cut, 8), before, pref),
         [pltpu.VMEM((ROWS, SUB, 64), F32), pltpu.VMEM((4, R, N), F32), pltpu.VMEM((PAD, N), F32)],
     )
-    got = [outs[0], *along_rows(outs[1:])]
+    got = [outs[0], along_row(outs[2], 2), along_row(outs[1], 1), along_row(outs[3], 3)]
     return pl.pallas_call(
         place_kernel,
         out_shape=jax.ShapeDtypeStruct((64, 64), F32),

time: 119 us -> 121 us (1.017)
  starting transfers between devices: 38.1 us -> 45.8 us
  waiting for transfers between devices: 36.5 us -> 30.8 us
    ppermute x6 -> x12, starting transfers between devices: 8.87 us -> 15.3 us  [along(): lax.ppermute(m, 'tm', [(i, i - i % n + (i + d * stride) % n) for i in ran...]
    ppermute x6 -> x12, waiting for transfers between devices: 13.1 us -> 7.98 us  [along(): lax.ppermute(m, 'tm', [(i, i - i % n + (i + d * stride) % n) for i in ran...]
    ppermute x7 -> x13, starting transfers between devices: 0.61 us -> 2.16 us  [other_core(): return lax.ppermute(m, 'tm', [(i, i ^ 1) for i in range(32)])]
    ppermute x7 -> x13, waiting for transfers between devices: 3.09 us -> 2.85 us  [other_core(): return lax.ppermute(m, 'tm', [(i, i ^ 1) for i in range(32)])]
  transfers between devices with their start and end apart: 32 -> 44, of which waited for: 19 -> 19; matrix products, arithmetic and copies ran while one was open for 0% -> 0% of each run, Pallas kernels for 11% -> 11%
where the time goes in v11:
time: 121 us; the launch traced here: 120 us
  starting transfers between devices  45.8 us (38%)
  waiting for transfers between devices  30.8 us (25%)
  Pallas kernels  26.7 us (22%)
  blocking collectives  16.7 us (14%)
    ppermute x19, starting transfers between devices, along_row(): return lax.ppermute(x, 'row', [(i, (i + d) % ROWS) for i in range(ROWS)])  28.4 us
    ppermute x19, waiting for transfers between devices, along_row(): return lax.ppermute(x, 'row', [(i, (i + d) % ROWS) for i in range(ROWS)])  19.9 us
    pallas_call x11, Pallas kernels, call(): pl.pallas_call(kernel, out_shape=[pltpu.VMEM(s, t) for s, t in outs], in_...  18.7 us
    all_to_all x1, blocking collectives, shards(): sums = lax.all_to_all(partial, 'tm', 0, 0, tiled=True).reshape(32, 16, N)  16.7 us
    ppermute x12, starting transfers between devices, along(): lax.ppermute(m, 'tm', [(i, i - i % n + (i + d * stride) % n) for i in ran...  15.3 us
    ppermute x12, waiting for transfers between devices, along(): lax.ppermute(m, 'tm', [(i, i - i % n + (i + d * stride) % n) for i in ran...  7.98 us
    pallas_call x1, Pallas kernels, binned(): pl.pallas_call(bin_kernel, out_shape=jax.ShapeDtypeStruct((n_bins // 4, N...  6.9 us
    ppermute x13, waiting for transfers between devices, other_core(): return lax.ppermute(m, 'tm', [(i, i ^ 1) for i in range(32)])  2.85 us
  transfers between devices with their start and end apart: 44, of which 19 were waited for; matrix products, arithmetic and copies ran while one was open for 0% of the time, Pallas kernels for 11%

profile of v11, /device:TPU:6, one launch (start us, length us, event | category | flops | bytes accessed | tf_op | source)
XLA Modules:
  0.0 120.4 jit_solution(8228452832020100667)
XLA Ops:
  0.1 2.5 %shard_map.67 = (f32[1536,256]{1,0:T(8,128)S(1)}, f32[1536,256]{1,0:T(8,128)S(1)}) custom-call(s32[4]{0:T(128)S(1)} %pad_add_fusion.idx, f32[4096,256]{1,0:T(8,128)} %bitcast.14), custom_call_target="tpu_custom_call" | custom-call | tf_op jit(solution)/shard_map/pallas_call | solution.py:77
  2.6 2.0 %collective-permute-start.2 = (f32[1536,256]{1,0:T(8,128)S(1)}, f32[1536,256]{1,0:T(8,128)S(1)}, u32[]{:S(2)}, u32[]{:S(2)}) collective-permute-start(f32[1536,256]{1,0:T(8,128)S(1)} %get-tuple-element.46), channel_id=1, source_target_pairs={{0,1},{1,2},{2,3},{3,0},{4,5},{5,6},{6,7},{7,4},{8,9},{9,10},{10,1... | collective-permute-start | bytes 4718600 | tf_op jit(solution)/shard_map/ppermute | solution.py:344
  4.6 2.2 %collective-permute-start.3 = (f32[1536,256]{1,0:T(8,128)S(1)}, f32[1536,256]{1,0:T(8,128)S(1)}, u32[]{:S(2)}, u32[]{:S(2)}) collective-permute-start(f32[1536,256]{1,0:T(8,128)S(1)} %get-tuple-element.47), channel_id=1, source_target_pairs={{0,3},{1,0},{2,1},{3,2},{4,7},{5,4},{6,5},{7,6},{8,11},{9,8},{10,9... | collective-permute-start | bytes 4718600 | tf_op jit(solution)/shard_map/ppermute | solution.py:344
  6.8 6.9 %shard_map.64 = f32[512,256]{1,0:T(8,128)S(1)} custom-call(s32[1,4096]{1,0:T(1,128)S(1)} %bitcast.12, f32[64,4096]{1,0:T(8,128)S(1)} %bitcast.11), custom_call_target="tpu_custom_call" | custom-call | tf_op jit(solution)/shard_map/pallas_call | solution.py:122
  13.7 16.7 %all_to_all.9.sums = f32[32,16,256]{2,1,0:T(8,128)S(1)} all-to-all(f32[32,16,256]{2,1,0:T(8,128)S(1)} %bitcast.10), channel_id=1, replica_groups=mesh['tm'=32,'row'=4] {'tm'}, dimensions={0} | all-to-all | bytes 1048576 | tf_op jit(solution)/shard_map/all_to_all | solution.py:364
  31.0 2.0 %collective-permute-start.1 = (f32[16,256]{1,0:T(8,128)S(1)}, f32[16,256]{1,0:T(8,128)S(1)}, u32[]{:S(2)}, u32[]{:S(2)}) collective-permute-start(f32[16,256]{1,0:T(8,128)S(1)} %shard_map.65.info.i0), channel_id=1, source_target_pairs={{0,3},{1,0},{2,1},{3,2},{4,7},{5,4},{6,5},{7,6},{8,11},{9,8},{10,9... | collective-permute-start | bytes 49160 | tf_op jit(solution)/shard_map/ppermute | solution.py:344
  33.1 1.8 %collective-permute-start.4 = (f32[16,256]{1,0:T(8,128)S(1)}, f32[16,256]{1,0:T(8,128)S(1)}, u32[]{:S(2)}, u32[]{:S(2)}) collective-permute-start(f32[16,256]{1,0:T(8,128)S(1)} %shard_map.65.info.i0), channel_id=1, source_target_pairs={{0,2},{1,3},{2,0},{3,1},{4,6},{5,7},{6,4},{7,5},{8,10},{9,11},{10,... | collective-permute-start | bytes 49160 | tf_op jit(solution)/shard_map/ppermute | solution.py:344
  34.9 3.0 %shard_map.66 = (f32[64,64,256]{2,1,0:T(8,128)S(1)}, f32[1024,256]{1,0:T(8,128)S(1)}) custom-call(s32[4]{0:T(128)S(1)} %pad_add_fusion.idx, f32[64,64,256]{2,1,0:T(8,128)} %gains.1, f32[4096,256]{1,0:T(8,128)} %bitcast.15, f32[16,256]{1,0:T(8,128)S(1)} %shard_map.65.info.i0), custom_call_target="tpu_custom_call" | custom-call | tf_op jit(solution)/shard_map/pallas_call | solution.py:77
  38.0 3.2 %collective-permute-done.1.r3 = f32[16,256]{1,0:T(8,128)S(1)} collective-permute-done((f32[16,256]{1,0:T(8,128)S(1)}, f32[16,256]{1,0:T(8,128)S(1)}, u32[]{:S(2)}, u32[]{:S(2)}) %collective-permute-start.1) | collective-permute-done | bytes 16416 | tf_op jit(solution)/shard_map/ppermute | solution.py:344
  44.1 2.1 %collective-permute-start.6 = (f32[512,256]{1,0:T(8,128)S(1)}, f32[512,256]{1,0:T(8,128)S(1)}, u32[]{:S(2)}, u32[]{:S(2)}) collective-permute-start(f32[512,256]{1,0:T(8,128)S(1)} %get-tuple-element.58), channel_id=1, source_target_pairs={{0,3},{1,0},{2,1},{3,2},{4,7},{5,4},{6,5},{7,6},{8,11},{9,8},{10,9... | collective-permute-start | bytes 1572872 | tf_op jit(solution)/shard_map/ppermute | solution.py:344
  46.2 1.6 %shard_map.69 = (f32[16,256]{1,0:T(8,128)S(1)}, f32[16,256]{1,0:T(8,128)S(1)}, f32[16,256]{1,0:T(8,128)S(1)}, f32[16,256]{1,0:T(8,128)S(1)}) custom-call(s32[4]{0:T(128)S(1)} %pad_add_fusion.idx, f32[64,64,256]{2,1,0:T(8,128)S(1)} %get-tuple-element.59.g, f32[16,256]{1,0:T(8,128)S(1)} %shard_map.65.info.i0, f32[16,256]{1,0:T(8,128)S(1)} %collective-permute-done.r1, ...), custom_call_target="tpu_custom_call" | custom-call | tf_op jit(solution)/shard_map/pallas_call | solution.py:77
  47.8 2.8 %collective-permute-start.8 = (f32[16,256]{1,0:T(8,128)S(1)}, f32[16,256]{1,0:T(8,128)S(1)}, u32[]{:S(2)}, u32[]{:S(2)}) collective-permute-start(f32[16,256]{1,0:T(8,128)S(1)} %get-tuple-element.65), channel_id=1, source_target_pairs={{0,2},{1,3},{2,0},{3,1},{4,6},{5,7},{6,4},{7,5},{8,10},{9,11},{10,... | collective-permute-start | bytes 49160 | tf_op jit(solution)/shard_map/ppermute | solution.py:344
  51.5 5.7 %collective-permute-done.7.b1 = f32[16,256]{1,0:T(8,128)S(1)} collective-permute-done((f32[16,256]{1,0:T(8,128)S(1)}, f32[16,256]{1,0:T(8,128)S(1)}, u32[]{:S(2)}, u32[]{:S(2)}) %collective-permute-start.7) | collective-permute-done | bytes 16416 | tf_op jit(solution)/shard_map/ppermute | solution.py:344
  58.3 3.7 %shard_map.70 = (f32[16,272,256]{2,1,0:T(8,128)S(1)}, f32[136,256]{1,0:T(8,128)S(1)}, f32[136,256]{1,0:T(8,128)S(1)}) custom-call(s32[4]{0:T(128)S(1)} %pad_add_fusion.idx, f32[1024,256]{1,0:T(8,128)S(1)} %get-tuple-element.50.own, f32[1536,256]{1,0:T(8,128)S(1)} %collective-permute-done.2.prev, f32[1536,256]{1,0:T(8,128)S(1)} %collective-permute-done.3.after, ...), custom_call_target="tpu_custom_call" | custom-call | tf_op jit(solution)/shard_map/pallas_call | solution.py:77
  63.0 2.3 %collective-permute-start.13 = (f32[136,256]{1,0:T(8,128)S(1)}, f32[136,256]{1,0:T(8,128)S(1)}, u32[]{:S(2)}, u32[]{:S(2)}) collective-permute-start(f32[136,256]{1,0:T(8,128)S(1)} %get-tuple-element.68.l0), channel_id=1, source_target_pairs={{0,3},{1,0},{2,1},{3,2},{4,7},{5,4},{6,5},{7,6},{8,11},{9,8},{10,9... | collective-permute-start | bytes 417800 | tf_op jit(solution)/shard_map/ppermute | solution.py:344
  67.3 2.4 %collective-permute-done.10.t1 = f32[136,256]{1,0:T(8,128)S(1)} collective-permute-done((f32[136,256]{1,0:T(8,128)S(1)}, f32[136,256]{1,0:T(8,128)S(1)}, u32[]{:S(2)}, u32[]{:S(2)}) %collective-permute-start.10) | collective-permute-done | bytes 139296 | tf_op jit(solution)/shard_map/ppermute | solution.py:344
  69.8 3.2 %collective-permute-start.14 = (f32[136,256]{1,0:T(8,128)S(1)}, f32[136,256]{1,0:T(8,128)S(1)}, u32[]{:S(2)}, u32[]{:S(2)}) collective-permute-start(f32[136,256]{1,0:T(8,128)S(1)} %collective-permute-done.13.l3), channel_id=1, source_target_pairs={{0,3},{1,0},{2,1},{3,2},{4,7},{5,4},{6,5},{7,6},{8,11},{9,8},{10,9... | collective-permute-start | bytes 417800 | tf_op jit(solution)/shard_map/ppermute | solution.py:344
  73.0 3.0 %collective-permute-done.12.t2 = f32[136,256]{1,0:T(8,128)S(1)} collective-permute-done((f32[136,256]{1,0:T(8,128)S(1)}, f32[136,256]{1,0:T(8,128)S(1)}, u32[]{:S(2)}, u32[]{:S(2)}) %collective-permute-start.12) | collective-permute-done | bytes 139296 | tf_op jit(solution)/shard_map/ppermute | solution.py:344
  80.0 1.6 %collective-permute-start.17 = (f32[72,256]{1,0:T(8,128)S(1)}, f32[72,256]{1,0:T(8,128)S(1)}, u32[]{:S(2)}, u32[]{:S(2)}) collective-permute-start(f32[72,256]{1,0:T(8,128)S(1)} %get-tuple-element.72), channel_id=1, source_target_pairs={{0,8},{4,12},{8,16},{12,20},{16,24},{20,28},{24,0},{28,4},{32,40},... | collective-permute-start | bytes 221192 | tf_op jit(solution)/shard_map/ppermute | solution.py:415
  81.7 1.7 %collective-permute-start.20 = (f32[64,256]{1,0:T(8,128)S(1)}, f32[64,256]{1,0:T(8,128)S(1)}, u32[]{:S(2)}, u32[]{:S(2)}) collective-permute-start(f32[64,256]{1,0:T(8,128)S(1)} %get-tuple-element.73), channel_id=1, source_target_pairs={{0,24},{4,28},{8,0},{12,4},{16,8},{20,12},{24,16},{28,20},{32,56},... | collective-permute-start | bytes 196616 | tf_op jit(solution)/shard_map/ppermute | solution.py:415
  83.3 1.8 %collective-permute-start.19 = (f32[72,256]{1,0:T(8,128)S(1)}, f32[72,256]{1,0:T(8,128)S(1)}, u32[]{:S(2)}, u32[]{:S(2)}) collective-permute-start(f32[72,256]{1,0:T(8,128)S(1)} %get-tuple-element.72), channel_id=1, source_target_pairs={{0,24},{4,28},{8,0},{12,4},{16,8},{20,12},{24,16},{28,20},{32,56},... | collective-permute-start | bytes 221192 | tf_op jit(solution)/shard_map/ppermute | solution.py:415
  86.1 1.6 %collective-permute-start.18 = (f32[64,256]{1,0:T(8,128)S(1)}, f32[64,256]{1,0:T(8,128)S(1)}, u32[]{:S(2)}, u32[]{:S(2)}) collective-permute-start(f32[64,256]{1,0:T(8,128)S(1)} %get-tuple-element.73), channel_id=1, source_target_pairs={{0,8},{4,12},{8,16},{12,20},{16,24},{20,28},{24,0},{28,4},{32,40},... | collective-permute-start | bytes 196616 | tf_op jit(solution)/shard_map/ppermute | solution.py:415
  87.7 1.7 %collective-permute-start.22 = (f32[64,256]{1,0:T(8,128)S(1)}, f32[64,256]{1,0:T(8,128)S(1)}, u32[]{:S(2)}, u32[]{:S(2)}) collective-permute-start(f32[64,256]{1,0:T(8,128)S(1)} %collective-permute-done.20.refs_3_), channel_id=1, source_target_pairs={{0,24},{4,28},{8,0},{12,4},{16,8},{20,12},{24,16},{28,20},{32,56},... | collective-permute-start | bytes 196616 | tf_op jit(solution)/shard_map/ppermute | solution.py:415
  89.6 2.5 %collective-permute-done.18.refs_1_ = f32[64,256]{1,0:T(8,128)S(1)} collective-permute-done((f32[64,256]{1,0:T(8,128)S(1)}, f32[64,256]{1,0:T(8,128)S(1)}, u32[]{:S(2)}, u32[]{:S(2)}) %collective-permute-start.18) | collective-permute-done | bytes 65568 | tf_op jit(solution)/shard_map/ppermute | solution.py:415
  98.3 1.7 %collective-permute-done.29.refs_0_ = f32[72,256]{1,0:T(8,128)S(1)} collective-permute-done((f32[72,256]{1,0:T(8,128)S(1)}, f32[72,256]{1,0:T(8,128)S(1)}, u32[]{:S(2)}, u32[]{:S(2)}) %collective-permute-start.29) | collective-permute-done | bytes 73760 | tf_op jit(solution)/shard_map/ppermute | solution.py:415
  99.9 1.7 %collective-permute-start.33 = (f32[72,256]{1,0:T(8,128)S(1)}, f32[72,256]{1,0:T(8,128)S(1)}, u32[]{:S(2)}, u32[]{:S(2)}) collective-permute-start(f32[72,256]{1,0:T(8,128)S(1)} %collective-permute-done.29.refs_0_), channel_id=1, source_target_pairs={{0,32},{4,36},{8,40},{12,44},{16,48},{20,52},{24,56},{28,60},{32,6... | collective-permute-start | bytes 221192 | tf_op jit(solution)/shard_map/ppermute | solution.py:415
  101.9 1.8 %collective-permute-start.34 = (f32[64,256]{1,0:T(8,128)S(1)}, f32[64,256]{1,0:T(8,128)S(1)}, u32[]{:S(2)}, u32[]{:S(2)}) collective-permute-start(f32[64,256]{1,0:T(8,128)S(1)} %collective-permute-done.32.refs_3_), channel_id=1, source_target_pairs={{0,96},{4,100},{8,104},{12,108},{16,112},{20,116},{24,120},{28,124... | collective-permute-start | bytes 196616 | tf_op jit(solution)/shard_map/ppermute | solution.py:415
  103.9 2.0 %collective-permute-done.30.refs_1_ = f32[64,256]{1,0:T(8,128)S(1)} collective-permute-done((f32[64,256]{1,0:T(8,128)S(1)}, f32[64,256]{1,0:T(8,128)S(1)}, u32[]{:S(2)}, u32[]{:S(2)}) %collective-permute-start.30) | collective-permute-done | bytes 65568 | tf_op jit(solution)/shard_map/ppermute | solution.py:415
  108.9 2.2 %shard_map.75 = (f32[16,64]{1,0:T(8,128)S(1)}, f32[16,64]{1,0:T(8,128)S(1)}, f32[16,64]{1,0:T(8,128)S(1)}, f32[16,64]{1,0:T(8,128)S(1)}) custom-call(s32[4]{0:T(128)S(1)} %pad_add_fusion.idx, f32[1,256]{1,0:T(1,128)S(1)} %bitcast.13, f32[72,256]{1,0:T(8,128)S(1)} %collective-permute-done.29.refs_0_, f32[64,256]{1,0:T(8,128)S(1)} %collective-permute-done.30.refs_1_, ...), custom_call_target="tpu_custom_call" | custom-call | tf_op jit(solution)/shard_map/pallas_call | solution.py:77
  111.1 1.6 %collective-permute-start.41 = (f32[16,64]{1,0:T(8,128)S(1)}, f32[16,64]{1,0:T(8,128)S(1)}, u32[]{:S(2)}, u32[]{:S(2)}) collective-permute-start(f32[16,64]{1,0:T(8,128)S(1)} %get-tuple-element.80), channel_id=1, source_target_pairs={{0,2},{1,3},{2,0},{3,1},{4,6},{5,7},{6,4},{7,5},{8,10},{9,11},{10,... | collective-permute-start | bytes 12296 | tf_op jit(solution)/shard_map/ppermute | solution.py:344
  112.7 2.9 %collective-permute-start.42 = (f32[16,64]{1,0:T(8,128)S(1)}, f32[16,64]{1,0:T(8,128)S(1)}, u32[]{:S(2)}, u32[]{:S(2)}) collective-permute-start(f32[16,64]{1,0:T(8,128)S(1)} %get-tuple-element.81), channel_id=1, source_target_pairs={{0,1},{1,2},{2,3},{3,0},{4,5},{5,6},{6,7},{7,4},{8,9},{9,10},{10,1... | collective-permute-start | bytes 12296 | tf_op jit(solution)/shard_map/ppermute | solution.py:344
  117.5 1.7 %collective-permute-done.43.r3 = f32[16,64]{1,0:T(8,128)S(1)} collective-permute-done((f32[16,64]{1,0:T(8,128)S(1)}, f32[16,64]{1,0:T(8,128)S(1)}, u32[]{:S(2)}, u32[]{:S(2)}) %collective-permute-start.43) | collective-permute-done | bytes 4128 | tf_op jit(solution)/shard_map/ppermute | solution.py:344
  (81 shorter events, 26.8 us)
Async XLA Ops:
  2.6 38.9 %collective-permute-start.2 = (f32[1536,256]{1,0:T(8,128)S(1)}, f32[1536,256]{1,0:T(8,128)S(1)}, u32[]{:S(2)}, u32[]{:S(2)}) collective-permute-start(f32[1536,256]{1,0:T(8,128)S(1)} %get-tuple-element.46), channel_id=1, source_target_pairs={{0,1},{1,2},{2,3},{3,0},{4,5},{5,6},{6,7},{7,4},{8,9},{9,10},{10,1... | collective-permute-start | bytes 4718600 | tf_op jit(solution)/shard_map/ppermute | solution.py:344
  4.6 36.9 %collective-permute-start.3 = (f32[1536,256]{1,0:T(8,128)S(1)}, f32[1536,256]{1,0:T(8,128)S(1)}, u32[]{:S(2)}, u32[]{:S(2)}) collective-permute-start(f32[1536,256]{1,0:T(8,128)S(1)} %get-tuple-element.47), channel_id=1, source_target_pairs={{0,3},{1,0},{2,1},{3,2},{4,7},{5,4},{6,5},{7,6},{8,11},{9,8},{10,9... | collective-permute-start | bytes 4718600 | tf_op jit(solution)/shard_map/ppermute | solution.py:344
  31.0 10.1 %collective-permute-start.1 = (f32[16,256]{1,0:T(8,128)S(1)}, f32[16,256]{1,0:T(8,128)S(1)}, u32[]{:S(2)}, u32[]{:S(2)}) collective-permute-start(f32[16,256]{1,0:T(8,128)S(1)} %shard_map.65.info.i0), channel_id=1, source_target_pairs={{0,3},{1,0},{2,1},{3,2},{4,7},{5,4},{6,5},{7,6},{8,11},{9,8},{10,9... | collective-permute-start | bytes 49160 | tf_op jit(solution)/shard_map/ppermute | solution.py:344
  33.0 8.4 %collective-permute-start = (f32[16,256]{1,0:T(8,128)S(1)}, f32[16,256]{1,0:T(8,128)S(1)}, u32[]{:S(2)}, u32[]{:S(2)}) collective-permute-start(f32[16,256]{1,0:T(8,128)S(1)} %shard_map.65.info.i0), channel_id=1, source_target_pairs={{0,1},{1,2},{2,3},{3,0},{4,5},{5,6},{6,7},{7,4},{8,9},{9,10},{10,1... | collective-permute-start | bytes 49160 | tf_op jit(solution)/shard_map/ppermute | solution.py:344
  33.1 9.8 %collective-permute-start.4 = (f32[16,256]{1,0:T(8,128)S(1)}, f32[16,256]{1,0:T(8,128)S(1)}, u32[]{:S(2)}, u32[]{:S(2)}) collective-permute-start(f32[16,256]{1,0:T(8,128)S(1)} %shard_map.65.info.i0), channel_id=1, source_target_pairs={{0,2},{1,3},{2,0},{3,1},{4,6},{5,7},{6,4},{7,5},{8,10},{9,11},{10,... | collective-permute-start | bytes 49160 | tf_op jit(solution)/shard_map/ppermute | solution.py:344
  43.0 15.3 %collective-permute-start.5 = (f32[512,256]{1,0:T(8,128)S(1)}, f32[512,256]{1,0:T(8,128)S(1)}, u32[]{:S(2)}, u32[]{:S(2)}) collective-permute-start(f32[512,256]{1,0:T(8,128)S(1)} %get-tuple-element.57), channel_id=1, source_target_pairs={{0,1},{1,2},{2,3},{3,0},{4,5},{5,6},{6,7},{7,4},{8,9},{9,10},{10,1... | collective-permute-start | bytes 1572872 | tf_op jit(solution)/shard_map/ppermute | solution.py:344
  44.1 14.2 %collective-permute-start.6 = (f32[512,256]{1,0:T(8,128)S(1)}, f32[512,256]{1,0:T(8,128)S(1)}, u32[]{:S(2)}, u32[]{:S(2)}) collective-permute-start(f32[512,256]{1,0:T(8,128)S(1)} %get-tuple-element.58), channel_id=1, source_target_pairs={{0,3},{1,0},{2,1},{3,2},{4,7},{5,4},{6,5},{7,6},{8,11},{9,8},{10,9... | collective-permute-start | bytes 1572872 | tf_op jit(solution)/shard_map/ppermute | solution.py:344
  47.8 9.4 %collective-permute-start.7 = (f32[16,256]{1,0:T(8,128)S(1)}, f32[16,256]{1,0:T(8,128)S(1)}, u32[]{:S(2)}, u32[]{:S(2)}) collective-permute-start(f32[16,256]{1,0:T(8,128)S(1)} %get-tuple-element.64), channel_id=1, source_target_pairs={{0,1},{1,2},{2,3},{3,0},{4,5},{5,6},{6,7},{7,4},{8,9},{9,10},{10,1... | collective-permute-start | bytes 49160 | tf_op jit(solution)/shard_map/ppermute | solution.py:344
  47.8 10.5 %collective-permute-start.8 = (f32[16,256]{1,0:T(8,128)S(1)}, f32[16,256]{1,0:T(8,128)S(1)}, u32[]{:S(2)}, u32[]{:S(2)}) collective-permute-start(f32[16,256]{1,0:T(8,128)S(1)} %get-tuple-element.65), channel_id=1, source_target_pairs={{0,2},{1,3},{2,0},{3,1},{4,6},{5,7},{6,4},{7,5},{8,10},{9,11},{10,... | collective-permute-start | bytes 49160 | tf_op jit(solution)/shard_map/ppermute | solution.py:344
  50.6 7.7 %collective-permute-start.9 = (f32[16,256]{1,0:T(8,128)S(1)}, f32[16,256]{1,0:T(8,128)S(1)}, u32[]{:S(2)}, u32[]{:S(2)}) collective-permute-start(f32[16,256]{1,0:T(8,128)S(1)} %get-tuple-element.66), channel_id=1, source_target_pairs={{0,3},{1,0},{2,1},{3,2},{4,7},{5,4},{6,5},{7,6},{8,11},{9,8},{10,9... | collective-permute-start | bytes 49160 | tf_op jit(solution)/shard_map/ppermute | solution.py:344
  62.0 7.8 %collective-permute-start.10 = (f32[136,256]{1,0:T(8,128)S(1)}, f32[136,256]{1,0:T(8,128)S(1)}, u32[]{:S(2)}, u32[]{:S(2)}) collective-permute-start(f32[136,256]{1,0:T(8,128)S(1)} %get-tuple-element.67.t0), channel_id=1, source_target_pairs={{0,1},{1,2},{2,3},{3,0},{4,5},{5,6},{6,7},{7,4},{8,9},{9,10},{10,1... | collective-permute-start | bytes 417800 | tf_op jit(solution)/shard_map/ppermute | solution.py:344
  63.0 6.7 %collective-permute-start.13 = (f32[136,256]{1,0:T(8,128)S(1)}, f32[136,256]{1,0:T(8,128)S(1)}, u32[]{:S(2)}, u32[]{:S(2)}) collective-permute-start(f32[136,256]{1,0:T(8,128)S(1)} %get-tuple-element.68.l0), channel_id=1, source_target_pairs={{0,3},{1,0},{2,1},{3,2},{4,7},{5,4},{6,5},{7,6},{8,11},{9,8},{10,9... | collective-permute-start | bytes 417800 | tf_op jit(solution)/shard_map/ppermute | solution.py:344
  65.3 7.7 %collective-permute-start.15 = (f32[136,256]{1,0:T(8,128)S(1)}, f32[136,256]{1,0:T(8,128)S(1)}, u32[]{:S(2)}, u32[]{:S(2)}) collective-permute-start(f32[136,256]{1,0:T(8,128)S(1)} %get-tuple-element.67.t0), channel_id=1, source_target_pairs={{0,3},{1,0},{2,1},{3,2},{4,7},{5,4},{6,5},{7,6},{8,11},{9,8},{10,9... | collective-permute-start | bytes 417800 | tf_op jit(solution)/shard_map/ppermute | solution.py:344
  66.1 6.9 %collective-permute-start.11 = (f32[136,256]{1,0:T(8,128)S(1)}, f32[136,256]{1,0:T(8,128)S(1)}, u32[]{:S(2)}, u32[]{:S(2)}) collective-permute-start(f32[136,256]{1,0:T(8,128)S(1)} %get-tuple-element.68.l0), channel_id=1, source_target_pairs={{0,1},{1,2},{2,3},{3,0},{4,5},{5,6},{6,7},{7,4},{8,9},{9,10},{10,1... | collective-permute-start | bytes 417800 | tf_op jit(solution)/shard_map/ppermute | solution.py:344
  69.8 6.3 %collective-permute-start.12 = (f32[136,256]{1,0:T(8,128)S(1)}, f32[136,256]{1,0:T(8,128)S(1)}, u32[]{:S(2)}, u32[]{:S(2)}) collective-permute-start(f32[136,256]{1,0:T(8,128)S(1)} %collective-permute-done.10.t1), channel_id=1, source_target_pairs={{0,1},{1,2},{2,3},{3,0},{4,5},{5,6},{6,7},{7,4},{8,9},{9,10},{10,1... | collective-permute-start | bytes 417800 | tf_op jit(solution)/shard_map/ppermute | solution.py:344
  69.8 6.3 %collective-permute-start.14 = (f32[136,256]{1,0:T(8,128)S(1)}, f32[136,256]{1,0:T(8,128)S(1)}, u32[]{:S(2)}, u32[]{:S(2)}) collective-permute-start(f32[136,256]{1,0:T(8,128)S(1)} %collective-permute-done.13.l3), channel_id=1, source_target_pairs={{0,3},{1,0},{2,1},{3,2},{4,7},{5,4},{6,5},{7,6},{8,11},{9,8},{10,9... | collective-permute-start | bytes 417800 | tf_op jit(solution)/shard_map/ppermute | solution.py:344
  80.0 5.8 %collective-permute-start.17 = (f32[72,256]{1,0:T(8,128)S(1)}, f32[72,256]{1,0:T(8,128)S(1)}, u32[]{:S(2)}, u32[]{:S(2)}) collective-permute-start(f32[72,256]{1,0:T(8,128)S(1)} %get-tuple-element.72), channel_id=1, source_target_pairs={{0,8},{4,12},{8,16},{12,20},{16,24},{20,28},{24,0},{28,4},{32,40},... | collective-permute-start | bytes 221192 | tf_op jit(solution)/shard_map/ppermute | solution.py:415
  81.7 6.0 %collective-permute-start.20 = (f32[64,256]{1,0:T(8,128)S(1)}, f32[64,256]{1,0:T(8,128)S(1)}, u32[]{:S(2)}, u32[]{:S(2)}) collective-permute-start(f32[64,256]{1,0:T(8,128)S(1)} %get-tuple-element.73), channel_id=1, source_target_pairs={{0,24},{4,28},{8,0},{12,4},{16,8},{20,12},{24,16},{28,20},{32,56},... | collective-permute-start | bytes 196616 | tf_op jit(solution)/shard_map/ppermute | solution.py:415
  83.3 6.0 %collective-permute-start.19 = (f32[72,256]{1,0:T(8,128)S(1)}, f32[72,256]{1,0:T(8,128)S(1)}, u32[]{:S(2)}, u32[]{:S(2)}) collective-permute-start(f32[72,256]{1,0:T(8,128)S(1)} %get-tuple-element.72), channel_id=1, source_target_pairs={{0,24},{4,28},{8,0},{12,4},{16,8},{20,12},{24,16},{28,20},{32,56},... | collective-permute-start | bytes 221192 | tf_op jit(solution)/shard_map/ppermute | solution.py:415
  85.8 6.3 %collective-permute-start.21 = (f32[72,256]{1,0:T(8,128)S(1)}, f32[72,256]{1,0:T(8,128)S(1)}, u32[]{:S(2)}, u32[]{:S(2)}) collective-permute-start(f32[72,256]{1,0:T(8,128)S(1)} %collective-permute-done.17.refs_0_), channel_id=1, source_target_pairs={{0,8},{4,12},{8,16},{12,20},{16,24},{20,28},{24,0},{28,4},{32,40},... | collective-permute-start | bytes 221192 | tf_op jit(solution)/shard_map/ppermute | solution.py:415
  86.1 6.0 %collective-permute-start.18 = (f32[64,256]{1,0:T(8,128)S(1)}, f32[64,256]{1,0:T(8,128)S(1)}, u32[]{:S(2)}, u32[]{:S(2)}) collective-permute-start(f32[64,256]{1,0:T(8,128)S(1)} %get-tuple-element.73), channel_id=1, source_target_pairs={{0,8},{4,12},{8,16},{12,20},{16,24},{20,28},{24,0},{28,4},{32,40},... | collective-permute-start | bytes 196616 | tf_op jit(solution)/shard_map/ppermute | solution.py:415
  87.7 4.9 %collective-permute-start.26 = (f32[64,256]{1,0:T(8,128)S(1)}, f32[64,256]{1,0:T(8,128)S(1)}, u32[]{:S(2)}, u32[]{:S(2)}) collective-permute-start(f32[64,256]{1,0:T(8,128)S(1)} %collective-permute-done.20.refs_3_), channel_id=1, source_target_pairs={{0,4},{4,0},{8,12},{12,8},{16,20},{20,16},{24,28},{28,24},{32,36},... | collective-permute-start | bytes 196616 | tf_op jit(solution)/shard_map/ppermute | solution.py:409
  87.7 5.0 %collective-permute-start.22 = (f32[64,256]{1,0:T(8,128)S(1)}, f32[64,256]{1,0:T(8,128)S(1)}, u32[]{:S(2)}, u32[]{:S(2)}) collective-permute-start(f32[64,256]{1,0:T(8,128)S(1)} %collective-permute-done.20.refs_3_), channel_id=1, source_target_pairs={{0,24},{4,28},{8,0},{12,4},{16,8},{20,12},{24,16},{28,20},{32,56},... | collective-permute-start | bytes 196616 | tf_op jit(solution)/shard_map/ppermute | solution.py:415
  89.3 4.5 %collective-permute-start.25 = (f32[72,256]{1,0:T(8,128)S(1)}, f32[72,256]{1,0:T(8,128)S(1)}, u32[]{:S(2)}, u32[]{:S(2)}) collective-permute-start(f32[72,256]{1,0:T(8,128)S(1)} %collective-permute-done.19.refs_2_), channel_id=1, source_target_pairs={{0,4},{4,0},{8,12},{12,8},{16,20},{20,16},{24,28},{28,24},{32,36},... | collective-permute-start | bytes 221192 | tf_op jit(solution)/shard_map/ppermute | solution.py:409
  95.3 4.6 %collective-permute-start.29 = (f32[72,256]{1,0:T(8,128)S(1)}, f32[72,256]{1,0:T(8,128)S(1)}, u32[]{:S(2)}, u32[]{:S(2)}) collective-permute-start(f32[72,256]{1,0:T(8,128)S(1)} %get-tuple-element.74), channel_id=1, source_target_pairs={{0,32},{4,36},{8,40},{12,44},{16,48},{20,52},{24,56},{28,60},{32,6... | collective-permute-start | bytes 221192 | tf_op jit(solution)/shard_map/ppermute | solution.py:415
  95.9 6.0 %collective-permute-start.32 = (f32[64,256]{1,0:T(8,128)S(1)}, f32[64,256]{1,0:T(8,128)S(1)}, u32[]{:S(2)}, u32[]{:S(2)}) collective-permute-start(f32[64,256]{1,0:T(8,128)S(1)} %get-tuple-element.75), channel_id=1, source_target_pairs={{0,96},{4,100},{8,104},{12,108},{16,112},{20,116},{24,120},{28,124... | collective-permute-start | bytes 196616 | tf_op jit(solution)/shard_map/ppermute | solution.py:415
  97.4 6.2 %collective-permute-start.31 = (f32[72,256]{1,0:T(8,128)S(1)}, f32[72,256]{1,0:T(8,128)S(1)}, u32[]{:S(2)}, u32[]{:S(2)}) collective-permute-start(f32[72,256]{1,0:T(8,128)S(1)} %get-tuple-element.74), channel_id=1, source_target_pairs={{0,96},{4,100},{8,104},{12,108},{16,112},{20,116},{24,120},{28,124... | collective-permute-start | bytes 221192 | tf_op jit(solution)/shard_map/ppermute | solution.py:415
  99.9 6.0 %collective-permute-start.33 = (f32[72,256]{1,0:T(8,128)S(1)}, f32[72,256]{1,0:T(8,128)S(1)}, u32[]{:S(2)}, u32[]{:S(2)}) collective-permute-start(f32[72,256]{1,0:T(8,128)S(1)} %collective-permute-done.29.refs_0_), channel_id=1, source_target_pairs={{0,32},{4,36},{8,40},{12,44},{16,48},{20,52},{24,56},{28,60},{32,6... | collective-permute-start | bytes 221192 | tf_op jit(solution)/shard_map/ppermute | solution.py:415
  101.9 5.7 %collective-permute-start.34 = (f32[64,256]{1,0:T(8,128)S(1)}, f32[64,256]{1,0:T(8,128)S(1)}, u32[]{:S(2)}, u32[]{:S(2)}) collective-permute-start(f32[64,256]{1,0:T(8,128)S(1)} %collective-permute-done.32.refs_3_), channel_id=1, source_target_pairs={{0,96},{4,100},{8,104},{12,108},{16,112},{20,116},{24,120},{28,124... | collective-permute-start | bytes 196616 | tf_op jit(solution)/shard_map/ppermute | solution.py:415
  103.7 4.8 %collective-permute-start.37 = (f32[72,256]{1,0:T(8,128)S(1)}, f32[72,256]{1,0:T(8,128)S(1)}, u32[]{:S(2)}, u32[]{:S(2)}) collective-permute-start(f32[72,256]{1,0:T(8,128)S(1)} %collective-permute-done.31.refs_2_), channel_id=1, source_target_pairs={{0,4},{4,0},{8,12},{12,8},{16,20},{20,16},{24,28},{28,24},{32,36},... | collective-permute-start | bytes 221192 | tf_op jit(solution)/shard_map/ppermute | solution.py:409
  111.1 5.2 %collective-permute-start.41 = (f32[16,64]{1,0:T(8,128)S(1)}, f32[16,64]{1,0:T(8,128)S(1)}, u32[]{:S(2)}, u32[]{:S(2)}) collective-permute-start(f32[16,64]{1,0:T(8,128)S(1)} %get-tuple-element.80), channel_id=1, source_target_pairs={{0,2},{1,3},{2,0},{3,1},{4,6},{5,7},{6,4},{7,5},{8,10},{9,11},{10,... | collective-permute-start | bytes 12296 | tf_op jit(solution)/shard_map/ppermute | solution.py:344
  112.7 4.9 %collective-permute-start.42 = (f32[16,64]{1,0:T(8,128)S(1)}, f32[16,64]{1,0:T(8,128)S(1)}, u32[]{:S(2)}, u32[]{:S(2)}) collective-permute-start(f32[16,64]{1,0:T(8,128)S(1)} %get-tuple-element.81), channel_id=1, source_target_pairs={{0,1},{1,2},{2,3},{3,0},{4,5},{5,6},{6,7},{7,4},{8,9},{9,10},{10,1... | collective-permute-start | bytes 12296 | tf_op jit(solution)/shard_map/ppermute | solution.py:344
  (16 other events, 100.2 us)

commit v12 on v10

--- a/solution.py
+++ b/solution.py
@@ -204,7 +204,7 @@
 
 
 def join(pos, c, mine, others, m_s):
-    for d, m, o in zip((3, 2, 1), mine, others):
+    for d, m, o in zip((3, 1, 2), mine, others):
         slot = lax.rem(pos - d + 4, 4)
         m_s[slot, half_rows(c), :] = m[...]
         m_s[slot, half_rows(1 - c), :] = o[...]
@@ -263,17 +263,20 @@
         o[...] = st_s[lax.rem(z + d, ROWS)]
 
 
-SENT = SUB + HALF_SUB
 COPIED = 4
 
 
-def send_kernel(idx, flat, ahead, back, sems):
+def send_kernel(idx, flat, ahead_far, back_far, ahead, back, sems):
     z = idx[Z]
     copies = []
-    for way, out in enumerate((ahead, back)):
-        for at in range(0, SENT, COPIED):
-            d, first = ((1, 3)[way], at) if at < SUB else (2, at - SUB + way * HALF_SUB)
-            source = lax.rem(z + d, ROWS) * (SUB * 64) + first * 64
+    for out, d, first, count in (
+        (ahead_far, 2, 0, HALF_SUB),
+        (back_far, 2, HALF_SUB, HALF_SUB),
+        (ahead, 1, 0, SUB),
+        (back, 3, 0, SUB),
+    ):
+        for at in range(0, count, COPIED):
+            source = lax.rem(z + d, ROWS) * (SUB * 64) + (first + at) * 64
             copies.append(
                 pltpu.make_async_copy(
                     flat.at[pl.ds(pl.multiple_of(source, 64), COPIED * 64)],
@@ -285,11 +288,6 @@
         copy.start()
     for copy in copies:
         copy.wait()
-
-
-def relay_kernel(idx, prev, after, p, a):
-    p[...] = prev[SUB * 64 :, :]
-    a[...] = after[SUB * 64 :, :]
 
 
 def stage_kernel(idx, gains, flat, info, staged, own, sems):
@@ -325,7 +323,7 @@
         o[:, 128:] = jnp.zeros((16, 128), F32)
 
 
-def place_kernel(idx, r0, r1, r2, r3, out):
+def place_kernel(idx, r0, r2, r1, r3, out):
     z = idx[Z]
     for d, r in enumerate((r0, r1, r2, r3)):
         slot = lax.rem(z - d + ROWS, ROWS)
@@ -346,9 +344,15 @@
     def along_rows(blocks):
         return [along_row(b, d) for d, b in enumerate(blocks, 1)]
 
-    ahead, back = call(
-        send_kernel, [(SENT * 64, N)] * 2, idx, (), [pltpu.SemaphoreType.DMA((2 * SENT // COPIED,))], far=(flat,)
-    )
+    *far, ahead, back = call(
+        send_kernel,
+        [(HALF_SUB * 64, N)] * 2 + [(SUB * 64, N)] * 2,
+        idx,
+        (),
+        [pltpu.SemaphoreType.DMA((3 * SUB // COPIED,))],
+        far=(flat,),
+    )
+    far = [along_row(f, d) for f, d in zip(far, (1, 3))]
     prev, after = along_row(ahead, 1), along_row(back, 3)
 
     rid = owner[:, 0] * 16 + step % 16 + 512 * (step // 16)
@@ -364,12 +368,10 @@
         [pltpu.SemaphoreType.DMA((2,))],
         far=(gains, flat),
     )
-    infos[0], infos[2], staged, own, prev, after, idx, prior = lax.optimization_barrier(
-        (infos[0], infos[2], staged, own, prev, after, idx, prior)
-    )
-    pieces = call(relay_kernel, [(HALF_SUB * 64, N)] * 2, idx, (prev, after))
-    pieces, infos = lax.optimization_barrier((pieces, infos))
-    relayed = [along_row(p, d) for p, d in zip(pieces, (1, 3))]
+    infos, staged, own, prev, after, far, idx, prior = lax.optimization_barrier(
+        (infos, staged, own, prev, after, far, idx, prior)
+    )
+    relayed = [along_row(f, d) for f, d in zip(far, (1, 3))]
     offs = call(
         offset_kernel,
         [(16, N)] * 4,
@@ -403,7 +405,7 @@
     def gathered(half, stride):
         n = 4 * stride
         got = [
-            lax.ppermute(half, "tm", [(i, i - i % n + (i + d * stride) % n) for i in range(32)]) for d in (3, 2, 1)
+            lax.ppermute(half, "tm", [(i, i - i % n + (i + d * stride) % n) for i in range(32)]) for d in (3, 1, 2)
         ]
         return *got, *[other_core(g) for g in got]
 
@@ -425,7 +427,7 @@
         (prior, *gathered(half, 8), before, pref),
         [pltpu.VMEM((ROWS, SUB, 64), F32), pltpu.VMEM((4, R, N), F32), pltpu.VMEM((PAD, N), F32)],
     )
-    got = [outs[0], *along_rows(outs[1:])]
+    got = [outs[0], along_row(outs[2], 2), along_row(outs[1], 1), along_row(outs[3], 3)]
     return pl.pallas_call(
         place_kernel,
         out_shape=jax.ShapeDtypeStruct((64, 64), F32),

time: 119 us -> 116 us (0.975)
  waiting for transfers between devices: 36.5 us -> 32.9 us
  starting transfers between devices: 38.1 us -> 40.3 us
    ppermute x6, waiting for transfers between devices: 13.1 us -> 10.9 us  [gathered(): lax.ppermute(half, 'tm', [(i, i - i % n + (i + d * stride) % n) for i in...]
    ppermute x19 -> x21, waiting for transfers between devices: 20.3 us -> 18.8 us  [along_row(): return lax.ppermute(x, 'row', [(i, (i + d) % ROWS) for i in range(ROWS)])]
    ppermute x6, starting transfers between devices: 8.87 us -> 10.1 us  [gathered(): lax.ppermute(half, 'tm', [(i, i - i % n + (i + d * stride) % n) for i in...]
    ppermute x19 -> x21, starting transfers between devices: 28.6 us -> 29.5 us  [along_row(): return lax.ppermute(x, 'row', [(i, (i + d) % ROWS) for i in range(ROWS)])]
    pallas_call x11 -> x10, Pallas kernels: 18.7 us -> 17.9 us  [call(): pl.pallas_call(kernel, out_shape=[pltpu.VMEM(s, t) for s, t in outs], in_...]
  transfers between devices with their start and end apart: 32 -> 34, of which waited for: 19 -> 19; matrix products, arithmetic and copies ran while one was open for 0% -> 0% of each run, Pallas kernels for 11% -> 11%
where the time goes in v12:
time: 116 us
  starting transfers between devices  40.3 us (35%)
  waiting for transfers between devices  32.9 us (28%)
  Pallas kernels  26 us (22%)
  blocking collectives  16.7 us (14%)
    ppermute x21, starting transfers between devices, along_row(): return lax.ppermute(x, 'row', [(i, (i + d) % ROWS) for i in range(ROWS)])  29.5 us
    ppermute x21, waiting for transfers between devices, along_row(): return lax.ppermute(x, 'row', [(i, (i + d) % ROWS) for i in range(ROWS)])  18.8 us
    pallas_call x10, Pallas kernels, call(): pl.pallas_call(kernel, out_shape=[pltpu.VMEM(s, t) for s, t in outs], in_...  17.9 us
    all_to_all x1, blocking collectives, shards(): sums = lax.all_to_all(partial, 'tm', 0, 0, tiled=True).reshape(32, 16, N)  16.7 us
    ppermute x6, waiting for transfers between devices, gathered(): lax.ppermute(half, 'tm', [(i, i - i % n + (i + d * stride) % n) for i in...  10.9 us
    ppermute x6, starting transfers between devices, gathered(): lax.ppermute(half, 'tm', [(i, i - i % n + (i + d * stride) % n) for i in...  10.1 us
    pallas_call x1, Pallas kernels, binned(): pl.pallas_call(bin_kernel, out_shape=jax.ShapeDtypeStruct((n_bins // 4, N...  6.91 us
    ppermute x7, waiting for transfers between devices, other_core(): return lax.ppermute(m, 'tm', [(i, i ^ 1) for i in range(32)])  3.09 us
  transfers between devices with their start and end apart: 34, of which 19 were waited for; matrix products, arithmetic and copies ran while one was open for 0% of the time, Pallas kernels for 11%

profile of v12, /device:TPU:6, one launch (start us, length us, event | category | flops | bytes accessed | tf_op | source)
XLA Modules:
  0.0 116.2 jit_solution(1136137923200626084)
XLA Ops:
  0.1 2.5 %shard_map.67 = (f32[512,256]{1,0:T(8,128)S(1)}, f32[512,256]{1,0:T(8,128)S(1)}, f32[1024,256]{1,0:T(8,128)S(1)}, f32[1024,256]{1,0:T(8,128)S(1)}) custom-call(s32[4]{0:T(128)S(1)} %pad_add_fusion.idx, f32[4096,256]{1,0:T(8,128)} %bitcast.14), custom_call_target="tpu_custom_call" | custom-call | tf_op jit(solution)/shard_map/pallas_call | solution.py:75
  2.6 2.0 %collective-permute-start.5 = (f32[512,256]{1,0:T(8,128)S(1)}, f32[512,256]{1,0:T(8,128)S(1)}, u32[]{:S(2)}, u32[]{:S(2)}) collective-permute-start(f32[512,256]{1,0:T(8,128)S(1)} %get-tuple-element.44), channel_id=1, source_target_pairs={{0,1},{1,2},{2,3},{3,0},{4,5},{5,6},{6,7},{7,4},{8,9},{9,10},{10,1... | collective-permute-start | bytes 1572872 | tf_op jit(solution)/shard_map/ppermute | solution.py:334
  4.6 2.2 %collective-permute-start.6 = (f32[512,256]{1,0:T(8,128)S(1)}, f32[512,256]{1,0:T(8,128)S(1)}, u32[]{:S(2)}, u32[]{:S(2)}) collective-permute-start(f32[512,256]{1,0:T(8,128)S(1)} %get-tuple-element.45), channel_id=1, source_target_pairs={{0,3},{1,0},{2,1},{3,2},{4,7},{5,4},{6,5},{7,6},{8,11},{9,8},{10,9... | collective-permute-start | bytes 1572872 | tf_op jit(solution)/shard_map/ppermute | solution.py:334
  6.8 3.2 %collective-permute-start.4 = (f32[1024,256]{1,0:T(8,128)S(1)}, f32[1024,256]{1,0:T(8,128)S(1)}, u32[]{:S(2)}, u32[]{:S(2)}) collective-permute-start(f32[1024,256]{1,0:T(8,128)S(1)} %get-tuple-element.43), channel_id=1, source_target_pairs={{0,3},{1,0},{2,1},{3,2},{4,7},{5,4},{6,5},{7,6},{8,11},{9,8},{10,9... | collective-permute-start | bytes 3145736 | tf_op jit(solution)/shard_map/ppermute | solution.py:334
  10.1 6.9 %shard_map.64 = f32[512,256]{1,0:T(8,128)S(1)} custom-call(s32[1,4096]{1,0:T(1,128)S(1)} %bitcast.12, f32[64,4096]{1,0:T(8,128)S(1)} %bitcast.11), custom_call_target="tpu_custom_call" | custom-call | tf_op jit(solution)/shard_map/pallas_call | solution.py:120
  17.0 16.7 %all_to_all.9.sums = f32[32,16,256]{2,1,0:T(8,128)S(1)} all-to-all(f32[32,16,256]{2,1,0:T(8,128)S(1)} %bitcast.10), channel_id=1, replica_groups=mesh['tm'=32,'row'=4] {'tm'}, dimensions={0} | all-to-all | bytes 1048576 | tf_op jit(solution)/shard_map/all_to_all | solution.py:360
  36.4 3.0 %shard_map.66 = (f32[64,64,256]{2,1,0:T(8,128)S(1)}, f32[1024,256]{1,0:T(8,128)S(1)}) custom-call(s32[4]{0:T(128)S(1)} %pad_add_fusion.idx, f32[64,64,256]{2,1,0:T(8,128)} %gains.1, f32[4096,256]{1,0:T(8,128)} %bitcast.15, f32[16,256]{1,0:T(8,128)S(1)} %shard_map.65.info.i0), custom_call_target="tpu_custom_call" | custom-call | tf_op jit(solution)/shard_map/pallas_call | solution.py:75
  39.5 1.7 %collective-permute-done.2.r3 = f32[16,256]{1,0:T(8,128)S(1)} collective-permute-done((f32[16,256]{1,0:T(8,128)S(1)}, f32[16,256]{1,0:T(8,128)S(1)}, u32[]{:S(2)}, u32[]{:S(2)}) %collective-permute-start.2) | collective-permute-done | bytes 16416 | tf_op jit(solution)/shard_map/ppermute | solution.py:334
  41.2 1.6 %collective-permute-done.1.r2 = f32[16,256]{1,0:T(8,128)S(1)} collective-permute-done((f32[16,256]{1,0:T(8,128)S(1)}, f32[16,256]{1,0:T(8,128)S(1)}, u32[]{:S(2)}, u32[]{:S(2)}) %collective-permute-start.1) | collective-permute-done | bytes 16416 | tf_op jit(solution)/shard_map/ppermute | solution.py:334
  42.8 1.4 %collective-permute-start.7 = (f32[512,256]{1,0:T(8,128)S(1)}, f32[512,256]{1,0:T(8,128)S(1)}, u32[]{:S(2)}, u32[]{:S(2)}) collective-permute-start(f32[512,256]{1,0:T(8,128)S(1)} %collective-permute-done.5), channel_id=1, source_target_pairs={{0,1},{1,2},{2,3},{3,0},{4,5},{5,6},{6,7},{7,4},{8,9},{9,10},{10,1... | collective-permute-start | bytes 1572872 | tf_op jit(solution)/shard_map/ppermute | solution.py:334
  44.2 1.9 %collective-permute-start.8 = (f32[512,256]{1,0:T(8,128)S(1)}, f32[512,256]{1,0:T(8,128)S(1)}, u32[]{:S(2)}, u32[]{:S(2)}) collective-permute-start(f32[512,256]{1,0:T(8,128)S(1)} %collective-permute-done.6), channel_id=1, source_target_pairs={{0,3},{1,0},{2,1},{3,2},{4,7},{5,4},{6,5},{7,6},{8,11},{9,8},{10,9... | collective-permute-start | bytes 1572872 | tf_op jit(solution)/shard_map/ppermute | solution.py:334
  46.1 1.6 %shard_map.68 = (f32[16,256]{1,0:T(8,128)S(1)}, f32[16,256]{1,0:T(8,128)S(1)}, f32[16,256]{1,0:T(8,128)S(1)}, f32[16,256]{1,0:T(8,128)S(1)}) custom-call(s32[4]{0:T(128)S(1)} %pad_add_fusion.idx, f32[64,64,256]{2,1,0:T(8,128)S(1)} %get-tuple-element.53.g, f32[16,256]{1,0:T(8,128)S(1)} %shard_map.65.info.i0, f32[16,256]{1,0:T(8,128)S(1)} %collective-permute-done.r1, ...), custom_call_target="tpu_custom_call" | custom-call | tf_op jit(solution)/shard_map/pallas_call | solution.py:75
  47.8 2.2 %collective-permute-start.10 = (f32[16,256]{1,0:T(8,128)S(1)}, f32[16,256]{1,0:T(8,128)S(1)}, u32[]{:S(2)}, u32[]{:S(2)}) collective-permute-start(f32[16,256]{1,0:T(8,128)S(1)} %get-tuple-element.59), channel_id=1, source_target_pairs={{0,2},{1,3},{2,0},{3,1},{4,6},{5,7},{6,4},{7,5},{8,10},{9,11},{10,... | collective-permute-start | bytes 49160 | tf_op jit(solution)/shard_map/ppermute | solution.py:334
  50.9 6.0 %collective-permute-done.9.b1 = f32[16,256]{1,0:T(8,128)S(1)} collective-permute-done((f32[16,256]{1,0:T(8,128)S(1)}, f32[16,256]{1,0:T(8,128)S(1)}, u32[]{:S(2)}, u32[]{:S(2)}) %collective-permute-start.9) | collective-permute-done | bytes 16416 | tf_op jit(solution)/shard_map/ppermute | solution.py:334
  57.7 3.7 %shard_map.69 = (f32[16,272,256]{2,1,0:T(8,128)S(1)}, f32[136,256]{1,0:T(8,128)S(1)}, f32[136,256]{1,0:T(8,128)S(1)}) custom-call(s32[4]{0:T(128)S(1)} %pad_add_fusion.idx, f32[1024,256]{1,0:T(8,128)S(1)} %get-tuple-element.48.own, f32[1024,256]{1,0:T(8,128)S(1)} %collective-permute-done.3.prev, f32[1024,256]{1,0:T(8,128)S(1)} %collective-permute-done.4.after, ...), custom_call_target="tpu_custom_call" | custom-call | tf_op jit(solution)/shard_map/pallas_call | solution.py:75
  62.4 2.3 %collective-permute-start.15 = (f32[136,256]{1,0:T(8,128)S(1)}, f32[136,256]{1,0:T(8,128)S(1)}, u32[]{:S(2)}, u32[]{:S(2)}) collective-permute-start(f32[136,256]{1,0:T(8,128)S(1)} %get-tuple-element.62.l0), channel_id=1, source_target_pairs={{0,3},{1,0},{2,1},{3,2},{4,7},{5,4},{6,5},{7,6},{8,11},{9,8},{10,9... | collective-permute-start | bytes 417800 | tf_op jit(solution)/shard_map/ppermute | solution.py:334
  66.7 2.5 %collective-permute-done.12.t1 = f32[136,256]{1,0:T(8,128)S(1)} collective-permute-done((f32[136,256]{1,0:T(8,128)S(1)}, f32[136,256]{1,0:T(8,128)S(1)}, u32[]{:S(2)}, u32[]{:S(2)}) %collective-permute-start.12) | collective-permute-done | bytes 139296 | tf_op jit(solution)/shard_map/ppermute | solution.py:334
  69.2 3.2 %collective-permute-start.16 = (f32[136,256]{1,0:T(8,128)S(1)}, f32[136,256]{1,0:T(8,128)S(1)}, u32[]{:S(2)}, u32[]{:S(2)}) collective-permute-start(f32[136,256]{1,0:T(8,128)S(1)} %collective-permute-done.15.l3), channel_id=1, source_target_pairs={{0,3},{1,0},{2,1},{3,2},{4,7},{5,4},{6,5},{7,6},{8,11},{9,8},{10,9... | collective-permute-start | bytes 417800 | tf_op jit(solution)/shard_map/ppermute | solution.py:334
  72.5 3.0 %collective-permute-done.14.t2 = f32[136,256]{1,0:T(8,128)S(1)} collective-permute-done((f32[136,256]{1,0:T(8,128)S(1)}, f32[136,256]{1,0:T(8,128)S(1)}, u32[]{:S(2)}, u32[]{:S(2)}) %collective-permute-start.14) | collective-permute-done | bytes 139296 | tf_op jit(solution)/shard_map/ppermute | solution.py:334
  76.9 1.5 %collective-permute-done.18.other = f32[272,256]{1,0:T(8,128)S(1)} collective-permute-done((f32[272,256]{1,0:T(8,128)S(1)}, f32[272,256]{1,0:T(8,128)S(1)}, u32[]{:S(2)}, u32[]{:S(2)}) %collective-permute-start.18) | collective-permute-done | bytes 278560 | tf_op jit(solution)/shard_map/ppermute | solution.py:403
  79.3 3.3 %collective-permute-start.21 = (f32[136,256]{1,0:T(8,128)S(1)}, f32[136,256]{1,0:T(8,128)S(1)}, u32[]{:S(2)}, u32[]{:S(2)}) collective-permute-start(f32[136,256]{1,0:T(8,128)S(1)} %get-tuple-element.66), channel_id=1, source_target_pairs={{0,16},{4,20},{8,24},{12,28},{16,0},{20,4},{24,8},{28,12},{32,48},... | collective-permute-start | bytes 417800 | tf_op jit(solution)/shard_map/ppermute | solution.py:408
  83.3 2.6 %collective-permute-start.19 = (f32[136,256]{1,0:T(8,128)S(1)}, f32[136,256]{1,0:T(8,128)S(1)}, u32[]{:S(2)}, u32[]{:S(2)}) collective-permute-start(f32[136,256]{1,0:T(8,128)S(1)} %get-tuple-element.66), channel_id=1, source_target_pairs={{0,24},{4,28},{8,0},{12,4},{16,8},{20,12},{24,16},{28,20},{32,56},... | collective-permute-start | bytes 417800 | tf_op jit(solution)/shard_map/ppermute | solution.py:408
  85.9 1.6 %collective-permute-done.21.h3 = f32[136,256]{1,0:T(8,128)S(1)} collective-permute-done((f32[136,256]{1,0:T(8,128)S(1)}, f32[136,256]{1,0:T(8,128)S(1)}, u32[]{:S(2)}, u32[]{:S(2)}) %collective-permute-start.21) | collective-permute-done | bytes 139296 | tf_op jit(solution)/shard_map/ppermute | solution.py:408
  87.4 2.5 %collective-permute-done.20.h2 = f32[136,256]{1,0:T(8,128)S(1)} collective-permute-done((f32[136,256]{1,0:T(8,128)S(1)}, f32[136,256]{1,0:T(8,128)S(1)}, u32[]{:S(2)}, u32[]{:S(2)}) %collective-permute-start.20) | collective-permute-done | bytes 139296 | tf_op jit(solution)/shard_map/ppermute | solution.py:408
  92.8 1.5 %collective-permute-start.27 = (f32[136,256]{1,0:T(8,128)S(1)}, f32[136,256]{1,0:T(8,128)S(1)}, u32[]{:S(2)}, u32[]{:S(2)}) collective-permute-start(f32[136,256]{1,0:T(8,128)S(1)} %get-tuple-element.67), channel_id=1, source_target_pairs={{0,64},{4,68},{8,72},{12,76},{16,80},{20,84},{24,88},{28,92},{32,9... | collective-permute-start | bytes 417800 | tf_op jit(solution)/shard_map/ppermute | solution.py:408
  94.2 2.1 %collective-permute-start.26 = (f32[136,256]{1,0:T(8,128)S(1)}, f32[136,256]{1,0:T(8,128)S(1)}, u32[]{:S(2)}, u32[]{:S(2)}) collective-permute-start(f32[136,256]{1,0:T(8,128)S(1)} %get-tuple-element.67), channel_id=1, source_target_pairs={{0,32},{4,36},{8,40},{12,44},{16,48},{20,52},{24,56},{28,60},{32,6... | collective-permute-start | bytes 417800 | tf_op jit(solution)/shard_map/ppermute | solution.py:408
  96.3 4.5 %collective-permute-done.27.h3 = f32[136,256]{1,0:T(8,128)S(1)} collective-permute-done((f32[136,256]{1,0:T(8,128)S(1)}, f32[136,256]{1,0:T(8,128)S(1)}, u32[]{:S(2)}, u32[]{:S(2)}) %collective-permute-start.27) | collective-permute-done | bytes 139296 | tf_op jit(solution)/shard_map/ppermute | solution.py:408
  101.4 2.0 %collective-permute-done.25.h1 = f32[136,256]{1,0:T(8,128)S(1)} collective-permute-done((f32[136,256]{1,0:T(8,128)S(1)}, f32[136,256]{1,0:T(8,128)S(1)}, u32[]{:S(2)}, u32[]{:S(2)}) %collective-permute-start.25) | collective-permute-done | bytes 139296 | tf_op jit(solution)/shard_map/ppermute | solution.py:408
  104.7 2.2 %shard_map.74 = (f32[16,64]{1,0:T(8,128)S(1)}, f32[16,64]{1,0:T(8,128)S(1)}, f32[16,64]{1,0:T(8,128)S(1)}, f32[16,64]{1,0:T(8,128)S(1)}) custom-call(s32[4]{0:T(128)S(1)} %pad_add_fusion.idx, f32[1,256]{1,0:T(1,128)S(1)} %bitcast.13, f32[136,256]{1,0:T(8,128)S(1)} %collective-permute-done.25.h1, f32[136,256]{1,0:T(8,128)S(1)} %collective-permute-done.26.h2, ...), custom_call_target="tpu_custom_call" | custom-call | tf_op jit(solution)/shard_map/pallas_call | solution.py:75
  106.9 1.6 %collective-permute-start.31 = (f32[16,64]{1,0:T(8,128)S(1)}, f32[16,64]{1,0:T(8,128)S(1)}, u32[]{:S(2)}, u32[]{:S(2)}) collective-permute-start(f32[16,64]{1,0:T(8,128)S(1)} %get-tuple-element.72), channel_id=1, source_target_pairs={{0,2},{1,3},{2,0},{3,1},{4,6},{5,7},{6,4},{7,5},{8,10},{9,11},{10,... | collective-permute-start | bytes 12296 | tf_op jit(solution)/shard_map/ppermute | solution.py:334
  108.5 2.9 %collective-permute-start.32 = (f32[16,64]{1,0:T(8,128)S(1)}, f32[16,64]{1,0:T(8,128)S(1)}, u32[]{:S(2)}, u32[]{:S(2)}) collective-permute-start(f32[16,64]{1,0:T(8,128)S(1)} %get-tuple-element.73), channel_id=1, source_target_pairs={{0,1},{1,2},{2,3},{3,0},{4,5},{5,6},{6,7},{7,4},{8,9},{9,10},{10,1... | collective-permute-start | bytes 12296 | tf_op jit(solution)/shard_map/ppermute | solution.py:334
  113.4 1.7 %collective-permute-done.33.r3 = f32[16,64]{1,0:T(8,128)S(1)} collective-permute-done((f32[16,64]{1,0:T(8,128)S(1)}, f32[16,64]{1,0:T(8,128)S(1)}, u32[]{:S(2)}, u32[]{:S(2)}) %collective-permute-start.33) | collective-permute-done | bytes 4128 | tf_op jit(solution)/shard_map/ppermute | solution.py:334
  (60 shorter events, 18.6 us)
Async XLA Ops:
  2.6 32.5 %collective-permute-start.5 = (f32[512,256]{1,0:T(8,128)S(1)}, f32[512,256]{1,0:T(8,128)S(1)}, u32[]{:S(2)}, u32[]{:S(2)}) collective-permute-start(f32[512,256]{1,0:T(8,128)S(1)} %get-tuple-element.44), channel_id=1, source_target_pairs={{0,1},{1,2},{2,3},{3,0},{4,5},{5,6},{6,7},{7,4},{8,9},{9,10},{10,1... | collective-permute-start | bytes 1572872 | tf_op jit(solution)/shard_map/ppermute | solution.py:334
  4.6 30.6 %collective-permute-start.6 = (f32[512,256]{1,0:T(8,128)S(1)}, f32[512,256]{1,0:T(8,128)S(1)}, u32[]{:S(2)}, u32[]{:S(2)}) collective-permute-start(f32[512,256]{1,0:T(8,128)S(1)} %get-tuple-element.45), channel_id=1, source_target_pairs={{0,3},{1,0},{2,1},{3,2},{4,7},{5,4},{6,5},{7,6},{8,11},{9,8},{10,9... | collective-permute-start | bytes 1572872 | tf_op jit(solution)/shard_map/ppermute | solution.py:334
  6.8 36.0 %collective-permute-start.3 = (f32[1024,256]{1,0:T(8,128)S(1)}, f32[1024,256]{1,0:T(8,128)S(1)}, u32[]{:S(2)}, u32[]{:S(2)}) collective-permute-start(f32[1024,256]{1,0:T(8,128)S(1)} %get-tuple-element.42), channel_id=1, source_target_pairs={{0,1},{1,2},{2,3},{3,0},{4,5},{5,6},{6,7},{7,4},{8,9},{9,10},{10,1... | collective-permute-start | bytes 3145736 | tf_op jit(solution)/shard_map/ppermute | solution.py:334
  6.8 36.0 %collective-permute-start.4 = (f32[1024,256]{1,0:T(8,128)S(1)}, f32[1024,256]{1,0:T(8,128)S(1)}, u32[]{:S(2)}, u32[]{:S(2)}) collective-permute-start(f32[1024,256]{1,0:T(8,128)S(1)} %get-tuple-element.43), channel_id=1, source_target_pairs={{0,3},{1,0},{2,1},{3,2},{4,7},{5,4},{6,5},{7,6},{8,11},{9,8},{10,9... | collective-permute-start | bytes 3145736 | tf_op jit(solution)/shard_map/ppermute | solution.py:334
  34.3 6.9 %collective-permute-start.2 = (f32[16,256]{1,0:T(8,128)S(1)}, f32[16,256]{1,0:T(8,128)S(1)}, u32[]{:S(2)}, u32[]{:S(2)}) collective-permute-start(f32[16,256]{1,0:T(8,128)S(1)} %shard_map.65.info.i0), channel_id=1, source_target_pairs={{0,3},{1,0},{2,1},{3,2},{4,7},{5,4},{6,5},{7,6},{8,11},{9,8},{10,9... | collective-permute-start | bytes 49160 | tf_op jit(solution)/shard_map/ppermute | solution.py:334
  35.1 7.7 %collective-permute-start.1 = (f32[16,256]{1,0:T(8,128)S(1)}, f32[16,256]{1,0:T(8,128)S(1)}, u32[]{:S(2)}, u32[]{:S(2)}) collective-permute-start(f32[16,256]{1,0:T(8,128)S(1)} %shard_map.65.info.i0), channel_id=1, source_target_pairs={{0,2},{1,3},{2,0},{3,1},{4,6},{5,7},{6,4},{7,5},{8,10},{9,11},{10,... | collective-permute-start | bytes 49160 | tf_op jit(solution)/shard_map/ppermute | solution.py:334
  35.2 7.6 %collective-permute-start = (f32[16,256]{1,0:T(8,128)S(1)}, f32[16,256]{1,0:T(8,128)S(1)}, u32[]{:S(2)}, u32[]{:S(2)}) collective-permute-start(f32[16,256]{1,0:T(8,128)S(1)} %shard_map.65.info.i0), channel_id=1, source_target_pairs={{0,1},{1,2},{2,3},{3,0},{4,5},{5,6},{6,7},{7,4},{8,9},{9,10},{10,1... | collective-permute-start | bytes 49160 | tf_op jit(solution)/shard_map/ppermute | solution.py:334
  42.8 14.9 %collective-permute-start.7 = (f32[512,256]{1,0:T(8,128)S(1)}, f32[512,256]{1,0:T(8,128)S(1)}, u32[]{:S(2)}, u32[]{:S(2)}) collective-permute-start(f32[512,256]{1,0:T(8,128)S(1)} %collective-permute-done.5), channel_id=1, source_target_pairs={{0,1},{1,2},{2,3},{3,0},{4,5},{5,6},{6,7},{7,4},{8,9},{9,10},{10,1... | collective-permute-start | bytes 1572872 | tf_op jit(solution)/shard_map/ppermute | solution.py:334
  44.2 13.5 %collective-permute-start.8 = (f32[512,256]{1,0:T(8,128)S(1)}, f32[512,256]{1,0:T(8,128)S(1)}, u32[]{:S(2)}, u32[]{:S(2)}) collective-permute-start(f32[512,256]{1,0:T(8,128)S(1)} %collective-permute-done.6), channel_id=1, source_target_pairs={{0,3},{1,0},{2,1},{3,2},{4,7},{5,4},{6,5},{7,6},{8,11},{9,8},{10,9... | collective-permute-start | bytes 1572872 | tf_op jit(solution)/shard_map/ppermute | solution.py:334
  47.7 9.3 %collective-permute-start.9 = (f32[16,256]{1,0:T(8,128)S(1)}, f32[16,256]{1,0:T(8,128)S(1)}, u32[]{:S(2)}, u32[]{:S(2)}) collective-permute-start(f32[16,256]{1,0:T(8,128)S(1)} %get-tuple-element.58), channel_id=1, source_target_pairs={{0,1},{1,2},{2,3},{3,0},{4,5},{5,6},{6,7},{7,4},{8,9},{9,10},{10,1... | collective-permute-start | bytes 49160 | tf_op jit(solution)/shard_map/ppermute | solution.py:334
  47.8 9.9 %collective-permute-start.10 = (f32[16,256]{1,0:T(8,128)S(1)}, f32[16,256]{1,0:T(8,128)S(1)}, u32[]{:S(2)}, u32[]{:S(2)}) collective-permute-start(f32[16,256]{1,0:T(8,128)S(1)} %get-tuple-element.59), channel_id=1, source_target_pairs={{0,2},{1,3},{2,0},{3,1},{4,6},{5,7},{6,4},{7,5},{8,10},{9,11},{10,... | collective-permute-start | bytes 49160 | tf_op jit(solution)/shard_map/ppermute | solution.py:334
  50.0 7.7 %collective-permute-start.11 = (f32[16,256]{1,0:T(8,128)S(1)}, f32[16,256]{1,0:T(8,128)S(1)}, u32[]{:S(2)}, u32[]{:S(2)}) collective-permute-start(f32[16,256]{1,0:T(8,128)S(1)} %get-tuple-element.60), channel_id=1, source_target_pairs={{0,3},{1,0},{2,1},{3,2},{4,7},{5,4},{6,5},{7,6},{8,11},{9,8},{10,9... | collective-permute-start | bytes 49160 | tf_op jit(solution)/shard_map/ppermute | solution.py:334
  61.4 7.8 %collective-permute-start.12 = (f32[136,256]{1,0:T(8,128)S(1)}, f32[136,256]{1,0:T(8,128)S(1)}, u32[]{:S(2)}, u32[]{:S(2)}) collective-permute-start(f32[136,256]{1,0:T(8,128)S(1)} %get-tuple-element.61.t0), channel_id=1, source_target_pairs={{0,1},{1,2},{2,3},{3,0},{4,5},{5,6},{6,7},{7,4},{8,9},{9,10},{10,1... | collective-permute-start | bytes 417800 | tf_op jit(solution)/shard_map/ppermute | solution.py:334
  62.4 6.8 %collective-permute-start.15 = (f32[136,256]{1,0:T(8,128)S(1)}, f32[136,256]{1,0:T(8,128)S(1)}, u32[]{:S(2)}, u32[]{:S(2)}) collective-permute-start(f32[136,256]{1,0:T(8,128)S(1)} %get-tuple-element.62.l0), channel_id=1, source_target_pairs={{0,3},{1,0},{2,1},{3,2},{4,7},{5,4},{6,5},{7,6},{8,11},{9,8},{10,9... | collective-permute-start | bytes 417800 | tf_op jit(solution)/shard_map/ppermute | solution.py:334
  64.7 7.8 %collective-permute-start.17 = (f32[136,256]{1,0:T(8,128)S(1)}, f32[136,256]{1,0:T(8,128)S(1)}, u32[]{:S(2)}, u32[]{:S(2)}) collective-permute-start(f32[136,256]{1,0:T(8,128)S(1)} %get-tuple-element.61.t0), channel_id=1, source_target_pairs={{0,3},{1,0},{2,1},{3,2},{4,7},{5,4},{6,5},{7,6},{8,11},{9,8},{10,9... | collective-permute-start | bytes 417800 | tf_op jit(solution)/shard_map/ppermute | solution.py:334
  65.9 6.6 %collective-permute-start.13 = (f32[136,256]{1,0:T(8,128)S(1)}, f32[136,256]{1,0:T(8,128)S(1)}, u32[]{:S(2)}, u32[]{:S(2)}) collective-permute-start(f32[136,256]{1,0:T(8,128)S(1)} %get-tuple-element.62.l0), channel_id=1, source_target_pairs={{0,1},{1,2},{2,3},{3,0},{4,5},{5,6},{6,7},{7,4},{8,9},{9,10},{10,1... | collective-permute-start | bytes 417800 | tf_op jit(solution)/shard_map/ppermute | solution.py:334
  69.2 6.3 %collective-permute-start.14 = (f32[136,256]{1,0:T(8,128)S(1)}, f32[136,256]{1,0:T(8,128)S(1)}, u32[]{:S(2)}, u32[]{:S(2)}) collective-permute-start(f32[136,256]{1,0:T(8,128)S(1)} %collective-permute-done.12.t1), channel_id=1, source_target_pairs={{0,1},{1,2},{2,3},{3,0},{4,5},{5,6},{6,7},{7,4},{8,9},{9,10},{10,1... | collective-permute-start | bytes 417800 | tf_op jit(solution)/shard_map/ppermute | solution.py:334
  69.2 6.3 %collective-permute-start.16 = (f32[136,256]{1,0:T(8,128)S(1)}, f32[136,256]{1,0:T(8,128)S(1)}, u32[]{:S(2)}, u32[]{:S(2)}) collective-permute-start(f32[136,256]{1,0:T(8,128)S(1)} %collective-permute-done.15.l3), channel_id=1, source_target_pairs={{0,3},{1,0},{2,1},{3,2},{4,7},{5,4},{6,5},{7,6},{8,11},{9,8},{10,9... | collective-permute-start | bytes 417800 | tf_op jit(solution)/shard_map/ppermute | solution.py:334
  76.8 1.6 %collective-permute-start.18 = (f32[272,256]{1,0:T(8,128)S(1)}, f32[272,256]{1,0:T(8,128)S(1)}, u32[]{:S(2)}, u32[]{:S(2)}) collective-permute-start(f32[272,256]{1,0:T(8,128)S(1)} %get-tuple-element.63.own), channel_id=1, source_target_pairs={{0,4},{4,0},{8,12},{12,8},{16,20},{20,16},{24,28},{28,24},{32,36},... | collective-permute-start | bytes 835592 | tf_op jit(solution)/shard_map/ppermute | solution.py:403
  79.3 8.1 %collective-permute-start.21 = (f32[136,256]{1,0:T(8,128)S(1)}, f32[136,256]{1,0:T(8,128)S(1)}, u32[]{:S(2)}, u32[]{:S(2)}) collective-permute-start(f32[136,256]{1,0:T(8,128)S(1)} %get-tuple-element.66), channel_id=1, source_target_pairs={{0,16},{4,20},{8,24},{12,28},{16,0},{20,4},{24,8},{28,12},{32,48},... | collective-permute-start | bytes 417800 | tf_op jit(solution)/shard_map/ppermute | solution.py:408
  82.6 7.3 %collective-permute-start.20 = (f32[136,256]{1,0:T(8,128)S(1)}, f32[136,256]{1,0:T(8,128)S(1)}, u32[]{:S(2)}, u32[]{:S(2)}) collective-permute-start(f32[136,256]{1,0:T(8,128)S(1)} %get-tuple-element.66), channel_id=1, source_target_pairs={{0,8},{4,12},{8,16},{12,20},{16,24},{20,28},{24,0},{28,4},{32,40},... | collective-permute-start | bytes 417800 | tf_op jit(solution)/shard_map/ppermute | solution.py:408
  83.3 6.8 %collective-permute-start.19 = (f32[136,256]{1,0:T(8,128)S(1)}, f32[136,256]{1,0:T(8,128)S(1)}, u32[]{:S(2)}, u32[]{:S(2)}) collective-permute-start(f32[136,256]{1,0:T(8,128)S(1)} %get-tuple-element.66), channel_id=1, source_target_pairs={{0,24},{4,28},{8,0},{12,4},{16,8},{20,12},{24,16},{28,20},{32,56},... | collective-permute-start | bytes 417800 | tf_op jit(solution)/shard_map/ppermute | solution.py:408
  87.4 3.0 %collective-permute-start.24 = (f32[136,256]{1,0:T(8,128)S(1)}, f32[136,256]{1,0:T(8,128)S(1)}, u32[]{:S(2)}, u32[]{:S(2)}) collective-permute-start(f32[136,256]{1,0:T(8,128)S(1)} %collective-permute-done.21.h3), channel_id=1, source_target_pairs={{0,4},{4,0},{8,12},{12,8},{16,20},{20,16},{24,28},{28,24},{32,36},... | collective-permute-start | bytes 417800 | tf_op jit(solution)/shard_map/ppermute | solution.py:403
  90.1 1.4 %collective-permute-start.22 = (f32[136,256]{1,0:T(8,128)S(1)}, f32[136,256]{1,0:T(8,128)S(1)}, u32[]{:S(2)}, u32[]{:S(2)}) collective-permute-start(f32[136,256]{1,0:T(8,128)S(1)} %collective-permute-done.19.h1), channel_id=1, source_target_pairs={{0,4},{4,0},{8,12},{12,8},{16,20},{20,16},{24,28},{28,24},{32,36},... | collective-permute-start | bytes 417800 | tf_op jit(solution)/shard_map/ppermute | solution.py:403
  92.8 8.1 %collective-permute-start.27 = (f32[136,256]{1,0:T(8,128)S(1)}, f32[136,256]{1,0:T(8,128)S(1)}, u32[]{:S(2)}, u32[]{:S(2)}) collective-permute-start(f32[136,256]{1,0:T(8,128)S(1)} %get-tuple-element.67), channel_id=1, source_target_pairs={{0,64},{4,68},{8,72},{12,76},{16,80},{20,84},{24,88},{28,92},{32,9... | collective-permute-start | bytes 417800 | tf_op jit(solution)/shard_map/ppermute | solution.py:408
  94.2 6.8 %collective-permute-start.26 = (f32[136,256]{1,0:T(8,128)S(1)}, f32[136,256]{1,0:T(8,128)S(1)}, u32[]{:S(2)}, u32[]{:S(2)}) collective-permute-start(f32[136,256]{1,0:T(8,128)S(1)} %get-tuple-element.67), channel_id=1, source_target_pairs={{0,32},{4,36},{8,40},{12,44},{16,48},{20,52},{24,56},{28,60},{32,6... | collective-permute-start | bytes 417800 | tf_op jit(solution)/shard_map/ppermute | solution.py:408
  96.3 7.0 %collective-permute-start.25 = (f32[136,256]{1,0:T(8,128)S(1)}, f32[136,256]{1,0:T(8,128)S(1)}, u32[]{:S(2)}, u32[]{:S(2)}) collective-permute-start(f32[136,256]{1,0:T(8,128)S(1)} %get-tuple-element.67), channel_id=1, source_target_pairs={{0,96},{4,100},{8,104},{12,108},{16,112},{20,116},{24,120},{28,124... | collective-permute-start | bytes 417800 | tf_op jit(solution)/shard_map/ppermute | solution.py:408
  100.8 3.4 %collective-permute-start.30 = (f32[136,256]{1,0:T(8,128)S(1)}, f32[136,256]{1,0:T(8,128)S(1)}, u32[]{:S(2)}, u32[]{:S(2)}) collective-permute-start(f32[136,256]{1,0:T(8,128)S(1)} %collective-permute-done.27.h3), channel_id=1, source_target_pairs={{0,4},{4,0},{8,12},{12,8},{16,20},{20,16},{24,28},{28,24},{32,36},... | collective-permute-start | bytes 417800 | tf_op jit(solution)/shard_map/ppermute | solution.py:403
  101.1 3.1 %collective-permute-start.29 = (f32[136,256]{1,0:T(8,128)S(1)}, f32[136,256]{1,0:T(8,128)S(1)}, u32[]{:S(2)}, u32[]{:S(2)}) collective-permute-start(f32[136,256]{1,0:T(8,128)S(1)} %collective-permute-done.26.h2), channel_id=1, source_target_pairs={{0,4},{4,0},{8,12},{12,8},{16,20},{20,16},{24,28},{28,24},{32,36},... | collective-permute-start | bytes 417800 | tf_op jit(solution)/shard_map/ppermute | solution.py:403
  106.9 5.2 %collective-permute-start.31 = (f32[16,64]{1,0:T(8,128)S(1)}, f32[16,64]{1,0:T(8,128)S(1)}, u32[]{:S(2)}, u32[]{:S(2)}) collective-permute-start(f32[16,64]{1,0:T(8,128)S(1)} %get-tuple-element.72), channel_id=1, source_target_pairs={{0,2},{1,3},{2,0},{3,1},{4,6},{5,7},{6,4},{7,5},{8,10},{9,11},{10,... | collective-permute-start | bytes 12296 | tf_op jit(solution)/shard_map/ppermute | solution.py:334
  108.5 4.9 %collective-permute-start.32 = (f32[16,64]{1,0:T(8,128)S(1)}, f32[16,64]{1,0:T(8,128)S(1)}, u32[]{:S(2)}, u32[]{:S(2)}) collective-permute-start(f32[16,64]{1,0:T(8,128)S(1)} %get-tuple-element.73), channel_id=1, source_target_pairs={{0,1},{1,2},{2,3},{3,0},{4,5},{5,6},{6,7},{7,4},{8,9},{9,10},{10,1... | collective-permute-start | bytes 12296 | tf_op jit(solution)/shard_map/ppermute | solution.py:334
  111.4 3.7 %collective-permute-start.33 = (f32[16,64]{1,0:T(8,128)S(1)}, f32[16,64]{1,0:T(8,128)S(1)}, u32[]{:S(2)}, u32[]{:S(2)}) collective-permute-start(f32[16,64]{1,0:T(8,128)S(1)} %get-tuple-element.74), channel_id=1, source_target_pairs={{0,3},{1,0},{2,1},{3,2},{4,7},{5,4},{6,5},{7,6},{8,11},{9,8},{10,9... | collective-permute-start | bytes 12296 | tf_op jit(solution)/shard_map/ppermute | solution.py:334
  (6 other events, 89.9 us)

commit v13 on v12

--- a/solution.py
+++ b/solution.py
@@ -131,20 +131,17 @@
     )(rid, observed)
 
 
-def assemble(z, own, prev, after, opposite, ah, al):
+def assemble(z, k, own, prev, after, opposite, ah, al):
     for d in range(ROWS):
-        slot = lax.rem(z - d + ROWS, ROWS)
-        rows = pl.ds(pl.multiple_of(slot * 64, 64), 64)
-        for k in range(SUB):
-            ref, at = ((own, k), (prev, k), (opposite[k // HALF_SUB], k % HALF_SUB), (after, k))[d]
-            hi, lo = split(ref[at * 64 : (at + 1) * 64, :])
-            ah[k, rows, :] = hi
-            al[k, rows, :] = lo
+        rows = pl.ds(pl.multiple_of(lax.rem(z - d + ROWS, ROWS) * 64, 64), 64)
+        ref, at = ((own, k), (prev, k), (opposite[k // HALF_SUB], k % HALF_SUB), (after, k))[d]
+        hi, lo = split(ref[at * 64 : (at + 1) * 64, :])
+        ah[k, rows, :] = hi
+        al[k, rows, :] = lo
 
 
 def compose_kernel(idx, own, prev, after, q1, q2, b0, b1, b2, b3, pref, top, low, ah, al, b_s):
     z = idx[Z]
-    assemble(z, own, prev, after, (q1, q2), ah, al)
     for d, b in enumerate((b0, b1, b2, b3)):
         b_s[lax.rem(z - d + ROWS, ROWS)] = b[...]
     b = jnp.concatenate([b_s[i, :, :64] for i in range(ROWS)], axis=1)
@@ -152,9 +149,13 @@
     eye = lax.broadcasted_iota(jnp.int32, (N, N), 0) == lax.broadcasted_iota(jnp.int32, (N, N), 1)
     eye = jnp.where(eye, 1.0, 0.0).astype(BF16)
     chains = range(SUB // SEG)
+    for c in chains:
+        assemble(z, c * SEG, own, prev, after, (q1, q2), ah, al)
     for t in range(SEG):
         for c in chains:
             k = c * SEG + t
+            if t + 1 < SEG:
+                assemble(z, k + 1, own, prev, after, (q1, q2), ah, al)
             shift = jnp.where(first, b[k : k + 1, :], 0.0)
             if t == 0:
                 pref[k, :N, :] = dot_nt(eye, ah[k]) + dot_nt(eye, al[k])
@@ -171,23 +172,11 @@
 
 
 def combine(pos, m_s, before):
-    m01 = then(m_s[0], m_s[1])
-    m23 = then(m_s[2], m_s[3])
-    before[...] = eye_map()
-
-    @pl.when(pos == 1)
-    def _():
-        before[...] = m_s[0]
-
-    @pl.when(pos == 2)
-    def _():
-        before[...] = m01
-
-    @pl.when(pos == 3)
-    def _():
-        before[...] = then(m01, m_s[2])
-
-    return then(m01, m23)
+    m0, m2 = m_s[0], m_s[2]
+    m01, m23 = then(m0, m_s[1]), then(m2, m_s[3])
+    total, m012 = then(m01, m23), then(m01, m2)
+    before[...] = jnp.where(pos == 0, eye_map(), jnp.where(pos == 1, m0, jnp.where(pos == 2, m01, m012)))
+    return total
 
 
 def four_kernel(idx, t0, l0, t1, l1, t2, l2, t3, l3, total, before, m_s):
@@ -235,11 +224,7 @@
     half[...] = total[half_rows(c), :]
 
 
-def fold_kernel(idx, first, second, out):
-    out[...] = then(first[...], second[...])
-
-
-def states_kernel(idx, prior, h1, h2, h3, g1, g2, g3, before, pref, o0, o1, o2, o3, st_s, m_s, s_s):
+def states_kernel(idx, prior, h1, h2, h3, g1, g2, g3, ybefore, before, pref, o0, o1, o2, o3, st_s, m_s, s_s):
     z, pos = idx[Z], idx[X]
     join(pos, idx[C], (h1, h2, h3), (g1, g2, g3), m_s)
     s_s[...] = jnp.where(lax.broadcasted_iota(jnp.int32, (PAD, N), 0) == 0, prior[...], 0.0)
@@ -249,7 +234,7 @@
         def _(i=i):
             s_s[...] = apply(s_s[...], m_s[i])
 
-    s = apply(s_s[...], before[...])
+    s = apply(apply(s_s[...], ybefore[...]), before[...])
     eye = lax.broadcasted_iota(jnp.int32, (N, N), 0) == lax.broadcasted_iota(jnp.int32, (N, N), 1)
     for end in range(SEG, SUB + 1, SEG):
         col = jnp.sum(jnp.where(eye, s[0:1, :], 0.0), axis=1, keepdims=True)
@@ -419,12 +404,11 @@
         (column, *gathered(half, 2)),
         [pltpu.VMEM((4, R, N), F32), pltpu.VMEM((R, N), F32)],
     )
-    (before,) = call(fold_kernel, [(R, N)], idx, (ybefore, before))
     outs = call(
         states_kernel,
         [(SUB, 64)] * 4,
         idx,
-        (prior, *gathered(half, 8), before, pref),
+        (prior, *gathered(half, 8), ybefore, before, pref),
         [pltpu.VMEM((ROWS, SUB, 64), F32), pltpu.VMEM((4, R, N), F32), pltpu.VMEM((PAD, N), F32)],
     )
     got = [outs[0], along_row(outs[2], 2), along_row(outs[1], 1), along_row(outs[3], 3)]

time: 116 us -> 116 us (level)
    pallas_call x10 -> x9, Pallas kernels: 17.9 us -> 17.3 us  [call(): pl.pallas_call(kernel, out_shape=[pltpu.VMEM(s, t) for s, t in outs], in_...]
  transfers between devices with their start and end apart: 34 -> 34, of which waited for: 19 -> 19; matrix products, arithmetic and copies ran while one was open for 0% -> 0% of each run, Pallas kernels for 11% -> 10%
where the time goes in v13:
time: 116 us
  starting transfers between devices  40.3 us (35%)
  waiting for transfers between devices  33.4 us (29%)
  Pallas kernels  25.4 us (22%)
  blocking collectives  16.7 us (14%)
    ppermute x21, starting transfers between devices, along_row(): return lax.ppermute(x, 'row', [(i, (i + d) % ROWS) for i in range(ROWS)])  29.5 us
    ppermute x21, waiting for transfers between devices, along_row(): return lax.ppermute(x, 'row', [(i, (i + d) % ROWS) for i in range(ROWS)])  18.6 us
    pallas_call x9, Pallas kernels, call(): pl.pallas_call(kernel, out_shape=[pltpu.VMEM(s, t) for s, t in outs], in_...  17.3 us
    all_to_all x1, blocking collectives, shards(): sums = lax.all_to_all(partial, 'tm', 0, 0, tiled=True).reshape(32, 16, N)  16.7 us
    ppermute x6, waiting for transfers between devices, gathered(): lax.ppermute(half, 'tm', [(i, i - i % n + (i + d * stride) % n) for i in...  10.9 us
    ppermute x6, starting transfers between devices, gathered(): lax.ppermute(half, 'tm', [(i, i - i % n + (i + d * stride) % n) for i in...  10.1 us
    pallas_call x1, Pallas kernels, binned(): pl.pallas_call(bin_kernel, out_shape=jax.ShapeDtypeStruct((n_bins // 4, N...  6.91 us
    ppermute x7, waiting for transfers between devices, other_core(): return lax.ppermute(m, 'tm', [(i, i ^ 1) for i in range(32)])  3.94 us
  transfers between devices with their start and end apart: 34, of which 19 were waited for; matrix products, arithmetic and copies ran while one was open for 0% of the time, Pallas kernels for 10%

profile of v13, /device:TPU:6, one launch (start us, length us, event | category | flops | bytes accessed | tf_op | source)
XLA Modules:
  0.0 116.2 jit_solution(18444150945850118884)
XLA Ops:
  0.1 2.5 %shard_map.67 = (f32[512,256]{1,0:T(8,128)S(1)}, f32[512,256]{1,0:T(8,128)S(1)}, f32[1024,256]{1,0:T(8,128)S(1)}, f32[1024,256]{1,0:T(8,128)S(1)}) custom-call(s32[4]{0:T(128)S(1)} %pad_add_fusion.idx, f32[4096,256]{1,0:T(8,128)} %bitcast.14), custom_call_target="tpu_custom_call" | custom-call | tf_op jit(solution)/shard_map/pallas_call | solution.py:75
  2.6 2.0 %collective-permute-start.5 = (f32[512,256]{1,0:T(8,128)S(1)}, f32[512,256]{1,0:T(8,128)S(1)}, u32[]{:S(2)}, u32[]{:S(2)}) collective-permute-start(f32[512,256]{1,0:T(8,128)S(1)} %get-tuple-element.44), channel_id=1, source_target_pairs={{0,1},{1,2},{2,3},{3,0},{4,5},{5,6},{6,7},{7,4},{8,9},{9,10},{10,1... | collective-permute-start | bytes 1572872 | tf_op jit(solution)/shard_map/ppermute | solution.py:319
  4.6 2.2 %collective-permute-start.6 = (f32[512,256]{1,0:T(8,128)S(1)}, f32[512,256]{1,0:T(8,128)S(1)}, u32[]{:S(2)}, u32[]{:S(2)}) collective-permute-start(f32[512,256]{1,0:T(8,128)S(1)} %get-tuple-element.45), channel_id=1, source_target_pairs={{0,3},{1,0},{2,1},{3,2},{4,7},{5,4},{6,5},{7,6},{8,11},{9,8},{10,9... | collective-permute-start | bytes 1572872 | tf_op jit(solution)/shard_map/ppermute | solution.py:319
  6.8 3.2 %collective-permute-start.4 = (f32[1024,256]{1,0:T(8,128)S(1)}, f32[1024,256]{1,0:T(8,128)S(1)}, u32[]{:S(2)}, u32[]{:S(2)}) collective-permute-start(f32[1024,256]{1,0:T(8,128)S(1)} %get-tuple-element.43), channel_id=1, source_target_pairs={{0,3},{1,0},{2,1},{3,2},{4,7},{5,4},{6,5},{7,6},{8,11},{9,8},{10,9... | collective-permute-start | bytes 3145736 | tf_op jit(solution)/shard_map/ppermute | solution.py:319
  10.1 6.9 %shard_map.64 = f32[512,256]{1,0:T(8,128)S(1)} custom-call(s32[1,4096]{1,0:T(1,128)S(1)} %bitcast.12, f32[64,4096]{1,0:T(8,128)S(1)} %bitcast.11), custom_call_target="tpu_custom_call" | custom-call | tf_op jit(solution)/shard_map/pallas_call | solution.py:120
  17.0 16.7 %all_to_all.9.sums = f32[32,16,256]{2,1,0:T(8,128)S(1)} all-to-all(f32[32,16,256]{2,1,0:T(8,128)S(1)} %bitcast.10), channel_id=1, replica_groups=mesh['tm'=32,'row'=4] {'tm'}, dimensions={0} | all-to-all | bytes 1048576 | tf_op jit(solution)/shard_map/all_to_all | solution.py:345
  36.4 3.0 %shard_map.66 = (f32[64,64,256]{2,1,0:T(8,128)S(1)}, f32[1024,256]{1,0:T(8,128)S(1)}) custom-call(s32[4]{0:T(128)S(1)} %pad_add_fusion.idx, f32[64,64,256]{2,1,0:T(8,128)} %gains.1, f32[4096,256]{1,0:T(8,128)} %bitcast.15, f32[16,256]{1,0:T(8,128)S(1)} %shard_map.65.info.i0), custom_call_target="tpu_custom_call" | custom-call | tf_op jit(solution)/shard_map/pallas_call | solution.py:75
  39.5 1.7 %collective-permute-done.2.r3 = f32[16,256]{1,0:T(8,128)S(1)} collective-permute-done((f32[16,256]{1,0:T(8,128)S(1)}, f32[16,256]{1,0:T(8,128)S(1)}, u32[]{:S(2)}, u32[]{:S(2)}) %collective-permute-start.2) | collective-permute-done | bytes 16416 | tf_op jit(solution)/shard_map/ppermute | solution.py:319
  41.2 1.6 %collective-permute-done.1.r2 = f32[16,256]{1,0:T(8,128)S(1)} collective-permute-done((f32[16,256]{1,0:T(8,128)S(1)}, f32[16,256]{1,0:T(8,128)S(1)}, u32[]{:S(2)}, u32[]{:S(2)}) %collective-permute-start.1) | collective-permute-done | bytes 16416 | tf_op jit(solution)/shard_map/ppermute | solution.py:319
  42.8 1.4 %collective-permute-start.7 = (f32[512,256]{1,0:T(8,128)S(1)}, f32[512,256]{1,0:T(8,128)S(1)}, u32[]{:S(2)}, u32[]{:S(2)}) collective-permute-start(f32[512,256]{1,0:T(8,128)S(1)} %collective-permute-done.5), channel_id=1, source_target_pairs={{0,1},{1,2},{2,3},{3,0},{4,5},{5,6},{6,7},{7,4},{8,9},{9,10},{10,1... | collective-permute-start | bytes 1572872 | tf_op jit(solution)/shard_map/ppermute | solution.py:319
  44.2 1.9 %collective-permute-start.8 = (f32[512,256]{1,0:T(8,128)S(1)}, f32[512,256]{1,0:T(8,128)S(1)}, u32[]{:S(2)}, u32[]{:S(2)}) collective-permute-start(f32[512,256]{1,0:T(8,128)S(1)} %collective-permute-done.6), channel_id=1, source_target_pairs={{0,3},{1,0},{2,1},{3,2},{4,7},{5,4},{6,5},{7,6},{8,11},{9,8},{10,9... | collective-permute-start | bytes 1572872 | tf_op jit(solution)/shard_map/ppermute | solution.py:319
  46.1 1.6 %shard_map.68 = (f32[16,256]{1,0:T(8,128)S(1)}, f32[16,256]{1,0:T(8,128)S(1)}, f32[16,256]{1,0:T(8,128)S(1)}, f32[16,256]{1,0:T(8,128)S(1)}) custom-call(s32[4]{0:T(128)S(1)} %pad_add_fusion.idx, f32[64,64,256]{2,1,0:T(8,128)S(1)} %get-tuple-element.53.g, f32[16,256]{1,0:T(8,128)S(1)} %shard_map.65.info.i0, f32[16,256]{1,0:T(8,128)S(1)} %collective-permute-done.r1, ...), custom_call_target="tpu_custom_call" | custom-call | tf_op jit(solution)/shard_map/pallas_call | solution.py:75
  47.8 2.2 %collective-permute-start.10 = (f32[16,256]{1,0:T(8,128)S(1)}, f32[16,256]{1,0:T(8,128)S(1)}, u32[]{:S(2)}, u32[]{:S(2)}) collective-permute-start(f32[16,256]{1,0:T(8,128)S(1)} %get-tuple-element.59), channel_id=1, source_target_pairs={{0,2},{1,3},{2,0},{3,1},{4,6},{5,7},{6,4},{7,5},{8,10},{9,11},{10,... | collective-permute-start | bytes 49160 | tf_op jit(solution)/shard_map/ppermute | solution.py:319
  50.9 6.0 %collective-permute-done.9.b1 = f32[16,256]{1,0:T(8,128)S(1)} collective-permute-done((f32[16,256]{1,0:T(8,128)S(1)}, f32[16,256]{1,0:T(8,128)S(1)}, u32[]{:S(2)}, u32[]{:S(2)}) %collective-permute-start.9) | collective-permute-done | bytes 16416 | tf_op jit(solution)/shard_map/ppermute | solution.py:319
  57.7 3.7 %shard_map.69 = (f32[16,272,256]{2,1,0:T(8,128)S(1)}, f32[136,256]{1,0:T(8,128)S(1)}, f32[136,256]{1,0:T(8,128)S(1)}) custom-call(s32[4]{0:T(128)S(1)} %pad_add_fusion.idx, f32[1024,256]{1,0:T(8,128)S(1)} %get-tuple-element.48.own, f32[1024,256]{1,0:T(8,128)S(1)} %collective-permute-done.3.prev, f32[1024,256]{1,0:T(8,128)S(1)} %collective-permute-done.4.after, ...), custom_call_target="tpu_custom_call" | custom-call | tf_op jit(solution)/shard_map/pallas_call | solution.py:75
  62.4 2.3 %collective-permute-start.15 = (f32[136,256]{1,0:T(8,128)S(1)}, f32[136,256]{1,0:T(8,128)S(1)}, u32[]{:S(2)}, u32[]{:S(2)}) collective-permute-start(f32[136,256]{1,0:T(8,128)S(1)} %get-tuple-element.62.l0), channel_id=1, source_target_pairs={{0,3},{1,0},{2,1},{3,2},{4,7},{5,4},{6,5},{7,6},{8,11},{9,8},{10,9... | collective-permute-start | bytes 417800 | tf_op jit(solution)/shard_map/ppermute | solution.py:319
  66.7 2.5 %collective-permute-done.12.t1 = f32[136,256]{1,0:T(8,128)S(1)} collective-permute-done((f32[136,256]{1,0:T(8,128)S(1)}, f32[136,256]{1,0:T(8,128)S(1)}, u32[]{:S(2)}, u32[]{:S(2)}) %collective-permute-start.12) | collective-permute-done | bytes 139296 | tf_op jit(solution)/shard_map/ppermute | solution.py:319
  69.2 3.2 %collective-permute-start.16 = (f32[136,256]{1,0:T(8,128)S(1)}, f32[136,256]{1,0:T(8,128)S(1)}, u32[]{:S(2)}, u32[]{:S(2)}) collective-permute-start(f32[136,256]{1,0:T(8,128)S(1)} %collective-permute-done.15.l3), channel_id=1, source_target_pairs={{0,3},{1,0},{2,1},{3,2},{4,7},{5,4},{6,5},{7,6},{8,11},{9,8},{10,9... | collective-permute-start | bytes 417800 | tf_op jit(solution)/shard_map/ppermute | solution.py:319
  72.5 3.0 %collective-permute-done.14.t2 = f32[136,256]{1,0:T(8,128)S(1)} collective-permute-done((f32[136,256]{1,0:T(8,128)S(1)}, f32[136,256]{1,0:T(8,128)S(1)}, u32[]{:S(2)}, u32[]{:S(2)}) %collective-permute-start.14) | collective-permute-done | bytes 139296 | tf_op jit(solution)/shard_map/ppermute | solution.py:319
  77.0 1.5 %collective-permute-done.18.other = f32[272,256]{1,0:T(8,128)S(1)} collective-permute-done((f32[272,256]{1,0:T(8,128)S(1)}, f32[272,256]{1,0:T(8,128)S(1)}, u32[]{:S(2)}, u32[]{:S(2)}) %collective-permute-start.18) | collective-permute-done | bytes 278560 | tf_op jit(solution)/shard_map/ppermute | solution.py:388
  79.4 3.3 %collective-permute-start.21 = (f32[136,256]{1,0:T(8,128)S(1)}, f32[136,256]{1,0:T(8,128)S(1)}, u32[]{:S(2)}, u32[]{:S(2)}) collective-permute-start(f32[136,256]{1,0:T(8,128)S(1)} %get-tuple-element.66), channel_id=1, source_target_pairs={{0,16},{4,20},{8,24},{12,28},{16,0},{20,4},{24,8},{28,12},{32,48},... | collective-permute-start | bytes 417800 | tf_op jit(solution)/shard_map/ppermute | solution.py:393
  83.3 2.6 %collective-permute-start.19 = (f32[136,256]{1,0:T(8,128)S(1)}, f32[136,256]{1,0:T(8,128)S(1)}, u32[]{:S(2)}, u32[]{:S(2)}) collective-permute-start(f32[136,256]{1,0:T(8,128)S(1)} %get-tuple-element.66), channel_id=1, source_target_pairs={{0,24},{4,28},{8,0},{12,4},{16,8},{20,12},{24,16},{28,20},{32,56},... | collective-permute-start | bytes 417800 | tf_op jit(solution)/shard_map/ppermute | solution.py:393
  85.9 1.6 %collective-permute-done.21.h3 = f32[136,256]{1,0:T(8,128)S(1)} collective-permute-done((f32[136,256]{1,0:T(8,128)S(1)}, f32[136,256]{1,0:T(8,128)S(1)}, u32[]{:S(2)}, u32[]{:S(2)}) %collective-permute-start.21) | collective-permute-done | bytes 139296 | tf_op jit(solution)/shard_map/ppermute | solution.py:393
  87.5 2.4 %collective-permute-done.20.h2 = f32[136,256]{1,0:T(8,128)S(1)} collective-permute-done((f32[136,256]{1,0:T(8,128)S(1)}, f32[136,256]{1,0:T(8,128)S(1)}, u32[]{:S(2)}, u32[]{:S(2)}) %collective-permute-start.20) | collective-permute-done | bytes 139296 | tf_op jit(solution)/shard_map/ppermute | solution.py:393
  92.9 1.5 %collective-permute-start.27 = (f32[136,256]{1,0:T(8,128)S(1)}, f32[136,256]{1,0:T(8,128)S(1)}, u32[]{:S(2)}, u32[]{:S(2)}) collective-permute-start(f32[136,256]{1,0:T(8,128)S(1)} %get-tuple-element.67), channel_id=1, source_target_pairs={{0,64},{4,68},{8,72},{12,76},{16,80},{20,84},{24,88},{28,92},{32,9... | collective-permute-start | bytes 417800 | tf_op jit(solution)/shard_map/ppermute | solution.py:393
  94.3 2.1 %collective-permute-start.26 = (f32[136,256]{1,0:T(8,128)S(1)}, f32[136,256]{1,0:T(8,128)S(1)}, u32[]{:S(2)}, u32[]{:S(2)}) collective-permute-start(f32[136,256]{1,0:T(8,128)S(1)} %get-tuple-element.67), channel_id=1, source_target_pairs={{0,32},{4,36},{8,40},{12,44},{16,48},{20,52},{24,56},{28,60},{32,6... | collective-permute-start | bytes 417800 | tf_op jit(solution)/shard_map/ppermute | solution.py:393
  96.4 4.5 %collective-permute-done.27.h3 = f32[136,256]{1,0:T(8,128)S(1)} collective-permute-done((f32[136,256]{1,0:T(8,128)S(1)}, f32[136,256]{1,0:T(8,128)S(1)}, u32[]{:S(2)}, u32[]{:S(2)}) %collective-permute-start.27) | collective-permute-done | bytes 139296 | tf_op jit(solution)/shard_map/ppermute | solution.py:393
  101.5 2.0 %collective-permute-done.25.h1 = f32[136,256]{1,0:T(8,128)S(1)} collective-permute-done((f32[136,256]{1,0:T(8,128)S(1)}, f32[136,256]{1,0:T(8,128)S(1)}, u32[]{:S(2)}, u32[]{:S(2)}) %collective-permute-start.25) | collective-permute-done | bytes 139296 | tf_op jit(solution)/shard_map/ppermute | solution.py:393
  104.8 2.4 %shard_map.73 = (f32[16,64]{1,0:T(8,128)S(1)}, f32[16,64]{1,0:T(8,128)S(1)}, f32[16,64]{1,0:T(8,128)S(1)}, f32[16,64]{1,0:T(8,128)S(1)}) custom-call(s32[4]{0:T(128)S(1)} %pad_add_fusion.idx, f32[1,256]{1,0:T(1,128)S(1)} %bitcast.13, f32[136,256]{1,0:T(8,128)S(1)} %collective-permute-done.25.h1, f32[136,256]{1,0:T(8,128)S(1)} %collective-permute-done.26.h2, ...), custom_call_target="tpu_custom_call" | custom-call | tf_op jit(solution)/shard_map/pallas_call | solution.py:75
  107.2 1.5 %collective-permute-start.31 = (f32[16,64]{1,0:T(8,128)S(1)}, f32[16,64]{1,0:T(8,128)S(1)}, u32[]{:S(2)}, u32[]{:S(2)}) collective-permute-start(f32[16,64]{1,0:T(8,128)S(1)} %get-tuple-element.72), channel_id=1, source_target_pairs={{0,2},{1,3},{2,0},{3,1},{4,6},{5,7},{6,4},{7,5},{8,10},{9,11},{10,... | collective-permute-start | bytes 12296 | tf_op jit(solution)/shard_map/ppermute | solution.py:319
  108.7 2.6 %collective-permute-start.32 = (f32[16,64]{1,0:T(8,128)S(1)}, f32[16,64]{1,0:T(8,128)S(1)}, u32[]{:S(2)}, u32[]{:S(2)}) collective-permute-start(f32[16,64]{1,0:T(8,128)S(1)} %get-tuple-element.73), channel_id=1, source_target_pairs={{0,1},{1,2},{2,3},{3,0},{4,5},{5,6},{6,7},{7,4},{8,9},{9,10},{10,1... | collective-permute-start | bytes 12296 | tf_op jit(solution)/shard_map/ppermute | solution.py:319
  113.6 1.4 %collective-permute-done.33.r3 = f32[16,64]{1,0:T(8,128)S(1)} collective-permute-done((f32[16,64]{1,0:T(8,128)S(1)}, f32[16,64]{1,0:T(8,128)S(1)}, u32[]{:S(2)}, u32[]{:S(2)}) %collective-permute-start.33) | collective-permute-done | bytes 4128 | tf_op jit(solution)/shard_map/ppermute | solution.py:319
  (59 shorter events, 19.0 us)
Async XLA Ops:
  2.6 32.5 %collective-permute-start.5 = (f32[512,256]{1,0:T(8,128)S(1)}, f32[512,256]{1,0:T(8,128)S(1)}, u32[]{:S(2)}, u32[]{:S(2)}) collective-permute-start(f32[512,256]{1,0:T(8,128)S(1)} %get-tuple-element.44), channel_id=1, source_target_pairs={{0,1},{1,2},{2,3},{3,0},{4,5},{5,6},{6,7},{7,4},{8,9},{9,10},{10,1... | collective-permute-start | bytes 1572872 | tf_op jit(solution)/shard_map/ppermute | solution.py:319
  4.6 30.6 %collective-permute-start.6 = (f32[512,256]{1,0:T(8,128)S(1)}, f32[512,256]{1,0:T(8,128)S(1)}, u32[]{:S(2)}, u32[]{:S(2)}) collective-permute-start(f32[512,256]{1,0:T(8,128)S(1)} %get-tuple-element.45), channel_id=1, source_target_pairs={{0,3},{1,0},{2,1},{3,2},{4,7},{5,4},{6,5},{7,6},{8,11},{9,8},{10,9... | collective-permute-start | bytes 1572872 | tf_op jit(solution)/shard_map/ppermute | solution.py:319
  6.8 36.0 %collective-permute-start.3 = (f32[1024,256]{1,0:T(8,128)S(1)}, f32[1024,256]{1,0:T(8,128)S(1)}, u32[]{:S(2)}, u32[]{:S(2)}) collective-permute-start(f32[1024,256]{1,0:T(8,128)S(1)} %get-tuple-element.42), channel_id=1, source_target_pairs={{0,1},{1,2},{2,3},{3,0},{4,5},{5,6},{6,7},{7,4},{8,9},{9,10},{10,1... | collective-permute-start | bytes 3145736 | tf_op jit(solution)/shard_map/ppermute | solution.py:319
  6.8 36.0 %collective-permute-start.4 = (f32[1024,256]{1,0:T(8,128)S(1)}, f32[1024,256]{1,0:T(8,128)S(1)}, u32[]{:S(2)}, u32[]{:S(2)}) collective-permute-start(f32[1024,256]{1,0:T(8,128)S(1)} %get-tuple-element.43), channel_id=1, source_target_pairs={{0,3},{1,0},{2,1},{3,2},{4,7},{5,4},{6,5},{7,6},{8,11},{9,8},{10,9... | collective-permute-start | bytes 3145736 | tf_op jit(solution)/shard_map/ppermute | solution.py:319
  34.3 6.9 %collective-permute-start.2 = (f32[16,256]{1,0:T(8,128)S(1)}, f32[16,256]{1,0:T(8,128)S(1)}, u32[]{:S(2)}, u32[]{:S(2)}) collective-permute-start(f32[16,256]{1,0:T(8,128)S(1)} %shard_map.65.info.i0), channel_id=1, source_target_pairs={{0,3},{1,0},{2,1},{3,2},{4,7},{5,4},{6,5},{7,6},{8,11},{9,8},{10,9... | collective-permute-start | bytes 49160 | tf_op jit(solution)/shard_map/ppermute | solution.py:319
  35.1 7.7 %collective-permute-start.1 = (f32[16,256]{1,0:T(8,128)S(1)}, f32[16,256]{1,0:T(8,128)S(1)}, u32[]{:S(2)}, u32[]{:S(2)}) collective-permute-start(f32[16,256]{1,0:T(8,128)S(1)} %shard_map.65.info.i0), channel_id=1, source_target_pairs={{0,2},{1,3},{2,0},{3,1},{4,6},{5,7},{6,4},{7,5},{8,10},{9,11},{10,... | collective-permute-start | bytes 49160 | tf_op jit(solution)/shard_map/ppermute | solution.py:319
  35.2 7.6 %collective-permute-start = (f32[16,256]{1,0:T(8,128)S(1)}, f32[16,256]{1,0:T(8,128)S(1)}, u32[]{:S(2)}, u32[]{:S(2)}) collective-permute-start(f32[16,256]{1,0:T(8,128)S(1)} %shard_map.65.info.i0), channel_id=1, source_target_pairs={{0,1},{1,2},{2,3},{3,0},{4,5},{5,6},{6,7},{7,4},{8,9},{9,10},{10,1... | collective-permute-start | bytes 49160 | tf_op jit(solution)/shard_map/ppermute | solution.py:319
  42.8 14.9 %collective-permute-start.7 = (f32[512,256]{1,0:T(8,128)S(1)}, f32[512,256]{1,0:T(8,128)S(1)}, u32[]{:S(2)}, u32[]{:S(2)}) collective-permute-start(f32[512,256]{1,0:T(8,128)S(1)} %collective-permute-done.5), channel_id=1, source_target_pairs={{0,1},{1,2},{2,3},{3,0},{4,5},{5,6},{6,7},{7,4},{8,9},{9,10},{10,1... | collective-permute-start | bytes 1572872 | tf_op jit(solution)/shard_map/ppermute | solution.py:319
  44.2 13.5 %collective-permute-start.8 = (f32[512,256]{1,0:T(8,128)S(1)}, f32[512,256]{1,0:T(8,128)S(1)}, u32[]{:S(2)}, u32[]{:S(2)}) collective-permute-start(f32[512,256]{1,0:T(8,128)S(1)} %collective-permute-done.6), channel_id=1, source_target_pairs={{0,3},{1,0},{2,1},{3,2},{4,7},{5,4},{6,5},{7,6},{8,11},{9,8},{10,9... | collective-permute-start | bytes 1572872 | tf_op jit(solution)/shard_map/ppermute | solution.py:319
  47.7 9.3 %collective-permute-start.9 = (f32[16,256]{1,0:T(8,128)S(1)}, f32[16,256]{1,0:T(8,128)S(1)}, u32[]{:S(2)}, u32[]{:S(2)}) collective-permute-start(f32[16,256]{1,0:T(8,128)S(1)} %get-tuple-element.58), channel_id=1, source_target_pairs={{0,1},{1,2},{2,3},{3,0},{4,5},{5,6},{6,7},{7,4},{8,9},{9,10},{10,1... | collective-permute-start | bytes 49160 | tf_op jit(solution)/shard_map/ppermute | solution.py:319
  47.8 9.9 %collective-permute-start.10 = (f32[16,256]{1,0:T(8,128)S(1)}, f32[16,256]{1,0:T(8,128)S(1)}, u32[]{:S(2)}, u32[]{:S(2)}) collective-permute-start(f32[16,256]{1,0:T(8,128)S(1)} %get-tuple-element.59), channel_id=1, source_target_pairs={{0,2},{1,3},{2,0},{3,1},{4,6},{5,7},{6,4},{7,5},{8,10},{9,11},{10,... | collective-permute-start | bytes 49160 | tf_op jit(solution)/shard_map/ppermute | solution.py:319
  50.0 7.7 %collective-permute-start.11 = (f32[16,256]{1,0:T(8,128)S(1)}, f32[16,256]{1,0:T(8,128)S(1)}, u32[]{:S(2)}, u32[]{:S(2)}) collective-permute-start(f32[16,256]{1,0:T(8,128)S(1)} %get-tuple-element.60), channel_id=1, source_target_pairs={{0,3},{1,0},{2,1},{3,2},{4,7},{5,4},{6,5},{7,6},{8,11},{9,8},{10,9... | collective-permute-start | bytes 49160 | tf_op jit(solution)/shard_map/ppermute | solution.py:319
  61.4 7.8 %collective-permute-start.12 = (f32[136,256]{1,0:T(8,128)S(1)}, f32[136,256]{1,0:T(8,128)S(1)}, u32[]{:S(2)}, u32[]{:S(2)}) collective-permute-start(f32[136,256]{1,0:T(8,128)S(1)} %get-tuple-element.61.t0), channel_id=1, source_target_pairs={{0,1},{1,2},{2,3},{3,0},{4,5},{5,6},{6,7},{7,4},{8,9},{9,10},{10,1... | collective-permute-start | bytes 417800 | tf_op jit(solution)/shard_map/ppermute | solution.py:319
  62.4 6.8 %collective-permute-start.15 = (f32[136,256]{1,0:T(8,128)S(1)}, f32[136,256]{1,0:T(8,128)S(1)}, u32[]{:S(2)}, u32[]{:S(2)}) collective-permute-start(f32[136,256]{1,0:T(8,128)S(1)} %get-tuple-element.62.l0), channel_id=1, source_target_pairs={{0,3},{1,0},{2,1},{3,2},{4,7},{5,4},{6,5},{7,6},{8,11},{9,8},{10,9... | collective-permute-start | bytes 417800 | tf_op jit(solution)/shard_map/ppermute | solution.py:319
  64.7 7.8 %collective-permute-start.17 = (f32[136,256]{1,0:T(8,128)S(1)}, f32[136,256]{1,0:T(8,128)S(1)}, u32[]{:S(2)}, u32[]{:S(2)}) collective-permute-start(f32[136,256]{1,0:T(8,128)S(1)} %get-tuple-element.61.t0), channel_id=1, source_target_pairs={{0,3},{1,0},{2,1},{3,2},{4,7},{5,4},{6,5},{7,6},{8,11},{9,8},{10,9... | collective-permute-start | bytes 417800 | tf_op jit(solution)/shard_map/ppermute | solution.py:319
  65.9 6.6 %collective-permute-start.13 = (f32[136,256]{1,0:T(8,128)S(1)}, f32[136,256]{1,0:T(8,128)S(1)}, u32[]{:S(2)}, u32[]{:S(2)}) collective-permute-start(f32[136,256]{1,0:T(8,128)S(1)} %get-tuple-element.62.l0), channel_id=1, source_target_pairs={{0,1},{1,2},{2,3},{3,0},{4,5},{5,6},{6,7},{7,4},{8,9},{9,10},{10,1... | collective-permute-start | bytes 417800 | tf_op jit(solution)/shard_map/ppermute | solution.py:319
  69.2 6.3 %collective-permute-start.14 = (f32[136,256]{1,0:T(8,128)S(1)}, f32[136,256]{1,0:T(8,128)S(1)}, u32[]{:S(2)}, u32[]{:S(2)}) collective-permute-start(f32[136,256]{1,0:T(8,128)S(1)} %collective-permute-done.12.t1), channel_id=1, source_target_pairs={{0,1},{1,2},{2,3},{3,0},{4,5},{5,6},{6,7},{7,4},{8,9},{9,10},{10,1... | collective-permute-start | bytes 417800 | tf_op jit(solution)/shard_map/ppermute | solution.py:319
  69.2 6.3 %collective-permute-start.16 = (f32[136,256]{1,0:T(8,128)S(1)}, f32[136,256]{1,0:T(8,128)S(1)}, u32[]{:S(2)}, u32[]{:S(2)}) collective-permute-start(f32[136,256]{1,0:T(8,128)S(1)} %collective-permute-done.15.l3), channel_id=1, source_target_pairs={{0,3},{1,0},{2,1},{3,2},{4,7},{5,4},{6,5},{7,6},{8,11},{9,8},{10,9... | collective-permute-start | bytes 417800 | tf_op jit(solution)/shard_map/ppermute | solution.py:319
  76.9 1.6 %collective-permute-start.18 = (f32[272,256]{1,0:T(8,128)S(1)}, f32[272,256]{1,0:T(8,128)S(1)}, u32[]{:S(2)}, u32[]{:S(2)}) collective-permute-start(f32[272,256]{1,0:T(8,128)S(1)} %get-tuple-element.63.own), channel_id=1, source_target_pairs={{0,4},{4,0},{8,12},{12,8},{16,20},{20,16},{24,28},{28,24},{32,36},... | collective-permute-start | bytes 835592 | tf_op jit(solution)/shard_map/ppermute | solution.py:388
  79.4 8.1 %collective-permute-start.21 = (f32[136,256]{1,0:T(8,128)S(1)}, f32[136,256]{1,0:T(8,128)S(1)}, u32[]{:S(2)}, u32[]{:S(2)}) collective-permute-start(f32[136,256]{1,0:T(8,128)S(1)} %get-tuple-element.66), channel_id=1, source_target_pairs={{0,16},{4,20},{8,24},{12,28},{16,0},{20,4},{24,8},{28,12},{32,48},... | collective-permute-start | bytes 417800 | tf_op jit(solution)/shard_map/ppermute | solution.py:393
  82.7 7.3 %collective-permute-start.20 = (f32[136,256]{1,0:T(8,128)S(1)}, f32[136,256]{1,0:T(8,128)S(1)}, u32[]{:S(2)}, u32[]{:S(2)}) collective-permute-start(f32[136,256]{1,0:T(8,128)S(1)} %get-tuple-element.66), channel_id=1, source_target_pairs={{0,8},{4,12},{8,16},{12,20},{16,24},{20,28},{24,0},{28,4},{32,40},... | collective-permute-start | bytes 417800 | tf_op jit(solution)/shard_map/ppermute | solution.py:393
  83.3 6.8 %collective-permute-start.19 = (f32[136,256]{1,0:T(8,128)S(1)}, f32[136,256]{1,0:T(8,128)S(1)}, u32[]{:S(2)}, u32[]{:S(2)}) collective-permute-start(f32[136,256]{1,0:T(8,128)S(1)} %get-tuple-element.66), channel_id=1, source_target_pairs={{0,24},{4,28},{8,0},{12,4},{16,8},{20,12},{24,16},{28,20},{32,56},... | collective-permute-start | bytes 417800 | tf_op jit(solution)/shard_map/ppermute | solution.py:393
  87.5 3.0 %collective-permute-start.24 = (f32[136,256]{1,0:T(8,128)S(1)}, f32[136,256]{1,0:T(8,128)S(1)}, u32[]{:S(2)}, u32[]{:S(2)}) collective-permute-start(f32[136,256]{1,0:T(8,128)S(1)} %collective-permute-done.21.h3), channel_id=1, source_target_pairs={{0,4},{4,0},{8,12},{12,8},{16,20},{20,16},{24,28},{28,24},{32,36},... | collective-permute-start | bytes 417800 | tf_op jit(solution)/shard_map/ppermute | solution.py:388
  90.1 1.4 %collective-permute-start.22 = (f32[136,256]{1,0:T(8,128)S(1)}, f32[136,256]{1,0:T(8,128)S(1)}, u32[]{:S(2)}, u32[]{:S(2)}) collective-permute-start(f32[136,256]{1,0:T(8,128)S(1)} %collective-permute-done.19.h1), channel_id=1, source_target_pairs={{0,4},{4,0},{8,12},{12,8},{16,20},{20,16},{24,28},{28,24},{32,36},... | collective-permute-start | bytes 417800 | tf_op jit(solution)/shard_map/ppermute | solution.py:388
  92.9 8.1 %collective-permute-start.27 = (f32[136,256]{1,0:T(8,128)S(1)}, f32[136,256]{1,0:T(8,128)S(1)}, u32[]{:S(2)}, u32[]{:S(2)}) collective-permute-start(f32[136,256]{1,0:T(8,128)S(1)} %get-tuple-element.67), channel_id=1, source_target_pairs={{0,64},{4,68},{8,72},{12,76},{16,80},{20,84},{24,88},{28,92},{32,9... | collective-permute-start | bytes 417800 | tf_op jit(solution)/shard_map/ppermute | solution.py:393
  94.3 6.8 %collective-permute-start.26 = (f32[136,256]{1,0:T(8,128)S(1)}, f32[136,256]{1,0:T(8,128)S(1)}, u32[]{:S(2)}, u32[]{:S(2)}) collective-permute-start(f32[136,256]{1,0:T(8,128)S(1)} %get-tuple-element.67), channel_id=1, source_target_pairs={{0,32},{4,36},{8,40},{12,44},{16,48},{20,52},{24,56},{28,60},{32,6... | collective-permute-start | bytes 417800 | tf_op jit(solution)/shard_map/ppermute | solution.py:393
  96.4 7.0 %collective-permute-start.25 = (f32[136,256]{1,0:T(8,128)S(1)}, f32[136,256]{1,0:T(8,128)S(1)}, u32[]{:S(2)}, u32[]{:S(2)}) collective-permute-start(f32[136,256]{1,0:T(8,128)S(1)} %get-tuple-element.67), channel_id=1, source_target_pairs={{0,96},{4,100},{8,104},{12,108},{16,112},{20,116},{24,120},{28,124... | collective-permute-start | bytes 417800 | tf_op jit(solution)/shard_map/ppermute | solution.py:393
  100.9 2.5 %collective-permute-start.30 = (f32[136,256]{1,0:T(8,128)S(1)}, f32[136,256]{1,0:T(8,128)S(1)}, u32[]{:S(2)}, u32[]{:S(2)}) collective-permute-start(f32[136,256]{1,0:T(8,128)S(1)} %collective-permute-done.27.h3), channel_id=1, source_target_pairs={{0,4},{4,0},{8,12},{12,8},{16,20},{20,16},{24,28},{28,24},{32,36},... | collective-permute-start | bytes 417800 | tf_op jit(solution)/shard_map/ppermute | solution.py:388
  101.2 2.3 %collective-permute-start.29 = (f32[136,256]{1,0:T(8,128)S(1)}, f32[136,256]{1,0:T(8,128)S(1)}, u32[]{:S(2)}, u32[]{:S(2)}) collective-permute-start(f32[136,256]{1,0:T(8,128)S(1)} %collective-permute-done.26.h2), channel_id=1, source_target_pairs={{0,4},{4,0},{8,12},{12,8},{16,20},{20,16},{24,28},{28,24},{32,36},... | collective-permute-start | bytes 417800 | tf_op jit(solution)/shard_map/ppermute | solution.py:388
  107.2 5.2 %collective-permute-start.31 = (f32[16,64]{1,0:T(8,128)S(1)}, f32[16,64]{1,0:T(8,128)S(1)}, u32[]{:S(2)}, u32[]{:S(2)}) collective-permute-start(f32[16,64]{1,0:T(8,128)S(1)} %get-tuple-element.72), channel_id=1, source_target_pairs={{0,2},{1,3},{2,0},{3,1},{4,6},{5,7},{6,4},{7,5},{8,10},{9,11},{10,... | collective-permute-start | bytes 12296 | tf_op jit(solution)/shard_map/ppermute | solution.py:319
  108.7 4.9 %collective-permute-start.32 = (f32[16,64]{1,0:T(8,128)S(1)}, f32[16,64]{1,0:T(8,128)S(1)}, u32[]{:S(2)}, u32[]{:S(2)}) collective-permute-start(f32[16,64]{1,0:T(8,128)S(1)} %get-tuple-element.73), channel_id=1, source_target_pairs={{0,1},{1,2},{2,3},{3,0},{4,5},{5,6},{6,7},{7,4},{8,9},{9,10},{10,1... | collective-permute-start | bytes 12296 | tf_op jit(solution)/shard_map/ppermute | solution.py:319
  111.4 3.7 %collective-permute-start.33 = (f32[16,64]{1,0:T(8,128)S(1)}, f32[16,64]{1,0:T(8,128)S(1)}, u32[]{:S(2)}, u32[]{:S(2)}) collective-permute-start(f32[16,64]{1,0:T(8,128)S(1)} %get-tuple-element.74), channel_id=1, source_target_pairs={{0,3},{1,0},{2,1},{3,2},{4,7},{5,4},{6,5},{7,6},{8,11},{9,8},{10,9... | collective-permute-start | bytes 12296 | tf_op jit(solution)/shard_map/ppermute | solution.py:319
  (6 other events, 90.0 us)

commit v14 on v12

--- a/solution.py
+++ b/solution.py
@@ -266,17 +266,11 @@
 COPIED = 4
 
 
-def send_kernel(idx, flat, ahead_far, back_far, ahead, back, sems):
-    z = idx[Z]
+def copied(idx, flat, wanted, sems):
     copies = []
-    for out, d, first, count in (
-        (ahead_far, 2, 0, HALF_SUB),
-        (back_far, 2, HALF_SUB, HALF_SUB),
-        (ahead, 1, 0, SUB),
-        (back, 3, 0, SUB),
-    ):
+    for out, d, first, count in wanted:
         for at in range(0, count, COPIED):
-            source = lax.rem(z + d, ROWS) * (SUB * 64) + (first + at) * 64
+            source = lax.rem(idx[Z] + d, ROWS) * (SUB * 64) + (first + at) * 64
             copies.append(
                 pltpu.make_async_copy(
                     flat.at[pl.ds(pl.multiple_of(source, 64), COPIED * 64)],
@@ -290,15 +284,18 @@
         copy.wait()
 
 
-def stage_kernel(idx, gains, flat, info, staged, own, sems):
-    copies = [
-        pltpu.make_async_copy(gains, staged, sems.at[0]),
-        pltpu.make_async_copy(flat.at[pl.ds(pl.multiple_of(idx[Z] * (SUB * 64), 64), SUB * 64)], own, sems.at[1]),
-    ]
-    for copy in copies:
-        copy.start()
-    for copy in copies:
-        copy.wait()
+def far_kernel(idx, flat, ahead, back, sems):
+    copied(idx, flat, ((ahead, 2, 0, HALF_SUB), (back, 2, HALF_SUB, HALF_SUB)), sems)
+
+
+def near_kernel(idx, flat, far_ahead, ahead, back, own, sems):
+    copied(idx, flat, ((ahead, 1, 0, SUB), (back, 3, 0, SUB), (own, 0, 0, SUB)), sems)
+
+
+def stage_kernel(idx, gains, info, staged, sem):
+    copy = pltpu.make_async_copy(gains, staged, sem)
+    copy.start()
+    copy.wait()
 
 
 def sum_kernel(idx, sums, info):
@@ -344,13 +341,10 @@
     def along_rows(blocks):
         return [along_row(b, d) for d, b in enumerate(blocks, 1)]
 
-    *far, ahead, back = call(
-        send_kernel,
-        [(HALF_SUB * 64, N)] * 2 + [(SUB * 64, N)] * 2,
-        idx,
-        (),
-        [pltpu.SemaphoreType.DMA((3 * SUB // COPIED,))],
-        far=(flat,),
+    dma = pltpu.SemaphoreType.DMA
+    far = call(far_kernel, [(HALF_SUB * 64, N)] * 2, idx, (), [dma((SUB // COPIED,))], far=(flat,))
+    ahead, back, own = call(
+        near_kernel, [(SUB * 64, N)] * 3, idx, far[:1], [dma((3 * SUB // COPIED,))], far=(flat,)
     )
     far = [along_row(f, d) for f, d in zip(far, (1, 3))]
     prev, after = along_row(ahead, 1), along_row(back, 3)
@@ -360,14 +354,7 @@
     sums = lax.all_to_all(partial, "tm", 0, 0, tiled=True).reshape(32, 16, N)
     (info,) = call(sum_kernel, [(16, N)], idx, (sums,))
     infos = along_rows([info] * 3)
-    staged, own = call(
-        stage_kernel,
-        [gains.shape, (SUB * 64, N)],
-        idx,
-        (info,),
-        [pltpu.SemaphoreType.DMA((2,))],
-        far=(gains, flat),
-    )
+    (staged,) = call(stage_kernel, [gains.shape], idx, (info,), [dma], far=(gains,))
     infos, staged, own, prev, after, far, idx, prior = lax.optimization_barrier(
         (infos, staged, own, prev, after, far, idx, prior)
     )

time: 116 us -> 117 us (level)
  waiting for transfers between devices: 32.9 us -> 30.2 us
  Pallas kernels: 26 us -> 27.4 us
  starting transfers between devices: 40.3 us -> 41.6 us
    ppermute x21, waiting for transfers between devices: 18.8 us -> 16 us  [along_row(): return lax.ppermute(x, 'row', [(i, (i + d) % ROWS) for i in range(ROWS)])]
    ppermute x21, starting transfers between devices: 29.5 us -> 31 us  [along_row(): return lax.ppermute(x, 'row', [(i, (i + d) % ROWS) for i in range(ROWS)])]
    pallas_call x10 -> x11, Pallas kernels: 17.9 us -> 19.4 us  [call(): pl.pallas_call(kernel, out_shape=[pltpu.VMEM(s, t) for s, t in outs], in_...]
  transfers between devices with their start and end apart: 34 -> 34, of which waited for: 19 -> 18; matrix products, arithmetic and copies ran while one was open for 0% -> 0% of each run, Pallas kernels for 11% -> 13%
where the time goes in v14:
time: 117 us; the launch traced here: 116 us
  starting transfers between devices  41.6 us (36%)
  waiting for transfers between devices  30.2 us (26%)
  Pallas kernels  27.4 us (23%)
  blocking collectives  16.7 us (14%)
    ppermute x21, starting transfers between devices, along_row(): return lax.ppermute(x, 'row', [(i, (i + d) % ROWS) for i in range(ROWS)])  31 us
    pallas_call x11, Pallas kernels, call(): pl.pallas_call(kernel, out_shape=[pltpu.VMEM(s, t) for s, t in outs], in_...  19.4 us
    all_to_all x1, blocking collectives, shards(): sums = lax.all_to_all(partial, 'tm', 0, 0, tiled=True).reshape(32, 16, N)  16.7 us
    ppermute x21, waiting for transfers between devices, along_row(): return lax.ppermute(x, 'row', [(i, (i + d) % ROWS) for i in range(ROWS)])  16 us
    ppermute x6, waiting for transfers between devices, gathered(): lax.ppermute(half, 'tm', [(i, i - i % n + (i + d * stride) % n) for i in...  11.1 us
    ppermute x6, starting transfers between devices, gathered(): lax.ppermute(half, 'tm', [(i, i - i % n + (i + d * stride) % n) for i in...  10.2 us
    pallas_call x1, Pallas kernels, binned(): pl.pallas_call(bin_kernel, out_shape=jax.ShapeDtypeStruct((n_bins // 4, N...  6.91 us
    ppermute x7, waiting for transfers between devices, other_core(): return lax.ppermute(m, 'tm', [(i, i ^ 1) for i in range(32)])  3.09 us
  transfers between devices with their start and end apart: 34, of which 18 were waited for; matrix products, arithmetic and copies ran while one was open for 0% of the time, Pallas kernels for 13%

profile of v14, /device:TPU:6, one launch (start us, length us, event | category | flops | bytes accessed | tf_op | source)
XLA Modules:
  0.0 116.2 jit_solution(11015228154308234596)
XLA Ops:
  0.1 1.8 %shard_map.67 = (f32[512,256]{1,0:T(8,128)S(1)}, f32[512,256]{1,0:T(8,128)S(1)}) custom-call(s32[4]{0:T(128)S(1)} %pad_add_fusion.idx, f32[4096,256]{1,0:T(8,128)} %bitcast.14), custom_call_target="tpu_custom_call" | custom-call | tf_op jit(solution)/shard_map/pallas_call | solution.py:75
  1.9 4.1 %collective-permute-start.6 = (f32[512,256]{1,0:T(8,128)S(1)}, f32[512,256]{1,0:T(8,128)S(1)}, u32[]{:S(2)}, u32[]{:S(2)}) collective-permute-start(f32[512,256]{1,0:T(8,128)S(1)} %get-tuple-element.43), channel_id=1, source_target_pairs={{0,3},{1,0},{2,1},{3,2},{4,7},{5,4},{6,5},{7,6},{8,11},{9,8},{10,9... | collective-permute-start | bytes 1572872 | tf_op jit(solution)/shard_map/ppermute | solution.py:331
  6.0 2.5 %shard_map.68 = (f32[1024,256]{1,0:T(8,128)S(1)}, f32[1024,256]{1,0:T(8,128)S(1)}, f32[1024,256]{1,0:T(8,128)S(1)}) custom-call(s32[4]{0:T(128)S(1)} %pad_add_fusion.idx, f32[4096,256]{1,0:T(8,128)} %bitcast.15, f32[512,256]{1,0:T(8,128)S(1)} %get-tuple-element.39.far_ahead), custom_call_target="tpu_custom_call" | custom-call | tf_op jit(solution)/shard_map/pallas_call | solution.py:75
  8.5 3.3 %collective-permute-start.4 = (f32[1024,256]{1,0:T(8,128)S(1)}, f32[1024,256]{1,0:T(8,128)S(1)}, u32[]{:S(2)}, u32[]{:S(2)}) collective-permute-start(f32[1024,256]{1,0:T(8,128)S(1)} %get-tuple-element.42), channel_id=1, source_target_pairs={{0,3},{1,0},{2,1},{3,2},{4,7},{5,4},{6,5},{7,6},{8,11},{9,8},{10,9... | collective-permute-start | bytes 3145736 | tf_op jit(solution)/shard_map/ppermute | solution.py:331
  11.9 6.9 %shard_map.64 = f32[512,256]{1,0:T(8,128)S(1)} custom-call(s32[1,4096]{1,0:T(1,128)S(1)} %bitcast.12, f32[64,4096]{1,0:T(8,128)S(1)} %bitcast.11), custom_call_target="tpu_custom_call" | custom-call | tf_op jit(solution)/shard_map/pallas_call | solution.py:120
  18.8 16.7 %all_to_all.9.sums = f32[32,16,256]{2,1,0:T(8,128)S(1)} all-to-all(f32[32,16,256]{2,1,0:T(8,128)S(1)} %bitcast.10), channel_id=1, replica_groups=mesh['tm'=32,'row'=4] {'tm'}, dimensions={0} | all-to-all | bytes 1048576 | tf_op jit(solution)/shard_map/all_to_all | solution.py:354
  36.1 2.0 %collective-permute-start.2 = (f32[16,256]{1,0:T(8,128)S(1)}, f32[16,256]{1,0:T(8,128)S(1)}, u32[]{:S(2)}, u32[]{:S(2)}) collective-permute-start(f32[16,256]{1,0:T(8,128)S(1)} %shard_map.65.info.i0), channel_id=1, source_target_pairs={{0,3},{1,0},{2,1},{3,2},{4,7},{5,4},{6,5},{7,6},{8,11},{9,8},{10,9... | collective-permute-start | bytes 49160 | tf_op jit(solution)/shard_map/ppermute | solution.py:331
  39.1 2.7 %shard_map.66.g = f32[64,64,256]{2,1,0:T(8,128)S(1)} custom-call(s32[4]{0:T(128)S(1)} %pad_add_fusion.idx, f32[64,64,256]{2,1,0:T(8,128)} %gains.1, f32[16,256]{1,0:T(8,128)S(1)} %shard_map.65.info.i0), custom_call_target="tpu_custom_call" | custom-call | tf_op jit(solution)/shard_map/pallas_call | solution.py:75
  41.8 1.5 %collective-permute-done.1.r2 = f32[16,256]{1,0:T(8,128)S(1)} collective-permute-done((f32[16,256]{1,0:T(8,128)S(1)}, f32[16,256]{1,0:T(8,128)S(1)}, u32[]{:S(2)}, u32[]{:S(2)}) %collective-permute-start.1) | collective-permute-done | bytes 16416 | tf_op jit(solution)/shard_map/ppermute | solution.py:331
  44.5 2.5 %collective-permute-start.8 = (f32[512,256]{1,0:T(8,128)S(1)}, f32[512,256]{1,0:T(8,128)S(1)}, u32[]{:S(2)}, u32[]{:S(2)}) collective-permute-start(f32[512,256]{1,0:T(8,128)S(1)} %collective-permute-done.6), channel_id=1, source_target_pairs={{0,3},{1,0},{2,1},{3,2},{4,7},{5,4},{6,5},{7,6},{8,11},{9,8},{10,9... | collective-permute-start | bytes 1572872 | tf_op jit(solution)/shard_map/ppermute | solution.py:331
  47.0 1.6 %shard_map.69 = (f32[16,256]{1,0:T(8,128)S(1)}, f32[16,256]{1,0:T(8,128)S(1)}, f32[16,256]{1,0:T(8,128)S(1)}, f32[16,256]{1,0:T(8,128)S(1)}) custom-call(s32[4]{0:T(128)S(1)} %pad_add_fusion.idx, f32[64,64,256]{2,1,0:T(8,128)S(1)} %shard_map.66.g, f32[16,256]{1,0:T(8,128)S(1)} %shard_map.65.info.i0, f32[16,256]{1,0:T(8,128)S(1)} %collective-permute-done.r1, ...), custom_call_target="tpu_custom_call" | custom-call | tf_op jit(solution)/shard_map/pallas_call | solution.py:75
  50.0 1.8 %collective-permute-start.11 = (f32[16,256]{1,0:T(8,128)S(1)}, f32[16,256]{1,0:T(8,128)S(1)}, u32[]{:S(2)}, u32[]{:S(2)}) collective-permute-start(f32[16,256]{1,0:T(8,128)S(1)} %get-tuple-element.58), channel_id=1, source_target_pairs={{0,3},{1,0},{2,1},{3,2},{4,7},{5,4},{6,5},{7,6},{8,11},{9,8},{10,9... | collective-permute-start | bytes 49160 | tf_op jit(solution)/shard_map/ppermute | solution.py:331
  51.8 6.9 %collective-permute-done.9.b1 = f32[16,256]{1,0:T(8,128)S(1)} collective-permute-done((f32[16,256]{1,0:T(8,128)S(1)}, f32[16,256]{1,0:T(8,128)S(1)}, u32[]{:S(2)}, u32[]{:S(2)}) %collective-permute-start.9) | collective-permute-done | bytes 16416 | tf_op jit(solution)/shard_map/ppermute | solution.py:331
  58.7 3.7 %shard_map.70 = (f32[16,272,256]{2,1,0:T(8,128)S(1)}, f32[136,256]{1,0:T(8,128)S(1)}, f32[136,256]{1,0:T(8,128)S(1)}) custom-call(s32[4]{0:T(128)S(1)} %pad_add_fusion.idx, f32[1024,256]{1,0:T(8,128)S(1)} %get-tuple-element.46.own, f32[1024,256]{1,0:T(8,128)S(1)} %collective-permute-done.3.prev, f32[1024,256]{1,0:T(8,128)S(1)} %collective-permute-done.4.after, ...), custom_call_target="tpu_custom_call" | custom-call | tf_op jit(solution)/shard_map/pallas_call | solution.py:75
  63.1 2.6 %collective-permute-start.15 = (f32[136,256]{1,0:T(8,128)S(1)}, f32[136,256]{1,0:T(8,128)S(1)}, u32[]{:S(2)}, u32[]{:S(2)}) collective-permute-start(f32[136,256]{1,0:T(8,128)S(1)} %get-tuple-element.60.l0), channel_id=1, source_target_pairs={{0,3},{1,0},{2,1},{3,2},{4,7},{5,4},{6,5},{7,6},{8,11},{9,8},{10,9... | collective-permute-start | bytes 417800 | tf_op jit(solution)/shard_map/ppermute | solution.py:331
  65.7 1.7 %collective-permute-start.17 = (f32[136,256]{1,0:T(8,128)S(1)}, f32[136,256]{1,0:T(8,128)S(1)}, u32[]{:S(2)}, u32[]{:S(2)}) collective-permute-start(f32[136,256]{1,0:T(8,128)S(1)} %get-tuple-element.59.t0), channel_id=1, source_target_pairs={{0,3},{1,0},{2,1},{3,2},{4,7},{5,4},{6,5},{7,6},{8,11},{9,8},{10,9... | collective-permute-start | bytes 417800 | tf_op jit(solution)/shard_map/ppermute | solution.py:331
  67.7 1.6 %collective-permute-done.12.t1 = f32[136,256]{1,0:T(8,128)S(1)} collective-permute-done((f32[136,256]{1,0:T(8,128)S(1)}, f32[136,256]{1,0:T(8,128)S(1)}, u32[]{:S(2)}, u32[]{:S(2)}) %collective-permute-start.12) | collective-permute-done | bytes 139296 | tf_op jit(solution)/shard_map/ppermute | solution.py:331
  69.3 3.2 %collective-permute-start.16 = (f32[136,256]{1,0:T(8,128)S(1)}, f32[136,256]{1,0:T(8,128)S(1)}, u32[]{:S(2)}, u32[]{:S(2)}) collective-permute-start(f32[136,256]{1,0:T(8,128)S(1)} %collective-permute-done.15.l3), channel_id=1, source_target_pairs={{0,3},{1,0},{2,1},{3,2},{4,7},{5,4},{6,5},{7,6},{8,11},{9,8},{10,9... | collective-permute-start | bytes 417800 | tf_op jit(solution)/shard_map/ppermute | solution.py:331
  73.7 1.9 %collective-permute-done.14.t2 = f32[136,256]{1,0:T(8,128)S(1)} collective-permute-done((f32[136,256]{1,0:T(8,128)S(1)}, f32[136,256]{1,0:T(8,128)S(1)}, u32[]{:S(2)}, u32[]{:S(2)}) %collective-permute-start.14) | collective-permute-done | bytes 139296 | tf_op jit(solution)/shard_map/ppermute | solution.py:331
  77.0 1.5 %collective-permute-done.18.other = f32[272,256]{1,0:T(8,128)S(1)} collective-permute-done((f32[272,256]{1,0:T(8,128)S(1)}, f32[272,256]{1,0:T(8,128)S(1)}, u32[]{:S(2)}, u32[]{:S(2)}) %collective-permute-start.18) | collective-permute-done | bytes 278560 | tf_op jit(solution)/shard_map/ppermute | solution.py:390
  79.4 3.3 %collective-permute-start.21 = (f32[136,256]{1,0:T(8,128)S(1)}, f32[136,256]{1,0:T(8,128)S(1)}, u32[]{:S(2)}, u32[]{:S(2)}) collective-permute-start(f32[136,256]{1,0:T(8,128)S(1)} %get-tuple-element.64), channel_id=1, source_target_pairs={{0,16},{4,20},{8,24},{12,28},{16,0},{20,4},{24,8},{28,12},{32,48},... | collective-permute-start | bytes 417800 | tf_op jit(solution)/shard_map/ppermute | solution.py:395
  83.3 2.6 %collective-permute-start.19 = (f32[136,256]{1,0:T(8,128)S(1)}, f32[136,256]{1,0:T(8,128)S(1)}, u32[]{:S(2)}, u32[]{:S(2)}) collective-permute-start(f32[136,256]{1,0:T(8,128)S(1)} %get-tuple-element.64), channel_id=1, source_target_pairs={{0,24},{4,28},{8,0},{12,4},{16,8},{20,12},{24,16},{28,20},{32,56},... | collective-permute-start | bytes 417800 | tf_op jit(solution)/shard_map/ppermute | solution.py:395
  85.9 1.6 %collective-permute-done.21.h3 = f32[136,256]{1,0:T(8,128)S(1)} collective-permute-done((f32[136,256]{1,0:T(8,128)S(1)}, f32[136,256]{1,0:T(8,128)S(1)}, u32[]{:S(2)}, u32[]{:S(2)}) %collective-permute-start.21) | collective-permute-done | bytes 139296 | tf_op jit(solution)/shard_map/ppermute | solution.py:395
  87.5 2.4 %collective-permute-done.20.h2 = f32[136,256]{1,0:T(8,128)S(1)} collective-permute-done((f32[136,256]{1,0:T(8,128)S(1)}, f32[136,256]{1,0:T(8,128)S(1)}, u32[]{:S(2)}, u32[]{:S(2)}) %collective-permute-start.20) | collective-permute-done | bytes 139296 | tf_op jit(solution)/shard_map/ppermute | solution.py:395
  92.8 1.6 %collective-permute-start.27 = (f32[136,256]{1,0:T(8,128)S(1)}, f32[136,256]{1,0:T(8,128)S(1)}, u32[]{:S(2)}, u32[]{:S(2)}) collective-permute-start(f32[136,256]{1,0:T(8,128)S(1)} %get-tuple-element.65), channel_id=1, source_target_pairs={{0,64},{4,68},{8,72},{12,76},{16,80},{20,84},{24,88},{28,92},{32,9... | collective-permute-start | bytes 417800 | tf_op jit(solution)/shard_map/ppermute | solution.py:395
  94.4 1.9 %collective-permute-start.26 = (f32[136,256]{1,0:T(8,128)S(1)}, f32[136,256]{1,0:T(8,128)S(1)}, u32[]{:S(2)}, u32[]{:S(2)}) collective-permute-start(f32[136,256]{1,0:T(8,128)S(1)} %get-tuple-element.65), channel_id=1, source_target_pairs={{0,32},{4,36},{8,40},{12,44},{16,48},{20,52},{24,56},{28,60},{32,6... | collective-permute-start | bytes 417800 | tf_op jit(solution)/shard_map/ppermute | solution.py:395
  96.5 4.4 %collective-permute-done.27.h3 = f32[136,256]{1,0:T(8,128)S(1)} collective-permute-done((f32[136,256]{1,0:T(8,128)S(1)}, f32[136,256]{1,0:T(8,128)S(1)}, u32[]{:S(2)}, u32[]{:S(2)}) %collective-permute-start.27) | collective-permute-done | bytes 139296 | tf_op jit(solution)/shard_map/ppermute | solution.py:395
  100.9 1.5 %collective-permute-done.26.h2 = f32[136,256]{1,0:T(8,128)S(1)} collective-permute-done((f32[136,256]{1,0:T(8,128)S(1)}, f32[136,256]{1,0:T(8,128)S(1)}, u32[]{:S(2)}, u32[]{:S(2)}) %collective-permute-start.26) | collective-permute-done | bytes 139296 | tf_op jit(solution)/shard_map/ppermute | solution.py:395
  104.8 2.2 %shard_map.75 = (f32[16,64]{1,0:T(8,128)S(1)}, f32[16,64]{1,0:T(8,128)S(1)}, f32[16,64]{1,0:T(8,128)S(1)}, f32[16,64]{1,0:T(8,128)S(1)}) custom-call(s32[4]{0:T(128)S(1)} %pad_add_fusion.idx, f32[1,256]{1,0:T(1,128)S(1)} %bitcast.13, f32[136,256]{1,0:T(8,128)S(1)} %collective-permute-done.25.h1, f32[136,256]{1,0:T(8,128)S(1)} %collective-permute-done.26.h2, ...), custom_call_target="tpu_custom_call" | custom-call | tf_op jit(solution)/shard_map/pallas_call | solution.py:75
  107.0 2.3 %collective-permute-start.31 = (f32[16,64]{1,0:T(8,128)S(1)}, f32[16,64]{1,0:T(8,128)S(1)}, u32[]{:S(2)}, u32[]{:S(2)}) collective-permute-start(f32[16,64]{1,0:T(8,128)S(1)} %get-tuple-element.70), channel_id=1, source_target_pairs={{0,2},{1,3},{2,0},{3,1},{4,6},{5,7},{6,4},{7,5},{8,10},{9,11},{10,... | collective-permute-start | bytes 12296 | tf_op jit(solution)/shard_map/ppermute | solution.py:331
  109.3 2.2 %collective-permute-start.32 = (f32[16,64]{1,0:T(8,128)S(1)}, f32[16,64]{1,0:T(8,128)S(1)}, u32[]{:S(2)}, u32[]{:S(2)}) collective-permute-start(f32[16,64]{1,0:T(8,128)S(1)} %get-tuple-element.71), channel_id=1, source_target_pairs={{0,1},{1,2},{2,3},{3,0},{4,5},{5,6},{6,7},{7,4},{8,9},{9,10},{10,1... | collective-permute-start | bytes 12296 | tf_op jit(solution)/shard_map/ppermute | solution.py:331
  112.5 1.6 %collective-permute-done.32.r1 = f32[16,64]{1,0:T(8,128)S(1)} collective-permute-done((f32[16,64]{1,0:T(8,128)S(1)}, f32[16,64]{1,0:T(8,128)S(1)}, u32[]{:S(2)}, u32[]{:S(2)}) %collective-permute-start.32) | collective-permute-done | bytes 4128 | tf_op jit(solution)/shard_map/ppermute | solution.py:331
  (61 shorter events, 18.0 us)
Async XLA Ops:
  1.9 36.3 %collective-permute-start.6 = (f32[512,256]{1,0:T(8,128)S(1)}, f32[512,256]{1,0:T(8,128)S(1)}, u32[]{:S(2)}, u32[]{:S(2)}) collective-permute-start(f32[512,256]{1,0:T(8,128)S(1)} %get-tuple-element.43), channel_id=1, source_target_pairs={{0,3},{1,0},{2,1},{3,2},{4,7},{5,4},{6,5},{7,6},{8,11},{9,8},{10,9... | collective-permute-start | bytes 1572872 | tf_op jit(solution)/shard_map/ppermute | solution.py:331
  6.0 32.2 %collective-permute-start.5 = (f32[512,256]{1,0:T(8,128)S(1)}, f32[512,256]{1,0:T(8,128)S(1)}, u32[]{:S(2)}, u32[]{:S(2)}) collective-permute-start(f32[512,256]{1,0:T(8,128)S(1)} %get-tuple-element.39.far_ahead), channel_id=1, source_target_pairs={{0,1},{1,2},{2,3},{3,0},{4,5},{5,6},{6,7},{7,4},{8,9},{9,10},{10,1... | collective-permute-start | bytes 1572872 | tf_op jit(solution)/shard_map/ppermute | solution.py:331
  8.5 35.3 %collective-permute-start.3 = (f32[1024,256]{1,0:T(8,128)S(1)}, f32[1024,256]{1,0:T(8,128)S(1)}, u32[]{:S(2)}, u32[]{:S(2)}) collective-permute-start(f32[1024,256]{1,0:T(8,128)S(1)} %get-tuple-element.41), channel_id=1, source_target_pairs={{0,1},{1,2},{2,3},{3,0},{4,5},{5,6},{6,7},{7,4},{8,9},{9,10},{10,1... | collective-permute-start | bytes 3145736 | tf_op jit(solution)/shard_map/ppermute | solution.py:331
  8.5 35.2 %collective-permute-start.4 = (f32[1024,256]{1,0:T(8,128)S(1)}, f32[1024,256]{1,0:T(8,128)S(1)}, u32[]{:S(2)}, u32[]{:S(2)}) collective-permute-start(f32[1024,256]{1,0:T(8,128)S(1)} %get-tuple-element.42), channel_id=1, source_target_pairs={{0,3},{1,0},{2,1},{3,2},{4,7},{5,4},{6,5},{7,6},{8,11},{9,8},{10,9... | collective-permute-start | bytes 3145736 | tf_op jit(solution)/shard_map/ppermute | solution.py:331
  36.1 5.7 %collective-permute-start.2 = (f32[16,256]{1,0:T(8,128)S(1)}, f32[16,256]{1,0:T(8,128)S(1)}, u32[]{:S(2)}, u32[]{:S(2)}) collective-permute-start(f32[16,256]{1,0:T(8,128)S(1)} %shard_map.65.info.i0), channel_id=1, source_target_pairs={{0,3},{1,0},{2,1},{3,2},{4,7},{5,4},{6,5},{7,6},{8,11},{9,8},{10,9... | collective-permute-start | bytes 49160 | tf_op jit(solution)/shard_map/ppermute | solution.py:331
  38.1 5.3 %collective-permute-start.1 = (f32[16,256]{1,0:T(8,128)S(1)}, f32[16,256]{1,0:T(8,128)S(1)}, u32[]{:S(2)}, u32[]{:S(2)}) collective-permute-start(f32[16,256]{1,0:T(8,128)S(1)} %shard_map.65.info.i0), channel_id=1, source_target_pairs={{0,2},{1,3},{2,0},{3,1},{4,6},{5,7},{6,4},{7,5},{8,10},{9,11},{10,... | collective-permute-start | bytes 49160 | tf_op jit(solution)/shard_map/ppermute | solution.py:331
  38.1 5.6 %collective-permute-start = (f32[16,256]{1,0:T(8,128)S(1)}, f32[16,256]{1,0:T(8,128)S(1)}, u32[]{:S(2)}, u32[]{:S(2)}) collective-permute-start(f32[16,256]{1,0:T(8,128)S(1)} %shard_map.65.info.i0), channel_id=1, source_target_pairs={{0,1},{1,2},{2,3},{3,0},{4,5},{5,6},{6,7},{7,4},{8,9},{9,10},{10,1... | collective-permute-start | bytes 49160 | tf_op jit(solution)/shard_map/ppermute | solution.py:331
  43.7 14.9 %collective-permute-start.7 = (f32[512,256]{1,0:T(8,128)S(1)}, f32[512,256]{1,0:T(8,128)S(1)}, u32[]{:S(2)}, u32[]{:S(2)}) collective-permute-start(f32[512,256]{1,0:T(8,128)S(1)} %collective-permute-done.5), channel_id=1, source_target_pairs={{0,1},{1,2},{2,3},{3,0},{4,5},{5,6},{6,7},{7,4},{8,9},{9,10},{10,1... | collective-permute-start | bytes 1572872 | tf_op jit(solution)/shard_map/ppermute | solution.py:331
  44.5 14.2 %collective-permute-start.8 = (f32[512,256]{1,0:T(8,128)S(1)}, f32[512,256]{1,0:T(8,128)S(1)}, u32[]{:S(2)}, u32[]{:S(2)}) collective-permute-start(f32[512,256]{1,0:T(8,128)S(1)} %collective-permute-done.6), channel_id=1, source_target_pairs={{0,3},{1,0},{2,1},{3,2},{4,7},{5,4},{6,5},{7,6},{8,11},{9,8},{10,9... | collective-permute-start | bytes 1572872 | tf_op jit(solution)/shard_map/ppermute | solution.py:331
  48.5 10.1 %collective-permute-start.9 = (f32[16,256]{1,0:T(8,128)S(1)}, f32[16,256]{1,0:T(8,128)S(1)}, u32[]{:S(2)}, u32[]{:S(2)}) collective-permute-start(f32[16,256]{1,0:T(8,128)S(1)} %get-tuple-element.56), channel_id=1, source_target_pairs={{0,1},{1,2},{2,3},{3,0},{4,5},{5,6},{6,7},{7,4},{8,9},{9,10},{10,1... | collective-permute-start | bytes 49160 | tf_op jit(solution)/shard_map/ppermute | solution.py:331
  48.6 10.1 %collective-permute-start.10 = (f32[16,256]{1,0:T(8,128)S(1)}, f32[16,256]{1,0:T(8,128)S(1)}, u32[]{:S(2)}, u32[]{:S(2)}) collective-permute-start(f32[16,256]{1,0:T(8,128)S(1)} %get-tuple-element.57), channel_id=1, source_target_pairs={{0,2},{1,3},{2,0},{3,1},{4,6},{5,7},{6,4},{7,5},{8,10},{9,11},{10,... | collective-permute-start | bytes 49160 | tf_op jit(solution)/shard_map/ppermute | solution.py:331
  50.0 8.6 %collective-permute-start.11 = (f32[16,256]{1,0:T(8,128)S(1)}, f32[16,256]{1,0:T(8,128)S(1)}, u32[]{:S(2)}, u32[]{:S(2)}) collective-permute-start(f32[16,256]{1,0:T(8,128)S(1)} %get-tuple-element.58), channel_id=1, source_target_pairs={{0,3},{1,0},{2,1},{3,2},{4,7},{5,4},{6,5},{7,6},{8,11},{9,8},{10,9... | collective-permute-start | bytes 49160 | tf_op jit(solution)/shard_map/ppermute | solution.py:331
  62.4 6.9 %collective-permute-start.12 = (f32[136,256]{1,0:T(8,128)S(1)}, f32[136,256]{1,0:T(8,128)S(1)}, u32[]{:S(2)}, u32[]{:S(2)}) collective-permute-start(f32[136,256]{1,0:T(8,128)S(1)} %get-tuple-element.59.t0), channel_id=1, source_target_pairs={{0,1},{1,2},{2,3},{3,0},{4,5},{5,6},{6,7},{7,4},{8,9},{9,10},{10,1... | collective-permute-start | bytes 417800 | tf_op jit(solution)/shard_map/ppermute | solution.py:331
  63.1 6.2 %collective-permute-start.15 = (f32[136,256]{1,0:T(8,128)S(1)}, f32[136,256]{1,0:T(8,128)S(1)}, u32[]{:S(2)}, u32[]{:S(2)}) collective-permute-start(f32[136,256]{1,0:T(8,128)S(1)} %get-tuple-element.60.l0), channel_id=1, source_target_pairs={{0,3},{1,0},{2,1},{3,2},{4,7},{5,4},{6,5},{7,6},{8,11},{9,8},{10,9... | collective-permute-start | bytes 417800 | tf_op jit(solution)/shard_map/ppermute | solution.py:331
  65.7 6.8 %collective-permute-start.17 = (f32[136,256]{1,0:T(8,128)S(1)}, f32[136,256]{1,0:T(8,128)S(1)}, u32[]{:S(2)}, u32[]{:S(2)}) collective-permute-start(f32[136,256]{1,0:T(8,128)S(1)} %get-tuple-element.59.t0), channel_id=1, source_target_pairs={{0,3},{1,0},{2,1},{3,2},{4,7},{5,4},{6,5},{7,6},{8,11},{9,8},{10,9... | collective-permute-start | bytes 417800 | tf_op jit(solution)/shard_map/ppermute | solution.py:331
  67.4 6.3 %collective-permute-start.13 = (f32[136,256]{1,0:T(8,128)S(1)}, f32[136,256]{1,0:T(8,128)S(1)}, u32[]{:S(2)}, u32[]{:S(2)}) collective-permute-start(f32[136,256]{1,0:T(8,128)S(1)} %get-tuple-element.60.l0), channel_id=1, source_target_pairs={{0,1},{1,2},{2,3},{3,0},{4,5},{5,6},{6,7},{7,4},{8,9},{9,10},{10,1... | collective-permute-start | bytes 417800 | tf_op jit(solution)/shard_map/ppermute | solution.py:331
  69.3 6.3 %collective-permute-start.14 = (f32[136,256]{1,0:T(8,128)S(1)}, f32[136,256]{1,0:T(8,128)S(1)}, u32[]{:S(2)}, u32[]{:S(2)}) collective-permute-start(f32[136,256]{1,0:T(8,128)S(1)} %collective-permute-done.12.t1), channel_id=1, source_target_pairs={{0,1},{1,2},{2,3},{3,0},{4,5},{5,6},{6,7},{7,4},{8,9},{9,10},{10,1... | collective-permute-start | bytes 417800 | tf_op jit(solution)/shard_map/ppermute | solution.py:331
  69.3 6.2 %collective-permute-start.16 = (f32[136,256]{1,0:T(8,128)S(1)}, f32[136,256]{1,0:T(8,128)S(1)}, u32[]{:S(2)}, u32[]{:S(2)}) collective-permute-start(f32[136,256]{1,0:T(8,128)S(1)} %collective-permute-done.15.l3), channel_id=1, source_target_pairs={{0,3},{1,0},{2,1},{3,2},{4,7},{5,4},{6,5},{7,6},{8,11},{9,8},{10,9... | collective-permute-start | bytes 417800 | tf_op jit(solution)/shard_map/ppermute | solution.py:331
  76.9 1.6 %collective-permute-start.18 = (f32[272,256]{1,0:T(8,128)S(1)}, f32[272,256]{1,0:T(8,128)S(1)}, u32[]{:S(2)}, u32[]{:S(2)}) collective-permute-start(f32[272,256]{1,0:T(8,128)S(1)} %get-tuple-element.61.own), channel_id=1, source_target_pairs={{0,4},{4,0},{8,12},{12,8},{16,20},{20,16},{24,28},{28,24},{32,36},... | collective-permute-start | bytes 835592 | tf_op jit(solution)/shard_map/ppermute | solution.py:390
  79.4 8.1 %collective-permute-start.21 = (f32[136,256]{1,0:T(8,128)S(1)}, f32[136,256]{1,0:T(8,128)S(1)}, u32[]{:S(2)}, u32[]{:S(2)}) collective-permute-start(f32[136,256]{1,0:T(8,128)S(1)} %get-tuple-element.64), channel_id=1, source_target_pairs={{0,16},{4,20},{8,24},{12,28},{16,0},{20,4},{24,8},{28,12},{32,48},... | collective-permute-start | bytes 417800 | tf_op jit(solution)/shard_map/ppermute | solution.py:395
  82.6 7.3 %collective-permute-start.20 = (f32[136,256]{1,0:T(8,128)S(1)}, f32[136,256]{1,0:T(8,128)S(1)}, u32[]{:S(2)}, u32[]{:S(2)}) collective-permute-start(f32[136,256]{1,0:T(8,128)S(1)} %get-tuple-element.64), channel_id=1, source_target_pairs={{0,8},{4,12},{8,16},{12,20},{16,24},{20,28},{24,0},{28,4},{32,40},... | collective-permute-start | bytes 417800 | tf_op jit(solution)/shard_map/ppermute | solution.py:395
  83.3 6.8 %collective-permute-start.19 = (f32[136,256]{1,0:T(8,128)S(1)}, f32[136,256]{1,0:T(8,128)S(1)}, u32[]{:S(2)}, u32[]{:S(2)}) collective-permute-start(f32[136,256]{1,0:T(8,128)S(1)} %get-tuple-element.64), channel_id=1, source_target_pairs={{0,24},{4,28},{8,0},{12,4},{16,8},{20,12},{24,16},{28,20},{32,56},... | collective-permute-start | bytes 417800 | tf_op jit(solution)/shard_map/ppermute | solution.py:395
  87.5 3.0 %collective-permute-start.24 = (f32[136,256]{1,0:T(8,128)S(1)}, f32[136,256]{1,0:T(8,128)S(1)}, u32[]{:S(2)}, u32[]{:S(2)}) collective-permute-start(f32[136,256]{1,0:T(8,128)S(1)} %collective-permute-done.21.h3), channel_id=1, source_target_pairs={{0,4},{4,0},{8,12},{12,8},{16,20},{20,16},{24,28},{28,24},{32,36},... | collective-permute-start | bytes 417800 | tf_op jit(solution)/shard_map/ppermute | solution.py:390
  90.1 1.4 %collective-permute-start.22 = (f32[136,256]{1,0:T(8,128)S(1)}, f32[136,256]{1,0:T(8,128)S(1)}, u32[]{:S(2)}, u32[]{:S(2)}) collective-permute-start(f32[136,256]{1,0:T(8,128)S(1)} %collective-permute-done.19.h1), channel_id=1, source_target_pairs={{0,4},{4,0},{8,12},{12,8},{16,20},{20,16},{24,28},{28,24},{32,36},... | collective-permute-start | bytes 417800 | tf_op jit(solution)/shard_map/ppermute | solution.py:390
  92.8 8.1 %collective-permute-start.27 = (f32[136,256]{1,0:T(8,128)S(1)}, f32[136,256]{1,0:T(8,128)S(1)}, u32[]{:S(2)}, u32[]{:S(2)}) collective-permute-start(f32[136,256]{1,0:T(8,128)S(1)} %get-tuple-element.65), channel_id=1, source_target_pairs={{0,64},{4,68},{8,72},{12,76},{16,80},{20,84},{24,88},{28,92},{32,9... | collective-permute-start | bytes 417800 | tf_op jit(solution)/shard_map/ppermute | solution.py:395
  94.4 8.0 %collective-permute-start.26 = (f32[136,256]{1,0:T(8,128)S(1)}, f32[136,256]{1,0:T(8,128)S(1)}, u32[]{:S(2)}, u32[]{:S(2)}) collective-permute-start(f32[136,256]{1,0:T(8,128)S(1)} %get-tuple-element.65), channel_id=1, source_target_pairs={{0,32},{4,36},{8,40},{12,44},{16,48},{20,52},{24,56},{28,60},{32,6... | collective-permute-start | bytes 417800 | tf_op jit(solution)/shard_map/ppermute | solution.py:395
  96.4 7.0 %collective-permute-start.25 = (f32[136,256]{1,0:T(8,128)S(1)}, f32[136,256]{1,0:T(8,128)S(1)}, u32[]{:S(2)}, u32[]{:S(2)}) collective-permute-start(f32[136,256]{1,0:T(8,128)S(1)} %get-tuple-element.65), channel_id=1, source_target_pairs={{0,96},{4,100},{8,104},{12,108},{16,112},{20,116},{24,120},{28,124... | collective-permute-start | bytes 417800 | tf_op jit(solution)/shard_map/ppermute | solution.py:395
  100.9 3.4 %collective-permute-start.30 = (f32[136,256]{1,0:T(8,128)S(1)}, f32[136,256]{1,0:T(8,128)S(1)}, u32[]{:S(2)}, u32[]{:S(2)}) collective-permute-start(f32[136,256]{1,0:T(8,128)S(1)} %collective-permute-done.27.h3), channel_id=1, source_target_pairs={{0,4},{4,0},{8,12},{12,8},{16,20},{20,16},{24,28},{28,24},{32,36},... | collective-permute-start | bytes 417800 | tf_op jit(solution)/shard_map/ppermute | solution.py:390
  102.4 1.8 %collective-permute-start.29 = (f32[136,256]{1,0:T(8,128)S(1)}, f32[136,256]{1,0:T(8,128)S(1)}, u32[]{:S(2)}, u32[]{:S(2)}) collective-permute-start(f32[136,256]{1,0:T(8,128)S(1)} %collective-permute-done.26.h2), channel_id=1, source_target_pairs={{0,4},{4,0},{8,12},{12,8},{16,20},{20,16},{24,28},{28,24},{32,36},... | collective-permute-start | bytes 417800 | tf_op jit(solution)/shard_map/ppermute | solution.py:390
  107.0 5.5 %collective-permute-start.31 = (f32[16,64]{1,0:T(8,128)S(1)}, f32[16,64]{1,0:T(8,128)S(1)}, u32[]{:S(2)}, u32[]{:S(2)}) collective-permute-start(f32[16,64]{1,0:T(8,128)S(1)} %get-tuple-element.70), channel_id=1, source_target_pairs={{0,2},{1,3},{2,0},{3,1},{4,6},{5,7},{6,4},{7,5},{8,10},{9,11},{10,... | collective-permute-start | bytes 12296 | tf_op jit(solution)/shard_map/ppermute | solution.py:331
  109.3 4.9 %collective-permute-start.32 = (f32[16,64]{1,0:T(8,128)S(1)}, f32[16,64]{1,0:T(8,128)S(1)}, u32[]{:S(2)}, u32[]{:S(2)}) collective-permute-start(f32[16,64]{1,0:T(8,128)S(1)} %get-tuple-element.71), channel_id=1, source_target_pairs={{0,1},{1,2},{2,3},{3,0},{4,5},{5,6},{6,7},{7,4},{8,9},{9,10},{10,1... | collective-permute-start | bytes 12296 | tf_op jit(solution)/shard_map/ppermute | solution.py:331
  111.4 3.7 %collective-permute-start.33 = (f32[16,64]{1,0:T(8,128)S(1)}, f32[16,64]{1,0:T(8,128)S(1)}, u32[]{:S(2)}, u32[]{:S(2)}) collective-permute-start(f32[16,64]{1,0:T(8,128)S(1)} %get-tuple-element.72), channel_id=1, source_target_pairs={{0,3},{1,0},{2,1},{3,2},{4,7},{5,4},{6,5},{7,6},{8,11},{9,8},{10,9... | collective-permute-start | bytes 12296 | tf_op jit(solution)/shard_map/ppermute | solution.py:331
  (6 other events, 94.3 us)

commit v15 on v12

--- a/solution.py
+++ b/solution.py
@@ -82,7 +82,7 @@
     )(idx, *[pltpu.with_memory_space_constraint(f, pltpu.HBM) for f in far], *[near(a) for a in args])
 
 
-BIN_M = 256
+BIN_M = 512
 
 
 def bin_kernel(rid_ref, obs_ref, out_ref, rhs, acc):
@@ -305,7 +305,7 @@
     info[...] = jnp.sum(sums[...], axis=0)
 
 
-def offset_kernel(idx, g, i0, r1, r2, r3, o0, o1, o2, o3, info_s, off_s):
+def offset_kernel(idx, g, i0, r1, r3, r2, o0, o1, o2, o3, info_s, off_s):
     z = idx[Z]
     info_s[z] = i0[...]
     for d, r in ((1, r1), (2, r2), (3, r3)):
@@ -359,7 +359,7 @@
     partial = binned(rid.reshape(1, -1), observed.T)
     sums = lax.all_to_all(partial, "tm", 0, 0, tiled=True).reshape(32, 16, N)
     (info,) = call(sum_kernel, [(16, N)], idx, (sums,))
-    infos = along_rows([info] * 3)
+    infos = [along_row(info, d) for d in (1, 3, 2)]
     staged, own = call(
         stage_kernel,
         [gains.shape, (SUB * 64, N)],

time: 116 us -> 116 us (level)
  transfers between devices with their start and end apart: 34 -> 34, of which waited for: 19 -> 18; matrix products, arithmetic and copies ran while one was open for 0% -> 0% of each run, Pallas kernels for 11% -> 10%
where the time goes in v15:
time: 116 us
  starting transfers between devices  41 us (35%)
  waiting for transfers between devices  33.3 us (29%)
  Pallas kernels  24.9 us (21%)
  blocking collectives  16.7 us (14%)
    ppermute x21, starting transfers between devices, along_row(): return lax.ppermute(x, 'row', [(i, (i + d) % ROWS) for i in range(ROWS)])  30.1 us
    ppermute x21, waiting for transfers between devices, along_row(): return lax.ppermute(x, 'row', [(i, (i + d) % ROWS) for i in range(ROWS)])  19.3 us
    pallas_call x10, Pallas kernels, call(): pl.pallas_call(kernel, out_shape=[pltpu.VMEM(s, t) for s, t in outs], in_...  17.9 us
    all_to_all x1, blocking collectives, shards(): sums = lax.all_to_all(partial, 'tm', 0, 0, tiled=True).reshape(32, 16, N)  16.7 us
    ppermute x6, waiting for transfers between devices, gathered(): lax.ppermute(half, 'tm', [(i, i - i % n + (i + d * stride) % n) for i in...  10.9 us
    ppermute x6, starting transfers between devices, gathered(): lax.ppermute(half, 'tm', [(i, i - i % n + (i + d * stride) % n) for i in...  10.1 us
    pallas_call x1, Pallas kernels, binned(): pl.pallas_call(bin_kernel, out_shape=jax.ShapeDtypeStruct((n_bins // 4, N...  5.84 us
    ppermute x7, waiting for transfers between devices, other_core(): return lax.ppermute(m, 'tm', [(i, i ^ 1) for i in range(32)])  3.09 us
  transfers between devices with their start and end apart: 34, of which 18 were waited for; matrix products, arithmetic and copies ran while one was open for 0% of the time, Pallas kernels for 10%

profile of v15, /device:TPU:6, one launch (start us, length us, event | category | flops | bytes accessed | tf_op | source)
XLA Modules:
  0.0 116.2 jit_solution(16813077813191029326)
XLA Ops:
  0.1 2.5 %shard_map.67 = (f32[512,256]{1,0:T(8,128)S(1)}, f32[512,256]{1,0:T(8,128)S(1)}, f32[1024,256]{1,0:T(8,128)S(1)}, f32[1024,256]{1,0:T(8,128)S(1)}) custom-call(s32[4]{0:T(128)S(1)} %pad_add_fusion.idx, f32[4096,256]{1,0:T(8,128)} %bitcast.14), custom_call_target="tpu_custom_call" | custom-call | tf_op jit(solution)/shard_map/pallas_call | solution.py:75
  2.6 2.0 %collective-permute-start.5 = (f32[512,256]{1,0:T(8,128)S(1)}, f32[512,256]{1,0:T(8,128)S(1)}, u32[]{:S(2)}, u32[]{:S(2)}) collective-permute-start(f32[512,256]{1,0:T(8,128)S(1)} %get-tuple-element.44), channel_id=1, source_target_pairs={{0,1},{1,2},{2,3},{3,0},{4,5},{5,6},{6,7},{7,4},{8,9},{9,10},{10,1... | collective-permute-start | bytes 1572872 | tf_op jit(solution)/shard_map/ppermute | solution.py:334
  4.6 2.2 %collective-permute-start.6 = (f32[512,256]{1,0:T(8,128)S(1)}, f32[512,256]{1,0:T(8,128)S(1)}, u32[]{:S(2)}, u32[]{:S(2)}) collective-permute-start(f32[512,256]{1,0:T(8,128)S(1)} %get-tuple-element.45), channel_id=1, source_target_pairs={{0,3},{1,0},{2,1},{3,2},{4,7},{5,4},{6,5},{7,6},{8,11},{9,8},{10,9... | collective-permute-start | bytes 1572872 | tf_op jit(solution)/shard_map/ppermute | solution.py:334
  6.8 3.2 %collective-permute-start.4 = (f32[1024,256]{1,0:T(8,128)S(1)}, f32[1024,256]{1,0:T(8,128)S(1)}, u32[]{:S(2)}, u32[]{:S(2)}) collective-permute-start(f32[1024,256]{1,0:T(8,128)S(1)} %get-tuple-element.43), channel_id=1, source_target_pairs={{0,3},{1,0},{2,1},{3,2},{4,7},{5,4},{6,5},{7,6},{8,11},{9,8},{10,9... | collective-permute-start | bytes 3145736 | tf_op jit(solution)/shard_map/ppermute | solution.py:334
  10.1 5.8 %shard_map.64 = f32[512,256]{1,0:T(8,128)S(1)} custom-call(s32[1,4096]{1,0:T(1,128)S(1)} %bitcast.12, f32[64,4096]{1,0:T(8,128)S(1)} %bitcast.11), custom_call_target="tpu_custom_call" | custom-call | tf_op jit(solution)/shard_map/pallas_call | solution.py:120
  15.9 16.7 %all_to_all.9.sums = f32[32,16,256]{2,1,0:T(8,128)S(1)} all-to-all(f32[32,16,256]{2,1,0:T(8,128)S(1)} %bitcast.10), channel_id=1, replica_groups=mesh['tm'=32,'row'=4] {'tm'}, dimensions={0} | all-to-all | bytes 1048576 | tf_op jit(solution)/shard_map/all_to_all | solution.py:360
  35.9 3.0 %shard_map.66 = (f32[64,64,256]{2,1,0:T(8,128)S(1)}, f32[1024,256]{1,0:T(8,128)S(1)}) custom-call(s32[4]{0:T(128)S(1)} %pad_add_fusion.idx, f32[64,64,256]{2,1,0:T(8,128)} %gains.1, f32[4096,256]{1,0:T(8,128)} %bitcast.15, f32[16,256]{1,0:T(8,128)S(1)} %shard_map.65.info.i0), custom_call_target="tpu_custom_call" | custom-call | tf_op jit(solution)/shard_map/pallas_call | solution.py:75
  38.9 3.9 %collective-permute-done.2.r2 = f32[16,256]{1,0:T(8,128)S(1)} collective-permute-done((f32[16,256]{1,0:T(8,128)S(1)}, f32[16,256]{1,0:T(8,128)S(1)}, u32[]{:S(2)}, u32[]{:S(2)}) %collective-permute-start.2) | collective-permute-done | bytes 16416 | tf_op jit(solution)/shard_map/ppermute | solution.py:334
  44.0 2.1 %collective-permute-start.8 = (f32[512,256]{1,0:T(8,128)S(1)}, f32[512,256]{1,0:T(8,128)S(1)}, u32[]{:S(2)}, u32[]{:S(2)}) collective-permute-start(f32[512,256]{1,0:T(8,128)S(1)} %collective-permute-done.6), channel_id=1, source_target_pairs={{0,3},{1,0},{2,1},{3,2},{4,7},{5,4},{6,5},{7,6},{8,11},{9,8},{10,9... | collective-permute-start | bytes 1572872 | tf_op jit(solution)/shard_map/ppermute | solution.py:334
  46.1 1.6 %shard_map.68 = (f32[16,256]{1,0:T(8,128)S(1)}, f32[16,256]{1,0:T(8,128)S(1)}, f32[16,256]{1,0:T(8,128)S(1)}, f32[16,256]{1,0:T(8,128)S(1)}) custom-call(s32[4]{0:T(128)S(1)} %pad_add_fusion.idx, f32[64,64,256]{2,1,0:T(8,128)S(1)} %get-tuple-element.53.g, f32[16,256]{1,0:T(8,128)S(1)} %shard_map.65.info.i0, f32[16,256]{1,0:T(8,128)S(1)} %collective-permute-done.r1, ...), custom_call_target="tpu_custom_call" | custom-call | tf_op jit(solution)/shard_map/pallas_call | solution.py:75
  47.7 2.3 %collective-permute-start.10 = (f32[16,256]{1,0:T(8,128)S(1)}, f32[16,256]{1,0:T(8,128)S(1)}, u32[]{:S(2)}, u32[]{:S(2)}) collective-permute-start(f32[16,256]{1,0:T(8,128)S(1)} %get-tuple-element.59), channel_id=1, source_target_pairs={{0,2},{1,3},{2,0},{3,1},{4,6},{5,7},{6,4},{7,5},{8,10},{9,11},{10,... | collective-permute-start | bytes 49160 | tf_op jit(solution)/shard_map/ppermute | solution.py:334
  51.0 5.9 %collective-permute-done.9.b1 = f32[16,256]{1,0:T(8,128)S(1)} collective-permute-done((f32[16,256]{1,0:T(8,128)S(1)}, f32[16,256]{1,0:T(8,128)S(1)}, u32[]{:S(2)}, u32[]{:S(2)}) %collective-permute-start.9) | collective-permute-done | bytes 16416 | tf_op jit(solution)/shard_map/ppermute | solution.py:334
  57.7 3.7 %shard_map.69 = (f32[16,272,256]{2,1,0:T(8,128)S(1)}, f32[136,256]{1,0:T(8,128)S(1)}, f32[136,256]{1,0:T(8,128)S(1)}) custom-call(s32[4]{0:T(128)S(1)} %pad_add_fusion.idx, f32[1024,256]{1,0:T(8,128)S(1)} %get-tuple-element.48.own, f32[1024,256]{1,0:T(8,128)S(1)} %collective-permute-done.3.prev, f32[1024,256]{1,0:T(8,128)S(1)} %collective-permute-done.4.after, ...), custom_call_target="tpu_custom_call" | custom-call | tf_op jit(solution)/shard_map/pallas_call | solution.py:75
  62.4 2.3 %collective-permute-start.15 = (f32[136,256]{1,0:T(8,128)S(1)}, f32[136,256]{1,0:T(8,128)S(1)}, u32[]{:S(2)}, u32[]{:S(2)}) collective-permute-start(f32[136,256]{1,0:T(8,128)S(1)} %get-tuple-element.62.l0), channel_id=1, source_target_pairs={{0,3},{1,0},{2,1},{3,2},{4,7},{5,4},{6,5},{7,6},{8,11},{9,8},{10,9... | collective-permute-start | bytes 417800 | tf_op jit(solution)/shard_map/ppermute | solution.py:334
  66.7 2.5 %collective-permute-done.12.t1 = f32[136,256]{1,0:T(8,128)S(1)} collective-permute-done((f32[136,256]{1,0:T(8,128)S(1)}, f32[136,256]{1,0:T(8,128)S(1)}, u32[]{:S(2)}, u32[]{:S(2)}) %collective-permute-start.12) | collective-permute-done | bytes 139296 | tf_op jit(solution)/shard_map/ppermute | solution.py:334
  69.2 3.2 %collective-permute-start.16 = (f32[136,256]{1,0:T(8,128)S(1)}, f32[136,256]{1,0:T(8,128)S(1)}, u32[]{:S(2)}, u32[]{:S(2)}) collective-permute-start(f32[136,256]{1,0:T(8,128)S(1)} %collective-permute-done.15.l3), channel_id=1, source_target_pairs={{0,3},{1,0},{2,1},{3,2},{4,7},{5,4},{6,5},{7,6},{8,11},{9,8},{10,9... | collective-permute-start | bytes 417800 | tf_op jit(solution)/shard_map/ppermute | solution.py:334
  72.5 3.0 %collective-permute-done.14.t2 = f32[136,256]{1,0:T(8,128)S(1)} collective-permute-done((f32[136,256]{1,0:T(8,128)S(1)}, f32[136,256]{1,0:T(8,128)S(1)}, u32[]{:S(2)}, u32[]{:S(2)}) %collective-permute-start.14) | collective-permute-done | bytes 139296 | tf_op jit(solution)/shard_map/ppermute | solution.py:334
  75.5 1.3 %shard_map.70 = (f32[272,256]{1,0:T(8,128)S(1)}, f32[272,256]{1,0:T(8,128)S(1)}) custom-call(s32[4]{0:T(128)S(1)} %pad_add_fusion.idx, f32[136,256]{1,0:T(8,128)S(1)} %get-tuple-element.61.t0, f32[136,256]{1,0:T(8,128)S(1)} %get-tuple-element.62.l0, f32[136,256]{1,0:T(8,128)S(1)} %collective-permute-done.12.t1, f32[136,256]{1,0:T(8,128)S(1)} %collective-permute-done.13.l1, ...), custom_call_target="tpu_custom_call" | custom-call | tf_op jit(solution)/shard_map/pallas_call | solution.py:75
  76.9 1.5 %collective-permute-done.18.other = f32[272,256]{1,0:T(8,128)S(1)} collective-permute-done((f32[272,256]{1,0:T(8,128)S(1)}, f32[272,256]{1,0:T(8,128)S(1)}, u32[]{:S(2)}, u32[]{:S(2)}) %collective-permute-start.18) | collective-permute-done | bytes 278560 | tf_op jit(solution)/shard_map/ppermute | solution.py:403
  79.3 3.3 %collective-permute-start.21 = (f32[136,256]{1,0:T(8,128)S(1)}, f32[136,256]{1,0:T(8,128)S(1)}, u32[]{:S(2)}, u32[]{:S(2)}) collective-permute-start(f32[136,256]{1,0:T(8,128)S(1)} %get-tuple-element.66), channel_id=1, source_target_pairs={{0,16},{4,20},{8,24},{12,28},{16,0},{20,4},{24,8},{28,12},{32,48},... | collective-permute-start | bytes 417800 | tf_op jit(solution)/shard_map/ppermute | solution.py:408
  83.3 2.6 %collective-permute-start.19 = (f32[136,256]{1,0:T(8,128)S(1)}, f32[136,256]{1,0:T(8,128)S(1)}, u32[]{:S(2)}, u32[]{:S(2)}) collective-permute-start(f32[136,256]{1,0:T(8,128)S(1)} %get-tuple-element.66), channel_id=1, source_target_pairs={{0,24},{4,28},{8,0},{12,4},{16,8},{20,12},{24,16},{28,20},{32,56},... | collective-permute-start | bytes 417800 | tf_op jit(solution)/shard_map/ppermute | solution.py:408
  85.8 1.6 %collective-permute-done.21.h3 = f32[136,256]{1,0:T(8,128)S(1)} collective-permute-done((f32[136,256]{1,0:T(8,128)S(1)}, f32[136,256]{1,0:T(8,128)S(1)}, u32[]{:S(2)}, u32[]{:S(2)}) %collective-permute-start.21) | collective-permute-done | bytes 139296 | tf_op jit(solution)/shard_map/ppermute | solution.py:408
  87.4 2.5 %collective-permute-done.20.h2 = f32[136,256]{1,0:T(8,128)S(1)} collective-permute-done((f32[136,256]{1,0:T(8,128)S(1)}, f32[136,256]{1,0:T(8,128)S(1)}, u32[]{:S(2)}, u32[]{:S(2)}) %collective-permute-start.20) | collective-permute-done | bytes 139296 | tf_op jit(solution)/shard_map/ppermute | solution.py:408
  91.4 1.3 %shard_map.72 = (f32[136,256]{1,0:T(8,128)S(1)}, f32[272,256]{1,0:T(8,128)S(1)}) custom-call(s32[4]{0:T(128)S(1)} %pad_add_fusion.idx, f32[272,256]{1,0:T(8,128)S(1)} %get-tuple-element.65.own, f32[136,256]{1,0:T(8,128)S(1)} %collective-permute-done.19.h1, f32[136,256]{1,0:T(8,128)S(1)} %collective-permute-done.20.h2, ...), custom_call_target="tpu_custom_call" | custom-call | tf_op jit(solution)/shard_map/pallas_call | solution.py:75
  92.7 1.5 %collective-permute-start.27 = (f32[136,256]{1,0:T(8,128)S(1)}, f32[136,256]{1,0:T(8,128)S(1)}, u32[]{:S(2)}, u32[]{:S(2)}) collective-permute-start(f32[136,256]{1,0:T(8,128)S(1)} %get-tuple-element.67), channel_id=1, source_target_pairs={{0,64},{4,68},{8,72},{12,76},{16,80},{20,84},{24,88},{28,92},{32,9... | collective-permute-start | bytes 417800 | tf_op jit(solution)/shard_map/ppermute | solution.py:408
  94.2 2.1 %collective-permute-start.26 = (f32[136,256]{1,0:T(8,128)S(1)}, f32[136,256]{1,0:T(8,128)S(1)}, u32[]{:S(2)}, u32[]{:S(2)}) collective-permute-start(f32[136,256]{1,0:T(8,128)S(1)} %get-tuple-element.67), channel_id=1, source_target_pairs={{0,32},{4,36},{8,40},{12,44},{16,48},{20,52},{24,56},{28,60},{32,6... | collective-permute-start | bytes 417800 | tf_op jit(solution)/shard_map/ppermute | solution.py:408
  96.3 4.5 %collective-permute-done.27.h3 = f32[136,256]{1,0:T(8,128)S(1)} collective-permute-done((f32[136,256]{1,0:T(8,128)S(1)}, f32[136,256]{1,0:T(8,128)S(1)}, u32[]{:S(2)}, u32[]{:S(2)}) %collective-permute-start.27) | collective-permute-done | bytes 139296 | tf_op jit(solution)/shard_map/ppermute | solution.py:408
  101.3 2.0 %collective-permute-done.25.h1 = f32[136,256]{1,0:T(8,128)S(1)} collective-permute-done((f32[136,256]{1,0:T(8,128)S(1)}, f32[136,256]{1,0:T(8,128)S(1)}, u32[]{:S(2)}, u32[]{:S(2)}) %collective-permute-start.25) | collective-permute-done | bytes 139296 | tf_op jit(solution)/shard_map/ppermute | solution.py:408
  104.7 2.2 %shard_map.74 = (f32[16,64]{1,0:T(8,128)S(1)}, f32[16,64]{1,0:T(8,128)S(1)}, f32[16,64]{1,0:T(8,128)S(1)}, f32[16,64]{1,0:T(8,128)S(1)}) custom-call(s32[4]{0:T(128)S(1)} %pad_add_fusion.idx, f32[1,256]{1,0:T(1,128)S(1)} %bitcast.13, f32[136,256]{1,0:T(8,128)S(1)} %collective-permute-done.25.h1, f32[136,256]{1,0:T(8,128)S(1)} %collective-permute-done.26.h2, ...), custom_call_target="tpu_custom_call" | custom-call | tf_op jit(solution)/shard_map/pallas_call | solution.py:75
  106.9 1.6 %collective-permute-start.31 = (f32[16,64]{1,0:T(8,128)S(1)}, f32[16,64]{1,0:T(8,128)S(1)}, u32[]{:S(2)}, u32[]{:S(2)}) collective-permute-start(f32[16,64]{1,0:T(8,128)S(1)} %get-tuple-element.72), channel_id=1, source_target_pairs={{0,2},{1,3},{2,0},{3,1},{4,6},{5,7},{6,4},{7,5},{8,10},{9,11},{10,... | collective-permute-start | bytes 12296 | tf_op jit(solution)/shard_map/ppermute | solution.py:334
  108.5 2.9 %collective-permute-start.32 = (f32[16,64]{1,0:T(8,128)S(1)}, f32[16,64]{1,0:T(8,128)S(1)}, u32[]{:S(2)}, u32[]{:S(2)}) collective-permute-start(f32[16,64]{1,0:T(8,128)S(1)} %get-tuple-element.73), channel_id=1, source_target_pairs={{0,1},{1,2},{2,3},{3,0},{4,5},{5,6},{6,7},{7,4},{8,9},{9,10},{10,1... | collective-permute-start | bytes 12296 | tf_op jit(solution)/shard_map/ppermute | solution.py:334
  113.3 1.7 %collective-permute-done.33.r3 = f32[16,64]{1,0:T(8,128)S(1)} collective-permute-done((f32[16,64]{1,0:T(8,128)S(1)}, f32[16,64]{1,0:T(8,128)S(1)}, u32[]{:S(2)}, u32[]{:S(2)}) %collective-permute-start.33) | collective-permute-done | bytes 4128 | tf_op jit(solution)/shard_map/ppermute | solution.py:334
  (60 shorter events, 17.7 us)
Async XLA Ops:
  2.6 31.3 %collective-permute-start.5 = (f32[512,256]{1,0:T(8,128)S(1)}, f32[512,256]{1,0:T(8,128)S(1)}, u32[]{:S(2)}, u32[]{:S(2)}) collective-permute-start(f32[512,256]{1,0:T(8,128)S(1)} %get-tuple-element.44), channel_id=1, source_target_pairs={{0,1},{1,2},{2,3},{3,0},{4,5},{5,6},{6,7},{7,4},{8,9},{9,10},{10,1... | collective-permute-start | bytes 1572872 | tf_op jit(solution)/shard_map/ppermute | solution.py:334
  4.6 30.2 %collective-permute-start.6 = (f32[512,256]{1,0:T(8,128)S(1)}, f32[512,256]{1,0:T(8,128)S(1)}, u32[]{:S(2)}, u32[]{:S(2)}) collective-permute-start(f32[512,256]{1,0:T(8,128)S(1)} %get-tuple-element.45), channel_id=1, source_target_pairs={{0,3},{1,0},{2,1},{3,2},{4,7},{5,4},{6,5},{7,6},{8,11},{9,8},{10,9... | collective-permute-start | bytes 1572872 | tf_op jit(solution)/shard_map/ppermute | solution.py:334
  6.8 36.0 %collective-permute-start.3 = (f32[1024,256]{1,0:T(8,128)S(1)}, f32[1024,256]{1,0:T(8,128)S(1)}, u32[]{:S(2)}, u32[]{:S(2)}) collective-permute-start(f32[1024,256]{1,0:T(8,128)S(1)} %get-tuple-element.42), channel_id=1, source_target_pairs={{0,1},{1,2},{2,3},{3,0},{4,5},{5,6},{6,7},{7,4},{8,9},{9,10},{10,1... | collective-permute-start | bytes 3145736 | tf_op jit(solution)/shard_map/ppermute | solution.py:334
  6.8 36.0 %collective-permute-start.4 = (f32[1024,256]{1,0:T(8,128)S(1)}, f32[1024,256]{1,0:T(8,128)S(1)}, u32[]{:S(2)}, u32[]{:S(2)}) collective-permute-start(f32[1024,256]{1,0:T(8,128)S(1)} %get-tuple-element.43), channel_id=1, source_target_pairs={{0,3},{1,0},{2,1},{3,2},{4,7},{5,4},{6,5},{7,6},{8,11},{9,8},{10,9... | collective-permute-start | bytes 3145736 | tf_op jit(solution)/shard_map/ppermute | solution.py:334
  33.2 9.6 %collective-permute-start.2 = (f32[16,256]{1,0:T(8,128)S(1)}, f32[16,256]{1,0:T(8,128)S(1)}, u32[]{:S(2)}, u32[]{:S(2)}) collective-permute-start(f32[16,256]{1,0:T(8,128)S(1)} %shard_map.65.info.i0), channel_id=1, source_target_pairs={{0,2},{1,3},{2,0},{3,1},{4,6},{5,7},{6,4},{7,5},{8,10},{9,11},{10,... | collective-permute-start | bytes 49160 | tf_op jit(solution)/shard_map/ppermute | solution.py:334
  33.8 8.9 %collective-permute-start.1 = (f32[16,256]{1,0:T(8,128)S(1)}, f32[16,256]{1,0:T(8,128)S(1)}, u32[]{:S(2)}, u32[]{:S(2)}) collective-permute-start(f32[16,256]{1,0:T(8,128)S(1)} %shard_map.65.info.i0), channel_id=1, source_target_pairs={{0,3},{1,0},{2,1},{3,2},{4,7},{5,4},{6,5},{7,6},{8,11},{9,8},{10,9... | collective-permute-start | bytes 49160 | tf_op jit(solution)/shard_map/ppermute | solution.py:334
  34.7 8.0 %collective-permute-start = (f32[16,256]{1,0:T(8,128)S(1)}, f32[16,256]{1,0:T(8,128)S(1)}, u32[]{:S(2)}, u32[]{:S(2)}) collective-permute-start(f32[16,256]{1,0:T(8,128)S(1)} %shard_map.65.info.i0), channel_id=1, source_target_pairs={{0,1},{1,2},{2,3},{3,0},{4,5},{5,6},{6,7},{7,4},{8,9},{9,10},{10,1... | collective-permute-start | bytes 49160 | tf_op jit(solution)/shard_map/ppermute | solution.py:334
  42.8 14.9 %collective-permute-start.7 = (f32[512,256]{1,0:T(8,128)S(1)}, f32[512,256]{1,0:T(8,128)S(1)}, u32[]{:S(2)}, u32[]{:S(2)}) collective-permute-start(f32[512,256]{1,0:T(8,128)S(1)} %collective-permute-done.5), channel_id=1, source_target_pairs={{0,1},{1,2},{2,3},{3,0},{4,5},{5,6},{6,7},{7,4},{8,9},{9,10},{10,1... | collective-permute-start | bytes 1572872 | tf_op jit(solution)/shard_map/ppermute | solution.py:334
  44.0 13.6 %collective-permute-start.8 = (f32[512,256]{1,0:T(8,128)S(1)}, f32[512,256]{1,0:T(8,128)S(1)}, u32[]{:S(2)}, u32[]{:S(2)}) collective-permute-start(f32[512,256]{1,0:T(8,128)S(1)} %collective-permute-done.6), channel_id=1, source_target_pairs={{0,3},{1,0},{2,1},{3,2},{4,7},{5,4},{6,5},{7,6},{8,11},{9,8},{10,9... | collective-permute-start | bytes 1572872 | tf_op jit(solution)/shard_map/ppermute | solution.py:334
  47.7 9.3 %collective-permute-start.9 = (f32[16,256]{1,0:T(8,128)S(1)}, f32[16,256]{1,0:T(8,128)S(1)}, u32[]{:S(2)}, u32[]{:S(2)}) collective-permute-start(f32[16,256]{1,0:T(8,128)S(1)} %get-tuple-element.58), channel_id=1, source_target_pairs={{0,1},{1,2},{2,3},{3,0},{4,5},{5,6},{6,7},{7,4},{8,9},{9,10},{10,1... | collective-permute-start | bytes 49160 | tf_op jit(solution)/shard_map/ppermute | solution.py:334
  47.7 9.9 %collective-permute-start.10 = (f32[16,256]{1,0:T(8,128)S(1)}, f32[16,256]{1,0:T(8,128)S(1)}, u32[]{:S(2)}, u32[]{:S(2)}) collective-permute-start(f32[16,256]{1,0:T(8,128)S(1)} %get-tuple-element.59), channel_id=1, source_target_pairs={{0,2},{1,3},{2,0},{3,1},{4,6},{5,7},{6,4},{7,5},{8,10},{9,11},{10,... | collective-permute-start | bytes 49160 | tf_op jit(solution)/shard_map/ppermute | solution.py:334
  50.0 7.7 %collective-permute-start.11 = (f32[16,256]{1,0:T(8,128)S(1)}, f32[16,256]{1,0:T(8,128)S(1)}, u32[]{:S(2)}, u32[]{:S(2)}) collective-permute-start(f32[16,256]{1,0:T(8,128)S(1)} %get-tuple-element.60), channel_id=1, source_target_pairs={{0,3},{1,0},{2,1},{3,2},{4,7},{5,4},{6,5},{7,6},{8,11},{9,8},{10,9... | collective-permute-start | bytes 49160 | tf_op jit(solution)/shard_map/ppermute | solution.py:334
  61.4 7.8 %collective-permute-start.12 = (f32[136,256]{1,0:T(8,128)S(1)}, f32[136,256]{1,0:T(8,128)S(1)}, u32[]{:S(2)}, u32[]{:S(2)}) collective-permute-start(f32[136,256]{1,0:T(8,128)S(1)} %get-tuple-element.61.t0), channel_id=1, source_target_pairs={{0,1},{1,2},{2,3},{3,0},{4,5},{5,6},{6,7},{7,4},{8,9},{9,10},{10,1... | collective-permute-start | bytes 417800 | tf_op jit(solution)/shard_map/ppermute | solution.py:334
  62.4 6.8 %collective-permute-start.15 = (f32[136,256]{1,0:T(8,128)S(1)}, f32[136,256]{1,0:T(8,128)S(1)}, u32[]{:S(2)}, u32[]{:S(2)}) collective-permute-start(f32[136,256]{1,0:T(8,128)S(1)} %get-tuple-element.62.l0), channel_id=1, source_target_pairs={{0,3},{1,0},{2,1},{3,2},{4,7},{5,4},{6,5},{7,6},{8,11},{9,8},{10,9... | collective-permute-start | bytes 417800 | tf_op jit(solution)/shard_map/ppermute | solution.py:334
  64.7 7.8 %collective-permute-start.17 = (f32[136,256]{1,0:T(8,128)S(1)}, f32[136,256]{1,0:T(8,128)S(1)}, u32[]{:S(2)}, u32[]{:S(2)}) collective-permute-start(f32[136,256]{1,0:T(8,128)S(1)} %get-tuple-element.61.t0), channel_id=1, source_target_pairs={{0,3},{1,0},{2,1},{3,2},{4,7},{5,4},{6,5},{7,6},{8,11},{9,8},{10,9... | collective-permute-start | bytes 417800 | tf_op jit(solution)/shard_map/ppermute | solution.py:334
  65.9 6.6 %collective-permute-start.13 = (f32[136,256]{1,0:T(8,128)S(1)}, f32[136,256]{1,0:T(8,128)S(1)}, u32[]{:S(2)}, u32[]{:S(2)}) collective-permute-start(f32[136,256]{1,0:T(8,128)S(1)} %get-tuple-element.62.l0), channel_id=1, source_target_pairs={{0,1},{1,2},{2,3},{3,0},{4,5},{5,6},{6,7},{7,4},{8,9},{9,10},{10,1... | collective-permute-start | bytes 417800 | tf_op jit(solution)/shard_map/ppermute | solution.py:334
  69.2 6.3 %collective-permute-start.14 = (f32[136,256]{1,0:T(8,128)S(1)}, f32[136,256]{1,0:T(8,128)S(1)}, u32[]{:S(2)}, u32[]{:S(2)}) collective-permute-start(f32[136,256]{1,0:T(8,128)S(1)} %collective-permute-done.12.t1), channel_id=1, source_target_pairs={{0,1},{1,2},{2,3},{3,0},{4,5},{5,6},{6,7},{7,4},{8,9},{9,10},{10,1... | collective-permute-start | bytes 417800 | tf_op jit(solution)/shard_map/ppermute | solution.py:334
  69.2 6.3 %collective-permute-start.16 = (f32[136,256]{1,0:T(8,128)S(1)}, f32[136,256]{1,0:T(8,128)S(1)}, u32[]{:S(2)}, u32[]{:S(2)}) collective-permute-start(f32[136,256]{1,0:T(8,128)S(1)} %collective-permute-done.15.l3), channel_id=1, source_target_pairs={{0,3},{1,0},{2,1},{3,2},{4,7},{5,4},{6,5},{7,6},{8,11},{9,8},{10,9... | collective-permute-start | bytes 417800 | tf_op jit(solution)/shard_map/ppermute | solution.py:334
  76.8 1.6 %collective-permute-start.18 = (f32[272,256]{1,0:T(8,128)S(1)}, f32[272,256]{1,0:T(8,128)S(1)}, u32[]{:S(2)}, u32[]{:S(2)}) collective-permute-start(f32[272,256]{1,0:T(8,128)S(1)} %get-tuple-element.63.own), channel_id=1, source_target_pairs={{0,4},{4,0},{8,12},{12,8},{16,20},{20,16},{24,28},{28,24},{32,36},... | collective-permute-start | bytes 835592 | tf_op jit(solution)/shard_map/ppermute | solution.py:403
  79.3 8.1 %collective-permute-start.21 = (f32[136,256]{1,0:T(8,128)S(1)}, f32[136,256]{1,0:T(8,128)S(1)}, u32[]{:S(2)}, u32[]{:S(2)}) collective-permute-start(f32[136,256]{1,0:T(8,128)S(1)} %get-tuple-element.66), channel_id=1, source_target_pairs={{0,16},{4,20},{8,24},{12,28},{16,0},{20,4},{24,8},{28,12},{32,48},... | collective-permute-start | bytes 417800 | tf_op jit(solution)/shard_map/ppermute | solution.py:408
  82.6 7.3 %collective-permute-start.20 = (f32[136,256]{1,0:T(8,128)S(1)}, f32[136,256]{1,0:T(8,128)S(1)}, u32[]{:S(2)}, u32[]{:S(2)}) collective-permute-start(f32[136,256]{1,0:T(8,128)S(1)} %get-tuple-element.66), channel_id=1, source_target_pairs={{0,8},{4,12},{8,16},{12,20},{16,24},{20,28},{24,0},{28,4},{32,40},... | collective-permute-start | bytes 417800 | tf_op jit(solution)/shard_map/ppermute | solution.py:408
  83.3 6.8 %collective-permute-start.19 = (f32[136,256]{1,0:T(8,128)S(1)}, f32[136,256]{1,0:T(8,128)S(1)}, u32[]{:S(2)}, u32[]{:S(2)}) collective-permute-start(f32[136,256]{1,0:T(8,128)S(1)} %get-tuple-element.66), channel_id=1, source_target_pairs={{0,24},{4,28},{8,0},{12,4},{16,8},{20,12},{24,16},{28,20},{32,56},... | collective-permute-start | bytes 417800 | tf_op jit(solution)/shard_map/ppermute | solution.py:408
  87.4 3.0 %collective-permute-start.24 = (f32[136,256]{1,0:T(8,128)S(1)}, f32[136,256]{1,0:T(8,128)S(1)}, u32[]{:S(2)}, u32[]{:S(2)}) collective-permute-start(f32[136,256]{1,0:T(8,128)S(1)} %collective-permute-done.21.h3), channel_id=1, source_target_pairs={{0,4},{4,0},{8,12},{12,8},{16,20},{20,16},{24,28},{28,24},{32,36},... | collective-permute-start | bytes 417800 | tf_op jit(solution)/shard_map/ppermute | solution.py:403
  90.1 1.4 %collective-permute-start.22 = (f32[136,256]{1,0:T(8,128)S(1)}, f32[136,256]{1,0:T(8,128)S(1)}, u32[]{:S(2)}, u32[]{:S(2)}) collective-permute-start(f32[136,256]{1,0:T(8,128)S(1)} %collective-permute-done.19.h1), channel_id=1, source_target_pairs={{0,4},{4,0},{8,12},{12,8},{16,20},{20,16},{24,28},{28,24},{32,36},... | collective-permute-start | bytes 417800 | tf_op jit(solution)/shard_map/ppermute | solution.py:403
  92.7 8.1 %collective-permute-start.27 = (f32[136,256]{1,0:T(8,128)S(1)}, f32[136,256]{1,0:T(8,128)S(1)}, u32[]{:S(2)}, u32[]{:S(2)}) collective-permute-start(f32[136,256]{1,0:T(8,128)S(1)} %get-tuple-element.67), channel_id=1, source_target_pairs={{0,64},{4,68},{8,72},{12,76},{16,80},{20,84},{24,88},{28,92},{32,9... | collective-permute-start | bytes 417800 | tf_op jit(solution)/shard_map/ppermute | solution.py:408
  94.2 6.8 %collective-permute-start.26 = (f32[136,256]{1,0:T(8,128)S(1)}, f32[136,256]{1,0:T(8,128)S(1)}, u32[]{:S(2)}, u32[]{:S(2)}) collective-permute-start(f32[136,256]{1,0:T(8,128)S(1)} %get-tuple-element.67), channel_id=1, source_target_pairs={{0,32},{4,36},{8,40},{12,44},{16,48},{20,52},{24,56},{28,60},{32,6... | collective-permute-start | bytes 417800 | tf_op jit(solution)/shard_map/ppermute | solution.py:408
  96.3 7.0 %collective-permute-start.25 = (f32[136,256]{1,0:T(8,128)S(1)}, f32[136,256]{1,0:T(8,128)S(1)}, u32[]{:S(2)}, u32[]{:S(2)}) collective-permute-start(f32[136,256]{1,0:T(8,128)S(1)} %get-tuple-element.67), channel_id=1, source_target_pairs={{0,96},{4,100},{8,104},{12,108},{16,112},{20,116},{24,120},{28,124... | collective-permute-start | bytes 417800 | tf_op jit(solution)/shard_map/ppermute | solution.py:408
  100.8 3.4 %collective-permute-start.30 = (f32[136,256]{1,0:T(8,128)S(1)}, f32[136,256]{1,0:T(8,128)S(1)}, u32[]{:S(2)}, u32[]{:S(2)}) collective-permute-start(f32[136,256]{1,0:T(8,128)S(1)} %collective-permute-done.27.h3), channel_id=1, source_target_pairs={{0,4},{4,0},{8,12},{12,8},{16,20},{20,16},{24,28},{28,24},{32,36},... | collective-permute-start | bytes 417800 | tf_op jit(solution)/shard_map/ppermute | solution.py:403
  101.0 3.2 %collective-permute-start.29 = (f32[136,256]{1,0:T(8,128)S(1)}, f32[136,256]{1,0:T(8,128)S(1)}, u32[]{:S(2)}, u32[]{:S(2)}) collective-permute-start(f32[136,256]{1,0:T(8,128)S(1)} %collective-permute-done.26.h2), channel_id=1, source_target_pairs={{0,4},{4,0},{8,12},{12,8},{16,20},{20,16},{24,28},{28,24},{32,36},... | collective-permute-start | bytes 417800 | tf_op jit(solution)/shard_map/ppermute | solution.py:403
  106.9 5.2 %collective-permute-start.31 = (f32[16,64]{1,0:T(8,128)S(1)}, f32[16,64]{1,0:T(8,128)S(1)}, u32[]{:S(2)}, u32[]{:S(2)}) collective-permute-start(f32[16,64]{1,0:T(8,128)S(1)} %get-tuple-element.72), channel_id=1, source_target_pairs={{0,2},{1,3},{2,0},{3,1},{4,6},{5,7},{6,4},{7,5},{8,10},{9,11},{10,... | collective-permute-start | bytes 12296 | tf_op jit(solution)/shard_map/ppermute | solution.py:334
  108.5 4.9 %collective-permute-start.32 = (f32[16,64]{1,0:T(8,128)S(1)}, f32[16,64]{1,0:T(8,128)S(1)}, u32[]{:S(2)}, u32[]{:S(2)}) collective-permute-start(f32[16,64]{1,0:T(8,128)S(1)} %get-tuple-element.73), channel_id=1, source_target_pairs={{0,1},{1,2},{2,3},{3,0},{4,5},{5,6},{6,7},{7,4},{8,9},{9,10},{10,1... | collective-permute-start | bytes 12296 | tf_op jit(solution)/shard_map/ppermute | solution.py:334
  111.4 3.7 %collective-permute-start.33 = (f32[16,64]{1,0:T(8,128)S(1)}, f32[16,64]{1,0:T(8,128)S(1)}, u32[]{:S(2)}, u32[]{:S(2)}) collective-permute-start(f32[16,64]{1,0:T(8,128)S(1)} %get-tuple-element.74), channel_id=1, source_target_pairs={{0,3},{1,0},{2,1},{3,2},{4,7},{5,4},{6,5},{7,6},{8,11},{9,8},{10,9... | collective-permute-start | bytes 12296 | tf_op jit(solution)/shard_map/ppermute | solution.py:334
  (6 other events, 89.8 us)

commit v16 on v15

--- a/solution.py
+++ b/solution.py
@@ -142,7 +142,7 @@
             al[k, rows, :] = lo
 
 
-def compose_kernel(idx, own, prev, after, q1, q2, b0, b1, b2, b3, pref, top, low, ah, al, b_s):
+def compose_kernel(idx, own, prev, after, q1, q2, b0, b2, b1, b3, pref, top, low, ah, al, b_s):
     z = idx[Z]
     assemble(z, own, prev, after, (q1, q2), ah, al)
     for d, b in enumerate((b0, b1, b2, b3)):
@@ -379,7 +379,7 @@
         (staged, info, *infos),
         [pltpu.VMEM((ROWS, 16, N), F32), pltpu.VMEM((ROWS, 16, 128), F32)],
     )
-    offs = [offs[0], *along_rows(offs[1:])]
+    offs = [offs[0], *[along_row(offs[d], d) for d in (2, 1, 3)]]
     pref, top, low = call(
         compose_kernel,
         [(SUB, R, N), (HALF, N), (HALF, N)],

time: 116 us -> 116 us (level)
  transfers between devices with their start and end apart: 34 -> 34, of which waited for: 18 -> 17; matrix products, arithmetic and copies ran while one was open for 0% -> 0% of each run, Pallas kernels for 10% -> 10%
where the time goes in v16:
time: 116 us
  starting transfers between devices  41.6 us (36%)
  waiting for transfers between devices  32.5 us (28%)
  Pallas kernels  24.9 us (21%)
  blocking collectives  16.7 us (14%)
    ppermute x21, starting transfers between devices, along_row(): return lax.ppermute(x, 'row', [(i, (i + d) % ROWS) for i in range(ROWS)])  30.8 us
    ppermute x21, waiting for transfers between devices, along_row(): return lax.ppermute(x, 'row', [(i, (i + d) % ROWS) for i in range(ROWS)])  18.5 us
    pallas_call x10, Pallas kernels, call(): pl.pallas_call(kernel, out_shape=[pltpu.VMEM(s, t) for s, t in outs], in_...  17.9 us
    all_to_all x1, blocking collectives, shards(): sums = lax.all_to_all(partial, 'tm', 0, 0, tiled=True).reshape(32, 16, N)  16.7 us
    ppermute x6, waiting for transfers between devices, gathered(): lax.ppermute(half, 'tm', [(i, i - i % n + (i + d * stride) % n) for i in...  10.9 us
    ppermute x6, starting transfers between devices, gathered(): lax.ppermute(half, 'tm', [(i, i - i % n + (i + d * stride) % n) for i in...  10.1 us
    pallas_call x1, Pallas kernels, binned(): pl.pallas_call(bin_kernel, out_shape=jax.ShapeDtypeStruct((n_bins // 4, N...  5.84 us
    ppermute x7, waiting for transfers between devices, other_core(): return lax.ppermute(m, 'tm', [(i, i ^ 1) for i in range(32)])  3.09 us
  transfers between devices with their start and end apart: 34, of which 17 were waited for; matrix products, arithmetic and copies ran while one was open for 0% of the time, Pallas kernels for 10%

profile of v16, /device:TPU:6, one launch (start us, length us, event | category | flops | bytes accessed | tf_op | source)
XLA Modules:
  0.0 116.0 jit_solution(14780258327379377421)
XLA Ops:
  0.1 2.5 %shard_map.67 = (f32[512,256]{1,0:T(8,128)S(1)}, f32[512,256]{1,0:T(8,128)S(1)}, f32[1024,256]{1,0:T(8,128)S(1)}, f32[1024,256]{1,0:T(8,128)S(1)}) custom-call(s32[4]{0:T(128)S(1)} %pad_add_fusion.idx, f32[4096,256]{1,0:T(8,128)} %bitcast.14), custom_call_target="tpu_custom_call" | custom-call | tf_op jit(solution)/shard_map/pallas_call | solution.py:75
  2.6 2.0 %collective-permute-start.5 = (f32[512,256]{1,0:T(8,128)S(1)}, f32[512,256]{1,0:T(8,128)S(1)}, u32[]{:S(2)}, u32[]{:S(2)}) collective-permute-start(f32[512,256]{1,0:T(8,128)S(1)} %get-tuple-element.44), channel_id=1, source_target_pairs={{0,1},{1,2},{2,3},{3,0},{4,5},{5,6},{6,7},{7,4},{8,9},{9,10},{10,1... | collective-permute-start | bytes 1572872 | tf_op jit(solution)/shard_map/ppermute | solution.py:334
  4.6 2.2 %collective-permute-start.6 = (f32[512,256]{1,0:T(8,128)S(1)}, f32[512,256]{1,0:T(8,128)S(1)}, u32[]{:S(2)}, u32[]{:S(2)}) collective-permute-start(f32[512,256]{1,0:T(8,128)S(1)} %get-tuple-element.45), channel_id=1, source_target_pairs={{0,3},{1,0},{2,1},{3,2},{4,7},{5,4},{6,5},{7,6},{8,11},{9,8},{10,9... | collective-permute-start | bytes 1572872 | tf_op jit(solution)/shard_map/ppermute | solution.py:334
  6.8 3.2 %collective-permute-start.4 = (f32[1024,256]{1,0:T(8,128)S(1)}, f32[1024,256]{1,0:T(8,128)S(1)}, u32[]{:S(2)}, u32[]{:S(2)}) collective-permute-start(f32[1024,256]{1,0:T(8,128)S(1)} %get-tuple-element.43), channel_id=1, source_target_pairs={{0,3},{1,0},{2,1},{3,2},{4,7},{5,4},{6,5},{7,6},{8,11},{9,8},{10,9... | collective-permute-start | bytes 3145736 | tf_op jit(solution)/shard_map/ppermute | solution.py:334
  10.1 5.8 %shard_map.64 = f32[512,256]{1,0:T(8,128)S(1)} custom-call(s32[1,4096]{1,0:T(1,128)S(1)} %bitcast.12, f32[64,4096]{1,0:T(8,128)S(1)} %bitcast.11), custom_call_target="tpu_custom_call" | custom-call | tf_op jit(solution)/shard_map/pallas_call | solution.py:120
  15.9 16.7 %all_to_all.9.sums = f32[32,16,256]{2,1,0:T(8,128)S(1)} all-to-all(f32[32,16,256]{2,1,0:T(8,128)S(1)} %bitcast.10), channel_id=1, replica_groups=mesh['tm'=32,'row'=4] {'tm'}, dimensions={0} | all-to-all | bytes 1048576 | tf_op jit(solution)/shard_map/all_to_all | solution.py:360
  35.9 3.0 %shard_map.66 = (f32[64,64,256]{2,1,0:T(8,128)S(1)}, f32[1024,256]{1,0:T(8,128)S(1)}) custom-call(s32[4]{0:T(128)S(1)} %pad_add_fusion.idx, f32[64,64,256]{2,1,0:T(8,128)} %gains.1, f32[4096,256]{1,0:T(8,128)} %bitcast.15, f32[16,256]{1,0:T(8,128)S(1)} %shard_map.65.info.i0), custom_call_target="tpu_custom_call" | custom-call | tf_op jit(solution)/shard_map/pallas_call | solution.py:75
  38.9 3.9 %collective-permute-done.2.r2 = f32[16,256]{1,0:T(8,128)S(1)} collective-permute-done((f32[16,256]{1,0:T(8,128)S(1)}, f32[16,256]{1,0:T(8,128)S(1)}, u32[]{:S(2)}, u32[]{:S(2)}) %collective-permute-start.2) | collective-permute-done | bytes 16416 | tf_op jit(solution)/shard_map/ppermute | solution.py:334
  44.0 2.1 %collective-permute-start.8 = (f32[512,256]{1,0:T(8,128)S(1)}, f32[512,256]{1,0:T(8,128)S(1)}, u32[]{:S(2)}, u32[]{:S(2)}) collective-permute-start(f32[512,256]{1,0:T(8,128)S(1)} %collective-permute-done.6), channel_id=1, source_target_pairs={{0,3},{1,0},{2,1},{3,2},{4,7},{5,4},{6,5},{7,6},{8,11},{9,8},{10,9... | collective-permute-start | bytes 1572872 | tf_op jit(solution)/shard_map/ppermute | solution.py:334
  46.1 1.6 %shard_map.68 = (f32[16,256]{1,0:T(8,128)S(1)}, f32[16,256]{1,0:T(8,128)S(1)}, f32[16,256]{1,0:T(8,128)S(1)}, f32[16,256]{1,0:T(8,128)S(1)}) custom-call(s32[4]{0:T(128)S(1)} %pad_add_fusion.idx, f32[64,64,256]{2,1,0:T(8,128)S(1)} %get-tuple-element.53.g, f32[16,256]{1,0:T(8,128)S(1)} %shard_map.65.info.i0, f32[16,256]{1,0:T(8,128)S(1)} %collective-permute-done.r1, ...), custom_call_target="tpu_custom_call" | custom-call | tf_op jit(solution)/shard_map/pallas_call | solution.py:75
  49.4 2.3 %collective-permute-start.11 = (f32[16,256]{1,0:T(8,128)S(1)}, f32[16,256]{1,0:T(8,128)S(1)}, u32[]{:S(2)}, u32[]{:S(2)}) collective-permute-start(f32[16,256]{1,0:T(8,128)S(1)} %get-tuple-element.60), channel_id=1, source_target_pairs={{0,3},{1,0},{2,1},{3,2},{4,7},{5,4},{6,5},{7,6},{8,11},{9,8},{10,9... | collective-permute-start | bytes 49160 | tf_op jit(solution)/shard_map/ppermute | solution.py:334
  51.7 5.8 %collective-permute-done.9.b2 = f32[16,256]{1,0:T(8,128)S(1)} collective-permute-done((f32[16,256]{1,0:T(8,128)S(1)}, f32[16,256]{1,0:T(8,128)S(1)}, u32[]{:S(2)}, u32[]{:S(2)}) %collective-permute-start.9) | collective-permute-done | bytes 16416 | tf_op jit(solution)/shard_map/ppermute | solution.py:334
  57.5 3.7 %shard_map.69 = (f32[16,272,256]{2,1,0:T(8,128)S(1)}, f32[136,256]{1,0:T(8,128)S(1)}, f32[136,256]{1,0:T(8,128)S(1)}) custom-call(s32[4]{0:T(128)S(1)} %pad_add_fusion.idx, f32[1024,256]{1,0:T(8,128)S(1)} %get-tuple-element.48.own, f32[1024,256]{1,0:T(8,128)S(1)} %collective-permute-done.3.prev, f32[1024,256]{1,0:T(8,128)S(1)} %collective-permute-done.4.after, ...), custom_call_target="tpu_custom_call" | custom-call | tf_op jit(solution)/shard_map/pallas_call | solution.py:75
  62.4 2.1 %collective-permute-start.15 = (f32[136,256]{1,0:T(8,128)S(1)}, f32[136,256]{1,0:T(8,128)S(1)}, u32[]{:S(2)}, u32[]{:S(2)}) collective-permute-start(f32[136,256]{1,0:T(8,128)S(1)} %get-tuple-element.62.l0), channel_id=1, source_target_pairs={{0,3},{1,0},{2,1},{3,2},{4,7},{5,4},{6,5},{7,6},{8,11},{9,8},{10,9... | collective-permute-start | bytes 417800 | tf_op jit(solution)/shard_map/ppermute | solution.py:334
  64.5 1.4 %collective-permute-start.17 = (f32[136,256]{1,0:T(8,128)S(1)}, f32[136,256]{1,0:T(8,128)S(1)}, u32[]{:S(2)}, u32[]{:S(2)}) collective-permute-start(f32[136,256]{1,0:T(8,128)S(1)} %get-tuple-element.61.t0), channel_id=1, source_target_pairs={{0,3},{1,0},{2,1},{3,2},{4,7},{5,4},{6,5},{7,6},{8,11},{9,8},{10,9... | collective-permute-start | bytes 417800 | tf_op jit(solution)/shard_map/ppermute | solution.py:334
  66.6 2.5 %collective-permute-done.12.t1 = f32[136,256]{1,0:T(8,128)S(1)} collective-permute-done((f32[136,256]{1,0:T(8,128)S(1)}, f32[136,256]{1,0:T(8,128)S(1)}, u32[]{:S(2)}, u32[]{:S(2)}) %collective-permute-start.12) | collective-permute-done | bytes 139296 | tf_op jit(solution)/shard_map/ppermute | solution.py:334
  69.1 3.2 %collective-permute-start.16 = (f32[136,256]{1,0:T(8,128)S(1)}, f32[136,256]{1,0:T(8,128)S(1)}, u32[]{:S(2)}, u32[]{:S(2)}) collective-permute-start(f32[136,256]{1,0:T(8,128)S(1)} %collective-permute-done.15.l3), channel_id=1, source_target_pairs={{0,3},{1,0},{2,1},{3,2},{4,7},{5,4},{6,5},{7,6},{8,11},{9,8},{10,9... | collective-permute-start | bytes 417800 | tf_op jit(solution)/shard_map/ppermute | solution.py:334
  72.3 3.0 %collective-permute-done.14.t2 = f32[136,256]{1,0:T(8,128)S(1)} collective-permute-done((f32[136,256]{1,0:T(8,128)S(1)}, f32[136,256]{1,0:T(8,128)S(1)}, u32[]{:S(2)}, u32[]{:S(2)}) %collective-permute-start.14) | collective-permute-done | bytes 139296 | tf_op jit(solution)/shard_map/ppermute | solution.py:334
  75.3 1.3 %shard_map.70 = (f32[272,256]{1,0:T(8,128)S(1)}, f32[272,256]{1,0:T(8,128)S(1)}) custom-call(s32[4]{0:T(128)S(1)} %pad_add_fusion.idx, f32[136,256]{1,0:T(8,128)S(1)} %get-tuple-element.61.t0, f32[136,256]{1,0:T(8,128)S(1)} %get-tuple-element.62.l0, f32[136,256]{1,0:T(8,128)S(1)} %collective-permute-done.12.t1, f32[136,256]{1,0:T(8,128)S(1)} %collective-permute-done.13.l1, ...), custom_call_target="tpu_custom_call" | custom-call | tf_op jit(solution)/shard_map/pallas_call | solution.py:75
  76.8 1.5 %collective-permute-done.18.other = f32[272,256]{1,0:T(8,128)S(1)} collective-permute-done((f32[272,256]{1,0:T(8,128)S(1)}, f32[272,256]{1,0:T(8,128)S(1)}, u32[]{:S(2)}, u32[]{:S(2)}) %collective-permute-start.18) | collective-permute-done | bytes 278560 | tf_op jit(solution)/shard_map/ppermute | solution.py:403
  79.2 3.3 %collective-permute-start.21 = (f32[136,256]{1,0:T(8,128)S(1)}, f32[136,256]{1,0:T(8,128)S(1)}, u32[]{:S(2)}, u32[]{:S(2)}) collective-permute-start(f32[136,256]{1,0:T(8,128)S(1)} %get-tuple-element.66), channel_id=1, source_target_pairs={{0,16},{4,20},{8,24},{12,28},{16,0},{20,4},{24,8},{28,12},{32,48},... | collective-permute-start | bytes 417800 | tf_op jit(solution)/shard_map/ppermute | solution.py:408
  83.1 2.6 %collective-permute-start.19 = (f32[136,256]{1,0:T(8,128)S(1)}, f32[136,256]{1,0:T(8,128)S(1)}, u32[]{:S(2)}, u32[]{:S(2)}) collective-permute-start(f32[136,256]{1,0:T(8,128)S(1)} %get-tuple-element.66), channel_id=1, source_target_pairs={{0,24},{4,28},{8,0},{12,4},{16,8},{20,12},{24,16},{28,20},{32,56},... | collective-permute-start | bytes 417800 | tf_op jit(solution)/shard_map/ppermute | solution.py:408
  85.7 1.6 %collective-permute-done.21.h3 = f32[136,256]{1,0:T(8,128)S(1)} collective-permute-done((f32[136,256]{1,0:T(8,128)S(1)}, f32[136,256]{1,0:T(8,128)S(1)}, u32[]{:S(2)}, u32[]{:S(2)}) %collective-permute-start.21) | collective-permute-done | bytes 139296 | tf_op jit(solution)/shard_map/ppermute | solution.py:408
  87.3 2.5 %collective-permute-done.20.h2 = f32[136,256]{1,0:T(8,128)S(1)} collective-permute-done((f32[136,256]{1,0:T(8,128)S(1)}, f32[136,256]{1,0:T(8,128)S(1)}, u32[]{:S(2)}, u32[]{:S(2)}) %collective-permute-start.20) | collective-permute-done | bytes 139296 | tf_op jit(solution)/shard_map/ppermute | solution.py:408
  92.6 1.5 %collective-permute-start.27 = (f32[136,256]{1,0:T(8,128)S(1)}, f32[136,256]{1,0:T(8,128)S(1)}, u32[]{:S(2)}, u32[]{:S(2)}) collective-permute-start(f32[136,256]{1,0:T(8,128)S(1)} %get-tuple-element.67), channel_id=1, source_target_pairs={{0,64},{4,68},{8,72},{12,76},{16,80},{20,84},{24,88},{28,92},{32,9... | collective-permute-start | bytes 417800 | tf_op jit(solution)/shard_map/ppermute | solution.py:408
  94.1 2.1 %collective-permute-start.26 = (f32[136,256]{1,0:T(8,128)S(1)}, f32[136,256]{1,0:T(8,128)S(1)}, u32[]{:S(2)}, u32[]{:S(2)}) collective-permute-start(f32[136,256]{1,0:T(8,128)S(1)} %get-tuple-element.67), channel_id=1, source_target_pairs={{0,32},{4,36},{8,40},{12,44},{16,48},{20,52},{24,56},{28,60},{32,6... | collective-permute-start | bytes 417800 | tf_op jit(solution)/shard_map/ppermute | solution.py:408
  96.2 4.5 %collective-permute-done.27.h3 = f32[136,256]{1,0:T(8,128)S(1)} collective-permute-done((f32[136,256]{1,0:T(8,128)S(1)}, f32[136,256]{1,0:T(8,128)S(1)}, u32[]{:S(2)}, u32[]{:S(2)}) %collective-permute-start.27) | collective-permute-done | bytes 139296 | tf_op jit(solution)/shard_map/ppermute | solution.py:408
  101.2 2.0 %collective-permute-done.25.h1 = f32[136,256]{1,0:T(8,128)S(1)} collective-permute-done((f32[136,256]{1,0:T(8,128)S(1)}, f32[136,256]{1,0:T(8,128)S(1)}, u32[]{:S(2)}, u32[]{:S(2)}) %collective-permute-start.25) | collective-permute-done | bytes 139296 | tf_op jit(solution)/shard_map/ppermute | solution.py:408
  104.5 2.2 %shard_map.74 = (f32[16,64]{1,0:T(8,128)S(1)}, f32[16,64]{1,0:T(8,128)S(1)}, f32[16,64]{1,0:T(8,128)S(1)}, f32[16,64]{1,0:T(8,128)S(1)}) custom-call(s32[4]{0:T(128)S(1)} %pad_add_fusion.idx, f32[1,256]{1,0:T(1,128)S(1)} %bitcast.13, f32[136,256]{1,0:T(8,128)S(1)} %collective-permute-done.25.h1, f32[136,256]{1,0:T(8,128)S(1)} %collective-permute-done.26.h2, ...), custom_call_target="tpu_custom_call" | custom-call | tf_op jit(solution)/shard_map/pallas_call | solution.py:75
  106.8 1.6 %collective-permute-start.31 = (f32[16,64]{1,0:T(8,128)S(1)}, f32[16,64]{1,0:T(8,128)S(1)}, u32[]{:S(2)}, u32[]{:S(2)}) collective-permute-start(f32[16,64]{1,0:T(8,128)S(1)} %get-tuple-element.72), channel_id=1, source_target_pairs={{0,2},{1,3},{2,0},{3,1},{4,6},{5,7},{6,4},{7,5},{8,10},{9,11},{10,... | collective-permute-start | bytes 12296 | tf_op jit(solution)/shard_map/ppermute | solution.py:334
  108.3 2.9 %collective-permute-start.32 = (f32[16,64]{1,0:T(8,128)S(1)}, f32[16,64]{1,0:T(8,128)S(1)}, u32[]{:S(2)}, u32[]{:S(2)}) collective-permute-start(f32[16,64]{1,0:T(8,128)S(1)} %get-tuple-element.73), channel_id=1, source_target_pairs={{0,1},{1,2},{2,3},{3,0},{4,5},{5,6},{6,7},{7,4},{8,9},{9,10},{10,1... | collective-permute-start | bytes 12296 | tf_op jit(solution)/shard_map/ppermute | solution.py:334
  113.2 1.7 %collective-permute-done.33.r3 = f32[16,64]{1,0:T(8,128)S(1)} collective-permute-done((f32[16,64]{1,0:T(8,128)S(1)}, f32[16,64]{1,0:T(8,128)S(1)}, u32[]{:S(2)}, u32[]{:S(2)}) %collective-permute-start.33) | collective-permute-done | bytes 4128 | tf_op jit(solution)/shard_map/ppermute | solution.py:334
  (60 shorter events, 17.7 us)
Async XLA Ops:
  2.6 31.3 %collective-permute-start.5 = (f32[512,256]{1,0:T(8,128)S(1)}, f32[512,256]{1,0:T(8,128)S(1)}, u32[]{:S(2)}, u32[]{:S(2)}) collective-permute-start(f32[512,256]{1,0:T(8,128)S(1)} %get-tuple-element.44), channel_id=1, source_target_pairs={{0,1},{1,2},{2,3},{3,0},{4,5},{5,6},{6,7},{7,4},{8,9},{9,10},{10,1... | collective-permute-start | bytes 1572872 | tf_op jit(solution)/shard_map/ppermute | solution.py:334
  4.6 30.2 %collective-permute-start.6 = (f32[512,256]{1,0:T(8,128)S(1)}, f32[512,256]{1,0:T(8,128)S(1)}, u32[]{:S(2)}, u32[]{:S(2)}) collective-permute-start(f32[512,256]{1,0:T(8,128)S(1)} %get-tuple-element.45), channel_id=1, source_target_pairs={{0,3},{1,0},{2,1},{3,2},{4,7},{5,4},{6,5},{7,6},{8,11},{9,8},{10,9... | collective-permute-start | bytes 1572872 | tf_op jit(solution)/shard_map/ppermute | solution.py:334
  6.8 36.0 %collective-permute-start.3 = (f32[1024,256]{1,0:T(8,128)S(1)}, f32[1024,256]{1,0:T(8,128)S(1)}, u32[]{:S(2)}, u32[]{:S(2)}) collective-permute-start(f32[1024,256]{1,0:T(8,128)S(1)} %get-tuple-element.42), channel_id=1, source_target_pairs={{0,1},{1,2},{2,3},{3,0},{4,5},{5,6},{6,7},{7,4},{8,9},{9,10},{10,1... | collective-permute-start | bytes 3145736 | tf_op jit(solution)/shard_map/ppermute | solution.py:334
  6.8 36.0 %collective-permute-start.4 = (f32[1024,256]{1,0:T(8,128)S(1)}, f32[1024,256]{1,0:T(8,128)S(1)}, u32[]{:S(2)}, u32[]{:S(2)}) collective-permute-start(f32[1024,256]{1,0:T(8,128)S(1)} %get-tuple-element.43), channel_id=1, source_target_pairs={{0,3},{1,0},{2,1},{3,2},{4,7},{5,4},{6,5},{7,6},{8,11},{9,8},{10,9... | collective-permute-start | bytes 3145736 | tf_op jit(solution)/shard_map/ppermute | solution.py:334
  33.2 9.6 %collective-permute-start.2 = (f32[16,256]{1,0:T(8,128)S(1)}, f32[16,256]{1,0:T(8,128)S(1)}, u32[]{:S(2)}, u32[]{:S(2)}) collective-permute-start(f32[16,256]{1,0:T(8,128)S(1)} %shard_map.65.info.i0), channel_id=1, source_target_pairs={{0,2},{1,3},{2,0},{3,1},{4,6},{5,7},{6,4},{7,5},{8,10},{9,11},{10,... | collective-permute-start | bytes 49160 | tf_op jit(solution)/shard_map/ppermute | solution.py:334
  33.8 8.9 %collective-permute-start.1 = (f32[16,256]{1,0:T(8,128)S(1)}, f32[16,256]{1,0:T(8,128)S(1)}, u32[]{:S(2)}, u32[]{:S(2)}) collective-permute-start(f32[16,256]{1,0:T(8,128)S(1)} %shard_map.65.info.i0), channel_id=1, source_target_pairs={{0,3},{1,0},{2,1},{3,2},{4,7},{5,4},{6,5},{7,6},{8,11},{9,8},{10,9... | collective-permute-start | bytes 49160 | tf_op jit(solution)/shard_map/ppermute | solution.py:334
  34.7 8.0 %collective-permute-start = (f32[16,256]{1,0:T(8,128)S(1)}, f32[16,256]{1,0:T(8,128)S(1)}, u32[]{:S(2)}, u32[]{:S(2)}) collective-permute-start(f32[16,256]{1,0:T(8,128)S(1)} %shard_map.65.info.i0), channel_id=1, source_target_pairs={{0,1},{1,2},{2,3},{3,0},{4,5},{5,6},{6,7},{7,4},{8,9},{9,10},{10,1... | collective-permute-start | bytes 49160 | tf_op jit(solution)/shard_map/ppermute | solution.py:334
  42.8 14.7 %collective-permute-start.7 = (f32[512,256]{1,0:T(8,128)S(1)}, f32[512,256]{1,0:T(8,128)S(1)}, u32[]{:S(2)}, u32[]{:S(2)}) collective-permute-start(f32[512,256]{1,0:T(8,128)S(1)} %collective-permute-done.5), channel_id=1, source_target_pairs={{0,1},{1,2},{2,3},{3,0},{4,5},{5,6},{6,7},{7,4},{8,9},{9,10},{10,1... | collective-permute-start | bytes 1572872 | tf_op jit(solution)/shard_map/ppermute | solution.py:334
  44.0 13.5 %collective-permute-start.8 = (f32[512,256]{1,0:T(8,128)S(1)}, f32[512,256]{1,0:T(8,128)S(1)}, u32[]{:S(2)}, u32[]{:S(2)}) collective-permute-start(f32[512,256]{1,0:T(8,128)S(1)} %collective-permute-done.6), channel_id=1, source_target_pairs={{0,3},{1,0},{2,1},{3,2},{4,7},{5,4},{6,5},{7,6},{8,11},{9,8},{10,9... | collective-permute-start | bytes 1572872 | tf_op jit(solution)/shard_map/ppermute | solution.py:334
  47.7 9.8 %collective-permute-start.9 = (f32[16,256]{1,0:T(8,128)S(1)}, f32[16,256]{1,0:T(8,128)S(1)}, u32[]{:S(2)}, u32[]{:S(2)}) collective-permute-start(f32[16,256]{1,0:T(8,128)S(1)} %get-tuple-element.58), channel_id=1, source_target_pairs={{0,2},{1,3},{2,0},{3,1},{4,6},{5,7},{6,4},{7,5},{8,10},{9,11},{10,... | collective-permute-start | bytes 49160 | tf_op jit(solution)/shard_map/ppermute | solution.py:334
  48.4 9.1 %collective-permute-start.10 = (f32[16,256]{1,0:T(8,128)S(1)}, f32[16,256]{1,0:T(8,128)S(1)}, u32[]{:S(2)}, u32[]{:S(2)}) collective-permute-start(f32[16,256]{1,0:T(8,128)S(1)} %get-tuple-element.59), channel_id=1, source_target_pairs={{0,1},{1,2},{2,3},{3,0},{4,5},{5,6},{6,7},{7,4},{8,9},{9,10},{10,1... | collective-permute-start | bytes 49160 | tf_op jit(solution)/shard_map/ppermute | solution.py:334
  49.4 8.1 %collective-permute-start.11 = (f32[16,256]{1,0:T(8,128)S(1)}, f32[16,256]{1,0:T(8,128)S(1)}, u32[]{:S(2)}, u32[]{:S(2)}) collective-permute-start(f32[16,256]{1,0:T(8,128)S(1)} %get-tuple-element.60), channel_id=1, source_target_pairs={{0,3},{1,0},{2,1},{3,2},{4,7},{5,4},{6,5},{7,6},{8,11},{9,8},{10,9... | collective-permute-start | bytes 49160 | tf_op jit(solution)/shard_map/ppermute | solution.py:334
  61.2 7.8 %collective-permute-start.12 = (f32[136,256]{1,0:T(8,128)S(1)}, f32[136,256]{1,0:T(8,128)S(1)}, u32[]{:S(2)}, u32[]{:S(2)}) collective-permute-start(f32[136,256]{1,0:T(8,128)S(1)} %get-tuple-element.61.t0), channel_id=1, source_target_pairs={{0,1},{1,2},{2,3},{3,0},{4,5},{5,6},{6,7},{7,4},{8,9},{9,10},{10,1... | collective-permute-start | bytes 417800 | tf_op jit(solution)/shard_map/ppermute | solution.py:334
  62.4 6.6 %collective-permute-start.15 = (f32[136,256]{1,0:T(8,128)S(1)}, f32[136,256]{1,0:T(8,128)S(1)}, u32[]{:S(2)}, u32[]{:S(2)}) collective-permute-start(f32[136,256]{1,0:T(8,128)S(1)} %get-tuple-element.62.l0), channel_id=1, source_target_pairs={{0,3},{1,0},{2,1},{3,2},{4,7},{5,4},{6,5},{7,6},{8,11},{9,8},{10,9... | collective-permute-start | bytes 417800 | tf_op jit(solution)/shard_map/ppermute | solution.py:334
  64.5 7.8 %collective-permute-start.17 = (f32[136,256]{1,0:T(8,128)S(1)}, f32[136,256]{1,0:T(8,128)S(1)}, u32[]{:S(2)}, u32[]{:S(2)}) collective-permute-start(f32[136,256]{1,0:T(8,128)S(1)} %get-tuple-element.61.t0), channel_id=1, source_target_pairs={{0,3},{1,0},{2,1},{3,2},{4,7},{5,4},{6,5},{7,6},{8,11},{9,8},{10,9... | collective-permute-start | bytes 417800 | tf_op jit(solution)/shard_map/ppermute | solution.py:334
  65.9 6.4 %collective-permute-start.13 = (f32[136,256]{1,0:T(8,128)S(1)}, f32[136,256]{1,0:T(8,128)S(1)}, u32[]{:S(2)}, u32[]{:S(2)}) collective-permute-start(f32[136,256]{1,0:T(8,128)S(1)} %get-tuple-element.62.l0), channel_id=1, source_target_pairs={{0,1},{1,2},{2,3},{3,0},{4,5},{5,6},{6,7},{7,4},{8,9},{9,10},{10,1... | collective-permute-start | bytes 417800 | tf_op jit(solution)/shard_map/ppermute | solution.py:334
  69.1 6.3 %collective-permute-start.14 = (f32[136,256]{1,0:T(8,128)S(1)}, f32[136,256]{1,0:T(8,128)S(1)}, u32[]{:S(2)}, u32[]{:S(2)}) collective-permute-start(f32[136,256]{1,0:T(8,128)S(1)} %collective-permute-done.12.t1), channel_id=1, source_target_pairs={{0,1},{1,2},{2,3},{3,0},{4,5},{5,6},{6,7},{7,4},{8,9},{9,10},{10,1... | collective-permute-start | bytes 417800 | tf_op jit(solution)/shard_map/ppermute | solution.py:334
  69.1 6.3 %collective-permute-start.16 = (f32[136,256]{1,0:T(8,128)S(1)}, f32[136,256]{1,0:T(8,128)S(1)}, u32[]{:S(2)}, u32[]{:S(2)}) collective-permute-start(f32[136,256]{1,0:T(8,128)S(1)} %collective-permute-done.15.l3), channel_id=1, source_target_pairs={{0,3},{1,0},{2,1},{3,2},{4,7},{5,4},{6,5},{7,6},{8,11},{9,8},{10,9... | collective-permute-start | bytes 417800 | tf_op jit(solution)/shard_map/ppermute | solution.py:334
  76.7 1.6 %collective-permute-start.18 = (f32[272,256]{1,0:T(8,128)S(1)}, f32[272,256]{1,0:T(8,128)S(1)}, u32[]{:S(2)}, u32[]{:S(2)}) collective-permute-start(f32[272,256]{1,0:T(8,128)S(1)} %get-tuple-element.63.own), channel_id=1, source_target_pairs={{0,4},{4,0},{8,12},{12,8},{16,20},{20,16},{24,28},{28,24},{32,36},... | collective-permute-start | bytes 835592 | tf_op jit(solution)/shard_map/ppermute | solution.py:403
  79.2 8.1 %collective-permute-start.21 = (f32[136,256]{1,0:T(8,128)S(1)}, f32[136,256]{1,0:T(8,128)S(1)}, u32[]{:S(2)}, u32[]{:S(2)}) collective-permute-start(f32[136,256]{1,0:T(8,128)S(1)} %get-tuple-element.66), channel_id=1, source_target_pairs={{0,16},{4,20},{8,24},{12,28},{16,0},{20,4},{24,8},{28,12},{32,48},... | collective-permute-start | bytes 417800 | tf_op jit(solution)/shard_map/ppermute | solution.py:408
  82.4 7.3 %collective-permute-start.20 = (f32[136,256]{1,0:T(8,128)S(1)}, f32[136,256]{1,0:T(8,128)S(1)}, u32[]{:S(2)}, u32[]{:S(2)}) collective-permute-start(f32[136,256]{1,0:T(8,128)S(1)} %get-tuple-element.66), channel_id=1, source_target_pairs={{0,8},{4,12},{8,16},{12,20},{16,24},{20,28},{24,0},{28,4},{32,40},... | collective-permute-start | bytes 417800 | tf_op jit(solution)/shard_map/ppermute | solution.py:408
  83.1 6.8 %collective-permute-start.19 = (f32[136,256]{1,0:T(8,128)S(1)}, f32[136,256]{1,0:T(8,128)S(1)}, u32[]{:S(2)}, u32[]{:S(2)}) collective-permute-start(f32[136,256]{1,0:T(8,128)S(1)} %get-tuple-element.66), channel_id=1, source_target_pairs={{0,24},{4,28},{8,0},{12,4},{16,8},{20,12},{24,16},{28,20},{32,56},... | collective-permute-start | bytes 417800 | tf_op jit(solution)/shard_map/ppermute | solution.py:408
  87.3 3.0 %collective-permute-start.24 = (f32[136,256]{1,0:T(8,128)S(1)}, f32[136,256]{1,0:T(8,128)S(1)}, u32[]{:S(2)}, u32[]{:S(2)}) collective-permute-start(f32[136,256]{1,0:T(8,128)S(1)} %collective-permute-done.21.h3), channel_id=1, source_target_pairs={{0,4},{4,0},{8,12},{12,8},{16,20},{20,16},{24,28},{28,24},{32,36},... | collective-permute-start | bytes 417800 | tf_op jit(solution)/shard_map/ppermute | solution.py:403
  89.9 1.4 %collective-permute-start.22 = (f32[136,256]{1,0:T(8,128)S(1)}, f32[136,256]{1,0:T(8,128)S(1)}, u32[]{:S(2)}, u32[]{:S(2)}) collective-permute-start(f32[136,256]{1,0:T(8,128)S(1)} %collective-permute-done.19.h1), channel_id=1, source_target_pairs={{0,4},{4,0},{8,12},{12,8},{16,20},{20,16},{24,28},{28,24},{32,36},... | collective-permute-start | bytes 417800 | tf_op jit(solution)/shard_map/ppermute | solution.py:403
  92.6 8.1 %collective-permute-start.27 = (f32[136,256]{1,0:T(8,128)S(1)}, f32[136,256]{1,0:T(8,128)S(1)}, u32[]{:S(2)}, u32[]{:S(2)}) collective-permute-start(f32[136,256]{1,0:T(8,128)S(1)} %get-tuple-element.67), channel_id=1, source_target_pairs={{0,64},{4,68},{8,72},{12,76},{16,80},{20,84},{24,88},{28,92},{32,9... | collective-permute-start | bytes 417800 | tf_op jit(solution)/shard_map/ppermute | solution.py:408
  94.1 6.8 %collective-permute-start.26 = (f32[136,256]{1,0:T(8,128)S(1)}, f32[136,256]{1,0:T(8,128)S(1)}, u32[]{:S(2)}, u32[]{:S(2)}) collective-permute-start(f32[136,256]{1,0:T(8,128)S(1)} %get-tuple-element.67), channel_id=1, source_target_pairs={{0,32},{4,36},{8,40},{12,44},{16,48},{20,52},{24,56},{28,60},{32,6... | collective-permute-start | bytes 417800 | tf_op jit(solution)/shard_map/ppermute | solution.py:408
  96.2 7.0 %collective-permute-start.25 = (f32[136,256]{1,0:T(8,128)S(1)}, f32[136,256]{1,0:T(8,128)S(1)}, u32[]{:S(2)}, u32[]{:S(2)}) collective-permute-start(f32[136,256]{1,0:T(8,128)S(1)} %get-tuple-element.67), channel_id=1, source_target_pairs={{0,96},{4,100},{8,104},{12,108},{16,112},{20,116},{24,120},{28,124... | collective-permute-start | bytes 417800 | tf_op jit(solution)/shard_map/ppermute | solution.py:408
  100.7 3.4 %collective-permute-start.30 = (f32[136,256]{1,0:T(8,128)S(1)}, f32[136,256]{1,0:T(8,128)S(1)}, u32[]{:S(2)}, u32[]{:S(2)}) collective-permute-start(f32[136,256]{1,0:T(8,128)S(1)} %collective-permute-done.27.h3), channel_id=1, source_target_pairs={{0,4},{4,0},{8,12},{12,8},{16,20},{20,16},{24,28},{28,24},{32,36},... | collective-permute-start | bytes 417800 | tf_op jit(solution)/shard_map/ppermute | solution.py:403
  100.8 3.2 %collective-permute-start.29 = (f32[136,256]{1,0:T(8,128)S(1)}, f32[136,256]{1,0:T(8,128)S(1)}, u32[]{:S(2)}, u32[]{:S(2)}) collective-permute-start(f32[136,256]{1,0:T(8,128)S(1)} %collective-permute-done.26.h2), channel_id=1, source_target_pairs={{0,4},{4,0},{8,12},{12,8},{16,20},{20,16},{24,28},{28,24},{32,36},... | collective-permute-start | bytes 417800 | tf_op jit(solution)/shard_map/ppermute | solution.py:403
  106.8 5.2 %collective-permute-start.31 = (f32[16,64]{1,0:T(8,128)S(1)}, f32[16,64]{1,0:T(8,128)S(1)}, u32[]{:S(2)}, u32[]{:S(2)}) collective-permute-start(f32[16,64]{1,0:T(8,128)S(1)} %get-tuple-element.72), channel_id=1, source_target_pairs={{0,2},{1,3},{2,0},{3,1},{4,6},{5,7},{6,4},{7,5},{8,10},{9,11},{10,... | collective-permute-start | bytes 12296 | tf_op jit(solution)/shard_map/ppermute | solution.py:334
  108.3 4.9 %collective-permute-start.32 = (f32[16,64]{1,0:T(8,128)S(1)}, f32[16,64]{1,0:T(8,128)S(1)}, u32[]{:S(2)}, u32[]{:S(2)}) collective-permute-start(f32[16,64]{1,0:T(8,128)S(1)} %get-tuple-element.73), channel_id=1, source_target_pairs={{0,1},{1,2},{2,3},{3,0},{4,5},{5,6},{6,7},{7,4},{8,9},{9,10},{10,1... | collective-permute-start | bytes 12296 | tf_op jit(solution)/shard_map/ppermute | solution.py:334
  111.2 3.7 %collective-permute-start.33 = (f32[16,64]{1,0:T(8,128)S(1)}, f32[16,64]{1,0:T(8,128)S(1)}, u32[]{:S(2)}, u32[]{:S(2)}) collective-permute-start(f32[16,64]{1,0:T(8,128)S(1)} %get-tuple-element.74), channel_id=1, source_target_pairs={{0,3},{1,0},{2,1},{3,2},{4,7},{5,4},{6,5},{7,6},{8,11},{9,8},{10,9... | collective-permute-start | bytes 12296 | tf_op jit(solution)/shard_map/ppermute | solution.py:334
  (6 other events, 89.7 us)
